TPU v7x, 32 devices: a whole 2x2x4 slice. The times are simulated.
32 devices in a mesh: dp: 16 (over z, x, core), tensor: 2 (over y).
Axes of the slice: x: 2, y: 2, z: 4, core: 2. Of those that a mesh axis runs over, the one named last changes fastest.
Arguments:
- block_input: bfloat16 [2, 64, 197, 768], P(None, 'dp'), may hold values from -6 to 6
- norm_gain: float32 [2, 2, 768], replicated, may hold values from 0.5 to 1.5
- row_bias: float32 [2, 3, 768], replicated, may hold values from -2 to 2
- qkv_weight: bfloat16 [2, 768, 3, 768], P(None, 'dp', None, 'tensor'), may hold values from -0.21875 to 0.21875
- qkv_bias: float32 [2, 2, 768], P(None, None, 'tensor'), may hold values from -2 to 2
- out_weight: bfloat16 [2, 768, 768], P(None, 'dp', 'tensor'), may hold values from -1.25 to 1.25
- mlp_in: bfloat16 [768, 3072], P('dp', 'tensor'), may hold values from -0.21875 to 0.21875
- mlp_in_bias: float32 [3072], P('tensor'), may hold values from -2 to 2
- mlp_out: bfloat16 [768, 3072], P('dp', 'tensor'), may hold values from -0.15625 to 0.15625
- mlp_out_bias: float32 [768], replicated, may hold values from -2 to 2
- router: float32 [768, 4], replicated, may hold values from -0.2 to 0.2
- expert_in: bfloat16 [768, 4, 3072], P('dp', None, 'tensor'), may hold values from -0.21875 to 0.21875
- expert_in_bias: float32 [4, 3072], P(None, 'tensor'), may hold values from -1.5 to 1.5
- expert_out: bfloat16 [768, 4, 3072], P('dp', None, 'tensor'), may hold values from -0.21875 to 0.21875
- expert_out_bias: float32 [4, 768], replicated, may hold values from -1.5 to 1.5
- routes: int32 [2, 64, 197, 2], P(None, 'dp'), may hold values from 0 to 3, as said below
- slot_index: int32 [2, 64, 197, 2], P(None, 'dp'), may hold values from 0 to 393, as said below
- out_grad: bfloat16 [2, 64, 197, 768], P(None, 'dp'), may hold values from -6 to 6
Outputs:
- block_output: bfloat16 [2, 64, 197, 768], P(None, 'dp')
- input_grad: float32 [2, 64, 197, 768], P(None, 'dp')
- norm_gain_grad: float32 [2, 2, 768], replicated
- row_bias_grad: float32 [2, 3, 768], replicated
- qkv_weight_grad: float32 [2, 768, 3, 768], P(None, 'dp', None, 'tensor')
- qkv_bias_grad: float32 [2, 2, 768], P(None, None, 'tensor')
- out_weight_grad: float32 [2, 768, 768], P(None, 'dp', 'tensor')
- mlp_in_grad: float32 [768, 3072], P('dp', 'tensor')
- mlp_in_bias_grad: float32 [3072], P('tensor')
- mlp_out_grad: float32 [768, 3072], P('dp', 'tensor')
- mlp_out_bias_grad: float32 [768], replicated
- router_grad: float32 [768, 4], replicated
- expert_in_grad: float32 [768, 4, 3072], P('dp', None, 'tensor')
- expert_in_bias_grad: float32 [4, 3072], P(None, 'tensor')
- expert_out_grad: float32 [768, 4, 3072], P('dp', None, 'tensor')
- expert_out_bias_grad: float32 [4, 768], replicated
Inputs may be any that keep to these rules, and one draw needn't show every extreme that they name: `routes`: in each micro-batch, the 4 images of each index of dp name every expert exactly 394 times, and a token's two experts differ. `slot_index`: in each micro-batch and each index of dp, the routes to one expert carry the slot numbers 0 to 393, each once.
All inputs are finite; a program needn't handle non-finite values.
Results may differ from a plain program's by a relative error of at most 0.018.
Values may be sent and summed in bfloat16 or wider, within the bound.
No kernel may reach another device: no remote copies, remote signals or barrier semaphores. Data moves between devices by JAX's collectives and lax.ppermute only.
A program may use at most 448 MiB of HBM per device.

v0:
```python
import jax
import jax.numpy as jnp
from jax import lax
from jax.sharding import PartitionSpec as P

HD = 64
CAP = 295


NORM_EPS = 1e-06
EXACT = lax.Precision.HIGHEST


def layer_norm(hidden, norm_gain, norm_shift):
    center = jnp.mean(hidden, axis=-1, keepdims=True)
    centred = hidden - center
    spread = jnp.mean(centred * centred, axis=-1, keepdims=True)
    return centred * lax.rsqrt(spread + NORM_EPS) * norm_gain + norm_shift


def norm_back(hidden, norm_gain, norm_shift, incoming):
    _, pullback = jax.vjp(layer_norm, hidden, norm_gain, norm_shift)
    return pullback(incoming)


def gelu_back(preact, incoming):
    _, pullback = jax.vjp(jax.nn.gelu, preact)
    return pullback(incoming)[0]


def fetch_first(parts):
    return (
        lax.all_gather(parts[0], "dp", axis=0, tiled=True),
        lax.all_gather(parts[1], "dp", axis=0, tiled=True),
        lax.all_gather(parts[2], "dp", axis=0, tiled=True),
        lax.all_gather(parts[3], "dp", axis=0, tiled=True),
    )


def fetch_second(parts):
    return (
        lax.all_gather(parts[0], "dp", axis=0, tiled=True),
        lax.all_gather(parts[1], "dp", axis=0, tiled=True),
        lax.all_gather(parts[2], "dp", axis=0, tiled=True),
        lax.all_gather(parts[3], "dp", axis=0, tiled=True),
    )


def branch_total(partial_value):
    return lax.psum(partial_value, "tensor")


def input_total(partial_value):
    return lax.psum(partial_value.astype(jnp.bfloat16), "tensor").astype(jnp.float32)


def scatter_first(grads):
    return (
        lax.psum_scatter(grads[0], "dp", scatter_dimension=0, tiled=True),
        lax.psum_scatter(grads[1], "dp", scatter_dimension=0, tiled=True),
        lax.psum_scatter(grads[2], "dp", scatter_dimension=0, tiled=True),
        lax.psum_scatter(grads[3], "dp", scatter_dimension=0, tiled=True),
    )


def scatter_second(grads):
    return (
        lax.psum_scatter(grads[0], "dp", scatter_dimension=0, tiled=True),
        lax.psum_scatter(grads[1], "dp", scatter_dimension=0, tiled=True),
        lax.psum_scatter(grads[2], "dp", scatter_dimension=0, tiled=True),
        lax.psum_scatter(grads[3], "dp", scatter_dimension=0, tiled=True),
    )


def add_grads(left, right):
    return tuple((first_term + second_term for first_term, second_term in zip(left, right)))


def attention_forward(
    hidden, norm_gain, norm_shift, qkv_weights, qkv_biases, out_matrix, out_biases, images
):
    normed = layer_norm(hidden, norm_gain, norm_shift)
    normed_low = normed.astype(jnp.bfloat16)
    projected = jnp.einsum(
        "td,dkf->tkf", normed_low, qkv_weights, preferred_element_type=jnp.float32
    )
    queries = (projected[:, 0] + qkv_biases[0]).astype(jnp.bfloat16)
    key_rows = projected[:, 1].astype(jnp.bfloat16)
    values = (projected[:, 2] + qkv_biases[1]).astype(jnp.bfloat16)
    local_heads = qkv_weights.shape[2] // HD
    head_shape = (images, -1, local_heads, HD)
    scores = jnp.einsum(
        "bqhe,bkhe->bhqk",
        queries.reshape(head_shape),
        key_rows.reshape(head_shape),
        preferred_element_type=jnp.float32,
    ) * HD ** (-0.5)
    row_max = jnp.max(scores, axis=-1, keepdims=True)
    weights = jnp.exp(scores - row_max)
    row_total = jnp.sum(weights, axis=-1, keepdims=True)
    attn_probs = (weights / row_total).astype(jnp.bfloat16)
    mixed_rows = jnp.einsum(
        "bhqk,bkhe->bqhe",
        attn_probs,
        values.reshape(head_shape),
        preferred_element_type=jnp.float32,
    )
    mixed_low = mixed_rows.reshape(hidden.shape[0], -1).astype(jnp.bfloat16)
    partial_value = jnp.einsum(
        "tf,of->to", mixed_low, out_matrix, preferred_element_type=jnp.float32
    )
    branch = branch_total(partial_value) + out_biases
    stored = (normed_low, queries, key_rows, values, row_max + jnp.log(row_total), mixed_low)
    return (hidden + branch, stored)


def attention_back(
    hidden, norm_gain, norm_shift, qkv_weights, out_matrix, stored, incoming, images
):
    normed_low, queries, key_rows, values, log_total, mixed_low = stored
    token_count = hidden.shape[0]
    grad_low = incoming.astype(jnp.bfloat16)
    out_bias_grad = jnp.sum(grad_low.astype(jnp.float32), axis=0)
    out_matrix_grad = jnp.einsum(
        "to,tf->of", grad_low, mixed_low, preferred_element_type=jnp.float32
    )
    mixed_grad = jnp.einsum(
        "to,of->tf", grad_low, out_matrix, preferred_element_type=jnp.float32
    ).astype(jnp.bfloat16)
    local_heads = qkv_weights.shape[2] // HD
    head_shape = (images, -1, local_heads, HD)
    query_heads = queries.reshape(head_shape)
    key_heads = key_rows.reshape(head_shape)
    value_heads = values.reshape(head_shape)
    mixed_heads = mixed_grad.reshape(head_shape)
    scores = jnp.einsum(
        "bqhe,bkhe->bhqk", query_heads, key_heads, preferred_element_type=jnp.float32
    ) * HD ** (-0.5)
    attn_probs = jnp.exp(scores - log_total)
    probs_grad = jnp.einsum(
        "bqhe,bkhe->bhqk", mixed_heads, value_heads, preferred_element_type=jnp.float32
    )
    score_grad = (
        attn_probs * (probs_grad - jnp.sum(attn_probs * probs_grad, axis=-1, keepdims=True))
    ).astype(jnp.bfloat16)
    query_grad = jnp.einsum(
        "bhqk,bkhe->bqhe", score_grad, key_heads, preferred_element_type=jnp.float32
    ) * HD ** (-0.5)
    key_grad = jnp.einsum(
        "bhqk,bqhe->bkhe", score_grad, query_heads, preferred_element_type=jnp.float32
    ) * HD ** (-0.5)
    value_grad = jnp.einsum(
        "bhqk,bqhe->bkhe",
        attn_probs.astype(jnp.bfloat16),
        mixed_heads,
        preferred_element_type=jnp.float32,
    )
    qkv_grad = jnp.stack(
        [
            query_grad.reshape(token_count, -1),
            key_grad.reshape(token_count, -1),
            value_grad.reshape(token_count, -1),
        ],
        axis=1,
    ).astype(jnp.bfloat16)
    column_sums = jnp.sum(qkv_grad.astype(jnp.float32), axis=0)
    qkv_bias_grad = jnp.stack([column_sums[0], column_sums[2]])
    qkv_matrix_grad = jnp.einsum(
        "td,tkf->dkf", normed_low, qkv_grad, preferred_element_type=jnp.float32
    )
    normed_grad = jnp.einsum(
        "tkf,dkf->td", qkv_grad, qkv_weights, preferred_element_type=jnp.float32
    )
    normed_grad = input_total(normed_grad)
    hidden_grad, gain_grad, shift_grad = norm_back(hidden, norm_gain, norm_shift, normed_grad)
    return (
        incoming + hidden_grad,
        (qkv_matrix_grad, out_matrix_grad, qkv_bias_grad, out_bias_grad, gain_grad, shift_grad),
    )


def dense_forward(hidden, norm_gain, norm_shift, in_matrix, in_biases, out_matrix, out_biases):
    normed_low = layer_norm(hidden, norm_gain, norm_shift).astype(jnp.bfloat16)
    preact = jnp.dot(normed_low, in_matrix, preferred_element_type=jnp.float32) + in_biases
    active = jax.nn.gelu(preact).astype(jnp.bfloat16)
    partial_value = jnp.einsum("tf,df->td", active, out_matrix, preferred_element_type=jnp.float32)
    return (hidden + branch_total(partial_value) + out_biases, (normed_low, preact, active))


def dense_back(hidden, norm_gain, norm_shift, in_matrix, out_matrix, stored, incoming):
    normed_low, preact, active = stored
    grad_low = incoming.astype(jnp.bfloat16)
    out_bias_grad = jnp.sum(grad_low.astype(jnp.float32), axis=0)
    out_matrix_grad = jnp.einsum("td,tf->df", grad_low, active, preferred_element_type=jnp.float32)
    active_grad = jnp.dot(grad_low, out_matrix, preferred_element_type=jnp.float32)
    preact_grad = gelu_back(preact, active_grad).astype(jnp.bfloat16)
    in_bias_grad = jnp.sum(preact_grad.astype(jnp.float32), axis=0)
    in_matrix_grad = jnp.einsum(
        "td,tf->df", normed_low, preact_grad, preferred_element_type=jnp.float32
    )
    normed_grad = jnp.einsum(
        "tf,df->td", preact_grad, in_matrix, preferred_element_type=jnp.float32
    )
    normed_grad = input_total(normed_grad)
    hidden_grad, gain_grad, shift_grad = norm_back(hidden, norm_gain, norm_shift, normed_grad)
    return (
        incoming + hidden_grad,
        (in_matrix_grad, out_matrix_grad, in_bias_grad, out_bias_grad, gain_grad, shift_grad),
    )


def dispatch_tables(route_ids, slot_ids, experts):
    token_count = route_ids.shape[0]
    kept_mask = slot_ids < CAP
    place_index = jnp.where(kept_mask, route_ids * CAP + slot_ids, experts * CAP)
    token_ids = jnp.broadcast_to(
        jnp.arange(token_count, dtype=jnp.int32)[:, None], (token_count, 2)
    )
    column_ids = jnp.broadcast_to(jnp.arange(2, dtype=jnp.int32)[None, :], (token_count, 2))
    owner_row = (
        jnp.zeros((experts * CAP,), jnp.int32)
        .at[place_index.reshape(-1)]
        .set(token_ids.reshape(-1), mode="drop")
    )
    column_pick = (
        jnp.zeros((experts * CAP,), jnp.int32)
        .at[place_index.reshape(-1)]
        .set(column_ids.reshape(-1), mode="drop")
    )
    safe_place = jnp.where(kept_mask, place_index, 0)
    return (kept_mask.astype(jnp.float32), owner_row, column_pick, safe_place)


def mixture_forward(
    hidden,
    norm_gain,
    norm_shift,
    router_matrix,
    in_matrix,
    in_biases,
    out_matrix,
    out_biases,
    route_ids,
    slot_ids,
):
    experts = router_matrix.shape[1]
    normed = layer_norm(hidden, norm_gain, norm_shift)
    normed_low = normed.astype(jnp.bfloat16)
    logits = jnp.dot(normed, router_matrix, precision=EXACT)
    logits = logits - jnp.max(logits, axis=-1, keepdims=True)
    weights = jnp.exp(logits)
    gate_probs = weights / jnp.sum(weights, axis=-1, keepdims=True)
    kept_float, owner_row, column_pick, safe_place = dispatch_tables(route_ids, slot_ids, experts)
    chosen = jnp.take_along_axis(gate_probs, route_ids, axis=1) * kept_float
    token_rows = normed_low[owner_row].reshape(experts, CAP, -1)
    preact = (
        jnp.einsum("ecd,def->ecf", token_rows, in_matrix, preferred_element_type=jnp.float32)
        + in_biases[:, None, :]
    )
    active = jax.nn.gelu(preact).astype(jnp.bfloat16)
    result = jnp.einsum(
        "ecf,def->ecd", active, out_matrix, preferred_element_type=jnp.float32
    ).reshape(experts * CAP, -1)
    partial_value = jnp.sum(chosen[:, :, None] * result[safe_place], axis=1)
    onehot = (route_ids[:, :, None] == jnp.arange(experts, dtype=jnp.int32)[None, None, :]).astype(
        jnp.float32
    )
    gate_matrix = jnp.sum(chosen[:, :, None] * onehot, axis=1)
    combined = branch_total(partial_value) + jnp.dot(gate_matrix, out_biases, precision=EXACT)
    stored = (
        normed,
        gate_probs,
        chosen,
        kept_float,
        owner_row,
        column_pick,
        safe_place,
        onehot,
        token_rows,
        preact,
        active,
        result,
    )
    return (hidden + combined, stored)


def mixture_back(
    hidden,
    norm_gain,
    norm_shift,
    router_matrix,
    in_matrix,
    out_matrix,
    out_biases,
    route_ids,
    stored,
    incoming,
):
    (
        normed,
        gate_probs,
        chosen,
        kept_float,
        owner_row,
        column_pick,
        safe_place,
        onehot,
        token_rows,
        preact,
        active,
        result,
    ) = stored
    experts = router_matrix.shape[1]
    gate_rows = chosen.reshape(-1)[owner_row * 2 + column_pick]
    result_grad = (
        (gate_rows[:, None] * incoming[owner_row]).astype(jnp.bfloat16).reshape(experts, CAP, -1)
    )
    out_bias_grad = jnp.sum(result_grad.astype(jnp.float32), axis=1)
    out_matrix_grad = jnp.einsum(
        "ecd,ecf->def", result_grad, active, preferred_element_type=jnp.float32
    )
    active_grad = jnp.einsum(
        "ecd,def->ecf", result_grad, out_matrix, preferred_element_type=jnp.float32
    )
    preact_grad = gelu_back(preact, active_grad).astype(jnp.bfloat16)
    in_bias_grad = jnp.sum(preact_grad.astype(jnp.float32), axis=1)
    in_matrix_grad = jnp.einsum(
        "ecd,ecf->def", token_rows, preact_grad, preferred_element_type=jnp.float32
    )
    rows_grad = jnp.einsum(
        "ecf,def->ecd", preact_grad, in_matrix, preferred_element_type=jnp.float32
    ).reshape(experts * CAP, -1)
    normed_part = jnp.sum(kept_float[:, :, None] * rows_grad[safe_place], axis=1)
    chosen_part = kept_float * jnp.sum(incoming[:, None, :] * result[safe_place], axis=2)
    normed_part, chosen_part = (
        lax.psum(normed_part.astype(jnp.bfloat16), "tensor").astype(jnp.float32),
        lax.psum(chosen_part.astype(jnp.bfloat16), "tensor").astype(jnp.float32),
    )
    bias_dots = jnp.take_along_axis(
        jnp.dot(incoming, out_biases.T, precision=EXACT), route_ids, axis=1
    )
    chosen_grad = chosen_part + kept_float * bias_dots
    probs_grad = jnp.sum(chosen_grad[:, :, None] * onehot, axis=1)
    logits_grad = gate_probs * (
        probs_grad - jnp.sum(gate_probs * probs_grad, axis=-1, keepdims=True)
    )
    router_grad = jnp.dot(normed.T, logits_grad, precision=EXACT)
    normed_grad = normed_part + jnp.dot(logits_grad, router_matrix.T, precision=EXACT)
    hidden_grad, gain_grad, shift_grad = norm_back(hidden, norm_gain, norm_shift, normed_grad)
    return (
        incoming + hidden_grad,
        (
            in_matrix_grad,
            out_matrix_grad,
            in_bias_grad,
            out_bias_grad,
            gain_grad,
            shift_grad,
            router_grad,
        ),
    )


def local(
    block_input,
    norm_gain,
    row_bias,
    qkv_weight,
    qkv_bias,
    out_weight,
    mlp_in,
    mlp_in_bias,
    mlp_out,
    mlp_out_bias,
    router,
    expert_in,
    expert_in_bias,
    expert_out,
    expert_out_bias,
    routes,
    slot_index,
    out_grad,
):
    micro_count, images, length, feature_width = block_input.shape
    token_count = images * length
    first_parts = (qkv_weight[0], out_weight[0], mlp_in, mlp_out)
    second_parts = (qkv_weight[1], out_weight[1], expert_in, expert_out)
    dp_count = lax.axis_size("dp")
    first_acc = tuple(
        (
            jnp.zeros((piece.shape[0] * dp_count,) + piece.shape[1:], jnp.float32)
            for piece in first_parts
        )
    )
    second_acc = tuple(
        (
            jnp.zeros((piece.shape[0] * dp_count,) + piece.shape[1:], jnp.float32)
            for piece in second_parts
        )
    )
    small_acc = tuple(
        (
            jnp.zeros(piece.shape, jnp.float32)
            for piece in (
                norm_gain,
                row_bias,
                qkv_bias,
                mlp_in_bias,
                mlp_out_bias,
                router,
                expert_in_bias,
                expert_out_bias,
            )
        )
    )
    results = []
    input_grads = []
    for micro_step in range(micro_count):
        layer_one = fetch_first(first_parts)
        hidden = block_input[micro_step].reshape(token_count, feature_width).astype(jnp.float32)
        after_one, stored_one = attention_forward(
            hidden,
            norm_gain[0, 0],
            row_bias[0, 0],
            layer_one[0],
            qkv_bias[0],
            layer_one[1],
            row_bias[0, 2],
            images,
        )
        after_ffn, stored_ffn = dense_forward(
            after_one,
            norm_gain[0, 1],
            row_bias[0, 1],
            layer_one[2],
            mlp_in_bias,
            layer_one[3],
            mlp_out_bias,
        )
        layer_two = fetch_second(second_parts)
        after_two, stored_two = attention_forward(
            after_ffn,
            norm_gain[1, 0],
            row_bias[1, 0],
            layer_two[0],
            qkv_bias[1],
            layer_two[1],
            row_bias[1, 2],
            images,
        )
        route_ids = routes[micro_step].reshape(token_count, 2)
        slot_ids = slot_index[micro_step].reshape(token_count, 2)
        layer_out, stored_moe = mixture_forward(
            after_two,
            norm_gain[1, 1],
            row_bias[1, 1],
            router,
            layer_two[2],
            expert_in_bias,
            layer_two[3],
            expert_out_bias,
            route_ids,
            slot_ids,
        )
        results.append(layer_out.astype(jnp.bfloat16).reshape(images, length, feature_width))
        incoming = out_grad[micro_step].reshape(token_count, feature_width).astype(jnp.float32)
        grad_two, moe_grads = mixture_back(
            after_two,
            norm_gain[1, 1],
            row_bias[1, 1],
            router,
            layer_two[2],
            layer_two[3],
            expert_out_bias,
            route_ids,
            stored_moe,
            incoming,
        )
        grad_ffn, att_two = attention_back(
            after_ffn,
            norm_gain[1, 0],
            row_bias[1, 0],
            layer_two[0],
            layer_two[1],
            stored_two,
            grad_two,
            images,
        )
        grad_one, ffn_grads = dense_back(
            after_one,
            norm_gain[0, 1],
            row_bias[0, 1],
            layer_one[2],
            layer_one[3],
            stored_ffn,
            grad_ffn,
        )
        grad_zero, att_one = attention_back(
            hidden,
            norm_gain[0, 0],
            row_bias[0, 0],
            layer_one[0],
            layer_one[1],
            stored_one,
            grad_one,
            images,
        )
        input_grads.append(grad_zero.reshape(images, length, feature_width))
        first_new = (att_one[0], att_one[1], ffn_grads[0], ffn_grads[1])
        second_new = (att_two[0], att_two[1], moe_grads[0], moe_grads[1])
        first_acc = add_grads(first_acc, first_new)
        second_acc = add_grads(second_acc, second_new)
        gain_new = jnp.stack(
            [jnp.stack([att_one[4], ffn_grads[4]]), jnp.stack([att_two[4], moe_grads[4]])]
        )
        shift_new = jnp.stack(
            [
                jnp.stack([att_one[5], ffn_grads[5], att_one[3]]),
                jnp.stack([att_two[5], moe_grads[5], att_two[3]]),
            ]
        )
        qkv_bias_new = jnp.stack([att_one[2], att_two[2]])
        small_new = (
            gain_new,
            shift_new,
            qkv_bias_new,
            ffn_grads[2],
            ffn_grads[3],
            moe_grads[6],
            moe_grads[2],
            moe_grads[3],
        )
        small_acc = add_grads(small_acc, small_new)
    first_done = scatter_first(first_acc)
    second_done = scatter_second(second_acc)
    (
        gain_sum,
        shift_sum,
        qkv_bias_sum,
        mlp_in_bias_sum,
        mlp_out_bias_sum,
        router_sum,
        expert_in_bias_sum,
        expert_out_bias_sum,
    ) = lax.psum(
        (
            small_acc[0],
            small_acc[1],
            small_acc[2],
            small_acc[3],
            small_acc[4],
            small_acc[5],
            small_acc[6],
            small_acc[7],
        ),
        "dp",
    )
    block_output = jnp.stack(results)
    input_grad = jnp.stack(input_grads)
    qkv_weight_grad = jnp.stack([first_done[0], second_done[0]])
    out_weight_grad = jnp.stack([first_done[1], second_done[1]])
    return (
        block_output,
        input_grad,
        gain_sum,
        shift_sum,
        qkv_weight_grad,
        qkv_bias_sum,
        out_weight_grad,
        first_done[2],
        mlp_in_bias_sum,
        first_done[3],
        mlp_out_bias_sum,
        router_sum,
        second_done[2],
        expert_in_bias_sum,
        second_done[3],
        expert_out_bias_sum,
    )


def solution(mesh):
    return jax.shard_map(
        local,
        mesh=mesh,
        in_specs=(
            P(None, "dp", None, None),
            P(),
            P(),
            P(None, "dp", None, "tensor"),
            P(None, None, "tensor"),
            P(None, "dp", "tensor"),
            P("dp", "tensor"),
            P("tensor"),
            P("dp", "tensor"),
            P(),
            P(),
            P("dp", None, "tensor"),
            P(None, "tensor"),
            P("dp", None, "tensor"),
            P(),
            P(None, "dp", None, None),
            P(None, "dp", None, None),
            P(None, "dp", None, None),
        ),
        out_specs=(
            P(None, "dp", None, None),
            P(None, "dp", None, None),
            P(),
            P(),
            P(None, "dp", None, "tensor"),
            P(None, None, "tensor"),
            P(None, "dp", "tensor"),
            P("dp", "tensor"),
            P("tensor"),
            P("dp", "tensor"),
            P(),
            P(),
            P("dp", None, "tensor"),
            P(None, "tensor"),
            P("dp", None, "tensor"),
            P(),
        ),
        check_vma=False,
    )
```

profile of v0, /device:TPU:0, one launch (start us, length us, event | category | flops | bytes accessed | tf_op | source)
XLA Modules:
  0.0 2848.2 jit_solution(7706571690532852692)
XLA Ops:
  36.6 26.5 all-gather.1
  118.8 13.3 copy.515
  149.4 118.9 %all-reduce.34.cloned.1.call-done = (f32[788,768]{1,0:T(8,128)}, f32[788,768]{1,0:T(8,128)}) async-done(((f32[788,768]{1,0:T(8,128)}, f32[788,768]{1,0:T(8,128)}), (f32[788,768]{1,0:T(8,128)}, f32[788,768]{1,0:T(8,128)})) %all-reduce.34.cloned.1.call-update) | async-done | bytes 4841488 | tf_op jit(solution)/shard_map/psum | solution.py:50
  274.4 38.9 %all-gather.11.cloned.1.call-done = bf16[768,1536]{1,0:T(8,128)(2,1)} async-done(((bf16[48,1536]{1,0:T(8,128)(2,1)}), bf16[768,1536]{1,0:T(8,128)(2,1)}) %all-gather.11.cloned.1.call-update) | async-done | bytes 2359312 | tf_op jit(solution)/shard_map/all_gather | solution.py:35
  325.0 31.6 %all-gather.13.cloned.1.call-done = bf16[768,1536]{1,0:T(8,128)(2,1)} async-done(((bf16[48,1536]{1,0:T(8,128)(2,1)}), bf16[768,1536]{1,0:T(8,128)(2,1)}) %all-gather.13.cloned.1.call-update) | async-done | bytes 2359312 | tf_op jit(solution)/shard_map/all_gather | solution.py:36
  369.9 22.4 all-gather.3
  392.3 98.5 %all-reduce.32.cloned.1.call-done = (f32[788,768]{1,0:T(8,128)}, f32[788,768]{1,0:T(8,128)}) async-done(((f32[788,768]{1,0:T(8,128)}, f32[788,768]{1,0:T(8,128)}), (f32[788,768]{1,0:T(8,128)}, f32[788,768]{1,0:T(8,128)})) %all-reduce.32.cloned.1.call-update) | async-done | bytes 4841488 | tf_op jit(solution)/shard_map/psum | solution.py:50
  496.9 37.4 %all-gather.21.cloned.1.call-done = bf16[1,768,3,384]{3,1,2,0:T(8,128)(2,1)} async-done(((bf16[1,48,3,384]{3,1,2,0:T(8,128)(2,1)}), bf16[1,768,3,384]{3,1,2,0:T(8,128)(2,1)}) %all-gather.21.cloned.1.call-update) | async-done | bytes 1769488 | tf_op jit(solution)/shard_map/all_gather | solution.py:42
  594.6 9.4 scatter_custom_fusion.3
  604.0 9.4 scatter_custom_fusion.1
  613.8 9.4 scatter_custom_fusion.2
  623.2 9.7 scatter_custom_fusion
  647.1 19.7 gather_fusion.13
  669.0 19.7 gather_fusion.12
  738.1 57.6 %all-gather.15.cloned.1.call-done = bf16[768,4,1536]{2,0,1:T(8,128)(2,1)} async-done(((bf16[48,4,1536]{2,0,1:T(8,128)(2,1)}), bf16[768,4,1536]{2,0,1:T(8,128)(2,1)}) %all-gather.15.cloned.1.call-update) | async-done | bytes 9437200 | tf_op jit(solution)/shard_map/all_gather | solution.py:44
  795.7 10.2 fusion.304
  805.9 71.7 %all-gather.17.cloned.1.call-done = bf16[768,4,1536]{2,0,1:T(8,128)(2,1)} async-done(((bf16[48,4,1536]{2,0,1:T(8,128)(2,1)}), bf16[768,4,1536]{2,0,1:T(8,128)(2,1)}) %all-gather.17.cloned.1.call-update) | async-done | bytes 9437200 | tf_op jit(solution)/shard_map/all_gather | solution.py:45
  877.6 11.4 fusion.273
  893.4 9.5 gather_fusion.3
  910.3 19.7 gather_fusion.11
  938.9 19.7 gather_fusion.10
  993.4 19.9 convert_reduce_fusion.1
  1028.0 9.5 gather_fusion.9
  1044.4 9.6 fusion.305
  1058.3 9.5 gather_fusion.6
  1075.2 9.4 multiply_reduce_fusion.5
  1084.6 9.6 multiply_reduce_fusion.7
  1094.3 12.2 fusion.272
  1106.5 13.6 multiply_reduce_fusion.4
  1124.4 9.5 gather_fusion.1
  1141.5 13.6 multiply_reduce_fusion.6
  1243.2 70.3 %all-reduce.40.cloned.1.call-done = (bf16[788,768]{1,0:T(8,128)(2,1)}, bf16[788,768]{1,0:T(8,128)(2,1)}) async-done(((bf16[788,768]{1,0:T(8,128)(2,1)}, bf16[788,768]{1,0:T(8,128)(2,1)}), (bf16[788,768]{1,0:T(8,128)(2,1)}, bf16[788,768]{1,0:T(8,128)(2,1)})) %all-reduce.40.cloned.1.call-update) | async-done | bytes 2420752 | tf_op jit(solution)/shard_map/psum | solution.py:54
  1342.2 70.0 %all-reduce.38.cloned.1.call-done = (bf16[788,768]{1,0:T(8,128)(2,1)}, bf16[788,768]{1,0:T(8,128)(2,1)}) async-done(((bf16[788,768]{1,0:T(8,128)(2,1)}, bf16[788,768]{1,0:T(8,128)(2,1)}), (bf16[788,768]{1,0:T(8,128)(2,1)}, bf16[788,768]{1,0:T(8,128)(2,1)})) %all-reduce.38.cloned.1.call-update) | async-done | bytes 2420752 | tf_op jit(solution)/shard_map/psum | solution.py:54
  1511.5 45.3 %all-reduce.36.cloned.1.call-done = (bf16[788,768]{1,0:T(8,128)(2,1)}, bf16[788,768]{1,0:T(8,128)(2,1)}) async-done(((bf16[788,768]{1,0:T(8,128)(2,1)}, bf16[788,768]{1,0:T(8,128)(2,1)}), (bf16[788,768]{1,0:T(8,128)(2,1)}, bf16[788,768]{1,0:T(8,128)(2,1)})) %all-reduce.36.cloned.1.call-update) | async-done | bytes 2420752 | tf_op jit(solution)/shard_map/psum | solution.py:54
  1574.1 11.5 fusion.312
  1592.8 14.5 add_bitcast_fusion.1
  1607.3 22.9 copy.639
  1630.2 12.1 fusion.271
  1642.3 16.1 add_bitcast_fusion
  1658.4 22.6 copy.640
  1725.9 18.7 reduce-scatter.13.cloned.1.call-done
  1744.5 61.2 %reduce-scatter.11.cloned.1.call-done = f32[48,384]{1,0:T(8,128)} async-done(((f32[768,384]{1,0:T(8,128)}), f32[48,384]{1,0:T(8,128)}) %reduce-scatter.11.cloned.1.call-update) | async-done | bytes 73744 | tf_op jit(solution)/shard_map/reduce_scatter | solution.py:60
  1827.0 70.1 %all-reduce.24.cloned.1.call-done = (f32[2,2,768]{2,1,0:T(2,128)}, f32[2,3,768]{2,1,0:T(4,128)}, f32[2,2,384]{2,1,0:T(2,128)}, f32[1536]{0:T(1024)}, f32[768]{0:...) async-done(((f32[2,2,768]{2,1,0:T(2,128)}, f32[2,3,768]{2,1,0:T(4,128)}, f32[2,2,384]{2,1,0:T(2,128)}, f32[1536]{0:T(1024)}, f32[768]{0:T(1024)}, ...) | async-done | bytes 95248 | tf_op jit(solution)/shard_map/psum | solution.py:545
  1898.5 73.3 %reduce-scatter.9.cloned.1.call-done = f32[48,3,384]{2,0,1:T(8,128)} async-done(((f32[768,3,384]{2,0,1:T(8,128)}), f32[48,3,384]{2,0,1:T(8,128)}) %reduce-scatter.9.cloned.1.call-update) | async-done | bytes 221200 | tf_op jit(solution)/shard_map/reduce_scatter | solution.py:68
  1971.7 70.8 %reduce-scatter.7.cloned.1.call-done = f32[48,3,384]{2,0,1:T(8,128)} async-done(((f32[768,3,384]{2,0,1:T(8,128)}), f32[48,3,384]{2,0,1:T(8,128)}) %reduce-scatter.7.cloned.1.call-update) | async-done | bytes 221200 | tf_op jit(solution)/shard_map/reduce_scatter | solution.py:59
  2044.4 632.6 %all-reduce.26.cloned.1.call-done = (f32[768,4,1536]{2,1,0:T(4,128)}, f32[768,4,1536]{2,1,0:T(4,128)}) async-done(((f32[768,4,1536]{2,1,0:T(4,128)}, f32[768,4,1536]{2,1,0:T(4,128)}), (f32[768,4,1536]{2,1,0:T(4,128)}, f32[768,4,1536]{2,1,0:T(4,128)})) %all-reduce.26.cloned.1.call-update) | async-done | bytes 37748752
  2681.7 75.8 %reduce-scatter.15.cloned.1.call-done = f32[48,1536]{1,0:T(8,128)} async-done(((f32[768,1536]{1,0:T(8,128)}), f32[48,1536]{1,0:T(8,128)}) %reduce-scatter.15.cloned.1.call-update) | async-done | bytes 294928 | tf_op jit(solution)/shard_map/reduce_scatter | solution.py:61
  2757.6 79.1 %reduce-scatter.17.cloned.1.call-done = f32[48,1536]{1,0:T(8,128)} async-done(((f32[768,1536]{1,0:T(8,128)}), f32[48,1536]{1,0:T(8,128)}) %reduce-scatter.17.cloned.1.call-update) | async-done | bytes 294928 | tf_op jit(solution)/shard_map/reduce_scatter | solution.py:62
  (1177 shorter events, 680.3 us)
Async XLA Ops:
  7.2 722.9 %copy-start = (f32[768,4]{0,1:T(4,128)S(1)}, f32[768,4]{0,1:T(4,128)}, u32[]{:S(2)}) copy-start(f32[768,4]{0,1:T(4,128)} %param.30) | copy-start | bytes 36868
  7.2 55.9 %all-gather.19.cloned.1.call-start = ((), (), s32[]{:S(2)}) async-start(), calls=%async_computation.16 | async-start | bytes 1880064 | tf_op jit(solution)/shard_map/all_gather | solution.py:33
  8.9 259.4 %all-reduce.34.cloned.1.call-start = ((), (), s32[]{:S(2)}) async-start(), calls=%async_computation.23 | async-start | bytes 9732096 | tf_op jit(solution)/shard_map/psum | solution.py:50
  16.5 251.8 %copy-start.34 = (f32[788,768]{1,0:T(8,128)}, f32[788,768]{1,0:T(8,128)S(1)}, u32[]{:S(2)}) copy-start(f32[788,768]{1,0:T(8,128)S(1)} %reshape.844) | copy-start | bytes 7262212
  35.9 284.6 %copy-start.235 = (f32[768]{0:T(1024)}, f32[768]{0:T(1024)S(1)}, u32[]{:S(2)}) copy-start(f32[768]{0:T(1024)S(1)} %get-tuple-element.140) | copy-start | bytes 9220
  35.9 505.0 %copy-start.217 = (f32[768]{0:T(1024)}, f32[768]{0:T(1024)S(1)}, u32[]{:S(2)}) copy-start(f32[768]{0:T(1024)S(1)} %get-tuple-element.142) | copy-start | bytes 9220
  36.6 283.9 %copy-start.311 = (f32[768]{0:T(1024)}, f32[768]{0:T(1024)S(1)}, u32[]{:S(2)}) copy-start(f32[768]{0:T(1024)S(1)} %get-tuple-element.135) | copy-start | bytes 9220
  36.6 504.4 %copy-start.315 = (f32[768]{0:T(1024)}, f32[768]{0:T(1024)S(1)}, u32[]{:S(2)}) copy-start(f32[768]{0:T(1024)S(1)} %get-tuple-element.134) | copy-start | bytes 9220
  148.0 165.3 %all-gather.11.cloned.1.call-start = ((), (), s32[]{:S(2)}) async-start(), calls=%async_computation.6 | async-start | bytes 2506752 | tf_op jit(solution)/shard_map/all_gather | solution.py:35
  148.8 207.8 %all-gather.13.cloned.1.call-start = ((), (), s32[]{:S(2)}) async-start(), calls=%async_computation.7 | async-start | bytes 2506752 | tf_op jit(solution)/shard_map/all_gather | solution.py:36
  149.4 341.5 %all-reduce.32.cloned.1.call-start = ((), (), s32[]{:S(2)}) async-start(), calls=%async_computation.22 | async-start | bytes 9732096 | tf_op jit(solution)/shard_map/psum | solution.py:50
  369.1 121.7 %copy-start.309 = (f32[768]{0:T(1024)S(1)}, f32[768]{0:T(1024)}, u32[]{:S(2)}) copy-start(f32[768]{0:T(1024)} %param.29) | copy-start | bytes 9220
  369.1 165.2 %all-gather.21.cloned.1.call-start = ((), (), s32[]{:S(2)}) async-start(), calls=%async_computation.17 | async-start | bytes 1880064 | tf_op jit(solution)/shard_map/all_gather | solution.py:42
  369.7 344.2 %all-reduce.30.cloned.1.call-start = ((), (), s32[]{:S(2)}) async-start(), calls=%async_computation.21 | async-start | bytes 9732096 | tf_op jit(solution)/shard_map/psum | solution.py:50
  589.8 206.0 %all-gather.15.cloned.1.call-start = ((), (), s32[]{:S(2)}) async-start(), calls=%async_computation.8 | async-start | bytes 10027008 | tf_op jit(solution)/shard_map/all_gather | solution.py:44
  591.7 285.9 %all-gather.17.cloned.1.call-start = ((), (), s32[]{:S(2)}) async-start(), calls=%async_computation.9 | async-start | bytes 10027008 | tf_op jit(solution)/shard_map/all_gather | solution.py:45
  592.8 570.4 %all-reduce.42.cloned.1.call-start = ((), (), s32[]{:S(2)}) async-start(), calls=%async_computation.27 | async-start | bytes 4866048 | tf_op jit(solution)/shard_map/psum | solution.py:336
  712.7 180.7 %copy-start.32 = (s32[2048]{0:T(1024)}, s32[2048]{0:T(1024)S(1)}, u32[]{:S(2)}) copy-start(s32[2048]{0:T(1024)S(1)} %get-tuple-element.329) | copy-start | bytes 24580
  734.4 175.8 %copy-start.168 = (f32[788,4]{0,1:T(4,128)}, f32[788,4]{0,1:T(4,128)S(1)}, u32[]{:S(2)}) copy-start(f32[788,4]{0,1:T(4,128)S(1)} %get-tuple-element.307) | copy-start | bytes 37828
  734.4 175.8 %copy-start.221 = (f32[788]{0:T(1024)}, f32[788]{0:T(1024)S(1)}, u32[]{:S(2)}) copy-start(f32[788]{0:T(1024)S(1)} %get-tuple-element.306) | copy-start | bytes 9460
  738.1 139.5 %copy-start.148 = (f32[4,1536]{1,0:T(4,128)S(1)}, f32[4,1536]{1,0:T(4,128)}, u32[]{:S(2)}) copy-start(f32[4,1536]{1,0:T(4,128)} %param.32) | copy-start | bytes 73732
  938.9 227.9 %copy-start.4 = (f32[788,4]{0,1:T(4,128)}, f32[788,4]{0,1:T(4,128)S(1)}, u32[]{:S(2)}) copy-start(f32[788,4]{0,1:T(4,128)S(1)} %fusion.211) | copy-start | bytes 37828
  1094.2 219.3 %all-reduce.40.cloned.1.call-start = ((), (), s32[]{:S(2)}) async-start(), calls=%async_computation.26 | async-start | bytes 4866048 | tf_op jit(solution)/shard_map/psum | solution.py:54
  1239.9 73.6 %copy-start.218 = (f32[768]{0:T(1024)S(1)}, f32[768]{0:T(1024)}, u32[]{:S(2)}) copy-start(f32[768]{0:T(1024)} %copy-done.217) | copy-start | bytes 9220
  1242.8 169.4 %all-reduce.38.cloned.1.call-start = ((), (), s32[]{:S(2)}) async-start(), calls=%async_computation.25 | async-start | bytes 4866048 | tf_op jit(solution)/shard_map/psum | solution.py:54
  1341.4 70.8 %copy-start.41 = (f32[788,768]{1,0:T(8,128)S(1)}, f32[788,768]{1,0:T(8,128)}, u32[]{:S(2)}) copy-start(f32[788,768]{1,0:T(8,128)} %copy-done.40) | copy-start | bytes 7262212
  1341.4 70.8 %copy-start.212 = (f32[788]{0:T(1024)S(1)}, f32[788]{0:T(1024)}, u32[]{:S(2)}) copy-start(f32[788]{0:T(1024)} %copy-done.211) | copy-start | bytes 9460
  1341.4 70.8 %copy-start.215 = (f32[788]{0:T(1024)S(1)}, f32[788]{0:T(1024)}, u32[]{:S(2)}) copy-start(f32[788]{0:T(1024)} %copy-done.214) | copy-start | bytes 9460
  1341.4 215.3 %all-reduce.36.cloned.1.call-start = ((), (), s32[]{:S(2)}) async-start(), calls=%async_computation.24 | async-start | bytes 4866048 | tf_op jit(solution)/shard_map/psum | solution.py:54
  1486.0 222.0 %all-reduce.28.cloned.1.call-start = ((), (), s32[]{:S(2)}) async-start(), calls=%async_computation.20 | async-start | bytes 9732096 | tf_op jit(solution)/shard_map/psum | solution.py:50
  1486.7 257.9 %reduce-scatter.13.cloned.1.call-start = ((), (), s32[]{:S(2)}) async-start(), calls=%async_computation.13 | async-start | bytes 1253376 | tf_op jit(solution)/shard_map/reduce_scatter | solution.py:69
  1503.8 301.9 %reduce-scatter.11.cloned.1.call-start = ((), (), s32[]{:S(2)}) async-start(), calls=%async_computation.12 | async-start | bytes 1253376 | tf_op jit(solution)/shard_map/reduce_scatter | solution.py:60
  1510.6 386.5 %all-reduce.24.cloned.1.call-start = ((), (), s32[]{:S(2)}) async-start(), calls=%async_computation.18 | async-start | bytes 208896 | tf_op jit(solution)/shard_map/psum | solution.py:545
  1566.0 405.7 %reduce-scatter.9.cloned.1.call-start = ((), (), s32[]{:S(2)}) async-start(), calls=%async_computation.11 | async-start | bytes 3760128 | tf_op jit(solution)/shard_map/reduce_scatter | solution.py:68
  1573.7 468.9 %reduce-scatter.7.cloned.1.call-start = ((), (), s32[]{:S(2)}) async-start(), calls=%async_computation.10 | async-start | bytes 3760128 | tf_op jit(solution)/shard_map/reduce_scatter | solution.py:59
  1592.6 1084.5 %all-reduce.26.cloned.1.call-start = ((), (), s32[]{:S(2)}) async-start(), calls=%async_computation.19 | async-start | bytes 75497472
  1681.1 1076.5 %reduce-scatter.15.cloned.1.call-start = ((), (), s32[]{:S(2)}) async-start(), calls=%async_computation.14 | async-start | bytes 5013504 | tf_op jit(solution)/shard_map/reduce_scatter | solution.py:61
  1692.0 1144.6 %reduce-scatter.17.cloned.1.call-start = ((), (), s32[]{:S(2)}) async-start(), calls=%async_computation.15 | async-start | bytes 5013504 | tf_op jit(solution)/shard_map/reduce_scatter | solution.py:62
  1723.5 83.9 %copy-start.37 = (f32[788,768]{1,0:T(8,128)S(1)}, f32[788,768]{1,0:T(8,128)}, u32[]{:S(2)}) copy-start(f32[788,768]{1,0:T(8,128)} %copy-done.34) | copy-start | bytes 7262212
  1723.5 83.8 %copy-start.277 = (f32[788]{0:T(1024)S(1)}, f32[788]{0:T(1024)}, u32[]{:S(2)}) copy-start(f32[788]{0:T(1024)} %copy-done.276) | copy-start | bytes 9460
  1723.5 83.8 %copy-start.279 = (f32[788]{0:T(1024)S(1)}, f32[788]{0:T(1024)}, u32[]{:S(2)}) copy-start(f32[788]{0:T(1024)} %copy-done.278) | copy-start | bytes 9460
  2044.4 792.3 %copy-start.305 = (f32[2,2,768]{2,1,0:T(2,128)S(1)}, f32[2,2,768]{2,1,0:T(2,128)}, u32[]{:S(2)}) copy-start(f32[2,2,768]{2,1,0:T(2,128)} %get-tuple-element.333) | copy-start | bytes 36868
  2044.4 792.9 %copy-start.308 = (f32[2,2,384]{2,1,0:T(2,128)S(1)}, f32[2,2,384]{2,1,0:T(2,128)}, u32[]{:S(2)}) copy-start(f32[2,2,384]{2,1,0:T(2,128)} %get-tuple-element.336) | copy-start | bytes 18436
  2044.4 793.5 %copy-start.306 = (f32[1536]{0:T(1024)S(1)}, f32[1536]{0:T(1024)}, u32[]{:S(2)}) copy-start(f32[1536]{0:T(1024)} %get-tuple-element.339) | copy-start | bytes 18436
  2044.4 794.1 %copy-start.310 = (f32[768]{0:T(1024)S(1)}, f32[768]{0:T(1024)}, u32[]{:S(2)}) copy-start(f32[768]{0:T(1024)} %get-tuple-element.341) | copy-start | bytes 9220
  2044.4 794.7 %copy-start.304 = (f32[768,4]{0,1:T(4,128)S(1)}, f32[768,4]{0,1:T(4,128)}, u32[]{:S(2)}) copy-start(f32[768,4]{0,1:T(4,128)} %get-tuple-element.342) | copy-start | bytes 36868
  2044.4 795.2 %copy-start.290 = (f32[4,1536]{1,0:T(4,128)S(1)}, f32[4,1536]{1,0:T(4,128)}, u32[]{:S(2)}) copy-start(f32[4,1536]{1,0:T(4,128)} %get-tuple-element.344) | copy-start | bytes 73732
  2677.0 163.3 %copy-start.303 = (f32[4,768]{1,0:T(4,128)S(1)}, f32[4,768]{1,0:T(4,128)}, u32[]{:S(2)}) copy-start(f32[4,768]{1,0:T(4,128)} %get-tuple-element.346) | copy-start | bytes 36868
  (322 other events, 2947.5 us)
Sparse Core Ops, SparseCore 0:
  10.9 44.6 all-gather.18
  148.2 120.1 all-reduce.33
  270.6 42.6 all-gather.10
  315.4 41.0 all-gather.12
  369.2 121.5 all-reduce.31
  493.6 40.7 all-gather.20
  589.9 121.6 all-reduce.29
  713.9 81.8 all-gather.14
  798.0 79.5 all-gather.16
  1094.3 68.7 all-reduce.41
  1242.9 70.5 all-reduce.39
  1341.6 70.5 all-reduce.37
  1486.1 70.5 all-reduce.35
  1559.1 122.9 all-reduce.27
  1686.1 58.3 reduce-scatter.12
  1748.6 57.1 reduce-scatter.10
  1811.2 85.9 all-reduce.23
  1900.8 70.8 reduce-scatter.8
  1975.6 66.9 reduce-scatter.6
  2046.8 630.2 all-reduce.25
  2681.9 75.5 reduce-scatter.14
  2762.0 74.6 reduce-scatter.16
where the time goes:
time: 2860 us; the launch traced here: 2850 us
  waiting for transfers between devices  1730 us (60%)
  local copies, waits for them, and re-layouts  537 us (19%)
  matrix products  350 us (12%)
  other arithmetic  159 us (6%)
  blocking collectives  54.3 us (2%)
    unnamed x23, waiting for transfers between devices  635 us
    psum x4, waiting for transfers between devices, branch_total(): return lax.psum(partial_value, 'tensor')  217 us
    psum x3, waiting for transfers between devices, input_total(): lax.psum(partial_value.astype(jnp.bfloat16), 'tensor').astype(jnp.float32)  186 us
    reduce_scatter x1, waiting for transfers between devices, scatter_first(): lax.psum_scatter(grads[3], 'dp', scatter_dimension=0, tiled=True)  79.1 us
    reduce_scatter x1, waiting for transfers between devices, scatter_first(): lax.psum_scatter(grads[2], 'dp', scatter_dimension=0, tiled=True)  75.8 us
    reduce_scatter x1, waiting for transfers between devices, scatter_second(): lax.psum_scatter(grads[0], 'dp', scatter_dimension=0, tiled=True)  73.3 us
    all_gather x1, waiting for transfers between devices, fetch_second(): lax.all_gather(parts[3], 'dp', axis=0, tiled=True)  71.7 us
    reduce_scatter x1, waiting for transfers between devices, scatter_first(): lax.psum_scatter(grads[0], 'dp', scatter_dimension=0, tiled=True)  70.8 us
  transfers between devices with their start and end apart: 22, of which 19 were waited for; matrix products, arithmetic and copies ran while one was open for 17% of the time, Pallas kernels for 0%

commit v1 on v0

v1 whole, which is shorter than its diff:
```python
import functools

import jax
import jax.numpy as jnp
from jax import lax
from jax.experimental import pallas as pl
from jax.experimental.pallas import tpu as pltpu
from jax.sharding import PartitionSpec as P

HD = 64
CAP = 295
NORM_EPS = 1e-06
EXACT = lax.Precision.HIGHEST
BF = jnp.bfloat16
F32 = jnp.float32
VMEM_LIMIT = 58 * 1024 * 1024
FF_BLOCK = 512
ROW_PAD = 16
GELU_SLOPE = 0.7978845608028654
GELU_CUBE = 0.044715


def round_up(value, unit):
    return -(-value // unit) * unit


def mm(left, right):
    return jnp.dot(left, right, preferred_element_type=F32)


def mm_bt(left, right):
    return lax.dot_general(left, right, (((1,), (1,)), ((), ())), preferred_element_type=F32)


def mm_at(left, right):
    return lax.dot_general(left, right, (((0,), (0,)), ((), ())), preferred_element_type=F32)


def norm_parts(hidden):
    center = jnp.mean(hidden, axis=-1, keepdims=True)
    centred = hidden - center
    spread = jnp.mean(centred * centred, axis=-1, keepdims=True)
    scale = lax.rsqrt(spread + NORM_EPS)
    return centred * scale, scale


def norm_pull(unit, scale, gain, incoming):
    wide = incoming * gain
    mean_wide = jnp.mean(wide, axis=-1, keepdims=True)
    mean_dot = jnp.mean(wide * unit, axis=-1, keepdims=True)
    hidden_grad = scale * (wide - mean_wide - unit * mean_dot)
    gain_grad = jnp.sum(incoming * unit, axis=0, keepdims=True)
    shift_grad = jnp.sum(incoming, axis=0, keepdims=True)
    return hidden_grad, gain_grad, shift_grad


def gelu_pair(preact):
    square = preact * preact
    inner = GELU_SLOPE * preact * (1.0 + GELU_CUBE * square)
    bend = jnp.tanh(inner)
    half = 0.5 * (1.0 + bend)
    active = preact * half
    slope = half + 0.5 * preact * (1.0 - bend * bend) * (
        GELU_SLOPE * (1.0 + 3.0 * GELU_CUBE * square)
    )
    return active, slope


def gelu_value(preact):
    square = preact * preact
    inner = GELU_SLOPE * preact * (1.0 + GELU_CUBE * square)
    return 0.5 * preact * (1.0 + jnp.tanh(inner))


def call(kernel, grid, in_specs, out_specs, out_shape, scratch, flops, traffic, name):
    return pl.pallas_call(
        kernel,
        grid=grid,
        in_specs=in_specs,
        out_specs=out_specs,
        out_shape=out_shape,
        scratch_shapes=scratch,
        name=name,
        compiler_params=pltpu.CompilerParams(
            vmem_limit_bytes=VMEM_LIMIT,
            dimension_semantics=("arbitrary",) * len(grid),
        ),
        cost_estimate=pl.CostEstimate(
            flops=int(flops), bytes_accessed=int(traffic), transcendentals=0
        ),
    )


def whole(shape):
    zeros = (0,) * len(shape)
    return pl.BlockSpec(shape, lambda *_: zeros, pipeline_mode=pl.Buffered(1))


def rows_of(block, width):
    return pl.BlockSpec((block, width), lambda step: (step, 0))


def attn_fwd_kernel(
    length, pad, heads, router_on,
    h_ref, g_ref, b_ref, w_ref, qb_ref, ob_ref, *rest,
):
    if router_on:
        g2_ref, b2_ref, rt_ref, sel_ref = rest[:4]
        qkv_ref, lse_ref, o_ref, a_ref, rb_ref, gp_ref, wt_ref = rest[4:]
    else:
        qkv_ref, lse_ref, o_ref, a_ref = rest
    width = h_ref.shape[1]
    images = h_ref.shape[0] // pad
    hidden = h_ref[...]
    unit, _ = norm_parts(hidden)
    normed = (unit * g_ref[...] + b_ref[...]).astype(BF)
    for part in range(3):
        cols = slice(part * width, (part + 1) * width)
        qkv_ref[:, cols] = (mm(normed, w_ref[:, cols]) + qb_ref[:, cols]).astype(BF)
    pairs = heads // 2
    lane = lax.broadcasted_iota(jnp.int32, (pad, 2 * HD), 1)
    key_row = lax.broadcasted_iota(jnp.int32, (pad, pad), 0)

    def pair_step(step, carry):
        image = step // pairs
        pair = step % pairs
        rows = pl.ds(pl.multiple_of(image * pad, ROW_PAD), pad)

        def col(part):
            return pl.ds(pl.multiple_of(part * width + pair * 2 * HD, 2 * HD), 2 * HD)

        query = qkv_ref[rows, col(0)] * HD ** (-0.5)
        key = qkv_ref[rows, col(1)]
        value = qkv_ref[rows, col(2)]
        mixed = []
        for half in range(2):
            mine = (lane >= HD) if half else (lane < HD)
            scores = mm_bt(key, jnp.where(mine, query, 0).astype(BF))
            scores = jnp.where(key_row < length, scores, -1e30)
            top = jnp.max(scores, axis=0, keepdims=True)
            weights = jnp.exp(scores - top)
            total = jnp.sum(weights, axis=0, keepdims=True)
            probs = (weights * (1.0 / total)).astype(BF)
            mixed.append(mm_at(probs, value))
            lse_ref[image, pl.ds(pair * 2 + half, 1), :] = top + jnp.log(total)
        o_ref[rows, col(0)] = jnp.where(lane < HD, mixed[0], mixed[1]).astype(BF)
        return carry

    lax.fori_loop(0, images * pairs, pair_step, 0)
    after = hidden + mm_bt(o_ref[...], w_ref[:, 3 * width :]) + ob_ref[...]
    a_ref[...] = after
    if router_on:
        unit2, _ = norm_parts(after)
        normed2 = unit2 * g2_ref[...] + b2_ref[...]
        rb_ref[...] = normed2.astype(BF)
        logits = jnp.dot(normed2, rt_ref[...], precision=EXACT, preferred_element_type=F32)
        lanes = lax.broadcasted_iota(jnp.int32, logits.shape, 1)
        live = lanes < router_on
        logits = jnp.where(live, logits, -1e30)
        gates = jnp.exp(logits - jnp.max(logits, axis=-1, keepdims=True))
        gates = gates / jnp.sum(gates, axis=-1, keepdims=True)
        gates = jnp.where(live, gates, 0.0)
        gp_ref[...] = gates
        first = jnp.sum(jnp.where(lanes == sel_ref[:, 0:1], gates, 0.0), axis=-1, keepdims=True)
        second = jnp.sum(jnp.where(lanes == sel_ref[:, 1:2], gates, 0.0), axis=-1, keepdims=True)
        wt_ref[...] = jnp.where(lanes == 0, first, jnp.where(lanes == 1, second, 0.0))


def attention_forward(hidden, gain, shift, weights, qkv_bias, out_bias, length, pad, router=None):
    rows, width = hidden.shape
    heads = width // HD
    block = rows // 2
    lse_rows = round_up(heads, 8)
    images = block // pad
    in_specs = [
        rows_of(block, width), whole((1, width)), whole((1, width)), whole((width, 4 * width)),
        whole((1, 3 * width)), whole((1, width)),
    ]
    args = [hidden, gain, shift, weights, qkv_bias, out_bias]
    out_specs = [
        rows_of(block, 3 * width),
        pl.BlockSpec((images, lse_rows, pad), lambda step: (step, 0, 0)),
        rows_of(block, width),
        rows_of(block, width),
    ]
    out_shape = [
        jax.ShapeDtypeStruct((rows, 3 * width), BF),
        jax.ShapeDtypeStruct((2 * images, lse_rows, pad), F32),
        jax.ShapeDtypeStruct((rows, width), BF),
        jax.ShapeDtypeStruct((rows, width), F32),
    ]
    router_on = 0
    if router is not None:
        gain2, shift2, router_wide, select, router_on = router
        lanes = router_wide.shape[1]
        in_specs += [whole((1, width)), whole((1, width)), whole((width, lanes)), rows_of(block, 2)]
        args += [gain2, shift2, router_wide, select]
        out_specs += [rows_of(block, width), rows_of(block, lanes), rows_of(block, lanes)]
        out_shape += [
            jax.ShapeDtypeStruct((rows, width), BF),
            jax.ShapeDtypeStruct((rows, lanes), F32),
            jax.ShapeDtypeStruct((rows, lanes), F32),
        ]
    return call(
        functools.partial(attn_fwd_kernel, length, pad, heads, router_on),
        (2,), in_specs, out_specs, out_shape, [],
        8.0 * rows * width * width + 16.0 * rows * pad * width, 12.0e6, "attn_fwd",
    )(*args)


def attn_bwd_kernel(
    length, pad, heads,
    da_ref, h_ref, g_ref, b_ref, w_ref, qkv_ref, lse_ref, o_ref,
    dh_ref, dwq_ref, dwo_ref, dqb_ref, dob_ref, dg_ref, db_ref,
    grad_sc, dqkv_sc, wq_acc, wo_acc,
):
    step_id = pl.program_id(0)
    last = pl.num_programs(0) - 1
    width = h_ref.shape[1]
    images = h_ref.shape[0] // pad
    pairs = heads // 2
    incoming = da_ref[...]
    low = incoming.astype(BF)
    out_bias_grad = jnp.sum(low.astype(F32), axis=0, keepdims=True)
    out_grad_part = mm_at(low, o_ref[...])
    grad_sc[...] = mm(low, w_ref[:, 3 * width :]).astype(BF)
    lane = lax.broadcasted_iota(jnp.int32, (pad, 2 * HD), 1)
    key_row = lax.broadcasted_iota(jnp.int32, (pad, pad), 0)

    def pair_step(step, carry):
        image = step // pairs
        pair = step % pairs
        rows = pl.ds(pl.multiple_of(image * pad, ROW_PAD), pad)

        def col(part):
            return pl.ds(pl.multiple_of(part * width + pair * 2 * HD, 2 * HD), 2 * HD)

        query = (qkv_ref[rows, col(0)] * HD ** (-0.5)).astype(BF)
        key = qkv_ref[rows, col(1)]
        value = qkv_ref[rows, col(2)]
        mixed = grad_sc[rows, col(0)]
        parts = []
        for half in range(2):
            mine = (lane >= HD) if half else (lane < HD)
            scores = mm_bt(key, jnp.where(mine, query, 0).astype(BF))
            total = lse_ref[image, pl.ds(pair * 2 + half, 1), :]
            probs = jnp.where(key_row < length, jnp.exp(scores - total), 0.0)
            probs_grad = mm_bt(value, jnp.where(mine, mixed, 0).astype(BF))
            product = probs * probs_grad
            delta = jnp.sum(product, axis=0, keepdims=True)
            score_grad = (product - probs * delta).astype(BF)
            parts.append((
                mm_at(score_grad, key) * HD ** (-0.5),
                mm(score_grad, query),
                mm(probs.astype(BF), mixed),
            ))
        for part in range(3):
            dqkv_sc[rows, col(part)] = jnp.where(
                lane < HD, parts[0][part], parts[1][part]
            ).astype(BF)
        return carry

    lax.fori_loop(0, images * pairs, pair_step, 0)
    unit, scale = norm_parts(h_ref[...])
    normed = (unit * g_ref[...] + b_ref[...]).astype(BF)
    normed_grad = None
    bias_parts = []
    first = step_id == 0
    for part in range(3):
        cols = slice(part * width, (part + 1) * width)
        grads = dqkv_sc[:, cols]
        term = mm_bt(grads, w_ref[:, cols])
        normed_grad = term if normed_grad is None else normed_grad + term
        piece = mm_at(normed, grads)
        bias_parts.append(jnp.sum(grads.astype(F32), axis=0, keepdims=True))

        @pl.when(first)
        def _():
            wq_acc[:, cols] = piece

        @pl.when(step_id == last)
        def _():
            dwq_ref[:, cols] = (wq_acc[:, cols] + piece).astype(BF)

    hidden_grad, gain_grad, shift_grad = norm_pull(unit, scale, g_ref[...], normed_grad)
    dh_ref[...] = incoming + hidden_grad

    @pl.when(first)
    def _():
        wo_acc[...] = out_grad_part
        dob_ref[...] = out_bias_grad
        dg_ref[...] = gain_grad
        db_ref[...] = shift_grad
        for part in range(3):
            dqb_ref[:, part * width : (part + 1) * width] = bias_parts[part]

    @pl.when(step_id == last)
    def _():
        dwo_ref[...] = (wo_acc[...] + out_grad_part).astype(BF)
        dob_ref[...] += out_bias_grad
        dg_ref[...] += gain_grad
        db_ref[...] += shift_grad
        for part in range(3):
            dqb_ref[:, part * width : (part + 1) * width] += bias_parts[part]


def attention_back(incoming, hidden, gain, shift, weights, stored, length, pad):
    qkv, lse, mixed = stored
    rows, width = hidden.shape
    heads = width // HD
    block = rows // 2
    images = block // pad
    lse_rows = lse.shape[1]
    return call(
        functools.partial(attn_bwd_kernel, length, pad, heads),
        (2,),
        [
            rows_of(block, width), rows_of(block, width), whole((1, width)), whole((1, width)),
            whole((width, 4 * width)), rows_of(block, 3 * width),
            pl.BlockSpec((images, lse_rows, pad), lambda step: (step, 0, 0)),
            rows_of(block, width),
        ],
        [
            rows_of(block, width), whole((width, 3 * width)), whole((width, width)),
            whole((1, 3 * width)), whole((1, width)), whole((1, width)), whole((1, width)),
        ],
        [
            jax.ShapeDtypeStruct((rows, width), F32),
            jax.ShapeDtypeStruct((width, 3 * width), BF),
            jax.ShapeDtypeStruct((width, width), BF),
            jax.ShapeDtypeStruct((1, 3 * width), F32),
            jax.ShapeDtypeStruct((1, width), F32),
            jax.ShapeDtypeStruct((1, width), F32),
            jax.ShapeDtypeStruct((1, width), F32),
        ],
        [
            pltpu.VMEM((block, width), BF),
            pltpu.VMEM((block, 3 * width), BF),
            pltpu.VMEM((width, 3 * width), F32),
            pltpu.VMEM((width, width), F32),
        ],
        16.0 * rows * width * width + 40.0 * rows * pad * width, 25.0e6, "attn_bwd",
    )(incoming, hidden, gain, shift, weights, qkv, lse, mixed)


def dense_fwd_kernel(a_ref, g_ref, b_ref, win_ref, wout_ref, bin_ref, bout_ref, x_ref, m_sc, acc):
    step = pl.program_id(0)

    @pl.when(step == 0)
    def _():
        unit, _ = norm_parts(a_ref[...])
        m_sc[...] = (unit * g_ref[...] + b_ref[...]).astype(BF)
        acc[...] = a_ref[...] + bout_ref[...]

    preact = mm(m_sc[...], win_ref[...]) + bin_ref[...]
    active = gelu_value(preact).astype(BF)
    acc[...] += mm_bt(active, wout_ref[...])

    @pl.when(step == pl.num_programs(0) - 1)
    def _():
        x_ref[...] = acc[...]


def dense_forward(hidden, gain, shift, weights, in_bias, out_bias):
    rows, width = hidden.shape
    ff = in_bias.shape[1]
    steps = ff // FF_BLOCK
    return call(
        dense_fwd_kernel, (steps,),
        [
            whole((rows, width)), whole((1, width)), whole((1, width)),
            pl.BlockSpec((width, FF_BLOCK), lambda c: (0, c)),
            pl.BlockSpec((width, FF_BLOCK), lambda c: (0, steps + c)),
            pl.BlockSpec((1, FF_BLOCK), lambda c: (0, c)),
            whole((1, width)),
        ],
        whole((rows, width)),
        jax.ShapeDtypeStruct((rows, width), F32),
        [pltpu.VMEM((rows, width), BF), pltpu.VMEM((rows, width), F32)],
        4.0 * rows * width * ff, 15.0e6, "dense_fwd",
    )(hidden, gain, shift, weights, weights, in_bias, out_bias)


def dense_bwd_kernel(
    dx_ref, a_ref, g_ref, b_ref, win_ref, wout_ref, bin_ref,
    da_ref, dwin_ref, dwout_ref, dbin_ref, dbout_ref, dg_ref, db_ref,
    m_sc, low_sc, acc,
):
    step = pl.program_id(0)

    @pl.when(step == 0)
    def _():
        unit, _ = norm_parts(a_ref[...])
        m_sc[...] = (unit * g_ref[...] + b_ref[...]).astype(BF)
        low = dx_ref[...].astype(BF)
        low_sc[...] = low
        dbout_ref[...] = jnp.sum(low.astype(F32), axis=0, keepdims=True)
        acc[...] = jnp.zeros_like(acc)

    normed = m_sc[...]
    low = low_sc[...]
    preact = mm(normed, win_ref[...]) + bin_ref[...]
    active, slope = gelu_pair(preact)
    preact_grad = (slope * mm(low, wout_ref[...])).astype(BF)
    dbin_ref[...] = jnp.sum(preact_grad.astype(F32), axis=0, keepdims=True)
    dwout_ref[...] = mm_at(low, active.astype(BF)).astype(BF)
    dwin_ref[...] = mm_at(normed, preact_grad).astype(BF)
    acc[...] += mm_bt(preact_grad, win_ref[...])

    @pl.when(step == pl.num_programs(0) - 1)
    def _():
        unit, scale = norm_parts(a_ref[...])
        hidden_grad, gain_grad, shift_grad = norm_pull(unit, scale, g_ref[...], acc[...])
        da_ref[...] = dx_ref[...] + hidden_grad
        dg_ref[...] = gain_grad
        db_ref[...] = shift_grad


def dense_back(incoming, hidden, gain, shift, weights, in_bias):
    rows, width = hidden.shape
    ff = in_bias.shape[1]
    steps = ff // FF_BLOCK
    col_block = pl.BlockSpec((width, FF_BLOCK), lambda c: (0, c))
    return call(
        dense_bwd_kernel, (steps,),
        [
            whole((rows, width)), whole((rows, width)), whole((1, width)), whole((1, width)),
            col_block,
            pl.BlockSpec((width, FF_BLOCK), lambda c: (0, steps + c)),
            pl.BlockSpec((1, FF_BLOCK), lambda c: (0, c)),
        ],
        [
            whole((rows, width)), col_block, col_block,
            pl.BlockSpec((1, FF_BLOCK), lambda c: (0, c)),
            whole((1, width)), whole((1, width)), whole((1, width)),
        ],
        [
            jax.ShapeDtypeStruct((rows, width), F32),
            jax.ShapeDtypeStruct((width, ff), BF),
            jax.ShapeDtypeStruct((width, ff), BF),
            jax.ShapeDtypeStruct((1, ff), F32),
            jax.ShapeDtypeStruct((1, width), F32),
            jax.ShapeDtypeStruct((1, width), F32),
            jax.ShapeDtypeStruct((1, width), F32),
        ],
        [
            pltpu.VMEM((rows, width), BF), pltpu.VMEM((rows, width), BF),
            pltpu.VMEM((rows, width), F32),
        ],
        10.0 * rows * width * ff, 35.0e6, "dense_bwd",
    )(incoming, hidden, gain, shift, weights, weights, in_bias)


def moe_kernel(
    micro, capp,
    rb_own, rb_oth, og_own, og_oth, dr_ref, dc_own, dc_oth, w_ref,
    win_ref, wout_ref, bin_ref, bout_ref,
    yc_own, yc_oth, rc_own, rc_oth, dg_own, dg_oth,
    dwin_ref, dwout_ref, dbin_ref, dbout_ref,
    b_sc, og_sc, dy_sc, w_sc, y_acc, r_acc, yo_acc, yt_acc, ro_acc, rt_acc,
):
    expert = pl.program_id(0)
    chunk = pl.program_id(1)
    last_expert = expert == pl.num_programs(0) - 1
    last_chunk = chunk == pl.num_programs(1) - 1
    half = rb_own.shape[1]

    @pl.when(chunk == 0)
    def _():
        for m in range(micro):
            slots = slice(m * capp, (m + 1) * capp)
            ids = lax.broadcasted_iota(jnp.int32, (capp, half), 0) + expert * capp
            tokens = None
            for side, (rb, og) in enumerate(((rb_own, og_own), (rb_oth, og_oth))):
                hit0 = dr_ref[m, 2 * side : 2 * side + 1, :] == ids
                hit1 = dr_ref[m, 2 * side + 1 : 2 * side + 2, :] == ids
                pick = jnp.where(hit0 | hit1, 1.0, 0.0).astype(BF)
                gate = jnp.sum(
                    jnp.where(hit0, w_ref[m, 2 * side : 2 * side + 1, :], 0.0)
                    + jnp.where(hit1, w_ref[m, 2 * side + 1 : 2 * side + 2, :], 0.0),
                    axis=-1, keepdims=True,
                )
                found = (mm(pick, rb[m]), mm(pick, og[m]), gate)
                tokens = found if tokens is None else tuple(
                    one + two for one, two in zip(tokens, found)
                )
            b_sc[slots, :] = tokens[0].astype(BF)
            og_sc[slots, :] = tokens[1].astype(BF)
            dy_sc[slots, :] = (tokens[1] * tokens[2]).astype(BF)
            w_sc[slots, :] = jnp.broadcast_to(tokens[2], (capp, w_sc.shape[1]))
        y_acc[...] = jnp.zeros_like(y_acc)
        r_acc[...] = jnp.zeros_like(r_acc)

    tokens = b_sc[...]
    low = dy_sc[...]
    preact = mm(tokens, win_ref[...]) + bin_ref[0]
    active, slope = gelu_pair(preact)
    active = active.astype(BF)
    preact_grad = (slope * mm(low, wout_ref[...])).astype(BF)
    dbin_ref[0] = jnp.sum(preact_grad.astype(F32), axis=0, keepdims=True)
    y_acc[...] += mm_bt(active, wout_ref[...])
    r_acc[...] += mm_bt(preact_grad, win_ref[...])
    dwout_ref[...] = mm_at(low, active).astype(BF)
    dwin_ref[...] = mm_at(tokens, preact_grad).astype(BF)

    @pl.when(last_chunk)
    def _():
        dbout_ref[0] = jnp.sum(dy_sc[...].astype(F32), axis=0, keepdims=True)
        for m in range(micro):
            slots = slice(m * capp, (m + 1) * capp)
            result = y_acc[slots, :] + 0.5 * bout_ref[0]
            dots = jnp.sum(og_sc[slots, :].astype(F32) * result, axis=-1, keepdims=True)
            lanes = lax.broadcasted_iota(jnp.int32, (capp, dg_own.shape[2]), 1)
            dots = jnp.where(lanes == expert, dots, 0.0)
            weighted = (w_sc[slots, 0:1] * result).astype(BF)
            rows_grad = r_acc[slots, :].astype(BF)
            ids = lax.broadcasted_iota(jnp.int32, (half, capp), 1) + expert * capp
            for dc, yc, rc, dg in (
                (dc_own, yo_acc, ro_acc, dg_own), (dc_oth, yt_acc, rt_acc, dg_oth)
            ):
                hit = (dc[m, :, 0:1] == ids) | (dc[m, :, 1:2] == ids)
                pick = jnp.where(hit, 1.0, 0.0)
                low_pick = pick.astype(BF)
                y_new = mm(low_pick, weighted)
                r_new = mm(low_pick, rows_grad)
                d_new = jnp.dot(pick, dots, precision=EXACT, preferred_element_type=F32)

                @pl.when(expert == 0)
                def _():
                    yc[m] = y_new
                    rc[m] = r_new
                    dg[m] = d_new

                @pl.when(expert > 0)
                def _():
                    yc[m] += y_new
                    rc[m] += r_new
                    dg[m] += d_new

    @pl.when(last_chunk & last_expert)
    def _():
        yc_own[...] = yo_acc[...].astype(BF)
        yc_oth[...] = yt_acc[...].astype(BF)
        rc_own[...] = ro_acc[...].astype(BF)
        rc_oth[...] = rt_acc[...].astype(BF)


def mixture(rows_own, rows_oth, grad_own, grad_oth, place_rows, place_own, place_oth, gates,
            weights, in_bias, out_bias, capp):
    micro, half, width = rows_own.shape
    experts, _, ff = in_bias.shape
    steps = ff // FF_BLOCK
    blocks = experts * steps
    lanes = 128
    slots = micro * capp
    w_block = (width, FF_BLOCK)
    group = (micro, half, width)
    return call(
        functools.partial(moe_kernel, micro, capp),
        (experts, steps),
        [
            whole(group), whole(group), whole(group), whole(group),
            whole(place_rows.shape), whole(place_own.shape), whole(place_oth.shape),
            whole(gates.shape),
            pl.BlockSpec(w_block, lambda e, c: (0, e * steps + c)),
            pl.BlockSpec(w_block, lambda e, c: (0, blocks + e * steps + c)),
            pl.BlockSpec((1, 1, FF_BLOCK), lambda e, c: (e, 0, c)),
            pl.BlockSpec((1, 1, width), lambda e, c: (e, 0, 0)),
        ],
        [
            whole(group), whole(group), whole(group), whole(group),
            whole((micro, half, lanes)), whole((micro, half, lanes)),
            pl.BlockSpec(w_block, lambda e, c: (0, e * steps + c)),
            pl.BlockSpec(w_block, lambda e, c: (0, e * steps + c)),
            pl.BlockSpec((1, 1, FF_BLOCK), lambda e, c: (e, 0, c)),
            pl.BlockSpec((1, 1, width), lambda e, c: (e, 0, 0)),
        ],
        [
            jax.ShapeDtypeStruct(group, BF), jax.ShapeDtypeStruct(group, BF),
            jax.ShapeDtypeStruct(group, BF), jax.ShapeDtypeStruct(group, BF),
            jax.ShapeDtypeStruct((micro, half, lanes), F32),
            jax.ShapeDtypeStruct((micro, half, lanes), F32),
            jax.ShapeDtypeStruct((width, experts * ff), BF),
            jax.ShapeDtypeStruct((width, experts * ff), BF),
            jax.ShapeDtypeStruct((experts, 1, ff), F32),
            jax.ShapeDtypeStruct((experts, 1, width), F32),
        ],
        [
            pltpu.VMEM((slots, width), BF), pltpu.VMEM((slots, width), BF),
            pltpu.VMEM((slots, width), BF), pltpu.VMEM((slots, 128), F32),
            pltpu.VMEM((slots, width), F32), pltpu.VMEM((slots, width), F32),
            pltpu.VMEM(group, F32), pltpu.VMEM(group, F32),
            pltpu.VMEM(group, F32), pltpu.VMEM(group, F32),
        ],
        12.0 * slots * experts * width * ff + 16.0 * experts * micro * capp * half * width,
        60.0e6, "experts",
    )(rows_own, rows_oth, grad_own, grad_oth, place_rows, place_own, place_oth, gates,
      weights, weights, in_bias, out_bias)


def gate_bwd_kernel(
    a_ref, og_ref, yo_ref, yr_ref, ro_ref, rr_ref, do_ref, dr_ref, gp_ref, rt_ref, g_ref, b_ref,
    out_ref, da_ref, drt_ref, dg_ref, db_ref,
):
    step = pl.program_id(0)
    after = a_ref[...]
    incoming = og_ref[...].astype(F32)
    out_ref[...] = (after + (yo_ref[...].astype(F32) + yr_ref[...].astype(F32))).astype(BF)
    gates = gp_ref[...]
    gate_grad = do_ref[...] + dr_ref[...]
    logit_grad = gates * (gate_grad - jnp.sum(gates * gate_grad, axis=-1, keepdims=True))
    unit, scale = norm_parts(after)
    normed = unit * g_ref[...] + b_ref[...]
    router_grad = lax.dot_general(
        logit_grad, normed, (((0,), (0,)), ((), ())), precision=EXACT, preferred_element_type=F32
    )
    normed_grad = ro_ref[...].astype(F32) + rr_ref[...].astype(F32)
    normed_grad += lax.dot_general(
        logit_grad, rt_ref[...], (((1,), (1,)), ((), ())), precision=EXACT,
        preferred_element_type=F32,
    )
    hidden_grad, gain_grad, shift_grad = norm_pull(unit, scale, g_ref[...], normed_grad)
    da_ref[...] = incoming + hidden_grad

    @pl.when(step == 0)
    def _():
        drt_ref[...] = router_grad
        dg_ref[...] = gain_grad
        db_ref[...] = shift_grad

    @pl.when(step > 0)
    def _():
        drt_ref[...] += router_grad
        dg_ref[...] += gain_grad
        db_ref[...] += shift_grad


def gate_back(after, incoming, y_own, y_got, r_own, r_got, d_own, d_got, gates, router, gain, shift):
    rows, width = after.shape
    lanes = gates.shape[1]
    block = rows // 2
    row = rows_of(block, width)
    row_low = rows_of(block, lanes)
    return call(
        gate_bwd_kernel, (2,),
        [
            row, row, row, row, row, row, row_low, row_low, row_low,
            whole((width, lanes)), whole((1, width)), whole((1, width)),
        ],
        [row, row, whole((lanes, width)), whole((1, width)), whole((1, width))],
        [
            jax.ShapeDtypeStruct((rows, width), BF),
            jax.ShapeDtypeStruct((rows, width), F32),
            jax.ShapeDtypeStruct((lanes, width), F32),
            jax.ShapeDtypeStruct((1, width), F32),
            jax.ShapeDtypeStruct((1, width), F32),
        ],
        [], 4.0 * rows * width * lanes, 14.0e6, "gate_bwd",
    )(after, incoming, y_own, y_got, r_own, r_got, d_own, d_got, gates, router, gain, shift)


def swap(value):
    return lax.ppermute(value, "tensor", [(0, 1), (1, 0)])


def in_order(mine, other, axis):
    first = lax.axis_index("tensor") == 0
    return jnp.stack([jnp.where(first, mine, other), jnp.where(first, other, mine)], axis=axis)


def gather_rows(share):
    return lax.all_gather(share, "dp", axis=0, tiled=True)


def scatter_rows(grad):
    return lax.psum_scatter(grad, "dp", scatter_dimension=0, tiled=True).astype(F32)


def join_halves(grad, parts):
    rows, total = grad.shape
    width = total // parts // 2
    halves = grad.reshape(rows, parts, 2, width)
    mine = lax.axis_index("tensor")
    kept = lax.dynamic_index_in_dim(halves, mine, 2, keepdims=False)
    sent = lax.dynamic_index_in_dim(halves, 1 - mine, 2, keepdims=False)
    return kept + swap(sent)


def own_half(value, axis):
    size = value.shape[axis] // 2
    return lax.dynamic_slice_in_dim(value, lax.axis_index("tensor") * size, size, axis)


def local(
    block_input, norm_gain, row_bias, qkv_weight, qkv_bias, out_weight, mlp_in, mlp_in_bias,
    mlp_out, mlp_out_bias, router, expert_in, expert_in_bias, expert_out, expert_out_bias,
    routes, slot_index, out_grad,
):
    micro, images, length, width = block_input.shape
    experts = router.shape[1]
    share_rows = mlp_in.shape[0]
    own_images = images // 2
    pad = round_up(length, ROW_PAD)
    half = own_images * pad
    rows = micro * half
    capp = round_up(CAP, ROW_PAD)
    side = lax.axis_index("tensor")

    def attn_share(layer):
        return jnp.concatenate(
            [qkv_weight[layer].reshape(share_rows, -1), out_weight[layer]], axis=1
        )

    def attn_full(layer):
        mine = attn_share(layer)
        other = swap(mine)
        full = in_order(mine.reshape(share_rows, 4, -1), other.reshape(share_rows, 4, -1), 2)
        return gather_rows(full.reshape(share_rows, -1))

    attn_one = attn_full(0)
    dense_mine = jnp.stack([mlp_in, mlp_out], axis=1)
    dense_full = in_order(dense_mine, swap(dense_mine), 2)
    dense_w = gather_rows(dense_full.reshape(share_rows, -1))
    attn_two = attn_full(1)
    expert_w = gather_rows(
        jnp.concatenate(
            [expert_in.reshape(share_rows, -1), expert_out.reshape(share_rows, -1)], axis=1
        )
    )

    def both(vector):
        joined = in_order(vector, swap(vector), vector.ndim - 1)
        return joined.reshape(vector.shape[:-1] + (-1,))

    biases = jnp.concatenate([qkv_bias.reshape(-1), mlp_in_bias])
    biases_other = swap(biases)
    bias_pair = in_order(biases, biases_other, 0)
    split = qkv_bias.size
    qkv_bias_full = jnp.moveaxis(
        bias_pair[:, :split].reshape((2,) + qkv_bias.shape), 0, 2
    ).reshape(qkv_bias.shape[:2] + (width,))
    mlp_bias_full = bias_pair[:, split:].reshape(1, -1)

    def qkv_bias_row(layer):
        zero = jnp.zeros((width,), F32)
        return jnp.concatenate(
            [qkv_bias_full[layer, 0], zero, qkv_bias_full[layer, 1]]
        ).reshape(1, -1)

    def padded(value, start):
        part = lax.dynamic_slice_in_dim(value, start, own_images, 1)
        return jnp.pad(part, ((0, 0), (0, 0), (0, pad - length), (0, 0)))

    mine_at = side * own_images
    other_at = (1 - side) * own_images
    hidden = padded(block_input, mine_at).astype(F32).reshape(rows, width)
    grad_own = padded(out_grad, mine_at).reshape(micro, half, width)
    grad_oth = padded(out_grad, other_at).reshape(micro, half, width)

    kept = slot_index < CAP
    place = jnp.where(kept, routes * capp + slot_index, -1)
    pick = jnp.where(kept, routes, -1)

    def lay(value, start):
        part = lax.dynamic_slice_in_dim(value, start, own_images, 1)
        part = jnp.pad(
            part, ((0, 0), (0, 0), (0, pad - length), (0, 0)), constant_values=-1
        )
        return part.reshape(micro, half, 2)

    place_own, place_oth = lay(place, mine_at), lay(place, other_at)
    place_rows = jnp.concatenate(
        [jnp.swapaxes(place_own, 1, 2), jnp.swapaxes(place_oth, 1, 2)], axis=1
    )
    select = lay(pick, mine_at).reshape(rows, 2)
    router_wide = jnp.pad(router, ((0, 0), (0, 128 - experts)))

    def row(vector):
        return vector.reshape(1, -1)

    qkv_one, lse_one, mix_one, after_one = attention_forward(
        hidden, row(norm_gain[0, 0]), row(row_bias[0, 0]), attn_one, qkv_bias_row(0),
        row(row_bias[0, 2]), length, pad,
    )
    after_ffn = dense_forward(
        after_one, row(norm_gain[0, 1]), row(row_bias[0, 1]), dense_w, mlp_bias_full,
        row(mlp_out_bias),
    )
    qkv_two, lse_two, mix_two, after_two, rows_own, gates, chosen = attention_forward(
        after_ffn, row(norm_gain[1, 0]), row(row_bias[1, 0]), attn_two, qkv_bias_row(1),
        row(row_bias[1, 2]), length, pad,
        (row(norm_gain[1, 1]), row(row_bias[1, 1]), router_wide, select, experts),
    )
    rows_oth = swap(rows_own)
    gate_own = jnp.swapaxes(chosen[:, :2].reshape(micro, half, 2), 1, 2)
    gate_oth = swap(gate_own)
    (
        y_own, y_oth, r_own, r_oth, d_own, d_oth, ein_grad, eout_grad, ein_bias, eout_bias,
    ) = mixture(
        rows_own.reshape(micro, half, width), rows_oth.reshape(micro, half, width),
        grad_own, grad_oth, place_rows, place_own, place_oth,
        jnp.concatenate([gate_own, gate_oth], axis=1),
        expert_w, expert_in_bias.reshape(experts, 1, -1), expert_out_bias.reshape(experts, 1, -1),
        capp,
    )
    y_got, r_got, d_got = swap(y_oth), swap(r_oth), swap(d_oth)

    def flat(value):
        return value.reshape(rows, value.shape[-1])

    out_own, grad_two, router_grad, gain_moe, shift_moe = gate_back(
        after_two, flat(grad_own), flat(y_own), flat(y_got), flat(r_own), flat(r_got),
        flat(d_own), flat(d_got), gates, router_wide,
        row(norm_gain[1, 1]), row(row_bias[1, 1]),
    )
    grad_ffn, wq_two, wo_two, qb_two, ob_two, gain_two, shift_two = attention_back(
        grad_two, after_ffn, row(norm_gain[1, 0]), row(row_bias[1, 0]), attn_two,
        (qkv_two, lse_two, mix_two), length, pad,
    )
    grad_one, win_grad, wout_grad, in_bias_grad, out_bias_grad, gain_ffn, shift_ffn = dense_back(
        grad_ffn, after_one, row(norm_gain[0, 1]), row(row_bias[0, 1]), dense_w, mlp_bias_full
    )
    grad_zero, wq_one, wo_one, qb_one, ob_one, gain_one, shift_one = attention_back(
        grad_one, hidden, row(norm_gain[0, 0]), row(row_bias[0, 0]), attn_one,
        (qkv_one, lse_one, mix_one), length, pad,
    )

    def images_of(value):
        value = value.astype(BF).reshape(micro, own_images, pad, width)[:, :, :length]
        return in_order(value, swap(value), 1).reshape(block_input.shape)

    block_output = images_of(out_own)
    input_grad = images_of(grad_zero).astype(F32)

    ein_done = scatter_rows(ein_grad).reshape(expert_in.shape)
    eout_done = scatter_rows(eout_grad).reshape(expert_out.shape)
    wq_two_done = join_halves(scatter_rows(wq_two), 3)
    wo_two_done = join_halves(scatter_rows(wo_two), 1)
    win_done = join_halves(scatter_rows(win_grad), 1).reshape(mlp_in.shape)
    wout_done = join_halves(scatter_rows(wout_grad), 1).reshape(mlp_out.shape)
    wq_one_done = join_halves(scatter_rows(wq_one), 3)
    wo_one_done = join_halves(scatter_rows(wo_one), 1)

    place_in = (side == jnp.arange(2)).astype(F32)
    ein_bias_wide = place_in[:, None, None] * ein_bias.reshape(1, experts, -1)
    small = lax.psum(
        (
            jnp.concatenate([gain_one, gain_ffn, gain_two, gain_moe]),
            jnp.concatenate([shift_one, shift_ffn, ob_one, shift_two, shift_moe, ob_two]),
            jnp.concatenate([qb_one, qb_two]),
            in_bias_grad,
            out_bias_grad,
            router_grad[:experts],
            ein_bias_wide,
            0.5 * eout_bias,
        ),
        ("dp", "tensor"),
    )
    gain_sum, shift_sum, qb_sum, in_bias_sum, out_bias_sum, router_sum, ein_sum, eout_sum = small
    qb_sum = own_half(qb_sum.reshape(2, 3, width), 2)
    return (
        block_output,
        input_grad,
        gain_sum.reshape(norm_gain.shape),
        shift_sum.reshape(row_bias.shape),
        jnp.stack([wq_one_done, wq_two_done]).reshape(qkv_weight.shape),
        jnp.stack([qb_sum[:, 0], qb_sum[:, 2]], axis=1),
        jnp.stack([wo_one_done, wo_two_done]).reshape(out_weight.shape),
        win_done,
        own_half(in_bias_sum.reshape(-1), 0),
        wout_done,
        out_bias_sum.reshape(-1),
        router_sum.T,
        ein_done,
        lax.dynamic_index_in_dim(ein_sum, side, 0, keepdims=False),
        eout_done,
        eout_sum.reshape(experts, width),
    )


def solution(mesh):
    return jax.shard_map(
        local,
        mesh=mesh,
        in_specs=(
            P(None, "dp", None, None), P(), P(), P(None, "dp", None, "tensor"),
            P(None, None, "tensor"), P(None, "dp", "tensor"), P("dp", "tensor"), P("tensor"),
            P("dp", "tensor"), P(), P(), P("dp", None, "tensor"), P(None, "tensor"),
            P("dp", None, "tensor"), P(), P(None, "dp", None, None), P(None, "dp", None, None),
            P(None, "dp", None, None),
        ),
        out_specs=(
            P(None, "dp", None, None), P(None, "dp", None, None), P(), P(),
            P(None, "dp", None, "tensor"), P(None, None, "tensor"), P(None, "dp", "tensor"),
            P("dp", "tensor"), P("tensor"), P("dp", "tensor"), P(), P(),
            P("dp", None, "tensor"), P(None, "tensor"), P("dp", None, "tensor"), P(),
        ),
        check_vma=False,
    )
```

time: 2860 us -> 1410 us (0.49)
  waiting for transfers between devices: 1730 us -> 970 us
  local copies, waits for them, and re-layouts: 537 us -> 68.2 us
  matrix products: 350 us -> 0 us
  Pallas kernels: 0 us -> 305 us
  other arithmetic: 159 us -> 17.4 us
  blocking collectives: 54.3 us -> 0 us
    unnamed x23 -> x13, waiting for transfers between devices: 635 us -> 4.86 us
    psum x9 -> x1, waiting for transfers between devices: 474 us -> 111 us  [local(): lax.psum((jnp.concatenate([gain_one, gain_ffn, gain_two, gain_moe]), jnp....]
    dot_general x82 -> x0, matrix products: 350 us -> none  [the longest x2 28.2 us: mixture_back(): jnp.einsum('ecd,ecf->def', result_grad, active, preferred_element_type=jn...]
    pallas_call x0 -> x8, Pallas kernels: none -> 305 us  [the longest x1 93.1 us: mixture(): call(functools.partial(moe_kernel, micro, capp), (experts, steps), [whole...]
    reduce_scatter x6 -> x8, waiting for transfers between devices: 379 us -> 603 us  [scatter_rows(): lax.psum_scatter(grad, 'dp', scatter_dimension=0, tiled=True).astype(F32)]
    gather x32 -> x0, local copies, waits for them, and re-layouts: 191 us -> none  [the longest x6 41.6 us: mixture_back(): jnp.take_along_axis(jnp.dot(incoming, out_biases.T, precision=EXACT), rou...]
    reduce_sum x43 -> x0, other arithmetic: 115 us -> none  [the longest x2 27.2 us: mixture_back(): jnp.sum(incoming[:, None, :] * result[safe_place], axis=2)]
    ppermute x0 -> x17, waiting for transfers between devices: none -> 108 us  [swap(): return lax.ppermute(value, 'tensor', [(0, 1), (1, 0)])]
  transfers between devices with their start and end apart: 22 -> 30, of which waited for: 19 -> 21; matrix products, arithmetic and copies ran while one was open for 17% -> 5% of each run, Pallas kernels for 0% -> 6%
where the time goes in v1:
time: 1410 us; the launch traced here: 1400 us
  waiting for transfers between devices  970 us (69%)
  Pallas kernels  305 us (22%)
  local copies, waits for them, and re-layouts  68.2 us (5%)
  starting transfers between devices  25.4 us (2%)
  other arithmetic  17.4 us (1%)
  between operations  15.2 us (1%)
    reduce_scatter x8, waiting for transfers between devices, scatter_rows(): lax.psum_scatter(grad, 'dp', scatter_dimension=0, tiled=True).astype(F32)  603 us
    all_gather x4, waiting for transfers between devices, gather_rows(): return lax.all_gather(share, 'dp', axis=0, tiled=True)  143 us
    psum x1, waiting for transfers between devices, local(): lax.psum((jnp.concatenate([gain_one, gain_ffn, gain_two, gain_moe]), jnp....  111 us
    ppermute x17, waiting for transfers between devices, swap(): return lax.ppermute(value, 'tensor', [(0, 1), (1, 0)])  108 us
    pallas_call x1, Pallas kernels, mixture(): call(functools.partial(moe_kernel, micro, capp), (experts, steps), [whole...  93.1 us
    pallas_call x2, Pallas kernels, attention_back(): call(functools.partial(attn_bwd_kernel, length, pad, heads), (2,), [rows_...  87 us
    pallas_call x2, Pallas kernels, attention_forward(): call(functools.partial(attn_fwd_kernel, length, pad, heads, router_on), (...  65.5 us
    pallas_call x1, Pallas kernels, dense_back(): call(dense_bwd_kernel, (steps,), [whole((rows, width)), whole((rows, widt...  33.4 us
  transfers between devices with their start and end apart: 30, of which 21 were waited for; matrix products, arithmetic and copies ran while one was open for 5% of the time, Pallas kernels for 6%

profile of v1, /device:TPU:0, one launch (start us, length us, event | category | flops | bytes accessed | tf_op | source)
XLA Modules:
  0.0 1402.0 jit_solution(17459941962916345734)
XLA Ops:
  9.1 3.0 collective-permute-start
  12.1 3.8 collective-permute-done
  17.7 1.8 collective-permute-start.2
  19.5 6.5 collective-permute-done.2
  29.7 3.7 collective-permute-done.3
  38.0 6.9 constant_dynamic-slice_fusion.15
  47.1 1.8 bitcast_convert_fusion.h_ref
  53.5 19.0 %all-gather.5.cloned.1.call-done.w_ref = bf16[768,3072]{1,0:T(8,128)(2,1)} async-done(((bf16[48,3072]{1,0:T(8,128)(2,1)}), bf16[768,3072]{1,0:T(8,128)(2,1)}) %all-gather.5.cloned.1.call-update) | async-done | bytes 4718608 | tf_op jit(solution)/shard_map/all_gather | solution.py:672
  72.5 30.0 %attn_fwd.2 = (bf16[832,2304]{1,0:T(8,128)(2,1)}, f32[4,16,208]{2,1,0:T(8,128)}, bf16[832,768]{1,0:T(8,128)(2,1)}, f32[832,768]{1,0:T(8,128)}) custom-call(f32[832,768]{1,0:T(8,128)} %bitcast_convert_fusion.h_ref, f32[1,768]{1,0:T(1,128)} %get-tuple-element.230.g_ref, f32[1,768]{1,0:T(1,128)} %get-tuple-element.224.b_ref, ...), custom_call_target="tpu_custom_call" | custom-call | flops 6052380672 | bytes 12000000 | tf_op jit(solution)/shard_map/attn_fwd/pallas_call | solution.py:204
  102.5 52.9 %all-gather.7.cloned.1.call-done.win_ref.wout_ref = bf16[768,6144]{1,0:T(8,128)(2,1)} async-done(((bf16[48,6144]{1,0:T(8,128)(2,1)}), bf16[768,6144]{1,0:T(8,128)(2,1)}) %all-gather.7.cloned.1.call-update) | async-done | bytes 9437200 | tf_op jit(solution)/shard_map/all_gather | solution.py:672
  155.4 15.8 %dense_fwd.1.h_ref = f32[832,768]{1,0:T(8,128)} custom-call(f32[832,768]{1,0:T(8,128)} %get-tuple-element.63.a_ref, f32[1,768]{1,0:T(1,128)} %get-tuple-element.229.g_ref, f32[1,768]{1,0:T(1,128)} %get-tuple-element.222.b_ref, bf16[768,6144]{1,0:T(8,128)(2,1)} %all-gather.7.cloned.1.call-done.win_ref.wout_ref, ...), custom_call_target="tpu_custom_call" | custom-call | flops 7851737088 | bytes 15000000 | tf_op jit(solution)/shard_map/dense_fwd/pallas_call | solution.py:368
  171.2 38.5 %all-gather.9.cloned.1.call-done.w_ref = bf16[768,3072]{1,0:T(8,128)(2,1)} async-done(((bf16[48,3072]{1,0:T(8,128)(2,1)}), bf16[768,3072]{1,0:T(8,128)(2,1)}) %all-gather.9.cloned.1.call-update) | async-done | bytes 4718608 | tf_op jit(solution)/shard_map/all_gather | solution.py:672
  209.6 35.5 %attn_fwd.3 = (bf16[832,2304]{1,0:T(8,128)(2,1)}, f32[4,16,208]{2,1,0:T(8,128)}, bf16[832,768]{1,0:T(8,128)(2,1)}, f32[832,768]{1,0:T(8,128)}, bf16[832,768]{1,0...) custom-call(f32[832,768]{1,0:T(8,128)} %dense_fwd.1.h_ref, f32[1,768]{1,0:T(1,128)} %get-tuple-element.231.g_ref, ...), custom_call_target="tpu_custom_call" | custom-call | flops 6052380672 | bytes 12000000 | tf_op jit(solution)/shard_map/attn_fwd/pallas_call | solution.py:204
  245.2 1.5 collective-permute-start.4
  255.6 20.3 %collective-permute-done.5 = f32[2,2,416]{2,1,0:T(2,128)S(1)} collective-permute-done((f32[2,2,416]{2,1,0:T(2,128)S(1)}, f32[2,2,416]{2,1,0:T(2,128)S(1)}, u32[]{:S(2)}, u32[]{:S(2)}) %collective-permute-start.5) | collective-permute-done | bytes 6688 | tf_op jit(solution)/shard_map/ppermute | solution.py:663
  276.5 32.8 %all-gather.11.cloned.1.call-done.win_ref.wout_ref = bf16[768,12288]{1,0:T(8,128)(2,1)} async-done(((bf16[48,12288]{1,0:T(8,128)(2,1)}), bf16[768,12288]{1,0:T(8,128)(2,1)}) %all-gather.11.cloned.1.call-update) | async-done | bytes 18874384 | tf_op jit(solution)/shard_map/all_gather | solution.py:672
  309.3 93.1 %experts.1 = (bf16[2,416,768]{2,1,0:T(8,128)(2,1)}, bf16[2,416,768]{2,1,0:T(8,128)(2,1)}, bf16[2,416,768]{2,1,0:T(8,128)(2,1)}, bf16[2,416,768]{2,1,0:T(8,128)(2...) custom-call(bf16[2,416,768]{2,1,0:T(8,128)(2,1)} %bitcast.203, ...), custom_call_target="tpu_custom_call" | custom-call | flops 46858764288 | bytes 60000000 | tf_op jit(solution)/shard_map/experts/pallas_call | solution.py:558
  402.4 1.5 collective-permute-start.6
  408.7 60.7 %collective-permute-done.8 = f32[2,416,128]{2,1,0:T(8,128)S(1)} collective-permute-done((f32[2,416,128]{2,1,0:T(8,128)}, f32[2,416,128]{2,1,0:T(8,128)S(1)}, u32[]{:S(2)}, u32[]{:S(2)}) %collective-permute-start.8) | collective-permute-done | bytes 426016 | tf_op jit(solution)/shard_map/ppermute | solution.py:663
  471.0 10.5 gate_bwd.1
  481.5 43.4 %attn_bwd.2 = (f32[832,768]{1,0:T(8,128)}, bf16[768,2304]{1,0:T(8,128)(2,1)}, bf16[768,768]{1,0:T(8,128)(2,1)}, f32[1,2304]{1,0:T(1,128)}, f32[1,768]{1,0:T(1,128)}, /*index=5*/f32[1,768]{1,0:T(1,128)}, f32[1,768]{1,0:T(1,128)}) custom-call(f32[832,768]{1,0:T(8,128)} %get-tuple-element.75.da_ref, f32[832,768]{1,0:T(8,128)} %dense_fwd.1.h_ref, ...), custom_call_target="tpu_custom_call" | custom-call | flops 13168017408 | bytes 25000000 | tf_op jit(solution)/shard_map/attn_bwd/pallas_call | solution.py:314
  525.0 33.4 %dense_bwd.1 = (f32[832,768]{1,0:T(8,128)}, bf16[768,3072]{1,0:T(8,128)(2,1)}, bf16[768,3072]{1,0:T(8,128)(2,1)}, f32[1,3072]{1,0:T(1,128)}, f32[1,768]{1,0:T(1,...) custom-call(f32[832,768]{1,0:T(8,128)} %get-tuple-element.79.dx_ref, f32[832,768]{1,0:T(8,128)} %get-tuple-element.63.a_ref, ...), custom_call_target="tpu_custom_call" | custom-call | flops 19629342720 | bytes 35000000 | tf_op jit(solution)/shard_map/dense_bwd/pallas_call | solution.py:424
  558.4 43.5 %attn_bwd.3 = (f32[832,768]{1,0:T(8,128)}, bf16[768,2304]{1,0:T(8,128)(2,1)}, bf16[768,768]{1,0:T(8,128)(2,1)}, f32[1,2304]{1,0:T(1,128)}, f32[1,768]{1,0:T(1,128)}, /*index=5*/f32[1,768]{1,0:T(1,128)}, f32[1,768]{1,0:T(1,128)}) custom-call(f32[832,768]{1,0:T(8,128)} %get-tuple-element.80.da_ref, f32[832,768]{1,0:T(8,128)} %bitcast_convert_fusion.h_ref, ...), custom_call_target="tpu_custom_call" | custom-call | flops 13168017408 | bytes 25000000 | tf_op jit(solution)/shard_map/attn_bwd/pallas_call | solution.py:314
  613.5 1.9 convert_element_type.31
  615.4 2.0 copy.151
  619.0 2.0 copy.147
  621.5 111.5 %all-reduce.10.cloned.1.call-done = (f32[2,2,768]{2,1,0:T(2,128)}, f32[2,3,768]{2,1,0:T(4,128)}, f32[2,3,768]{2,1,0:T(4,128)}, f32[1,3072]{1,0:T(1,128)}, f32[76...) async-done(((f32[2,2,768]{2,1,0:T(2,128)}, f32[2,3,768]{2,1,0:T(4,128)}, f32[2,3,768]{2,1,0:T(4,128)}, f32[1,3072]{1,0:T(1,128)}, ...) | async-done | bytes 138256 | tf_op jit(solution)/shard_map/psum | solution.py:846
  740.6 4.1 copy.160
  746.5 2.4 copy.159
  748.8 48.9 %reduce-scatter.13.cloned.1.call-done = bf16[48,768]{1,0:T(8,128)(2,1)} async-done(((bf16[768,768]{1,0:T(8,128)(2,1)}), bf16[48,768]{1,0:T(8,128)(2,1)}) %reduce-scatter.13.cloned.1.call-update) | async-done | bytes 73744 | tf_op jit(solution)/shard_map/reduce_scatter | solution.py:676
  798.8 1.5 collective-permute-start.13
  800.4 59.1 %reduce-scatter.15.cloned.1.call-done = bf16[48,768]{1,0:T(8,128)(2,1)} async-done(((bf16[768,768]{1,0:T(8,128)(2,1)}), bf16[48,768]{1,0:T(8,128)(2,1)}) %reduce-scatter.15.cloned.1.call-update) | async-done | bytes 73744 | tf_op jit(solution)/shard_map/reduce_scatter | solution.py:676
  860.5 1.6 collective-permute-start.14
  862.1 2.8 collective-permute-done.14
  865.0 65.9 %reduce-scatter.9.cloned.1.call-done = bf16[48,2304]{1,0:T(8,128)(2,1)} async-done(((bf16[768,2304]{1,0:T(8,128)(2,1)}), bf16[48,2304]{1,0:T(8,128)(2,1)}) %reduce-scatter.9.cloned.1.call-update) | async-done | bytes 221200 | tf_op jit(solution)/shard_map/reduce_scatter | solution.py:676
  934.6 67.6 %reduce-scatter.11.cloned.1.call-done = bf16[48,2304]{1,0:T(8,128)(2,1)} async-done(((bf16[768,2304]{1,0:T(8,128)(2,1)}), bf16[48,2304]{1,0:T(8,128)(2,1)}) %reduce-scatter.11.cloned.1.call-update) | async-done | bytes 221200 | tf_op jit(solution)/shard_map/reduce_scatter | solution.py:676
  1003.8 1.5 collective-permute-start.12
  1005.3 4.5 collective-permute-done.12
  1009.8 71.1 %reduce-scatter.19.cloned.1.call-done = bf16[48,3072]{1,0:T(8,128)(2,1)} async-done(((bf16[768,3072]{1,0:T(8,128)(2,1)}), bf16[48,3072]{1,0:T(8,128)(2,1)}) %reduce-scatter.19.cloned.1.call-update) | async-done | bytes 294928 | tf_op jit(solution)/shard_map/reduce_scatter | solution.py:676
  1080.9 1.5 reshape.361
  1083.0 1.5 collective-permute-start.16
  1085.4 74.1 %reduce-scatter.17.cloned.1.call-done = bf16[48,3072]{1,0:T(8,128)(2,1)} async-done(((bf16[768,3072]{1,0:T(8,128)(2,1)}), bf16[48,3072]{1,0:T(8,128)(2,1)}) %reduce-scatter.17.cloned.1.call-update) | async-done | bytes 294928 | tf_op jit(solution)/shard_map/reduce_scatter | solution.py:676
  1159.5 1.5 reshape.359
  1163.8 5.5 collective-permute-done.15
  1170.1 104.3 %reduce-scatter.21.cloned.1.call-done = bf16[48,6144]{1,0:T(8,128)(2,1)} async-done(((bf16[768,6144]{1,0:T(8,128)(2,1)}), bf16[48,6144]{1,0:T(8,128)(2,1)}) %reduce-scatter.21.cloned.1.call-update) | async-done | bytes 589840 | tf_op jit(solution)/shard_map/reduce_scatter | solution.py:676
  1274.4 3.0 reshape.363
  1277.4 112.2 %reduce-scatter.23.cloned.1.call-done = bf16[48,6144]{1,0:T(8,128)(2,1)} async-done(((bf16[768,6144]{1,0:T(8,128)(2,1)}), bf16[48,6144]{1,0:T(8,128)(2,1)}) %reduce-scatter.23.cloned.1.call-update) | async-done | bytes 589840 | tf_op jit(solution)/shard_map/reduce_scatter | solution.py:676
  1389.6 3.0 reshape.365
  (231 shorter events, 71.8 us)
Async XLA Ops:
  7.2 65.3 %all-gather.5.cloned.1.call-start = ((), (), s32[]{:S(2)}) async-start(), calls=%async_computation.8 | async-start | bytes 5013504 | tf_op jit(solution)/shard_map/all_gather | solution.py:672
  9.1 6.9 collective-permute-start
  17.6 137.8 %all-gather.7.cloned.1.call-start = ((), (), s32[]{:S(2)}) async-start(), calls=%async_computation.9 | async-start | bytes 10027008 | tf_op jit(solution)/shard_map/all_gather | solution.py:672
  17.7 8.3 collective-permute-start.2
  28.0 181.6 %all-gather.9.cloned.1.call-start = ((), (), s32[]{:S(2)}) async-start(), calls=%async_computation.10 | async-start | bytes 5013504 | tf_op jit(solution)/shard_map/all_gather | solution.py:672
  28.2 5.2 collective-permute-start.3
  35.0 274.2 %all-gather.11.cloned.1.call-start = ((), (), s32[]{:S(2)}) async-start(), calls=%async_computation.11 | async-start | bytes 20054016 | tf_op jit(solution)/shard_map/all_gather | solution.py:672
  36.4 696.5 %all-reduce.10.cloned.1.call-start = ((), (), s32[]{:S(2)}) async-start(), calls=%async_computation.20 | async-start | bytes 303104 | tf_op jit(solution)/shard_map/psum | solution.py:846
  36.6 15.0 %collective-permute-start.1 = (f32[3072]{0:T(1024)S(1)}, f32[3072]{0:T(1024)S(1)}, u32[]{:S(2)}, u32[]{:S(2)}) collective-permute-start(f32[3072]{0:T(1024)S(1)} %constant_dynamic-update-slice_fusion), channel_id=1, source_target_pairs={{0,1},{1,0},{2,3},{3,2},{4,5},{5,4},{6,7},{7,6},{8,9},{9,8},{10,11... | collective-permute-start | bytes 36872 | tf_op jit(solution)/shard_map/ppermute | solution.py:663
  45.1 1.9 copy-start.11
  47.1 2.7 copy-start.14
  245.2 31.3 %collective-permute-start.4 = (bf16[832,768]{1,0:T(8,128)(2,1)}, bf16[832,768]{1,0:T(8,128)(2,1)}, u32[]{:S(2)}, u32[]{:S(2)}) collective-permute-start(bf16[832,768]{1,0:T(8,128)(2,1)} %get-tuple-element.65), channel_id=1, source_target_pairs={{0,1},{1,0},{2,3},{3,2},{4,5},{5,4},{6,7},{7,6},{8,9},{9,8},{10,11... | collective-permute-start | bytes 3833864 | tf_op jit(solution)/shard_map/ppermute | solution.py:663
  247.0 3.6 copy-start.1
  249.2 2.7 copy-start.2
  250.6 25.3 %collective-permute-start.5 = (f32[2,2,416]{2,1,0:T(2,128)S(1)}, f32[2,2,416]{2,1,0:T(2,128)S(1)}, u32[]{:S(2)}, u32[]{:S(2)}) collective-permute-start(f32[2,2,416]{2,1,0:T(2,128)S(1)} %bitcast.199), channel_id=1, source_target_pairs={{0,1},{1,0},{2,3},{3,2},{4,5},{5,4},{6,7},{7,6},{8,9},{9,8},{10,11... | collective-permute-start | bytes 19976 | tf_op jit(solution)/shard_map/ppermute | solution.py:663
  402.4 67.0 %collective-permute-start.6 = (bf16[2,416,768]{2,1,0:T(8,128)(2,1)}, bf16[2,416,768]{2,1,0:T(8,128)(2,1)S(1)}, u32[]{:S(2)}, u32[]{:S(2)}) collective-permute-start(bf16[2,416,768]{2,1,0:T(8,128)(2,1)} %get-tuple-element.68), channel_id=1, source_target_pairs={{0,1},{1,0},{2,3},{3,2},{4,5},{5,4},{6,7},{7,6},{8,9},{9,8},{10,11... | collective-permute-start | bytes 3833864 | tf_op jit(solution)/shard_map/ppermute | solution.py:663
  403.9 65.5 %collective-permute-start.7 = (bf16[2,416,768]{2,1,0:T(8,128)(2,1)}, bf16[2,416,768]{2,1,0:T(8,128)(2,1)S(1)}, u32[]{:S(2)}, u32[]{:S(2)}) collective-permute-start(bf16[2,416,768]{2,1,0:T(8,128)(2,1)} %get-tuple-element.70), channel_id=1, source_target_pairs={{0,1},{1,0},{2,3},{3,2},{4,5},{5,4},{6,7},{7,6},{8,9},{9,8},{10,11... | collective-permute-start | bytes 3833864 | tf_op jit(solution)/shard_map/ppermute | solution.py:663
  404.5 64.9 %collective-permute-start.8 = (f32[2,416,128]{2,1,0:T(8,128)}, f32[2,416,128]{2,1,0:T(8,128)S(1)}, u32[]{:S(2)}, u32[]{:S(2)}) collective-permute-start(f32[2,416,128]{2,1,0:T(8,128)} %get-tuple-element.72), channel_id=1, source_target_pairs={{0,1},{1,0},{2,3},{3,2},{4,5},{5,4},{6,7},{7,6},{8,9},{9,8},{10,11... | collective-permute-start | bytes 1277960 | tf_op jit(solution)/shard_map/ppermute | solution.py:663
  558.3 43.6 %copy-start.20 = (f32[1,2304]{1,0:T(1,128)S(1)}, f32[1,2304]{1,0:T(1,128)}, u32[]{:S(2)}) copy-start(f32[1,2304]{1,0:T(1,128)} %get-tuple-element.98) | copy-start | bytes 27652
  558.4 45.0 %copy-start.29 = (f32[1,768]{1,0:T(1,128)S(1)}, f32[1,768]{1,0:T(1,128)}, u32[]{:S(2)}) copy-start(f32[1,768]{1,0:T(1,128)} %get-tuple-element.93) | copy-start | bytes 9220
  558.4 45.0 %copy-start.30 = (f32[1,768]{1,0:T(1,128)S(1)}, f32[1,768]{1,0:T(1,128)}, u32[]{:S(2)}) copy-start(f32[1,768]{1,0:T(1,128)} %get-tuple-element.94) | copy-start | bytes 9220
  558.4 45.0 %copy-start.31 = (f32[1,768]{1,0:T(1,128)S(1)}, f32[1,768]{1,0:T(1,128)}, u32[]{:S(2)}) copy-start(f32[1,768]{1,0:T(1,128)} %get-tuple-element.92) | copy-start | bytes 9220
  558.4 45.0 %copy-start.32 = (f32[1,768]{1,0:T(1,128)S(1)}, f32[1,768]{1,0:T(1,128)}, u32[]{:S(2)}) copy-start(f32[1,768]{1,0:T(1,128)} %get-tuple-element.90) | copy-start | bytes 9220
  558.4 46.3 %copy-start.25 = (f32[1,768]{1,0:T(1,128)S(1)}, f32[1,768]{1,0:T(1,128)}, u32[]{:S(2)}) copy-start(f32[1,768]{1,0:T(1,128)} %get-tuple-element.88) | copy-start | bytes 9220
  558.4 46.3 %copy-start.26 = (f32[1,768]{1,0:T(1,128)S(1)}, f32[1,768]{1,0:T(1,128)}, u32[]{:S(2)}) copy-start(f32[1,768]{1,0:T(1,128)} %get-tuple-element.87) | copy-start | bytes 9220
  558.4 46.3 %copy-start.27 = (f32[1,768]{1,0:T(1,128)S(1)}, f32[1,768]{1,0:T(1,128)}, u32[]{:S(2)}) copy-start(f32[1,768]{1,0:T(1,128)} %get-tuple-element.86) | copy-start | bytes 9220
  558.4 48.9 %copy-start.28 = (f32[1,768]{1,0:T(1,128)S(1)}, f32[1,768]{1,0:T(1,128)}, u32[]{:S(2)}) copy-start(f32[1,768]{1,0:T(1,128)} %get-tuple-element.104) | copy-start | bytes 9220
  608.0 189.7 %reduce-scatter.13.cloned.1.call-start = ((), (), s32[]{:S(2)}) async-start(), calls=%async_computation.14 | async-start | bytes 1253376 | tf_op jit(solution)/shard_map/reduce_scatter | solution.py:676
  608.6 250.8 %reduce-scatter.15.cloned.1.call-start = ((), (), s32[]{:S(2)}) async-start(), calls=%async_computation.15 | async-start | bytes 1253376 | tf_op jit(solution)/shard_map/reduce_scatter | solution.py:676
  609.3 321.5 %reduce-scatter.9.cloned.1.call-start = ((), (), s32[]{:S(2)}) async-start(), calls=%async_computation.12 | async-start | bytes 3760128 | tf_op jit(solution)/shard_map/reduce_scatter | solution.py:676
  610.1 392.1 %reduce-scatter.11.cloned.1.call-start = ((), (), s32[]{:S(2)}) async-start(), calls=%async_computation.13 | async-start | bytes 3760128 | tf_op jit(solution)/shard_map/reduce_scatter | solution.py:676
  610.8 470.1 %reduce-scatter.19.cloned.1.call-start = ((), (), s32[]{:S(2)}) async-start(), calls=%async_computation.17 | async-start | bytes 5013504 | tf_op jit(solution)/shard_map/reduce_scatter | solution.py:676
  611.4 548.1 %reduce-scatter.17.cloned.1.call-start = ((), (), s32[]{:S(2)}) async-start(), calls=%async_computation.16 | async-start | bytes 5013504 | tf_op jit(solution)/shard_map/reduce_scatter | solution.py:676
  612.1 662.3 %reduce-scatter.21.cloned.1.call-start = ((), (), s32[]{:S(2)}) async-start(), calls=%async_computation.18 | async-start | bytes 10027008 | tf_op jit(solution)/shard_map/reduce_scatter | solution.py:676
  612.7 776.9 %reduce-scatter.23.cloned.1.call-start = ((), (), s32[]{:S(2)}) async-start(), calls=%async_computation.19 | async-start | bytes 10027008 | tf_op jit(solution)/shard_map/reduce_scatter | solution.py:676
  615.4 3.4 copy-start
  617.4 121.0 %collective-permute-start.10 = (bf16[2,2,197,768]{3,1,2,0:T(2,128)(2,1)}, bf16[2,2,197,768]{3,1,2,0:T(2,128)(2,1)}, u32[]{:S(2)}, u32[]{:S(2)}) collective-permute-start(bf16[2,2,197,768]{3,1,2,0:T(2,128)(2,1)} %copy.151), channel_id=1, source_target_pairs={{0,1},{1,0},{2,3},{3,2},{4,5},{5,4},{6,7},{7,6},{8,9},{9,8},{10,11... | collective-permute-start | bytes 3631112 | tf_op jit(solution)/shard_map/ppermute | solution.py:663
  620.9 123.8 %collective-permute-start.9 = (bf16[2,2,197,768]{3,1,2,0:T(2,128)(2,1)}, bf16[2,2,197,768]{3,1,2,0:T(2,128)(2,1)}, u32[]{:S(2)}, u32[]{:S(2)}) collective-permute-start(bf16[2,2,197,768]{3,1,2,0:T(2,128)(2,1)} %copy.147), channel_id=1, source_target_pairs={{0,1},{1,0},{2,3},{3,2},{4,5},{5,4},{6,7},{7,6},{8,9},{9,8},{10,11... | collective-permute-start | bytes 3631112 | tf_op jit(solution)/shard_map/ppermute | solution.py:663
  798.8 63.3 %collective-permute-start.13 = (f32[48,1,384]{2,0,1:T(8,128)S(1)}, f32[48,1,384]{2,0,1:T(8,128)S(1)}, u32[]{:S(2)}, u32[]{:S(2)}) collective-permute-start(f32[48,1,384]{2,0,1:T(8,128)S(1)} %bitcast.193), channel_id=1, source_target_pairs={{0,1},{1,0},{2,3},{3,2},{4,5},{5,4},{6,7},{7,6},{8,9},{9,8},{10,11... | collective-permute-start | bytes 221192 | tf_op jit(solution)/shard_map/ppermute | solution.py:663
  860.5 4.4 collective-permute-start.14
  932.4 72.8 %collective-permute-start.11 = (f32[48,3,384]{2,0,1:T(8,128)S(1)}, f32[48,3,384]{2,0,1:T(8,128)S(1)}, u32[]{:S(2)}, u32[]{:S(2)}) collective-permute-start(f32[48,3,384]{2,0,1:T(8,128)S(1)} %bitcast.190), channel_id=1, source_target_pairs={{0,1},{1,0},{2,3},{3,2},{4,5},{5,4},{6,7},{7,6},{8,9},{9,8},{10,11... | collective-permute-start | bytes 663560 | tf_op jit(solution)/shard_map/ppermute | solution.py:663
  1003.8 6.0 collective-permute-start.12
  1083.0 80.1 %collective-permute-start.16 = (f32[48,1,1536]{2,0,1:T(8,128)S(1)}, f32[48,1,1536]{2,0,1:T(8,128)S(1)}, u32[]{:S(2)}, u32[]{:S(2)}) collective-permute-start(f32[48,1,1536]{2,0,1:T(8,128)S(1)} %bitcast.188), channel_id=1, source_target_pairs={{0,1},{1,0},{2,3},{3,2},{4,5},{5,4},{6,7},{7,6},{8,9},{9,8},{10,11... | collective-permute-start | bytes 884744 | tf_op jit(solution)/shard_map/ppermute | solution.py:663
  1161.6 7.8 collective-permute-start.15
  1277.4 115.2 %copy-start.19 = (f32[2,2,768]{2,1,0:T(2,128)S(1)}, f32[2,2,768]{2,1,0:T(2,128)}, u32[]{:S(2)}) copy-start(f32[2,2,768]{2,1,0:T(2,128)} %get-tuple-element.238) | copy-start | bytes 36868
  1277.4 115.8 %copy-start.24 = (f32[768]{0:T(1024)S(1)}, f32[768]{0:T(1024)}, u32[]{:S(2)}) copy-start(f32[768]{0:T(1024)} %get-tuple-element.246) | copy-start | bytes 9220
  1277.4 116.4 %copy-start.18 = (f32[768,4]{0,1:T(4,128)S(1)}, f32[768,4]{0,1:T(4,128)}, u32[]{:S(2)}) copy-start(f32[768,4]{0,1:T(4,128)} %get-tuple-element.247) | copy-start | bytes 36868
  1277.4 117.0 %copy-start.17 = (f32[4,768]{1,0:T(4,128)S(1)}, f32[4,768]{1,0:T(4,128)}, u32[]{:S(2)}) copy-start(f32[4,768]{1,0:T(4,128)} %get-tuple-element.251) | copy-start | bytes 36868
  (15 other events, 21.1 us)
Sparse Core Ops, SparseCore 0:
  17.7 54.6 all-gather.4
  75.3 80.0 all-gather.6
  158.2 51.3 all-gather.8
  211.7 97.5 all-gather.10
  608.1 124.7 all-reduce.9
  737.4 60.2 reduce-scatter.12
  802.3 57.0 reduce-scatter.14
  863.8 67.0 reduce-scatter.8
  935.2 66.9 reduce-scatter.10
  1006.4 74.4 reduce-scatter.18
  1084.8 74.6 reduce-scatter.16
  1164.0 110.3 reduce-scatter.20
  1278.5 111.0 reduce-scatter.22

commit v2 on v1

--- a/solution.py
+++ b/solution.py
@@ -72,14 +72,24 @@
     return 0.5 * preact * (1.0 + jnp.tanh(inner))
 
 
-def call(kernel, grid, in_specs, out_specs, out_shape, scratch, flops, traffic, name):
-    return pl.pallas_call(
-        kernel,
-        grid=grid,
-        in_specs=in_specs,
-        out_specs=out_specs,
+def call(kernel, grid, in_specs, out_specs, out_shape, scratch, flops, traffic, name,
+         after=(), prefetch=0):
+    taken = prefetch + len(in_specs)
+    skipped = len(after)
+
+    def body(*refs):
+        kernel(*refs[:taken], *refs[taken + skipped :])
+
+    made = pl.pallas_call(
+        body,
+        grid_spec=pltpu.PrefetchScalarGridSpec(
+            num_scalar_prefetch=prefetch,
+            grid=grid,
+            in_specs=list(in_specs) + [pl.BlockSpec(memory_space=pl.ANY)] * skipped,
+            out_specs=out_specs,
+            scratch_shapes=scratch,
+        ),
         out_shape=out_shape,
-        scratch_shapes=scratch,
         name=name,
         compiler_params=pltpu.CompilerParams(
             vmem_limit_bytes=VMEM_LIMIT,
@@ -89,6 +99,27 @@
             flops=int(flops), bytes_accessed=int(traffic), transcendentals=0
         ),
     )
+    return lambda *args: made(*args, *after)
+
+
+def grad_shape(devices, width, columns):
+    rows = width // devices
+    if rows % ROW_PAD:
+        return (2, width, columns)
+    return (devices, 2, rows, columns)
+
+
+def grad_block(shape, columns, index):
+    block = shape[:-1] + (columns,)
+    zeros = (0,) * (len(shape) - 1)
+    return pl.BlockSpec(block, lambda *at: zeros + (index(*at),))
+
+
+def put_grad(ref, part, cols, value):
+    if len(ref.shape) == 3:
+        ref[part, :, cols] = value
+    else:
+        ref[:, part, :, cols] = value.reshape(ref.shape[0], ref.shape[2], value.shape[1])
 
 
 def whole(shape):
@@ -166,14 +197,22 @@
         wt_ref[...] = jnp.where(lanes == 0, first, jnp.where(lanes == 1, second, 0.0))
 
 
-def attention_forward(hidden, gain, shift, weights, qkv_bias, out_bias, length, pad, router=None):
+def layer_block(width, layer):
+    return pl.BlockSpec(
+        (width, 4 * width), lambda *_: (0, layer), pipeline_mode=pl.Buffered(1)
+    )
+
+
+def attention_forward(
+    hidden, gain, shift, weights, layer, qkv_bias, out_bias, length, pad, router=None
+):
     rows, width = hidden.shape
     heads = width // HD
     block = rows // 2
     lse_rows = round_up(heads, 8)
     images = block // pad
     in_specs = [
-        rows_of(block, width), whole((1, width)), whole((1, width)), whole((width, 4 * width)),
+        rows_of(block, width), whole((1, width)), whole((1, width)), layer_block(width, layer),
         whole((1, 3 * width)), whole((1, width)),
     ]
     args = [hidden, gain, shift, weights, qkv_bias, out_bias]
@@ -208,22 +247,15 @@
     )(*args)
 
 
-def attn_bwd_kernel(
-    length, pad, heads,
-    da_ref, h_ref, g_ref, b_ref, w_ref, qkv_ref, lse_ref, o_ref,
-    dh_ref, dwq_ref, dwo_ref, dqb_ref, dob_ref, dg_ref, db_ref,
-    grad_sc, dqkv_sc, wq_acc, wo_acc,
+def attn_core_kernel(
+    length, pad, heads, da_ref, wo_ref, qkv_ref, lse_ref, dqkv_ref, low_ref, grad_sc,
 ):
-    step_id = pl.program_id(0)
-    last = pl.num_programs(0) - 1
-    width = h_ref.shape[1]
-    images = h_ref.shape[0] // pad
+    width = da_ref.shape[1]
+    images = da_ref.shape[0] // pad
     pairs = heads // 2
-    incoming = da_ref[...]
-    low = incoming.astype(BF)
-    out_bias_grad = jnp.sum(low.astype(F32), axis=0, keepdims=True)
-    out_grad_part = mm_at(low, o_ref[...])
-    grad_sc[...] = mm(low, w_ref[:, 3 * width :]).astype(BF)
+    low = da_ref[...].astype(BF)
+    low_ref[...] = low
+    grad_sc[...] = mm(low, wo_ref[...]).astype(BF)
     lane = lax.broadcasted_iota(jnp.int32, (pad, 2 * HD), 1)
     key_row = lax.broadcasted_iota(jnp.int32, (pad, pad), 0)
 
@@ -255,92 +287,115 @@
                 mm(probs.astype(BF), mixed),
             ))
         for part in range(3):
-            dqkv_sc[rows, col(part)] = jnp.where(
+            dqkv_ref[rows, col(part)] = jnp.where(
                 lane < HD, parts[0][part], parts[1][part]
             ).astype(BF)
         return carry
 
     lax.fori_loop(0, images * pairs, pair_step, 0)
-    unit, scale = norm_parts(h_ref[...])
-    normed = (unit * g_ref[...] + b_ref[...]).astype(BF)
-    normed_grad = None
-    bias_parts = []
-    first = step_id == 0
-    for part in range(3):
-        cols = slice(part * width, (part + 1) * width)
-        grads = dqkv_sc[:, cols]
-        term = mm_bt(grads, w_ref[:, cols])
-        normed_grad = term if normed_grad is None else normed_grad + term
-        piece = mm_at(normed, grads)
-        bias_parts.append(jnp.sum(grads.astype(F32), axis=0, keepdims=True))
-
-        @pl.when(first)
-        def _():
-            wq_acc[:, cols] = piece
-
-        @pl.when(step_id == last)
-        def _():
-            dwq_ref[:, cols] = (wq_acc[:, cols] + piece).astype(BF)
-
-    hidden_grad, gain_grad, shift_grad = norm_pull(unit, scale, g_ref[...], normed_grad)
-    dh_ref[...] = incoming + hidden_grad
-
-    @pl.when(first)
-    def _():
-        wo_acc[...] = out_grad_part
-        dob_ref[...] = out_bias_grad
-        dg_ref[...] = gain_grad
-        db_ref[...] = shift_grad
-        for part in range(3):
-            dqb_ref[:, part * width : (part + 1) * width] = bias_parts[part]
-
-    @pl.when(step_id == last)
-    def _():
-        dwo_ref[...] = (wo_acc[...] + out_grad_part).astype(BF)
-        dob_ref[...] += out_bias_grad
-        dg_ref[...] += gain_grad
-        db_ref[...] += shift_grad
-        for part in range(3):
-            dqb_ref[:, part * width : (part + 1) * width] += bias_parts[part]
-
-
-def attention_back(incoming, hidden, gain, shift, weights, stored, length, pad):
-    qkv, lse, mixed = stored
-    rows, width = hidden.shape
+
+
+def attention_core_back(incoming, weights, layer, stored, length, pad, which, after=()):
+    qkv, lse, _ = stored
+    rows, width = incoming.shape
     heads = width // HD
     block = rows // 2
     images = block // pad
     lse_rows = lse.shape[1]
     return call(
-        functools.partial(attn_bwd_kernel, length, pad, heads),
-        (2,),
+        functools.partial(attn_core_kernel, length, pad, heads),
+        (1,),
         [
-            rows_of(block, width), rows_of(block, width), whole((1, width)), whole((1, width)),
-            whole((width, 4 * width)), rows_of(block, 3 * width),
-            pl.BlockSpec((images, lse_rows, pad), lambda step: (step, 0, 0)),
-            rows_of(block, width),
+            pl.BlockSpec((block, width), lambda step: (which, 0)),
+            pl.BlockSpec((width, width), lambda step: (0, 4 * layer + 3)),
+            pl.BlockSpec((block, 3 * width), lambda step: (which, 0)),
+            pl.BlockSpec((images, lse_rows, pad), lambda step: (which, 0, 0)),
+        ],
+        [whole((block, 3 * width)), whole((block, width))],
+        [
+            jax.ShapeDtypeStruct((block, 3 * width), BF),
+            jax.ShapeDtypeStruct((block, width), BF),
+        ],
+        [pltpu.VMEM((block, width), BF)],
+        2.0 * block * width * width + 20.0 * block * pad * width * 4, 8.0e6, "attn_core",
+        after,
+    )(incoming, weights, qkv, lse)
+
+
+def attn_grad_kernel(
+    da_ref, h_ref, g_ref, b_ref, w_ref, dq0_ref, dq1_ref, low0_ref, low1_ref, o_ref,
+    dh_ref, dw_ref, dqb_ref, dob_ref, dg_ref, db_ref,
+):
+    width = h_ref.shape[1]
+    block = dq0_ref.shape[0]
+    gain = g_ref[...]
+    unit, scale = norm_parts(h_ref[...])
+    normed = (unit * gain + b_ref[...]).astype(BF)
+    half = (slice(0, block), slice(block, 2 * block))
+    normed_grad = [None, None]
+    for part in range(3):
+        cols = slice(part * width, (part + 1) * width)
+        piece = None
+        sums = None
+        for side, ref in enumerate((dq0_ref, dq1_ref)):
+            grads = ref[:, cols]
+            term = mm_bt(grads, w_ref[:, cols])
+            normed_grad[side] = term if part == 0 else normed_grad[side] + term
+            outer = mm_at(normed[half[side]], grads)
+            total = jnp.sum(grads.astype(F32), axis=0, keepdims=True)
+            piece = outer if side == 0 else piece + outer
+            sums = total if side == 0 else sums + total
+        at = (part % 2) * width
+        put_grad(dw_ref, part // 2, slice(at, at + width), piece.astype(BF))
+        dqb_ref[:, cols] = sums
+    low0, low1 = low0_ref[...], low1_ref[...]
+    piece = mm_at(low0, o_ref[half[0], :]) + mm_at(low1, o_ref[half[1], :])
+    put_grad(dw_ref, 1, slice(width, 2 * width), piece.astype(BF))
+    dob_ref[...] = jnp.sum(low0.astype(F32), axis=0, keepdims=True) + jnp.sum(
+        low1.astype(F32), axis=0, keepdims=True
+    )
+    for side in range(2):
+        hidden_grad, gain_grad, shift_grad = norm_pull(
+            unit[half[side]], scale[half[side]], gain, normed_grad[side]
+        )
+        dh_ref[half[side], :] = da_ref[half[side], :] + hidden_grad
+        if side == 0:
+            dg_ref[...] = gain_grad
+            db_ref[...] = shift_grad
+        else:
+            dg_ref[...] += gain_grad
+            db_ref[...] += shift_grad
+
+
+def attention_grad(
+    incoming, hidden, gain, shift, weights, layer, cores, mixed, devices, after=()
+):
+    rows, width = hidden.shape
+    shape = grad_shape(devices, width, 2 * width)
+    block = rows // 2
+    return call(
+        attn_grad_kernel, (1,),
+        [
+            whole((rows, width)), whole((rows, width)), whole((1, width)), whole((1, width)),
+            layer_block(width, layer), whole((block, 3 * width)), whole((block, 3 * width)),
+            whole((block, width)), whole((block, width)), whole((rows, width)),
         ],
         [
-            rows_of(block, width), whole((width, 3 * width)), whole((width, width)),
-            whole((1, 3 * width)), whole((1, width)), whole((1, width)), whole((1, width)),
+            whole((rows, width)), whole(shape), whole((1, 3 * width)),
+            whole((1, width)), whole((1, width)), whole((1, width)),
         ],
         [
             jax.ShapeDtypeStruct((rows, width), F32),
-            jax.ShapeDtypeStruct((width, 3 * width), BF),
-            jax.ShapeDtypeStruct((width, width), BF),
+            jax.ShapeDtypeStruct(shape, BF),
             jax.ShapeDtypeStruct((1, 3 * width), F32),
             jax.ShapeDtypeStruct((1, width), F32),
             jax.ShapeDtypeStruct((1, width), F32),
             jax.ShapeDtypeStruct((1, width), F32),
         ],
-        [
-            pltpu.VMEM((block, width), BF),
-            pltpu.VMEM((block, 3 * width), BF),
-            pltpu.VMEM((width, 3 * width), F32),
-            pltpu.VMEM((width, width), F32),
-        ],
-        16.0 * rows * width * width + 40.0 * rows * pad * width, 25.0e6, "attn_bwd",
-    )(incoming, hidden, gain, shift, weights, qkv, lse, mixed)
+        [],
+        14.0 * rows * width * width, 25.0e6, "attn_grad", after,
+    )(incoming, hidden, gain, shift, weights, cores[0][0], cores[1][0], cores[0][1],
+      cores[1][1], mixed)
 
 
 def dense_fwd_kernel(a_ref, g_ref, b_ref, win_ref, wout_ref, bin_ref, bout_ref, x_ref, m_sc, acc):
@@ -361,16 +416,17 @@
         x_ref[...] = acc[...]
 
 
-def dense_forward(hidden, gain, shift, weights, in_bias, out_bias):
+def dense_forward(hidden, gain, shift, weights, at, in_bias, out_bias):
     rows, width = hidden.shape
     ff = in_bias.shape[1]
     steps = ff // FF_BLOCK
+    start = at // FF_BLOCK
     return call(
         dense_fwd_kernel, (steps,),
         [
             whole((rows, width)), whole((1, width)), whole((1, width)),
-            pl.BlockSpec((width, FF_BLOCK), lambda c: (0, c)),
-            pl.BlockSpec((width, FF_BLOCK), lambda c: (0, steps + c)),
+            pl.BlockSpec((width, FF_BLOCK), lambda c: (0, start + c)),
+            pl.BlockSpec((width, FF_BLOCK), lambda c: (0, start + steps + c)),
             pl.BlockSpec((1, FF_BLOCK), lambda c: (0, c)),
             whole((1, width)),
         ],
@@ -382,20 +438,23 @@
 
 
 def dense_bwd_kernel(
-    dx_ref, a_ref, g_ref, b_ref, win_ref, wout_ref, bin_ref,
-    da_ref, dwin_ref, dwout_ref, dbin_ref, dbout_ref, dg_ref, db_ref,
-    m_sc, low_sc, acc,
+    last_call, dx_ref, a_ref, g_ref, b_ref, win_ref, wout_ref, bin_ref, *rest,
 ):
+    if last_call:
+        part_ref, da_ref, dw_ref, dbin_ref, dbout_ref, dg_ref, db_ref, m_sc, low_sc, acc = rest
+    else:
+        part_ref, dw_ref, dbin_ref, m_sc, low_sc, acc = rest
     step = pl.program_id(0)
 
     @pl.when(step == 0)
     def _():
         unit, _ = norm_parts(a_ref[...])
         m_sc[...] = (unit * g_ref[...] + b_ref[...]).astype(BF)
-        low = dx_ref[...].astype(BF)
-        low_sc[...] = low
-        dbout_ref[...] = jnp.sum(low.astype(F32), axis=0, keepdims=True)
-        acc[...] = jnp.zeros_like(acc)
+        low_sc[...] = dx_ref[...].astype(BF)
+        if last_call:
+            acc[...] = part_ref[...]
+        else:
+            acc[...] = jnp.zeros_like(acc)
 
     normed = m_sc[...]
     low = low_sc[...]
@@ -403,65 +462,80 @@
     active, slope = gelu_pair(preact)
     preact_grad = (slope * mm(low, wout_ref[...])).astype(BF)
     dbin_ref[...] = jnp.sum(preact_grad.astype(F32), axis=0, keepdims=True)
-    dwout_ref[...] = mm_at(low, active.astype(BF)).astype(BF)
-    dwin_ref[...] = mm_at(normed, preact_grad).astype(BF)
+    every = slice(None)
+    put_grad(dw_ref, 1, every, mm_at(low, active.astype(BF)).astype(BF))
+    put_grad(dw_ref, 0, every, mm_at(normed, preact_grad).astype(BF))
     acc[...] += mm_bt(preact_grad, win_ref[...])
 
     @pl.when(step == pl.num_programs(0) - 1)
     def _():
+        if not last_call:
+            part_ref[...] = acc[...]
+            return
         unit, scale = norm_parts(a_ref[...])
         hidden_grad, gain_grad, shift_grad = norm_pull(unit, scale, g_ref[...], acc[...])
         da_ref[...] = dx_ref[...] + hidden_grad
+        dbout_ref[...] = jnp.sum(low_sc[...].astype(F32), axis=0, keepdims=True)
         dg_ref[...] = gain_grad
         db_ref[...] = shift_grad
 
 
-def dense_back(incoming, hidden, gain, shift, weights, in_bias):
+def dense_back(incoming, hidden, gain, shift, weights, at, in_bias, devices, part, after=()):
     rows, width = hidden.shape
     ff = in_bias.shape[1]
-    steps = ff // FF_BLOCK
-    col_block = pl.BlockSpec((width, FF_BLOCK), lambda c: (0, c))
+    steps = ff // FF_BLOCK // 2
+    last_call = part is not None
+    first = steps if last_call else 0
+    shape = grad_shape(devices, width, ff // 2)
+    start = at // FF_BLOCK + first
+    in_specs = [
+        whole((rows, width)), whole((rows, width)), whole((1, width)), whole((1, width)),
+        pl.BlockSpec((width, FF_BLOCK), lambda c: (0, start + c)),
+        pl.BlockSpec((width, FF_BLOCK), lambda c: (0, start + 2 * steps + c)),
+        pl.BlockSpec((1, FF_BLOCK), lambda c: (0, first + c)),
+    ]
+    wide = jax.ShapeDtypeStruct((rows, width), F32)
+    short = jax.ShapeDtypeStruct((1, width), F32)
+    grads = [
+        jax.ShapeDtypeStruct(shape, BF), jax.ShapeDtypeStruct((1, ff // 2), F32),
+    ]
+    grad_specs = [
+        grad_block(shape, FF_BLOCK, lambda c: c), pl.BlockSpec((1, FF_BLOCK), lambda c: (0, c)),
+    ]
+    args = [incoming, hidden, gain, shift, weights, weights, in_bias]
+    if last_call:
+        in_specs.append(whole((rows, width)))
+        args.append(part)
+        out_specs = [whole((rows, width))] + grad_specs + [whole((1, width))] * 3
+        out_shape = [wide] + grads + [short] * 3
+    else:
+        out_specs = [whole((rows, width))] + grad_specs
+        out_shape = [wide] + grads
     return call(
-        dense_bwd_kernel, (steps,),
-        [
-            whole((rows, width)), whole((rows, width)), whole((1, width)), whole((1, width)),
-            col_block,
-            pl.BlockSpec((width, FF_BLOCK), lambda c: (0, steps + c)),
-            pl.BlockSpec((1, FF_BLOCK), lambda c: (0, c)),
-        ],
-        [
-            whole((rows, width)), col_block, col_block,
-            pl.BlockSpec((1, FF_BLOCK), lambda c: (0, c)),
-            whole((1, width)), whole((1, width)), whole((1, width)),
-        ],
-        [
-            jax.ShapeDtypeStruct((rows, width), F32),
-            jax.ShapeDtypeStruct((width, ff), BF),
-            jax.ShapeDtypeStruct((width, ff), BF),
-            jax.ShapeDtypeStruct((1, ff), F32),
-            jax.ShapeDtypeStruct((1, width), F32),
-            jax.ShapeDtypeStruct((1, width), F32),
-            jax.ShapeDtypeStruct((1, width), F32),
-        ],
+        functools.partial(dense_bwd_kernel, last_call), (steps,), in_specs, out_specs, out_shape,
         [
             pltpu.VMEM((rows, width), BF), pltpu.VMEM((rows, width), BF),
             pltpu.VMEM((rows, width), F32),
         ],
-        10.0 * rows * width * ff, 35.0e6, "dense_bwd",
-    )(incoming, hidden, gain, shift, weights, weights, in_bias)
+        5.0 * rows * width * ff, 25.0e6, "dense_bwd", after,
+    )(*args)
 
 
 def moe_kernel(
-    micro, capp,
+    micro, capp, base, resumed,
     rb_own, rb_oth, og_own, og_oth, dr_ref, dc_own, dc_oth, w_ref,
-    win_ref, wout_ref, bin_ref, bout_ref,
-    yc_own, yc_oth, rc_own, rc_oth, dg_own, dg_oth,
-    dwin_ref, dwout_ref, dbin_ref, dbout_ref,
-    b_sc, og_sc, dy_sc, w_sc, y_acc, r_acc, yo_acc, yt_acc, ro_acc, rt_acc,
+    win_ref, wout_ref, bin_ref, bout_ref, *rest,
 ):
-    expert = pl.program_id(0)
+    before = rest[:6] if resumed else ()
+    (
+        yc_own, yc_oth, rc_own, rc_oth, dg_own, dg_oth,
+        dw_ref, dbin_ref, dbout_ref,
+        b_sc, og_sc, dy_sc, w_sc, y_acc, r_acc, yo_acc, yt_acc, ro_acc, rt_acc,
+    ) = rest[len(before):]
+    expert = pl.program_id(0) + base
+    fresh = pl.program_id(0) == 0
     chunk = pl.program_id(1)
-    last_expert = expert == pl.num_programs(0) - 1
+    last_expert = pl.program_id(0) == pl.num_programs(0) - 1
     last_chunk = chunk == pl.num_programs(1) - 1
     half = rb_own.shape[1]
 
@@ -500,8 +574,19 @@
     dbin_ref[0] = jnp.sum(preact_grad.astype(F32), axis=0, keepdims=True)
     y_acc[...] += mm_bt(active, wout_ref[...])
     r_acc[...] += mm_bt(preact_grad, win_ref[...])
-    dwout_ref[...] = mm_at(low, active).astype(BF)
-    dwin_ref[...] = mm_at(tokens, preact_grad).astype(BF)
+    every = slice(None)
+    put_grad(dw_ref, 1, every, mm_at(low, active).astype(BF))
+    put_grad(dw_ref, 0, every, mm_at(tokens, preact_grad).astype(BF))
+
+    if resumed:
+        @pl.when(fresh & (chunk == 0))
+        def _():
+            yo_acc[...] = before[0][...].astype(F32)
+            yt_acc[...] = before[1][...].astype(F32)
+            ro_acc[...] = before[2][...].astype(F32)
+            rt_acc[...] = before[3][...].astype(F32)
+            dg_own[...] = before[4][...]
+            dg_oth[...] = before[5][...]
 
     @pl.when(last_chunk)
     def _():
@@ -525,13 +610,19 @@
                 r_new = mm(low_pick, rows_grad)
                 d_new = jnp.dot(pick, dots, precision=EXACT, preferred_element_type=F32)
 
-                @pl.when(expert == 0)
+                if resumed:
+                    yc[m] += y_new
+                    rc[m] += r_new
+                    dg[m] += d_new
+                    continue
+
+                @pl.when(fresh)
                 def _():
                     yc[m] = y_new
                     rc[m] = r_new
                     dg[m] = d_new
 
-                @pl.when(expert > 0)
+                @pl.when(jnp.logical_not(fresh))
                 def _():
                     yc[m] += y_new
                     rc[m] += r_new
@@ -546,44 +637,41 @@
 
 
 def mixture(rows_own, rows_oth, grad_own, grad_oth, place_rows, place_own, place_oth, gates,
-            weights, in_bias, out_bias, capp):
+            weights, in_bias, out_bias, capp, base, count, devices, before=(), after=()):
     micro, half, width = rows_own.shape
     experts, _, ff = in_bias.shape
     steps = ff // FF_BLOCK
     blocks = experts * steps
+    first = base * steps
     lanes = 128
     slots = micro * capp
     w_block = (width, FF_BLOCK)
     group = (micro, half, width)
+    dots = (micro, half, lanes)
+    shape = grad_shape(devices, width, count * ff)
+    sums = [jax.ShapeDtypeStruct(group, BF)] * 4 + [jax.ShapeDtypeStruct(dots, F32)] * 2
+    sum_specs = [whole(group)] * 4 + [whole(dots)] * 2
     return call(
-        functools.partial(moe_kernel, micro, capp),
-        (experts, steps),
+        functools.partial(moe_kernel, micro, capp, base, bool(before)),
+        (count, steps),
         [
             whole(group), whole(group), whole(group), whole(group),
             whole(place_rows.shape), whole(place_own.shape), whole(place_oth.shape),
             whole(gates.shape),
-            pl.BlockSpec(w_block, lambda e, c: (0, e * steps + c)),
-            pl.BlockSpec(w_block, lambda e, c: (0, blocks + e * steps + c)),
+            pl.BlockSpec(w_block, lambda e, c: (0, first + e * steps + c)),
+            pl.BlockSpec(w_block, lambda e, c: (0, blocks + first + e * steps + c)),
+            pl.BlockSpec((1, 1, FF_BLOCK), lambda e, c: (base + e, 0, c)),
+            pl.BlockSpec((1, 1, width), lambda e, c: (base + e, 0, 0)),
+        ] + (sum_specs if before else []),
+        sum_specs + [
+            grad_block(shape, FF_BLOCK, lambda e, c: e * steps + c),
             pl.BlockSpec((1, 1, FF_BLOCK), lambda e, c: (e, 0, c)),
             pl.BlockSpec((1, 1, width), lambda e, c: (e, 0, 0)),
         ],
-        [
-            whole(group), whole(group), whole(group), whole(group),
-            whole((micro, half, lanes)), whole((micro, half, lanes)),
-            pl.BlockSpec(w_block, lambda e, c: (0, e * steps + c)),
-            pl.BlockSpec(w_block, lambda e, c: (0, e * steps + c)),
-            pl.BlockSpec((1, 1, FF_BLOCK), lambda e, c: (e, 0, c)),
-            pl.BlockSpec((1, 1, width), lambda e, c: (e, 0, 0)),
-        ],
-        [
-            jax.ShapeDtypeStruct(group, BF), jax.ShapeDtypeStruct(group, BF),
-            jax.ShapeDtypeStruct(group, BF), jax.ShapeDtypeStruct(group, BF),
-            jax.ShapeDtypeStruct((micro, half, lanes), F32),
-            jax.ShapeDtypeStruct((micro, half, lanes), F32),
-            jax.ShapeDtypeStruct((width, experts * ff), BF),
-            jax.ShapeDtypeStruct((width, experts * ff), BF),
-            jax.ShapeDtypeStruct((experts, 1, ff), F32),
-            jax.ShapeDtypeStruct((experts, 1, width), F32),
+        sums + [
+            jax.ShapeDtypeStruct(shape, BF),
+            jax.ShapeDtypeStruct((count, 1, ff), F32),
+            jax.ShapeDtypeStruct((count, 1, width), F32),
         ],
         [
             pltpu.VMEM((slots, width), BF), pltpu.VMEM((slots, width), BF),
@@ -592,20 +680,20 @@
             pltpu.VMEM(group, F32), pltpu.VMEM(group, F32),
             pltpu.VMEM(group, F32), pltpu.VMEM(group, F32),
         ],
-        12.0 * slots * experts * width * ff + 16.0 * experts * micro * capp * half * width,
-        60.0e6, "experts",
+        12.0 * slots * count * width * ff + 16.0 * count * micro * capp * half * width,
+        15.0e6 * count, "experts", after,
     )(rows_own, rows_oth, grad_own, grad_oth, place_rows, place_own, place_oth, gates,
-      weights, weights, in_bias, out_bias)
+      weights, weights, in_bias, out_bias, *before)
 
 
 def gate_bwd_kernel(
-    a_ref, og_ref, yo_ref, yr_ref, ro_ref, rr_ref, do_ref, dr_ref, gp_ref, rt_ref, g_ref, b_ref,
-    out_ref, da_ref, drt_ref, dg_ref, db_ref,
+    a_ref, og_ref, yt_ref, ro_ref, rr_ref, do_ref, dr_ref, gp_ref, rt_ref, g_ref, b_ref,
+    y_ref, da_ref, drt_ref, dg_ref, db_ref,
 ):
     step = pl.program_id(0)
     after = a_ref[...]
     incoming = og_ref[...].astype(F32)
-    out_ref[...] = (after + (yo_ref[...].astype(F32) + yr_ref[...].astype(F32))).astype(BF)
+    y_ref[...] = yt_ref[...]
     gates = gp_ref[...]
     gate_grad = do_ref[...] + dr_ref[...]
     logit_grad = gates * (gate_grad - jnp.sum(gates * gate_grad, axis=-1, keepdims=True))
@@ -635,7 +723,7 @@
         db_ref[...] += shift_grad
 
 
-def gate_back(after, incoming, y_own, y_got, r_own, r_got, d_own, d_got, gates, router, gain, shift):
+def gate_back(after, incoming, y_oth, r_own, r_got, d_own, d_got, gates, router, gain, shift):
     rows, width = after.shape
     lanes = gates.shape[1]
     block = rows // 2
@@ -644,7 +732,7 @@
     return call(
         gate_bwd_kernel, (2,),
         [
-            row, row, row, row, row, row, row_low, row_low, row_low,
+            row, row, row, row, row, row_low, row_low, row_low,
             whole((width, lanes)), whole((1, width)), whole((1, width)),
         ],
         [row, row, whole((lanes, width)), whole((1, width)), whole((1, width))],
@@ -656,7 +744,7 @@
             jax.ShapeDtypeStruct((1, width), F32),
         ],
         [], 4.0 * rows * width * lanes, 14.0e6, "gate_bwd",
-    )(after, incoming, y_own, y_got, r_own, r_got, d_own, d_got, gates, router, gain, shift)
+    )(after, incoming, y_oth, r_own, r_got, d_own, d_got, gates, router, gain, shift)
 
 
 def swap(value):
@@ -672,17 +760,128 @@
     return lax.all_gather(share, "dp", axis=0, tiled=True)
 
 
-def scatter_rows(grad):
-    return lax.psum_scatter(grad, "dp", scatter_dimension=0, tiled=True).astype(F32)
-
-
-def join_halves(grad, parts):
-    rows, total = grad.shape
-    width = total // parts // 2
-    halves = grad.reshape(rows, parts, 2, width)
+def chip_ring(chips):
+    if chips == 8:
+        return [0, 2, 4, 6, 7, 5, 3, 1]
+    return list(range(chips))
+
+
+def ring_add_kernel(kind, at_ref, *refs):
+    def chunk(grads, given):
+        return grads[0, 0].astype(F32) + given[0].astype(F32)
+
+    if kind == 0:
+        grads, given, ahead, behind = refs
+        total = chunk(grads, given).astype(BF)
+        ahead[...] = total[0]
+        behind[...] = total[1]
+    elif kind == 3:
+        grads, given, got_a, got_b, out = refs
+        out[...] = chunk(grads, given) + (got_a[...].astype(F32) + got_b[...].astype(F32))
+    else:
+        grads_a, given_a, grads_b, given_b, got_a, got_b, ahead, behind = refs
+        one, two = chunk(grads_a, given_a), chunk(grads_b, given_b)
+        if kind == 1:
+            ahead[0] = (one[0] + got_a[...].astype(F32)).astype(BF)
+            ahead[1] = one[1].astype(BF)
+            behind[0] = two[0].astype(BF)
+            behind[1] = (two[1] + got_b[...].astype(F32)).astype(BF)
+        else:
+            ahead[...] = (one + got_a[...].astype(F32)).astype(BF)
+            behind[...] = (two + got_b[...].astype(F32)).astype(BF)
+
+
+class RingSum:
+    def __init__(self, grad):
+        count = lax.axis_size("dp")
+        self.chips = count // 2
+        self.ring = chip_ring(self.chips)
+        position = [self.ring.index(chip) for chip in range(self.chips)]
+        me = lax.axis_index("dp")
+        self.core = me % 2
+        self.here = jnp.array(position, jnp.int32)[me // 2]
+        self.pieces = grad.reshape((self.chips, 2) + grad.shape[1:])
+        self.away = self.chips // 2
+        sent = lax.dynamic_index_in_dim(self.pieces, 1 - self.core, 1, keepdims=False)
+        self.messages = (sent,)
+        self.given = lax.ppermute(sent, "dp", [(at, at ^ 1) for at in range(count)])
+        self.got = ()
+        self.result = None
+
+    def send(self, value, step):
+        pairs = [
+            (self.ring[at] * 2 + side, self.ring[(at + step) % self.chips] * 2 + side)
+            for at in range(self.chips)
+            for side in range(2)
+        ]
+        return lax.ppermute(value, "dp", pairs)
+
+    def step(self, after=()):
+        table = jnp.array(self.ring, jnp.int32)
+        away = self.away
+        chips = [table[(self.here + away) % self.chips], table[(self.here - away) % self.chips]]
+        places = jnp.stack([self.core, *chips]).astype(jnp.int32)
+        one, rows, columns = self.pieces.shape[2:]
+        shape = (one, rows, columns)
+
+        def chunk_specs(which):
+            return [
+                pl.BlockSpec((1, 1) + shape, lambda _, at: (at[1 + which], at[0], 0, 0, 0)),
+                pl.BlockSpec((1,) + shape, lambda _, at: (at[1 + which], 0, 0, 0)),
+            ]
+
+        far = self.chips // 2
+        kind = 3 if away == 0 else 0 if away == far else 1 if away == far - 1 else 2
+        two_ways = kind in (1, 2)
+        in_specs = chunk_specs(0) + (chunk_specs(1) if two_ways else [])
+        args = [self.pieces, self.given] * (2 if two_ways else 1) + list(self.got)
+        in_specs += [whole(got.shape) for got in self.got]
+        out = shape if kind else shape[1:]
+        kinds = [jax.ShapeDtypeStruct(out, F32 if kind == 3 else BF)] * (1 if kind == 3 else 2)
+        sums = call(
+            functools.partial(ring_add_kernel, kind), (1,), in_specs,
+            [whole(out)] * len(kinds), kinds, [], 0, 1.0e6, "ring_add", after, prefetch=1,
+        )(places, *args)
+        self.away -= 1
+        if kind == 3:
+            self.result = sums[0]
+            self.messages = ()
+            return
+        self.messages = tuple(sums)
+        self.got = (self.send(sums[0], 1), self.send(sums[1], -1))
+
+
+class PlainSum:
+    def __init__(self, grad):
+        axis = 1 if grad.ndim == 3 else 0
+        done = lax.psum_scatter(grad, "dp", scatter_dimension=axis, tiled=True)
+        self.result = done.reshape((2,) + done.shape[-2:]).astype(F32)
+        self.messages = ()
+
+    def step(self, after=()):
+        return
+
+
+def sum_small(vector):
+    vector = vector + swap(vector)
+    count = lax.axis_size("dp")
+    step = 1
+    while step < count:
+        vector = vector + lax.ppermute(vector, "dp", [(at, at ^ step) for at in range(count)])
+        step *= 2
+    return vector
+
+
+def join_halves(parts):
     mine = lax.axis_index("tensor")
-    kept = lax.dynamic_index_in_dim(halves, mine, 2, keepdims=False)
-    sent = lax.dynamic_index_in_dim(halves, 1 - mine, 2, keepdims=False)
+    rows = parts[0].shape[0]
+    pairs = [part.reshape(rows, 2, -1) for part in parts]
+    sent = jnp.concatenate(
+        [lax.dynamic_index_in_dim(pair, 1 - mine, 1, keepdims=False) for pair in pairs], axis=1
+    )
+    kept = jnp.concatenate(
+        [lax.dynamic_index_in_dim(pair, mine, 1, keepdims=False) for pair in pairs], axis=1
+    )
     return kept + swap(sent)
 
 
@@ -711,26 +910,33 @@
             [qkv_weight[layer].reshape(share_rows, -1), out_weight[layer]], axis=1
         )
 
-    def attn_full(layer):
-        mine = attn_share(layer)
-        other = swap(mine)
-        full = in_order(mine.reshape(share_rows, 4, -1), other.reshape(share_rows, 4, -1), 2)
-        return gather_rows(full.reshape(share_rows, -1))
-
-    attn_one = attn_full(0)
-    dense_mine = jnp.stack([mlp_in, mlp_out], axis=1)
-    dense_full = in_order(dense_mine, swap(dense_mine), 2)
-    dense_w = gather_rows(dense_full.reshape(share_rows, -1))
-    attn_two = attn_full(1)
+    first_mine = jnp.concatenate(
+        [attn_share(0), attn_share(1), mlp_in, mlp_out], axis=1
+    )
+    first_other = swap(first_mine)
+    attn_columns = 8 * (width // 2)
+
+    def whole_columns(value, other, parts):
+        pair = in_order(
+            value.reshape(share_rows, parts, -1), other.reshape(share_rows, parts, -1), 2
+        )
+        return pair.reshape(share_rows, -1)
+
+    first_w = gather_rows(
+        jnp.concatenate(
+            [
+                whole_columns(first_mine[:, :attn_columns], first_other[:, :attn_columns], 8),
+                whole_columns(first_mine[:, attn_columns:], first_other[:, attn_columns:], 2),
+            ],
+            axis=1,
+        )
+    )
+    dense_at = 2 * attn_columns
     expert_w = gather_rows(
         jnp.concatenate(
             [expert_in.reshape(share_rows, -1), expert_out.reshape(share_rows, -1)], axis=1
         )
     )
-
-    def both(vector):
-        joined = in_order(vector, swap(vector), vector.ndim - 1)
-        return joined.reshape(vector.shape[:-1] + (-1,))
 
     biases = jnp.concatenate([qkv_bias.reshape(-1), mlp_in_bias])
     biases_other = swap(biases)
@@ -779,51 +985,103 @@
         return vector.reshape(1, -1)
 
     qkv_one, lse_one, mix_one, after_one = attention_forward(
-        hidden, row(norm_gain[0, 0]), row(row_bias[0, 0]), attn_one, qkv_bias_row(0),
+        hidden, row(norm_gain[0, 0]), row(row_bias[0, 0]), first_w, 0, qkv_bias_row(0),
         row(row_bias[0, 2]), length, pad,
     )
     after_ffn = dense_forward(
-        after_one, row(norm_gain[0, 1]), row(row_bias[0, 1]), dense_w, mlp_bias_full,
+        after_one, row(norm_gain[0, 1]), row(row_bias[0, 1]), first_w, dense_at, mlp_bias_full,
         row(mlp_out_bias),
     )
     qkv_two, lse_two, mix_two, after_two, rows_own, gates, chosen = attention_forward(
-        after_ffn, row(norm_gain[1, 0]), row(row_bias[1, 0]), attn_two, qkv_bias_row(1),
+        after_ffn, row(norm_gain[1, 0]), row(row_bias[1, 0]), first_w, 1, qkv_bias_row(1),
         row(row_bias[1, 2]), length, pad,
         (row(norm_gain[1, 1]), row(row_bias[1, 1]), router_wide, select, experts),
     )
     rows_oth = swap(rows_own)
     gate_own = jnp.swapaxes(chosen[:, :2].reshape(micro, half, 2), 1, 2)
     gate_oth = swap(gate_own)
-    (
-        y_own, y_oth, r_own, r_oth, d_own, d_oth, ein_grad, eout_grad, ein_bias, eout_bias,
-    ) = mixture(
-        rows_own.reshape(micro, half, width), rows_oth.reshape(micro, half, width),
-        grad_own, grad_oth, place_rows, place_own, place_oth,
-        jnp.concatenate([gate_own, gate_oth], axis=1),
-        expert_w, expert_in_bias.reshape(experts, 1, -1), expert_out_bias.reshape(experts, 1, -1),
-        capp,
-    )
-    y_got, r_got, d_got = swap(y_oth), swap(r_oth), swap(d_oth)
+    gate_pair = jnp.concatenate([gate_own, gate_oth], axis=1)
+    devices = lax.axis_size("dp")
+    sum_over = PlainSum if len(grad_shape(devices, width, width)) == 3 else RingSum
+    sums, expert_sums, ein_biases, eout_biases = (), [], [], []
+    per_call = experts // 2
+    for base in range(0, experts, per_call):
+        found = mixture(
+            rows_own.reshape(micro, half, width), rows_oth.reshape(micro, half, width),
+            grad_own, grad_oth, place_rows, place_own, place_oth, gate_pair, expert_w,
+            expert_in_bias.reshape(experts, 1, -1), expert_out_bias.reshape(experts, 1, -1),
+            capp, base, per_call, devices, sums,
+        )
+        sums = tuple(found[:6])
+        expert_sums.append(PlainSum(found[6]))
+        ein_biases.append(found[7])
+        eout_biases.append(found[8])
+    y_own, y_oth, r_own, r_oth, d_own, d_oth = sums
+    ein_bias = jnp.concatenate(ein_biases)
+    eout_bias = jnp.concatenate(eout_biases)
+    r_got, d_got = swap(r_oth), swap(d_oth)
 
     def flat(value):
         return value.reshape(rows, value.shape[-1])
 
-    out_own, grad_two, router_grad, gain_moe, shift_moe = gate_back(
-        after_two, flat(grad_own), flat(y_own), flat(y_got), flat(r_own), flat(r_got),
+    y_sent, grad_two, router_grad, gain_moe, shift_moe = gate_back(
+        after_two, flat(grad_own), flat(y_oth), flat(r_own), flat(r_got),
         flat(d_own), flat(d_got), gates, router_wide,
         row(norm_gain[1, 1]), row(row_bias[1, 1]),
     )
-    grad_ffn, wq_two, wo_two, qb_two, ob_two, gain_two, shift_two = attention_back(
-        grad_two, after_ffn, row(norm_gain[1, 0]), row(row_bias[1, 0]), attn_two,
-        (qkv_two, lse_two, mix_two), length, pad,
-    )
-    grad_one, win_grad, wout_grad, in_bias_grad, out_bias_grad, gain_ffn, shift_ffn = dense_back(
-        grad_ffn, after_one, row(norm_gain[0, 1]), row(row_bias[0, 1]), dense_w, mlp_bias_full
-    )
-    grad_zero, wq_one, wo_one, qb_one, ob_one, gain_one, shift_one = attention_back(
-        grad_one, hidden, row(norm_gain[0, 0]), row(row_bias[0, 0]), attn_one,
-        (qkv_one, lse_one, mix_one), length, pad,
-    )
+    y_got = swap(y_sent)
+    out_own = after_two + (flat(y_own).astype(F32) + y_got.astype(F32))
+
+    stored_two = (qkv_two, lse_two, mix_two)
+    cores = [
+        attention_core_back(grad_two, first_w, 1, stored_two, length, pad, which)
+        for which in range(2)
+    ]
+    grad_ffn, w_two, qb_two, ob_two, gain_two, shift_two = attention_grad(
+        grad_two, after_ffn, row(norm_gain[1, 0]), row(row_bias[1, 0]), first_w, 1, cores,
+        mix_two, devices,
+    )
+    sum_two = sum_over(w_two)
+    dense_args = (
+        grad_ffn, after_one, row(norm_gain[0, 1]), row(row_bias[0, 1]), first_w, dense_at,
+        mlp_bias_full, devices,
+    )
+    part, dense_low, in_bias_low = dense_back(*dense_args, None, sum_two.messages)
+    sum_low = sum_over(dense_low)
+    sum_two.step((in_bias_low,))
+    (
+        grad_one, dense_high, in_bias_high, out_bias_grad, gain_ffn, shift_ffn,
+    ) = dense_back(*dense_args, part, sum_two.messages + sum_low.messages)
+    sum_high = sum_over(dense_high)
+    done = (in_bias_high,)
+    sum_two.step(done)
+    sum_low.step(done)
+    stored_one = (qkv_one, lse_one, mix_one)
+    cores = []
+    for which in range(2):
+        flying = sum_two.messages + sum_low.messages + sum_high.messages
+        cores.append(
+            attention_core_back(
+                grad_one, first_w, 0, stored_one, length, pad, which, flying
+            )
+        )
+        done = (cores[-1][1],)
+        sum_two.step(done)
+        sum_low.step(done)
+        sum_high.step(done)
+    flying = sum_two.messages + sum_low.messages + sum_high.messages
+    grad_zero, w_one, qb_one, ob_one, gain_one, shift_one = attention_grad(
+        grad_one, hidden, row(norm_gain[0, 0]), row(row_bias[0, 0]), first_w, 0, cores,
+        mix_one, devices, flying,
+    )
+    sum_one = sum_over(w_one)
+    done = (qb_one,)
+    for _ in range(devices // 2):
+        for chain in (sum_two, sum_low, sum_high, sum_one):
+            if chain.result is None:
+                chain.step(done)
+        done = ()
+    in_bias_grad = jnp.concatenate([in_bias_low, in_bias_high], axis=1)
 
     def images_of(value):
         value = value.astype(BF).reshape(micro, own_images, pad, width)[:, :, :length]
@@ -832,48 +1090,65 @@
     block_output = images_of(out_own)
     input_grad = images_of(grad_zero).astype(F32)
 
-    ein_done = scatter_rows(ein_grad).reshape(expert_in.shape)
-    eout_done = scatter_rows(eout_grad).reshape(expert_out.shape)
-    wq_two_done = join_halves(scatter_rows(wq_two), 3)
-    wo_two_done = join_halves(scatter_rows(wo_two), 1)
-    win_done = join_halves(scatter_rows(win_grad), 1).reshape(mlp_in.shape)
-    wout_done = join_halves(scatter_rows(wout_grad), 1).reshape(mlp_out.shape)
-    wq_one_done = join_halves(scatter_rows(wq_one), 3)
-    wo_one_done = join_halves(scatter_rows(wo_one), 1)
+    expert_grads = jnp.concatenate(
+        [chain.result.reshape(2, share_rows, per_call, -1) for chain in expert_sums], axis=2
+    )
+
+    def attn_done(done):
+        return join_halves(
+            [done[0, :, :width], done[0, :, width:], done[1, :, :width], done[1, :, width:]]
+        )
+
+    attn_grads = [attn_done(sum_one.result), attn_done(sum_two.result)]
+    dense_done = join_halves(
+        [
+            jnp.concatenate([sum_low.result[part], sum_high.result[part]], axis=1)
+            for part in range(2)
+        ]
+    )
+    split_at = 3 * width // 2
 
     place_in = (side == jnp.arange(2)).astype(F32)
     ein_bias_wide = place_in[:, None, None] * ein_bias.reshape(1, experts, -1)
-    small = lax.psum(
-        (
-            jnp.concatenate([gain_one, gain_ffn, gain_two, gain_moe]),
-            jnp.concatenate([shift_one, shift_ffn, ob_one, shift_two, shift_moe, ob_two]),
-            jnp.concatenate([qb_one, qb_two]),
-            in_bias_grad,
-            out_bias_grad,
-            router_grad[:experts],
-            ein_bias_wide,
-            0.5 * eout_bias,
-        ),
-        ("dp", "tensor"),
-    )
-    gain_sum, shift_sum, qb_sum, in_bias_sum, out_bias_sum, router_sum, ein_sum, eout_sum = small
+    late = [gain_one, shift_one, ob_one, qb_one]
+    early = [
+        gain_ffn, gain_two, gain_moe, shift_ffn, shift_two, shift_moe, ob_two, qb_two,
+        in_bias_grad, out_bias_grad, router_grad[:experts], ein_bias_wide, 0.5 * eout_bias,
+    ]
+
+    def sum_list(values):
+        total = sum_small(jnp.concatenate([value.reshape(-1) for value in values]))
+        parts, at = [], 0
+        for value in values:
+            parts.append(total[at : at + value.size].reshape(value.shape))
+            at += value.size
+        return parts
+
+    gain_one, shift_one, ob_one, qb_one = sum_list(late)
+    (
+        gain_ffn, gain_two, gain_moe, shift_ffn, shift_two, shift_moe, ob_two, qb_two,
+        in_bias_sum, out_bias_sum, router_sum, ein_sum, eout_sum,
+    ) = sum_list(early)
+    gain_sum = jnp.concatenate([gain_one, gain_ffn, gain_two, gain_moe])
+    shift_sum = jnp.concatenate([shift_one, shift_ffn, ob_one, shift_two, shift_moe, ob_two])
+    qb_sum = jnp.concatenate([qb_one, qb_two])
     qb_sum = own_half(qb_sum.reshape(2, 3, width), 2)
     return (
         block_output,
         input_grad,
         gain_sum.reshape(norm_gain.shape),
         shift_sum.reshape(row_bias.shape),
-        jnp.stack([wq_one_done, wq_two_done]).reshape(qkv_weight.shape),
+        jnp.stack([part[:, :split_at] for part in attn_grads]).reshape(qkv_weight.shape),
         jnp.stack([qb_sum[:, 0], qb_sum[:, 2]], axis=1),
-        jnp.stack([wo_one_done, wo_two_done]).reshape(out_weight.shape),
-        win_done,
+        jnp.stack([part[:, split_at:] for part in attn_grads]),
+        dense_done[:, : mlp_in.shape[1]],
         own_half(in_bias_sum.reshape(-1), 0),
-        wout_done,
+        dense_done[:, mlp_in.shape[1] :],
         out_bias_sum.reshape(-1),
         router_sum.T,
-        ein_done,
+        expert_grads[0],
         lax.dynamic_index_in_dim(ein_sum, side, 0, keepdims=False),
-        eout_done,
+        expert_grads[1],
         eout_sum.reshape(experts, width),
     )
 

time: 1410 us -> 811 us (0.58)
  waiting for transfers between devices: 970 us -> 204 us
  Pallas kernels: 305 us -> 383 us
  starting transfers between devices: 25.4 us -> 69 us
  local copies, waits for them, and re-layouts: 68.2 us -> 91.3 us
  other arithmetic: 17.4 us -> 31.7 us
    reduce_scatter x8 -> x2, waiting for transfers between devices: 603 us -> 0.02 us  [__init__(): done = lax.psum_scatter(grad, 'dp', scatter_dimension=axis, tiled=True)]
    psum x1 -> x0, waiting for transfers between devices: 111 us -> none  [local(): lax.psum((jnp.concatenate([gain_one, gain_ffn, gain_two, gain_moe]), jnp....]
    pallas_call x8 -> x34, Pallas kernels: 305 us -> 383 us  [call(): return lambda *args: made(*args, *after)]
    all_gather x4 -> x2, waiting for transfers between devices: 143 us -> 81 us  [gather_rows(): return lax.all_gather(share, 'dp', axis=0, tiled=True)]
    ppermute x0 -> x44, starting transfers between devices: none -> 51.8 us  [the longest x32 40.4 us: send(): return lax.ppermute(value, 'dp', pairs)]
    ppermute x0 -> x44, waiting for transfers between devices: none -> 39.2 us  [the longest x32 24.8 us: send(): return lax.ppermute(value, 'dp', pairs)]
    ppermute x17 -> x14, waiting for transfers between devices: 108 us -> 83.5 us  [swap(): return lax.ppermute(value, 'tensor', [(0, 1), (1, 0)])]
    reshape x12 -> x14, local copies, waits for them, and re-layouts: 17.1 us -> 0.96 us  [the longest x2 0.89 us: whole_columns(): return pair.reshape(share_rows, -1)]
  transfers between devices with their start and end apart: 30 -> 62, of which waited for: 21 -> 25; matrix products, arithmetic and copies ran while one was open for 5% -> 11% of each run, Pallas kernels for 6% -> 36%
where the time goes in v2:
time: 811 us; the launch traced here: 802 us
  Pallas kernels  383 us (47%)
  waiting for transfers between devices  204 us (25%)
  local copies, waits for them, and re-layouts  91.3 us (11%)
  starting transfers between devices  69 us (9%)
  other arithmetic  31.7 us (4%)
  between operations  23.2 us (3%)
    pallas_call x34, Pallas kernels, call(): return lambda *args: made(*args, *after)  383 us
    ppermute x14, waiting for transfers between devices, swap(): return lax.ppermute(value, 'tensor', [(0, 1), (1, 0)])  83.5 us
    all_gather x2, waiting for transfers between devices, gather_rows(): return lax.all_gather(share, 'dp', axis=0, tiled=True)  81 us
    ppermute x32, starting transfers between devices, send(): return lax.ppermute(value, 'dp', pairs)  40.4 us
    unnamed x223, local copies, waits for them, and re-layouts  31 us
    ppermute x32, waiting for transfers between devices, send(): return lax.ppermute(value, 'dp', pairs)  24.8 us
    ppermute x14, starting transfers between devices, swap(): return lax.ppermute(value, 'tensor', [(0, 1), (1, 0)])  16.8 us
  transfers between devices with their start and end apart: 62, of which 25 were waited for; matrix products, arithmetic and copies ran while one was open for 11% of the time, Pallas kernels for 36%

profile of v2, /device:TPU:0, one launch (start us, length us, event | category | flops | bytes accessed | tf_op | source)
XLA Modules:
  0.0 802.3 jit_solution(3430082290930770941)
XLA Ops:
  8.7 3.0 collective-permute-start
  11.7 13.3 %collective-permute-done = bf16[48,6144]{1,0:T(8,128)(2,1)S(1)} collective-permute-done((bf16[48,6144]{1,0:T(8,128)(2,1)S(1)}, bf16[48,6144]{1,0:T(8,128)(2,1)S(1)}, u32[]{:S(2)}, u32[]{:S(2)}) %collective-permute-start) | collective-permute-done | bytes 589856 | tf_op jit(solution)/shard_map/ppermute | solution.py:751
  35.3 6.9 constant_dynamic-slice_fusion.18
  50.7 81.0 %all-gather.3.cloned.1.call-done.refs_3_.refs_4_.refs_1_.refs_5_ = bf16[768,12288]{1,0:T(8,128)(2,1)} async-done(((bf16[48,12288]{1,0:T(8,128)(2,1)}), bf16[768,12288]{1,0:T(8,128)(2,1)}) %all-gather.3.cloned.1.call-update) | async-done | bytes 18874384 | tf_op jit(solution)/shard_map/all_gather | solution.py:760
  131.7 30.0 %attn_fwd.2 = (bf16[832,2304]{1,0:T(8,128)(2,1)}, f32[4,16,208]{2,1,0:T(8,128)}, bf16[832,768]{1,0:T(8,128)(2,1)}, f32[832,768]{1,0:T(8,128)}) custom-call(f32[832,768]{1,0:T(8,128)} %bitcast_convert_fusion.refs_0_.refs_1_, f32[1,768]{1,0:T(1,128)} %get-tuple-element.360.refs_1_.refs_2_, f32[1,768]{1,0:T(1,128)} %get-tuple-element.352.refs_2_.refs_3_, ...), custom_call_target="tpu_custom_call" | custom-call | flops 6052380672 | bytes 12000000 | tf_op jit(solution)/shard_map/attn_fwd/pallas_call | solution.py:102
  161.7 16.0 %dense_fwd.1.refs_0_.refs_1_ = f32[832,768]{1,0:T(8,128)} custom-call(f32[832,768]{1,0:T(8,128)} %get-tuple-element.111.refs_0_.refs_1_, f32[1,768]{1,0:T(1,128)} %get-tuple-element.359.refs_1_.refs_2_, f32[1,768]{1,0:T(1,128)} %get-tuple-element.350.refs_2_.refs_3_, bf16[768,12288]{1,0:T(8,128)(2,1)} %all-gather.3.cloned.1.call-done.refs_3_.refs_4_.refs_1_.refs_5_, ...), custom_call_target="tpu_custom_call" | custom-call | flops 7851737088 | bytes 15000000 | tf_op jit(solution)/shard_map/dense_fwd/pallas_call | solution.py:102
  177.7 35.7 %attn_fwd.3 = (bf16[832,2304]{1,0:T(8,128)(2,1)}, f32[4,16,208]{2,1,0:T(8,128)}, bf16[832,768]{1,0:T(8,128)(2,1)}, f32[832,768]{1,0:T(8,128)}, bf16[832,768]{1,0...) custom-call(f32[832,768]{1,0:T(8,128)} %dense_fwd.1.refs_0_.refs_1_, ...), custom_call_target="tpu_custom_call" | custom-call | flops 6052380672 | bytes 12000000 | tf_op jit(solution)/shard_map/attn_fwd/pallas_call | solution.py:102
  223.9 20.0 %collective-permute-done.3 = f32[2,2,416]{2,1,0:T(2,128)S(1)} collective-permute-done((f32[2,2,416]{2,1,0:T(2,128)S(1)}, f32[2,2,416]{2,1,0:T(2,128)S(1)}, u32[]{:S(2)}, u32[]{:S(2)}) %collective-permute-start.3) | collective-permute-done | bytes 6688 | tf_op jit(solution)/shard_map/ppermute | solution.py:751
  244.5 50.2 %experts.2 = (bf16[2,416,768]{2,1,0:T(8,128)(2,1)}, bf16[2,416,768]{2,1,0:T(8,128)(2,1)}, bf16[2,416,768]{2,1,0:T(8,128)(2,1)}, bf16[2,416,768]{2,1,0:T(8,128)(2...) custom-call(bf16[2,416,768]{2,1,0:T(8,128)(2,1)} %bitcast.283, ...), custom_call_target="tpu_custom_call" | custom-call | flops 23429382144 | bytes 30000000 | tf_op jit(solution)/shard_map/experts/pallas_call | solution.py:102
  294.7 48.2 %experts.3 = (bf16[2,416,768]{2,1,0:T(8,128)(2,1)}, bf16[2,416,768]{2,1,0:T(8,128)(2,1)}, bf16[2,416,768]{2,1,0:T(8,128)(2,1)}, bf16[2,416,768]{2,1,0:T(8,128)(2...) custom-call(bf16[2,416,768]{2,1,0:T(8,128)(2,1)} %bitcast.284, ...), custom_call_target="tpu_custom_call" | custom-call | flops 23429382144 | bytes 30000000 | tf_op jit(solution)/shard_map/experts/pallas_call | solution.py:102
  356.0 25.9 %collective-permute-done.5 = f32[2,416,128]{2,1,0:T(8,128)S(1)} collective-permute-done((f32[2,416,128]{2,1,0:T(8,128)S(1)}, f32[2,416,128]{2,1,0:T(8,128)S(1)}, u32[]{:S(2)}, u32[]{:S(2)}) %collective-permute-start.5) | collective-permute-done | bytes 426016 | tf_op jit(solution)/shard_map/ppermute | solution.py:751
  383.0 9.9 %gate_bwd.1 = (bf16[832,768]{1,0:T(8,128)(2,1)}, f32[832,768]{1,0:T(8,128)}, f32[128,768]{1,0:T(8,128)}, f32[1,768]{1,0:T(1,128)}, f32[1,768]{1,0:T(1,128)}) custom-call(f32[832,768]{1,0:T(8,128)} %get-tuple-element.112.refs_0_, bf16[832,768]{1,0:T(8,128)(2,1)} %bitcast.229, bf16[832,768]{1,0:T(8,128)(2,1)} %bitcast.238, bf16[832,768]{1,0:T(8,128)(2,1)} %bitcast.239, ...), custom_call_target="tpu_custom_call" | custom-call | flops 327155712 | bytes 14000000 | tf_op jit(solution)/shard_map/gate_bwd/pallas_call | solution.py:102
  393.0 15.1 %attn_core.4 = (bf16[416,2304]{1,0:T(8,128)(2,1)}, bf16[416,768]{1,0:T(8,128)(2,1)}) custom-call(f32[832,768]{1,0:T(8,128)} %get-tuple-element.129.refs_0_, bf16[768,12288]{1,0:T(8,128)(2,1)} %all-gather.3.cloned.1.call-done.refs_3_.refs_4_.refs_1_.refs_5_, bf16[832,2304]{1,0:T(8,128)(2,1)} %get-tuple-element.130.refs_2_, ...), custom_call_target="tpu_custom_call" | custom-call | flops 5807013888 | bytes 8000000 | tf_op jit(solution)/shard_map/attn_core/pallas_call | solution.py:102
  408.1 15.3 %attn_core.5 = (bf16[416,2304]{1,0:T(8,128)(2,1)}, bf16[416,768]{1,0:T(8,128)(2,1)}) custom-call(f32[832,768]{1,0:T(8,128)} %get-tuple-element.129.refs_0_, bf16[768,12288]{1,0:T(8,128)(2,1)} %all-gather.3.cloned.1.call-done.refs_3_.refs_4_.refs_1_.refs_5_, bf16[832,2304]{1,0:T(8,128)(2,1)} %get-tuple-element.130.refs_2_, ...), custom_call_target="tpu_custom_call" | custom-call | flops 5807013888 | bytes 8000000 | tf_op jit(solution)/shard_map/attn_core/pallas_call | solution.py:102
  423.4 17.2 %attn_grad.2 = (f32[832,768]{1,0:T(8,128)}, bf16[16,2,48,1536]{3,2,1,0:T(8,128)(2,1)}, f32[1,2304]{1,0:T(1,128)}, f32[1,768]{1,0:T(1,128)}, f32[1,768]{1,0:T(1,128)}, /*index=5*/f32[1,768]{1,0:T(1,128)}) custom-call(f32[832,768]{1,0:T(8,128)} %get-tuple-element.129.refs_0_, f32[832,768]{1,0:T(8,128)} %dense_fwd.1.refs_0_.refs_1_, ...), custom_call_target="tpu_custom_call" | custom-call | flops 6870269952 | bytes 25000000 | tf_op jit(solution)/shard_map/attn_grad/pallas_call | solution.py:102
  440.6 3.3 dynamic-slice_bitcast_fusion.3.refs_7_
  445.6 19.4 %dense_bwd.2 = (f32[832,768]{1,0:T(8,128)}, bf16[16,2,48,1536]{3,2,1,0:T(8,128)(2,1)}, f32[1,1536]{1,0:T(1,128)}) custom-call(f32[832,768]{1,0:T(8,128)} %get-tuple-element.137.refs_0_, f32[832,768]{1,0:T(8,128)} %get-tuple-element.111.refs_0_.refs_1_, f32[1,768]{1,0:T(1,128)} %get-tuple-element.359.refs_1_.refs_2_, ...), custom_call_target="tpu_custom_call" | custom-call | flops 9814671360 | bytes 25000000 | tf_op jit(solution)/shard_map/dense_bwd/pallas_call | solution.py:102
  465.0 3.6 dynamic-slice_bitcast_fusion.2.refs_10_
  469.7 5.1 collective-permute-done.6
  474.9 3.3 fusion.1
  485.7 21.7 %dense_bwd.3 = (f32[832,768]{1,0:T(8,128)}, bf16[16,2,48,1536]{3,2,1,0:T(8,128)(2,1)}, f32[1,1536]{1,0:T(1,128)}, f32[1,768]{1,0:T(1,128)}, f32[1,768]{1,0:T(1,128)}, /*index=5*/f32[1,768]{1,0:T(1,128)}) custom-call(f32[832,768]{1,0:T(8,128)} %get-tuple-element.137.refs_0_, f32[832,768]{1,0:T(8,128)} %get-tuple-element.111.refs_0_.refs_1_, ...), custom_call_target="tpu_custom_call" | custom-call | flops 9814671360 | bytes 25000000 | tf_op jit(solution)/shard_map/dense_bwd/pallas_call | solution.py:102
  507.5 3.4 dynamic-slice_bitcast_fusion.1.refs_8_
  526.6 3.2 collective-permute-done.10.refs_6_
  534.4 15.2 %attn_core.6 = (bf16[416,2304]{1,0:T(8,128)(2,1)}, bf16[416,768]{1,0:T(8,128)(2,1)}) custom-call(f32[832,768]{1,0:T(8,128)} %get-tuple-element.144.refs_0_, bf16[768,12288]{1,0:T(8,128)(2,1)} %all-gather.3.cloned.1.call-done.refs_3_.refs_4_.refs_1_.refs_5_, bf16[832,2304]{1,0:T(8,128)(2,1)} %get-tuple-element.145.refs_2_, ...), custom_call_target="tpu_custom_call" | custom-call | flops 5807013888 | bytes 8000000 | tf_op jit(solution)/shard_map/attn_core/pallas_call | solution.py:102
  552.8 3.0 ring_add.24
  558.8 3.1 select_bitcast_fusion.3
  563.8 3.0 ring_add.23
  567.7 8.6 %collective-permute-done.32 = f32[29952]{0:T(1024)S(1)} collective-permute-done((f32[29952]{0:T(1024)S(1)}, f32[29952]{0:T(1024)S(1)}, u32[]{:S(2)}, u32[]{:S(2)}) %collective-permute-start.32) | collective-permute-done | bytes 119840 | tf_op jit(solution)/shard_map/ppermute | solution.py:870
  576.2 8.0 collective-permute-start.18
  590.1 15.3 %attn_core.7 = (bf16[416,2304]{1,0:T(8,128)(2,1)}, bf16[416,768]{1,0:T(8,128)(2,1)}) custom-call(f32[832,768]{1,0:T(8,128)} %get-tuple-element.144.refs_0_, bf16[768,12288]{1,0:T(8,128)(2,1)} %all-gather.3.cloned.1.call-done.refs_3_.refs_4_.refs_1_.refs_5_, bf16[832,2304]{1,0:T(8,128)(2,1)} %get-tuple-element.145.refs_2_, ...), custom_call_target="tpu_custom_call" | custom-call | flops 5807013888 | bytes 8000000 | tf_op jit(solution)/shard_map/attn_core/pallas_call | solution.py:102
  605.5 4.0 collective-permute-start.33
  609.5 3.0 ring_add.27
  613.9 3.0 ring_add.26
  621.1 17.1 %attn_grad.3 = (f32[832,768]{1,0:T(8,128)}, bf16[16,2,48,1536]{3,2,1,0:T(8,128)(2,1)}, f32[1,2304]{1,0:T(1,128)}, f32[1,768]{1,0:T(1,128)}, f32[1,768]{1,0:T(1,128)}, /*index=5*/f32[1,768]{1,0:T(1,128)}) custom-call(f32[832,768]{1,0:T(8,128)} %get-tuple-element.144.refs_0_, f32[832,768]{1,0:T(8,128)} %bitcast_convert_fusion.refs_0_.refs_1_, ...), custom_call_target="tpu_custom_call" | custom-call | flops 6870269952 | bytes 25000000 | tf_op jit(solution)/shard_map/attn_grad/pallas_call | solution.py:102
  659.8 3.5 dynamic-slice_bitcast_fusion
  666.5 3.5 collective-permute-done.28
  681.4 3.1 ring_add.35
  689.0 3.0 ring_add.37
  700.2 3.0 collective-permute-done.53.refs_5_
  704.6 3.0 ring_add.38
  709.6 12.4 %collective-permute-done.46 = f32[48,1536]{1,0:T(8,128)S(1)} collective-permute-done((f32[48,1536]{1,0:T(8,128)S(1)}, f32[48,1536]{1,0:T(8,128)S(1)}, u32[]{:S(2)}, u32[]{:S(2)}) %collective-permute-start.46) | collective-permute-done | bytes 294944 | tf_op jit(solution)/shard_map/ppermute | solution.py:751
  733.6 3.2 collective-permute-done.35.refs_5_
  744.2 3.9 collective-permute-done.37.refs_5_
  749.8 3.0 ring_add.31
  757.0 4.1 copy.179
  762.5 3.0 ring_add.32
  767.8 4.7 collective-permute-done.41.refs_3_
  781.7 4.9 collective-permute-done.43
  (513 shorter events, 187.0 us)
Async XLA Ops:
  7.2 124.5 %all-gather.3.cloned.1.call-start = ((), (), s32[]{:S(2)}) async-start(), calls=%async_computation.2 | async-start | bytes 20054016 | tf_op jit(solution)/shard_map/all_gather | solution.py:760
  8.7 16.4 %collective-permute-start = (bf16[48,6144]{1,0:T(8,128)(2,1)S(1)}, bf16[48,6144]{1,0:T(8,128)(2,1)S(1)}, u32[]{:S(2)}, u32[]{:S(2)}) collective-permute-start(bf16[48,6144]{1,0:T(8,128)(2,1)S(1)} %get-tuple-element.324), channel_id=1, source_target_pairs={{0,1},{1,0},{2,3},{3,2},{4,5},{5,4},{6,7},{7,6},{8,9},{9,8},{10,11... | collective-permute-start | bytes 1769480 | tf_op jit(solution)/shard_map/ppermute | solution.py:751
  31.1 213.4 %all-gather.5.cloned.1.call-start = ((), (), s32[]{:S(2)}) async-start(), calls=%async_computation.3 | async-start | bytes 20054016 | tf_op jit(solution)/shard_map/all_gather | solution.py:760
  33.4 755.1 %reduce-scatter.5.cloned.1.call-start = ((), (), s32[]{:S(2)}) async-start(), calls=%async_computation.5 | async-start | bytes 10027008 | tf_op jit(solution)/shard_map/reduce_scatter | solution.py:857
  33.5 15.2 %collective-permute-start.1 = (f32[3072]{0:T(1024)S(1)}, f32[3072]{0:T(1024)S(1)}, u32[]{:S(2)}, u32[]{:S(2)}) collective-permute-start(f32[3072]{0:T(1024)S(1)} %constant_dynamic-update-slice_fusion.10), channel_id=1, source_target_pairs={{0,1},{1,0},{2,3},{3,2},{4,5},{5,4},{6,7},{7,6},{8,9},{9,8},{10,11... | collective-permute-start | bytes 36872 | tf_op jit(solution)/shard_map/ppermute | solution.py:751
  213.4 31.1 %collective-permute-start.2 = (bf16[832,768]{1,0:T(8,128)(2,1)}, bf16[832,768]{1,0:T(8,128)(2,1)}, u32[]{:S(2)}, u32[]{:S(2)}) collective-permute-start(bf16[832,768]{1,0:T(8,128)(2,1)} %get-tuple-element.113), channel_id=1, source_target_pairs={{0,1},{1,0},{2,3},{3,2},{4,5},{5,4},{6,7},{7,6},{8,9},{9,8},{10,11... | collective-permute-start | bytes 3833864 | tf_op jit(solution)/shard_map/ppermute | solution.py:751
  218.8 25.1 %collective-permute-start.3 = (f32[2,2,416]{2,1,0:T(2,128)S(1)}, f32[2,2,416]{2,1,0:T(2,128)S(1)}, u32[]{:S(2)}, u32[]{:S(2)}) collective-permute-start(f32[2,2,416]{2,1,0:T(2,128)S(1)} %bitcast.280), channel_id=1, source_target_pairs={{0,1},{1,0},{2,3},{3,2},{4,5},{5,4},{6,7},{7,6},{8,9},{9,8},{10,11... | collective-permute-start | bytes 19976 | tf_op jit(solution)/shard_map/ppermute | solution.py:751
  342.9 447.7 %reduce-scatter.3.cloned.1.call-start = ((), (), s32[]{:S(2)}) async-start(), calls=%async_computation.4 | async-start | bytes 10027008 | tf_op jit(solution)/shard_map/reduce_scatter | solution.py:857
  343.2 38.7 %collective-permute-start.4 = (bf16[2,416,768]{2,1,0:T(8,128)(2,1)}, bf16[2,416,768]{2,1,0:T(8,128)(2,1)S(1)}, u32[]{:S(2)}, u32[]{:S(2)}) collective-permute-start(bf16[2,416,768]{2,1,0:T(8,128)(2,1)} %get-tuple-element.124), channel_id=1, source_target_pairs={{0,1},{1,0},{2,3},{3,2},{4,5},{5,4},{6,7},{7,6},{8,9},{9,8},{10,11... | collective-permute-start | bytes 3833864 | tf_op jit(solution)/shard_map/ppermute | solution.py:751
  344.7 37.1 %collective-permute-start.5 = (f32[2,416,128]{2,1,0:T(8,128)S(1)}, f32[2,416,128]{2,1,0:T(8,128)S(1)}, u32[]{:S(2)}, u32[]{:S(2)}) collective-permute-start(f32[2,416,128]{2,1,0:T(8,128)S(1)} %copy-done.84), channel_id=1, source_target_pairs={{0,1},{1,0},{2,3},{3,2},{4,5},{5,4},{6,7},{7,6},{8,9},{9,8},{10,11... | collective-permute-start | bytes 1277960 | tf_op jit(solution)/shard_map/ppermute | solution.py:751
  443.9 37.9 %collective-permute-start.8 = (bf16[8,2,48,1536]{3,2,1,0:T(8,128)(2,1)}, bf16[8,2,48,1536]{3,2,1,0:T(8,128)(2,1)S(1)}, u32[]{:S(2)}, u32[]{:S(2)}) collective-permute-start(bf16[8,2,48,1536]{3,2,1,0:T(8,128)(2,1)} %dynamic-slice_bitcast_fusion.3.refs_7_), channel_id=1, source_target_pairs={{0,2},{2,0},{4,6},{6,4},{8,10},{10,8},{12,14},{14,12},{16,18},{18,... | collective-permute-start | bytes 7077896 | tf_op jit(solution)/shard_map/ppermute | solution.py:807
  444.0 30.8 %collective-permute-start.6 = (bf16[832,768]{1,0:T(8,128)(2,1)}, bf16[832,768]{1,0:T(8,128)(2,1)}, u32[]{:S(2)}, u32[]{:S(2)}) collective-permute-start(bf16[832,768]{1,0:T(8,128)(2,1)} %get-tuple-element.128), channel_id=1, source_target_pairs={{0,1},{1,0},{2,3},{3,2},{4,5},{5,4},{6,7},{7,6},{8,9},{9,8},{10,11... | collective-permute-start | bytes 3833864 | tf_op jit(solution)/shard_map/ppermute | solution.py:751
  468.6 49.8 %collective-permute-start.11 = (bf16[8,2,48,1536]{3,2,1,0:T(8,128)(2,1)}, bf16[8,2,48,1536]{3,2,1,0:T(8,128)(2,1)}, u32[]{:S(2)}, u32[]{:S(2)}) collective-permute-start(bf16[8,2,48,1536]{3,2,1,0:T(8,128)(2,1)} %dynamic-slice_bitcast_fusion.2.refs_10_), channel_id=1, source_target_pairs={{0,2},{2,0},{4,6},{6,4},{8,10},{10,8},{12,14},{14,12},{16,18},{18,... | collective-permute-start | bytes 7077896 | tf_op jit(solution)/shard_map/ppermute | solution.py:807
  480.2 77.1 %collective-permute-start.7 = (bf16[2,2,197,768]{3,1,2,0:T(2,128)(2,1)}, bf16[2,2,197,768]{3,1,2,0:T(2,128)(2,1)}, u32[]{:S(2)}, u32[]{:S(2)}) collective-permute-start(bf16[2,2,197,768]{3,1,2,0:T(2,128)(2,1)} %copy.170), channel_id=1, source_target_pairs={{0,1},{1,0},{2,3},{3,2},{4,5},{5,4},{6,7},{7,6},{8,9},{9,8},{10,11... | collective-permute-start | bytes 3631112 | tf_op jit(solution)/shard_map/ppermute | solution.py:751
  510.8 73.4 %collective-permute-start.16 = (bf16[8,2,48,1536]{3,2,1,0:T(8,128)(2,1)}, bf16[8,2,48,1536]{3,2,1,0:T(8,128)(2,1)S(1)}, u32[]{:S(2)}, u32[]{:S(2)}) collective-permute-start(bf16[8,2,48,1536]{3,2,1,0:T(8,128)(2,1)} %dynamic-slice_bitcast_fusion.1.refs_8_), channel_id=1, source_target_pairs={{0,2},{2,0},{4,6},{6,4},{8,10},{10,8},{12,14},{14,12},{16,18},{18,... | collective-permute-start | bytes 7077896 | tf_op jit(solution)/shard_map/ppermute | solution.py:807
  514.8 10.1 %collective-permute-start.9 = (bf16[48,1536]{1,0:T(8,128)(2,1)S(1)}, bf16[48,1536]{1,0:T(8,128)(2,1)S(1)}, u32[]{:S(2)}, u32[]{:S(2)}) collective-permute-start(bf16[48,1536]{1,0:T(8,128)(2,1)S(1)} %copy-done.47), channel_id=1, source_target_pairs={{0,8},{2,10},{8,16},{10,18},{16,24},{18,26},{24,28},{26,30},{28,20... | collective-permute-start | bytes 442376 | tf_op jit(solution)/shard_map/ppermute | solution.py:817
  516.9 12.9 %collective-permute-start.10 = (bf16[48,1536]{1,0:T(8,128)(2,1)S(1)}, bf16[48,1536]{1,0:T(8,128)(2,1)S(1)}, u32[]{:S(2)}, u32[]{:S(2)}) collective-permute-start(bf16[48,1536]{1,0:T(8,128)(2,1)S(1)} %copy-done.46), channel_id=1, source_target_pairs={{0,4},{2,6},{8,0},{10,2},{16,8},{18,10},{24,16},{26,18},{28,24},{3... | collective-permute-start | bytes 442376 | tf_op jit(solution)/shard_map/ppermute | solution.py:817
  518.5 15.0 %collective-permute-start.30 = (f32[29952]{0:T(1024)S(1)}, f32[29952]{0:T(1024)S(1)}, u32[]{:S(2)}, u32[]{:S(2)}) collective-permute-start(f32[29952]{0:T(1024)S(1)} %add.479), channel_id=1, source_target_pairs={{0,2},{2,0},{4,6},{6,4},{8,10},{10,8},{12,14},{14,12},{16,18},{18,... | collective-permute-start | bytes 359432 | tf_op jit(solution)/shard_map/ppermute | solution.py:870
  524.8 24.7 %collective-permute-start.14 = (bf16[48,1536]{1,0:T(8,128)(2,1)}, bf16[48,1536]{1,0:T(8,128)(2,1)S(1)}, u32[]{:S(2)}, u32[]{:S(2)}) collective-permute-start(bf16[48,1536]{1,0:T(8,128)(2,1)} %get-tuple-element.150.refs_6_), channel_id=1, source_target_pairs={{0,8},{2,10},{8,16},{10,18},{16,24},{18,26},{24,28},{26,30},{28,20... | collective-permute-start | bytes 442376 | tf_op jit(solution)/shard_map/ppermute | solution.py:817
  529.9 22.3 %collective-permute-start.15 = (bf16[48,1536]{1,0:T(8,128)(2,1)}, bf16[48,1536]{1,0:T(8,128)(2,1)S(1)}, u32[]{:S(2)}, u32[]{:S(2)}) collective-permute-start(bf16[48,1536]{1,0:T(8,128)(2,1)} %get-tuple-element.151.refs_7_), channel_id=1, source_target_pairs={{0,4},{2,6},{8,0},{10,2},{16,8},{18,10},{24,16},{26,18},{28,24},{3... | collective-permute-start | bytes 442376 | tf_op jit(solution)/shard_map/ppermute | solution.py:817
  533.4 22.4 %collective-permute-start.31 = (f32[29952]{0:T(1024)S(1)}, f32[29952]{0:T(1024)S(1)}, u32[]{:S(2)}, u32[]{:S(2)}) collective-permute-start(f32[29952]{0:T(1024)S(1)} %add.480), channel_id=1, source_target_pairs={{0,4},{2,6},{4,0},{6,2},{8,12},{10,14},{12,8},{14,10},{16,20},{18,... | collective-permute-start | bytes 359432 | tf_op jit(solution)/shard_map/ppermute | solution.py:870
  549.6 12.3 %collective-permute-start.12 = (bf16[2,48,1536]{2,1,0:T(8,128)(2,1)S(1)}, bf16[2,48,1536]{2,1,0:T(8,128)(2,1)S(1)}, u32[]{:S(2)}, u32[]{:S(2)}) collective-permute-start(bf16[2,48,1536]{2,1,0:T(8,128)(2,1)S(1)} %copy-done.20), channel_id=1, source_target_pairs={{0,8},{2,10},{8,16},{10,18},{16,24},{18,26},{24,28},{26,30},{28,20... | collective-permute-start | bytes 884744 | tf_op jit(solution)/shard_map/ppermute | solution.py:817
  552.2 10.9 %collective-permute-start.13 = (bf16[2,48,1536]{2,1,0:T(8,128)(2,1)S(1)}, bf16[2,48,1536]{2,1,0:T(8,128)(2,1)S(1)}, u32[]{:S(2)}, u32[]{:S(2)}) collective-permute-start(bf16[2,48,1536]{2,1,0:T(8,128)(2,1)S(1)} %copy-done.19), channel_id=1, source_target_pairs={{0,4},{2,6},{8,0},{10,2},{16,8},{18,10},{24,16},{26,18},{28,24},{3... | collective-permute-start | bytes 884744 | tf_op jit(solution)/shard_map/ppermute | solution.py:817
  555.9 32.2 %collective-permute-start.19 = (bf16[2,48,1536]{2,1,0:T(8,128)(2,1)}, bf16[2,48,1536]{2,1,0:T(8,128)(2,1)S(1)}, u32[]{:S(2)}, u32[]{:S(2)}) collective-permute-start(bf16[2,48,1536]{2,1,0:T(8,128)(2,1)} %get-tuple-element.157.refs_6_), channel_id=1, source_target_pairs={{0,8},{2,10},{8,16},{10,18},{16,24},{18,26},{24,28},{26,30},{28,20... | collective-permute-start | bytes 884744 | tf_op jit(solution)/shard_map/ppermute | solution.py:817
  557.3 18.9 %collective-permute-start.32 = (f32[29952]{0:T(1024)S(1)}, f32[29952]{0:T(1024)S(1)}, u32[]{:S(2)}, u32[]{:S(2)}) collective-permute-start(f32[29952]{0:T(1024)S(1)} %add.481), channel_id=1, source_target_pairs={{0,8},{2,10},{4,12},{6,14},{8,0},{10,2},{12,4},{14,6},{16,24},{18,... | collective-permute-start | bytes 359432 | tf_op jit(solution)/shard_map/ppermute | solution.py:870
  561.9 43.6 %collective-permute-start.20 = (bf16[2,48,1536]{2,1,0:T(8,128)(2,1)S(1)}, bf16[2,48,1536]{2,1,0:T(8,128)(2,1)S(1)}, u32[]{:S(2)}, u32[]{:S(2)}) collective-permute-start(bf16[2,48,1536]{2,1,0:T(8,128)(2,1)S(1)} %copy-done.34), channel_id=1, source_target_pairs={{0,4},{2,6},{8,0},{10,2},{16,8},{18,10},{24,16},{26,18},{28,24},{3... | collective-permute-start | bytes 884744 | tf_op jit(solution)/shard_map/ppermute | solution.py:817
  566.8 45.7 %collective-permute-start.17 = (bf16[2,48,1536]{2,1,0:T(8,128)(2,1)}, bf16[2,48,1536]{2,1,0:T(8,128)(2,1)S(1)}, u32[]{:S(2)}, u32[]{:S(2)}) collective-permute-start(bf16[2,48,1536]{2,1,0:T(8,128)(2,1)} %get-tuple-element.155.refs_4_), channel_id=1, source_target_pairs={{0,8},{2,10},{8,16},{10,18},{16,24},{18,26},{24,28},{26,30},{28,20... | collective-permute-start | bytes 884744 | tf_op jit(solution)/shard_map/ppermute | solution.py:817
  576.2 36.3 %collective-permute-start.18 = (bf16[2,48,1536]{2,1,0:T(8,128)(2,1)}, bf16[2,48,1536]{2,1,0:T(8,128)(2,1)S(1)}, u32[]{:S(2)}, u32[]{:S(2)}) collective-permute-start(bf16[2,48,1536]{2,1,0:T(8,128)(2,1)} %get-tuple-element.156.refs_5_), channel_id=1, source_target_pairs={{0,4},{2,6},{8,0},{10,2},{16,8},{18,10},{24,16},{26,18},{28,24},{3... | collective-permute-start | bytes 884744 | tf_op jit(solution)/shard_map/ppermute | solution.py:817
  588.1 28.8 %collective-permute-start.21 = (bf16[48,1536]{1,0:T(8,128)(2,1)}, bf16[48,1536]{1,0:T(8,128)(2,1)S(1)}, u32[]{:S(2)}, u32[]{:S(2)}) collective-permute-start(bf16[48,1536]{1,0:T(8,128)(2,1)} %get-tuple-element.159.refs_8_), channel_id=1, source_target_pairs={{0,8},{2,10},{8,16},{10,18},{16,24},{18,26},{24,28},{26,30},{28,20... | collective-permute-start | bytes 442376 | tf_op jit(solution)/shard_map/ppermute | solution.py:817
  588.1 28.8 %collective-permute-start.22 = (bf16[48,1536]{1,0:T(8,128)(2,1)}, bf16[48,1536]{1,0:T(8,128)(2,1)S(1)}, u32[]{:S(2)}, u32[]{:S(2)}) collective-permute-start(bf16[48,1536]{1,0:T(8,128)(2,1)} %get-tuple-element.160.refs_9_), channel_id=1, source_target_pairs={{0,4},{2,6},{8,0},{10,2},{16,8},{18,10},{24,16},{26,18},{28,24},{3... | collective-permute-start | bytes 442376 | tf_op jit(solution)/shard_map/ppermute | solution.py:817
  605.5 38.3 %collective-permute-start.33 = (f32[29952]{0:T(1024)S(1)}, f32[29952]{0:T(1024)S(1)}, u32[]{:S(2)}, u32[]{:S(2)}) collective-permute-start(f32[29952]{0:T(1024)S(1)} %add.482), channel_id=1, source_target_pairs={{0,16},{2,18},{4,20},{6,22},{8,24},{10,26},{12,28},{14,30},{16,0},... | collective-permute-start | bytes 359432 | tf_op jit(solution)/shard_map/ppermute | solution.py:870
  650.0 9.0 %collective-permute-start.27 = (f32[4608]{0:T(1024)S(1)}, f32[4608]{0:T(1024)S(1)}, u32[]{:S(2)}, u32[]{:S(2)}) collective-permute-start(f32[4608]{0:T(1024)S(1)} %add.476), channel_id=1, source_target_pairs={{0,8},{2,10},{4,12},{6,14},{8,0},{10,2},{12,4},{14,6},{16,24},{18,... | collective-permute-start | bytes 55304 | tf_op jit(solution)/shard_map/ppermute | solution.py:870
  654.6 17.4 %collective-permute-start.44 = (bf16[2,48,1536]{2,1,0:T(8,128)(2,1)S(1)}, bf16[2,48,1536]{2,1,0:T(8,128)(2,1)S(1)}, u32[]{:S(2)}, u32[]{:S(2)}) collective-permute-start(bf16[2,48,1536]{2,1,0:T(8,128)(2,1)S(1)} %copy-done.18), channel_id=1, source_target_pairs={{0,8},{2,10},{8,16},{10,18},{16,24},{18,26},{24,28},{26,30},{28,20... | collective-permute-start | bytes 884744 | tf_op jit(solution)/shard_map/ppermute | solution.py:817
  654.6 19.4 %collective-permute-start.45 = (bf16[2,48,1536]{2,1,0:T(8,128)(2,1)S(1)}, bf16[2,48,1536]{2,1,0:T(8,128)(2,1)}, u32[]{:S(2)}, u32[]{:S(2)}) collective-permute-start(bf16[2,48,1536]{2,1,0:T(8,128)(2,1)S(1)} %copy-done.17), channel_id=1, source_target_pairs={{0,4},{2,6},{8,0},{10,2},{16,8},{18,10},{24,16},{26,18},{28,24},{3... | collective-permute-start | bytes 884744 | tf_op jit(solution)/shard_map/ppermute | solution.py:817
  656.6 24.8 %collective-permute-start.47 = (bf16[2,48,1536]{2,1,0:T(8,128)(2,1)}, bf16[2,48,1536]{2,1,0:T(8,128)(2,1)}, u32[]{:S(2)}, u32[]{:S(2)}) collective-permute-start(bf16[2,48,1536]{2,1,0:T(8,128)(2,1)} %get-tuple-element.166.refs_12_), channel_id=1, source_target_pairs={{0,8},{2,10},{8,16},{10,18},{16,24},{18,26},{24,28},{26,30},{28,20... | collective-permute-start | bytes 884744 | tf_op jit(solution)/shard_map/ppermute | solution.py:817
  656.7 24.8 %collective-permute-start.48 = (bf16[2,48,1536]{2,1,0:T(8,128)(2,1)}, bf16[2,48,1536]{2,1,0:T(8,128)(2,1)}, u32[]{:S(2)}, u32[]{:S(2)}) collective-permute-start(bf16[2,48,1536]{2,1,0:T(8,128)(2,1)} %get-tuple-element.167.refs_13_), channel_id=1, source_target_pairs={{0,4},{2,6},{8,0},{10,2},{16,8},{18,10},{24,16},{26,18},{28,24},{3... | collective-permute-start | bytes 884744 | tf_op jit(solution)/shard_map/ppermute | solution.py:817
  659.0 10.9 %collective-permute-start.28 = (f32[4608]{0:T(1024)S(1)}, f32[4608]{0:T(1024)S(1)}, u32[]{:S(2)}, u32[]{:S(2)}) collective-permute-start(f32[4608]{0:T(1024)S(1)} %add.477), channel_id=1, source_target_pairs={{0,16},{2,18},{4,20},{6,22},{8,24},{10,26},{12,28},{14,30},{16,0},... | collective-permute-start | bytes 55304 | tf_op jit(solution)/shard_map/ppermute | solution.py:870
  670.0 16.9 %collective-permute-start.51 = (bf16[2,48,1536]{2,1,0:T(8,128)(2,1)}, bf16[2,48,1536]{2,1,0:T(8,128)(2,1)}, u32[]{:S(2)}, u32[]{:S(2)}) collective-permute-start(bf16[2,48,1536]{2,1,0:T(8,128)(2,1)} %get-tuple-element.168.refs_14_), channel_id=1, source_target_pairs={{0,8},{2,10},{8,16},{10,18},{16,24},{18,26},{24,28},{26,30},{28,20... | collective-permute-start | bytes 884744 | tf_op jit(solution)/shard_map/ppermute | solution.py:817
  672.0 15.9 %collective-permute-start.52 = (bf16[2,48,1536]{2,1,0:T(8,128)(2,1)S(1)}, bf16[2,48,1536]{2,1,0:T(8,128)(2,1)}, u32[]{:S(2)}, u32[]{:S(2)}) collective-permute-start(bf16[2,48,1536]{2,1,0:T(8,128)(2,1)S(1)} %copy-done.16), channel_id=1, source_target_pairs={{0,4},{2,6},{8,0},{10,2},{16,8},{18,10},{24,16},{26,18},{28,24},{3... | collective-permute-start | bytes 884744 | tf_op jit(solution)/shard_map/ppermute | solution.py:817
  674.1 53.4 %collective-permute-start.34 = (bf16[8,2,48,1536]{3,2,1,0:T(8,128)(2,1)}, bf16[8,2,48,1536]{3,2,1,0:T(8,128)(2,1)S(1)}, u32[]{:S(2)}, u32[]{:S(2)}) collective-permute-start(bf16[8,2,48,1536]{3,2,1,0:T(8,128)(2,1)} %dynamic-slice_bitcast_fusion), channel_id=1, source_target_pairs={{0,2},{2,0},{4,6},{6,4},{8,10},{10,8},{12,14},{14,12},{16,18},{18,... | collective-permute-start | bytes 7077896 | tf_op jit(solution)/shard_map/ppermute | solution.py:807
  684.6 9.6 %collective-permute-start.49 = (bf16[2,48,1536]{2,1,0:T(8,128)(2,1)}, bf16[2,48,1536]{2,1,0:T(8,128)(2,1)S(1)}, u32[]{:S(2)}, u32[]{:S(2)}) collective-permute-start(bf16[2,48,1536]{2,1,0:T(8,128)(2,1)} %get-tuple-element.198), channel_id=1, source_target_pairs={{0,8},{2,10},{8,16},{10,18},{16,24},{18,26},{24,28},{26,30},{28,20... | collective-permute-start | bytes 884744 | tf_op jit(solution)/shard_map/ppermute | solution.py:817
  684.6 9.9 %collective-permute-start.50 = (bf16[2,48,1536]{2,1,0:T(8,128)(2,1)}, bf16[2,48,1536]{2,1,0:T(8,128)(2,1)S(1)}, u32[]{:S(2)}, u32[]{:S(2)}) collective-permute-start(bf16[2,48,1536]{2,1,0:T(8,128)(2,1)} %get-tuple-element.199), channel_id=1, source_target_pairs={{0,4},{2,6},{8,0},{10,2},{16,8},{18,10},{24,16},{26,18},{28,24},{3... | collective-permute-start | bytes 884744 | tf_op jit(solution)/shard_map/ppermute | solution.py:817
  686.9 67.9 %collective-permute-start.23 = (bf16[2,2,197,768]{3,1,2,0:T(2,128)(2,1)}, bf16[2,2,197,768]{3,1,2,0:T(2,128)(2,1)}, u32[]{:S(2)}, u32[]{:S(2)}) collective-permute-start(bf16[2,2,197,768]{3,1,2,0:T(2,128)(2,1)} %copy.174), channel_id=1, source_target_pairs={{0,1},{1,0},{2,3},{3,2},{4,5},{5,4},{6,7},{7,6},{8,9},{9,8},{10,11... | collective-permute-start | bytes 3631112 | tf_op jit(solution)/shard_map/ppermute | solution.py:751
  687.9 34.1 %collective-permute-start.46 = (f32[48,1536]{1,0:T(8,128)S(1)}, f32[48,1536]{1,0:T(8,128)S(1)}, u32[]{:S(2)}, u32[]{:S(2)}) collective-permute-start(f32[48,1536]{1,0:T(8,128)S(1)} %pad_maximum_fusion.9), channel_id=1, source_target_pairs={{0,1},{1,0},{2,3},{3,2},{4,5},{5,4},{6,7},{7,6},{8,9},{9,8},{10,11... | collective-permute-start | bytes 884744 | tf_op jit(solution)/shard_map/ppermute | solution.py:751
  694.2 8.9 %collective-permute-start.53 = (bf16[2,48,1536]{2,1,0:T(8,128)(2,1)}, bf16[2,48,1536]{2,1,0:T(8,128)(2,1)S(1)}, u32[]{:S(2)}, u32[]{:S(2)}) collective-permute-start(bf16[2,48,1536]{2,1,0:T(8,128)(2,1)} %get-tuple-element.200), channel_id=1, source_target_pairs={{0,8},{2,10},{8,16},{10,18},{16,24},{18,26},{24,28},{26,30},{28,20... | collective-permute-start | bytes 884744 | tf_op jit(solution)/shard_map/ppermute | solution.py:817
  707.6 14.4 %collective-permute-start.55 = (bf16[2,48,1536]{2,1,0:T(8,128)(2,1)}, bf16[2,48,1536]{2,1,0:T(8,128)(2,1)S(1)}, u32[]{:S(2)}, u32[]{:S(2)}) collective-permute-start(bf16[2,48,1536]{2,1,0:T(8,128)(2,1)} %get-tuple-element.202), channel_id=1, source_target_pairs={{0,8},{2,10},{8,16},{10,18},{16,24},{18,26},{24,28},{26,30},{28,20... | collective-permute-start | bytes 884744 | tf_op jit(solution)/shard_map/ppermute | solution.py:817
  708.2 13.9 %collective-permute-start.56 = (bf16[2,48,1536]{2,1,0:T(8,128)(2,1)}, bf16[2,48,1536]{2,1,0:T(8,128)(2,1)S(1)}, u32[]{:S(2)}, u32[]{:S(2)}) collective-permute-start(bf16[2,48,1536]{2,1,0:T(8,128)(2,1)} %get-tuple-element.203), channel_id=1, source_target_pairs={{0,4},{2,6},{8,0},{10,2},{16,8},{18,10},{24,16},{26,18},{28,24},{3... | collective-permute-start | bytes 884744 | tf_op jit(solution)/shard_map/ppermute | solution.py:817
  743.1 24.6 %collective-permute-start.57 = (f32[48,3072]{1,0:T(8,128)S(1)}, f32[48,3072]{1,0:T(8,128)S(1)}, u32[]{:S(2)}, u32[]{:S(2)}) collective-permute-start(f32[48,3072]{1,0:T(8,128)S(1)} %pad_maximum_fusion.6), channel_id=1, source_target_pairs={{0,1},{1,0},{2,3},{3,2},{4,5},{5,4},{6,7},{7,6},{8,9},{9,8},{10,11... | collective-permute-start | bytes 1769480 | tf_op jit(solution)/shard_map/ppermute | solution.py:751
  (100 other events, 415.4 us)
Sparse Core Ops, SparseCore 0:
  31.2 100.4 all-gather.2
  133.8 98.9 all-gather.4
  343.1 111.3 reduce-scatter.4
  459.0 136.5 reduce-scatter.2

commit v3 on v2

v3 whole, which is shorter than its diff:
```python
import functools

import jax
import jax.numpy as jnp
from jax import lax
from jax.experimental import pallas as pl
from jax.experimental.pallas import tpu as pltpu
from jax.sharding import PartitionSpec as P

HD = 64
CAP = 295
NORM_EPS = 1e-06
EXACT = lax.Precision.HIGHEST
BF = jnp.bfloat16
F32 = jnp.float32
VMEM_LIMIT = 58 * 1024 * 1024
FF_BLOCK = 512
ROW_PAD = 16
GELU_SLOPE = 0.7978845608028654
GELU_CUBE = 0.044715


def round_up(value, unit):
    return -(-value // unit) * unit


def mm(left, right):
    return jnp.dot(left, right, preferred_element_type=F32)


def mm_bt(left, right):
    return lax.dot_general(left, right, (((1,), (1,)), ((), ())), preferred_element_type=F32)


def mm_at(left, right):
    return lax.dot_general(left, right, (((0,), (0,)), ((), ())), preferred_element_type=F32)


def norm_parts(hidden):
    center = jnp.mean(hidden, axis=-1, keepdims=True)
    centred = hidden - center
    spread = jnp.mean(centred * centred, axis=-1, keepdims=True)
    scale = lax.rsqrt(spread + NORM_EPS)
    return centred * scale, scale


def norm_pull(unit, scale, gain, incoming):
    wide = incoming * gain
    mean_wide = jnp.mean(wide, axis=-1, keepdims=True)
    mean_dot = jnp.mean(wide * unit, axis=-1, keepdims=True)
    hidden_grad = scale * (wide - mean_wide - unit * mean_dot)
    gain_grad = jnp.sum(incoming * unit, axis=0, keepdims=True)
    shift_grad = jnp.sum(incoming, axis=0, keepdims=True)
    return hidden_grad, gain_grad, shift_grad


def gelu_pair(preact):
    square = preact * preact
    inner = GELU_SLOPE * preact * (1.0 + GELU_CUBE * square)
    bend = jnp.tanh(inner)
    half = 0.5 * (1.0 + bend)
    active = preact * half
    slope = half + 0.5 * preact * (1.0 - bend * bend) * (
        GELU_SLOPE * (1.0 + 3.0 * GELU_CUBE * square)
    )
    return active, slope


def gelu_value(preact):
    square = preact * preact
    inner = GELU_SLOPE * preact * (1.0 + GELU_CUBE * square)
    return 0.5 * preact * (1.0 + jnp.tanh(inner))


def call(kernel, grid, in_specs, out_specs, out_shape, scratch, flops, traffic, name,
         after=(), prefetch=0):
    taken = prefetch + len(in_specs)
    skipped = len(after)

    def body(*refs):
        kernel(*refs[:taken], *refs[taken + skipped :])

    made = pl.pallas_call(
        body,
        grid_spec=pltpu.PrefetchScalarGridSpec(
            num_scalar_prefetch=prefetch,
            grid=grid,
            in_specs=list(in_specs) + [pl.BlockSpec(memory_space=pl.ANY)] * skipped,
            out_specs=out_specs,
            scratch_shapes=scratch,
        ),
        out_shape=out_shape,
        name=name,
        compiler_params=pltpu.CompilerParams(
            vmem_limit_bytes=VMEM_LIMIT,
            dimension_semantics=("arbitrary",) * len(grid),
        ),
        cost_estimate=pl.CostEstimate(
            flops=int(flops), bytes_accessed=int(traffic), transcendentals=0
        ),
    )
    return lambda *args: made(*args, *after)


def whole_tiles(devices, width):
    return (width // devices) % ROW_PAD == 0


def grad_shapes(devices, width, columns, split):
    if not whole_tiles(devices, width):
        return [(2, width, columns)]
    if split:
        return [(devices // 2, 2, width // devices, columns)] * 2
    return [(devices, 2, width // devices, columns)]


def grad_block(shape, columns, index):
    block = shape[:-1] + (columns,)
    zeros = (0,) * (len(shape) - 1)
    return pl.BlockSpec(block, lambda *at: zeros + (index(*at),))


def put_grad(refs, core_ref, part, cols, value):
    ref = refs[0]
    if len(refs) == 2:
        pieces = value.reshape(ref.shape[0], 2, ref.shape[2], value.shape[1])
        core = core_ref[0]

        @pl.when(core == 0)
        def _():
            refs[0][:, part, :, cols] = pieces[:, 0]
            refs[1][:, part, :, cols] = pieces[:, 1]

        @pl.when(core != 0)
        def _():
            refs[0][:, part, :, cols] = pieces[:, 1]
            refs[1][:, part, :, cols] = pieces[:, 0]
    elif len(ref.shape) == 3:
        ref[part, :, cols] = value
    else:
        ref[:, part, :, cols] = value.reshape(ref.shape[0], ref.shape[2], value.shape[1])


def flat_rows(value):
    return value.reshape(-1, value.shape[-1])


def weight_spec(weights, sides, columns, index):
    devices, _, rows, _ = weights.shape
    return pl.BlockSpec(
        (devices, sides, rows, columns), index, pipeline_mode=pl.Buffered(1)
    )


def whole(shape):
    zeros = (0,) * len(shape)
    return pl.BlockSpec(shape, lambda *_: zeros, pipeline_mode=pl.Buffered(1))


def rows_of(block, width):
    return pl.BlockSpec((block, width), lambda step, *_: (step, 0))


def half_of(value, block, which):
    at = which if value.shape[0] > block else 0
    rest = (0,) * (value.ndim - 1)
    return pl.BlockSpec((block,) + value.shape[1:], lambda *_: (at,) + rest)


def attn_fwd_kernel(
    length, pad, heads, router_on,
    h_ref, g_ref, b_ref, w_ref, qb_ref, ob_ref, *rest,
):
    if router_on:
        g2_ref, b2_ref, rt_ref, sel_ref = rest[:4]
        qkv_ref, lse_ref, o_ref, a_ref, rb_ref, gp_ref, wt_ref = rest[4:]
    else:
        qkv_ref, lse_ref, o_ref, a_ref = rest
    width = h_ref.shape[1]
    images = h_ref.shape[0] // pad
    hidden = h_ref[...]
    unit, _ = norm_parts(hidden)
    normed = (unit * g_ref[...] + b_ref[...]).astype(BF)
    third = width // 2
    for t in range(2):
        cols = slice(t * 3 * third, (t + 1) * 3 * third)
        matrix = flat_rows(w_ref[:, t, :, : 3 * third])
        qkv_ref[:, cols] = (mm(normed, matrix) + qb_ref[:, cols]).astype(BF)
    pairs = heads // 2
    lane = lax.broadcasted_iota(jnp.int32, (pad, 2 * HD), 1)
    key_row = lax.broadcasted_iota(jnp.int32, (pad, pad), 0)

    def pair_step(step, carry):
        image = step // pairs
        pair = step % pairs
        rows = pl.ds(pl.multiple_of(image * pad, ROW_PAD), pad)

        def col(part):
            side = pair // (pairs // 2)
            at = (side * 3 + part) * (width // 2) + (pair % (pairs // 2)) * 2 * HD
            return pl.ds(pl.multiple_of(at, 2 * HD), 2 * HD)

        place = pl.ds(pl.multiple_of(pair * 2 * HD, 2 * HD), 2 * HD)

        query = qkv_ref[rows, col(0)] * HD ** (-0.5)
        key = qkv_ref[rows, col(1)]
        value = qkv_ref[rows, col(2)]
        mixed = []
        for half in range(2):
            mine = (lane >= HD) if half else (lane < HD)
            scores = mm_bt(key, jnp.where(mine, query, 0).astype(BF))
            scores = jnp.where(key_row < length, scores, -1e30)
            top = jnp.max(scores, axis=0, keepdims=True)
            weights = jnp.exp(scores - top)
            total = jnp.sum(weights, axis=0, keepdims=True)
            probs = (weights * (1.0 / total)).astype(BF)
            mixed.append(mm_at(probs, value))
            lse_ref[image, pl.ds(pair * 2 + half, 1), :] = top + jnp.log(total)
        o_ref[rows, place] = jnp.where(lane < HD, mixed[0], mixed[1]).astype(BF)
        return carry

    lax.fori_loop(0, images * pairs, pair_step, 0)
    out_matrix = jnp.concatenate(
        [flat_rows(w_ref[:, t, :, 3 * third :]) for t in range(2)], axis=1
    )
    after = hidden + mm_bt(o_ref[...], out_matrix) + ob_ref[...]
    a_ref[...] = after
    if router_on:
        unit2, _ = norm_parts(after)
        normed2 = unit2 * g2_ref[...] + b2_ref[...]
        rb_ref[...] = normed2.astype(BF)
        logits = jnp.dot(normed2, rt_ref[...], precision=EXACT, preferred_element_type=F32)
        lanes = lax.broadcasted_iota(jnp.int32, logits.shape, 1)
        live = lanes < router_on
        logits = jnp.where(live, logits, -1e30)
        gates = jnp.exp(logits - jnp.max(logits, axis=-1, keepdims=True))
        gates = gates / jnp.sum(gates, axis=-1, keepdims=True)
        gates = jnp.where(live, gates, 0.0)
        gp_ref[...] = gates
        first = jnp.sum(jnp.where(lanes == sel_ref[:, 0:1], gates, 0.0), axis=-1, keepdims=True)
        second = jnp.sum(jnp.where(lanes == sel_ref[:, 1:2], gates, 0.0), axis=-1, keepdims=True)
        wt_ref[...] = jnp.where(lanes == 0, first, jnp.where(lanes == 1, second, 0.0))


def attention_forward(
    hidden, gain, shift, weights, layer, qkv_bias, out_bias, length, pad, start, count,
    router=None,
):
    micro = 2
    rows, width = hidden.shape
    heads = width // HD
    block = rows // micro
    lse_rows = round_up(heads, 8)
    images = block // pad
    made = count * block
    in_specs = [
        pl.BlockSpec((block, width), lambda step: (start + step, 0)),
        whole((1, width)), whole((1, width)),
        weight_spec(weights, 2, 2 * width, lambda *_: (0, 0, 0, layer)),
        whole((1, 3 * width)), whole((1, width)),
    ]
    args = [hidden, gain, shift, weights, qkv_bias, out_bias]
    out_specs = [
        rows_of(block, 3 * width),
        pl.BlockSpec((images, lse_rows, pad), lambda step: (step, 0, 0)),
        rows_of(block, width),
        rows_of(block, width),
    ]
    out_shape = [
        jax.ShapeDtypeStruct((made, 3 * width), BF),
        jax.ShapeDtypeStruct((count * images, lse_rows, pad), F32),
        jax.ShapeDtypeStruct((made, width), BF),
        jax.ShapeDtypeStruct((made, width), F32),
    ]
    router_on = 0
    if router is not None:
        gain2, shift2, router_wide, select, router_on = router
        lanes = router_wide.shape[1]
        in_specs += [
            whole((1, width)), whole((1, width)), whole((width, lanes)),
            pl.BlockSpec((block, 2), lambda step: (start + step, 0)),
        ]
        args += [gain2, shift2, router_wide, select]
        out_specs += [rows_of(block, width), rows_of(block, lanes), rows_of(block, lanes)]
        out_shape += [
            jax.ShapeDtypeStruct((made, width), BF),
            jax.ShapeDtypeStruct((made, lanes), F32),
            jax.ShapeDtypeStruct((made, lanes), F32),
        ]
    return call(
        functools.partial(attn_fwd_kernel, length, pad, heads, router_on),
        (count,), in_specs, out_specs, out_shape, [],
        8.0 * made * width * width + 16.0 * made * pad * width, 12.0e6, "attn_fwd",
    )(*args)


def attn_core_kernel(
    length, pad, heads, da_ref, wo_ref, qkv_ref, lse_ref, dqkv_ref, low_ref, grad_sc,
):
    width = da_ref.shape[1]
    images = da_ref.shape[0] // pad
    pairs = heads // 2
    low = da_ref[...].astype(BF)
    low_ref[...] = low
    out_matrix = jnp.concatenate([flat_rows(wo_ref[:, t]) for t in range(2)], axis=1)
    grad_sc[...] = mm(low, out_matrix).astype(BF)
    lane = lax.broadcasted_iota(jnp.int32, (pad, 2 * HD), 1)
    key_row = lax.broadcasted_iota(jnp.int32, (pad, pad), 0)

    def pair_step(step, carry):
        image = step // pairs
        pair = step % pairs
        rows = pl.ds(pl.multiple_of(image * pad, ROW_PAD), pad)

        def col(part):
            side = pair // (pairs // 2)
            at = (side * 3 + part) * (width // 2) + (pair % (pairs // 2)) * 2 * HD
            return pl.ds(pl.multiple_of(at, 2 * HD), 2 * HD)

        place = pl.ds(pl.multiple_of(pair * 2 * HD, 2 * HD), 2 * HD)

        query = (qkv_ref[rows, col(0)] * HD ** (-0.5)).astype(BF)
        key = qkv_ref[rows, col(1)]
        value = qkv_ref[rows, col(2)]
        mixed = grad_sc[rows, place]
        parts = []
        for half in range(2):
            mine = (lane >= HD) if half else (lane < HD)
            scores = mm_bt(key, jnp.where(mine, query, 0).astype(BF))
            total = lse_ref[image, pl.ds(pair * 2 + half, 1), :]
            probs = jnp.where(key_row < length, jnp.exp(scores - total), 0.0)
            probs_grad = mm_bt(value, jnp.where(mine, mixed, 0).astype(BF))
            product = probs * probs_grad
            delta = jnp.sum(product, axis=0, keepdims=True)
            score_grad = (product - probs * delta).astype(BF)
            parts.append((
                mm_at(score_grad, key) * HD ** (-0.5),
                mm(score_grad, query),
                mm(probs.astype(BF), mixed),
            ))
        for part in range(3):
            dqkv_ref[rows, col(part)] = jnp.where(
                lane < HD, parts[0][part], parts[1][part]
            ).astype(BF)
        return carry

    lax.fori_loop(0, images * pairs, pair_step, 0)


def attention_core_back(incoming, weights, layer, stored, length, pad, which, after=()):
    qkv, lse, block = stored
    width = incoming.shape[1]
    heads = width // HD
    images = block // pad
    return call(
        functools.partial(attn_core_kernel, length, pad, heads),
        (1,),
        [
            half_of(incoming, block, which),
            weight_spec(weights, 2, width // 2, lambda *_: (0, 0, 0, 4 * layer + 3)),
            half_of(qkv, block, which),
            half_of(lse, images, which),
        ],
        [whole((block, 3 * width)), whole((block, width))],
        [
            jax.ShapeDtypeStruct((block, 3 * width), BF),
            jax.ShapeDtypeStruct((block, width), BF),
        ],
        [pltpu.VMEM((block, width), BF)],
        2.0 * block * width * width + 20.0 * block * pad * width * 4, 8.0e6, "attn_core",
        after,
    )(incoming, weights, qkv, lse)


def attn_grad_kernel(
    core_ref, da0_ref, da1_ref, h_ref, g_ref, b_ref, w_ref, dq0_ref, dq1_ref,
    low0_ref, low1_ref, o0_ref, o1_ref, *outs,
):
    dw_refs = outs[: len(outs) - 5]
    dh_ref, dqb_ref, dob_ref, dg_ref, db_ref = outs[len(outs) - 5 :]
    width = h_ref.shape[1]
    block = dq0_ref.shape[0]
    gain = g_ref[...]
    unit, scale = norm_parts(h_ref[...])
    normed = (unit * gain + b_ref[...]).astype(BF)
    half = (slice(0, block), slice(block, 2 * block))
    third = width // 2
    normed_grad = [None, None]
    for t in range(2):
        cols = slice(t * 3 * third, (t + 1) * 3 * third)
        matrix = flat_rows(w_ref[:, t, :, : 3 * third])
        piece = sums = mix = None
        sides = ((dq0_ref, low0_ref, o0_ref), (dq1_ref, low1_ref, o1_ref))
        for side, (dq_ref, low_ref, o_ref) in enumerate(sides):
            grads = dq_ref[:, cols]
            term = mm_bt(grads, matrix)
            normed_grad[side] = term if t == 0 else normed_grad[side] + term
            outer = mm_at(normed[half[side]], grads)
            total = jnp.sum(grads.astype(F32), axis=0, keepdims=True)
            out = mm_at(low_ref[...], o_ref[:, t * third : (t + 1) * third])
            piece = outer if side == 0 else piece + outer
            sums = total if side == 0 else sums + total
            mix = out if side == 0 else mix + out
        put_grad(dw_refs, core_ref, t, slice(0, 3 * third), piece.astype(BF))
        put_grad(dw_refs, core_ref, t, slice(3 * third, 4 * third), mix.astype(BF))
        dqb_ref[:, cols] = sums
    dob_ref[...] = jnp.sum(low0_ref[...].astype(F32), axis=0, keepdims=True) + jnp.sum(
        low1_ref[...].astype(F32), axis=0, keepdims=True
    )
    for side, da_ref in enumerate((da0_ref, da1_ref)):
        hidden_grad, gain_grad, shift_grad = norm_pull(
            unit[half[side]], scale[half[side]], gain, normed_grad[side]
        )
        dh_ref[half[side], :] = (da_ref[...] + hidden_grad).astype(dh_ref.dtype)
        if side == 0:
            dg_ref[...] = gain_grad
            db_ref[...] = shift_grad
        else:
            dg_ref[...] += gain_grad
            db_ref[...] += shift_grad


def attention_grad(
    core, incoming, hidden, gain, shift, weights, layer, cores, mixed, devices, split, kind,
    after=(),
):
    rows, width = hidden.shape
    shapes = grad_shapes(devices, width, 2 * width, split)
    block = rows // 2
    short = jax.ShapeDtypeStruct((1, width), F32)
    made = call(
        attn_grad_kernel, (1,),
        [
            half_of(incoming[0], block, 0), half_of(incoming[1], block, 1),
            whole((rows, width)), whole((1, width)), whole((1, width)),
            weight_spec(weights, 2, 2 * width, lambda *_: (0, 0, 0, layer)),
            whole((block, 3 * width)), whole((block, 3 * width)),
            whole((block, width)), whole((block, width)),
            half_of(mixed[0], block, 0), half_of(mixed[1], block, 1),
        ],
        [whole(shape) for shape in shapes] + [
            whole((rows, width)), whole((1, 3 * width)),
            whole((1, width)), whole((1, width)), whole((1, width)),
        ],
        [jax.ShapeDtypeStruct(shape, BF) for shape in shapes] + [
            jax.ShapeDtypeStruct((rows, width), kind),
            jax.ShapeDtypeStruct((1, 3 * width), F32),
            short, short, short,
        ],
        [],
        14.0 * rows * width * width, 25.0e6, "attn_grad", after, prefetch=1,
    )(core, *incoming, hidden, gain, shift, weights, cores[0][0], cores[1][0], cores[0][1],
      cores[1][1], *mixed)
    return made[: len(shapes)], made[len(shapes) :]


def dense_fwd_kernel(a_ref, g_ref, b_ref, win_ref, wout_ref, bin_ref, bout_ref, x_ref, m_sc, acc):
    step = pl.program_id(0)

    @pl.when(step == 0)
    def _():
        unit, _ = norm_parts(a_ref[...])
        m_sc[...] = (unit * g_ref[...] + b_ref[...]).astype(BF)
        acc[...] = a_ref[...] + bout_ref[...]

    preact = mm(m_sc[...], flat_rows(win_ref[...])) + bin_ref[...]
    active = gelu_value(preact).astype(BF)
    acc[...] += mm_bt(active, flat_rows(wout_ref[...]))

    @pl.when(step == pl.num_programs(0) - 1)
    def _():
        x_ref[...] = acc[...]


def dense_specs(weights, at, ff):
    devices, _, rows, _ = weights.shape
    steps = ff // 2 // FF_BLOCK
    block = (devices, 1, rows, FF_BLOCK)
    start = at // FF_BLOCK
    return [
        pl.BlockSpec(block, lambda c, *_: (0, c // steps, 0, start + c % steps)),
        pl.BlockSpec(block, lambda c, *_: (0, c // steps, 0, start + steps + c % steps)),
        pl.BlockSpec((1, FF_BLOCK), lambda c, *_: (0, c)),
    ]


def dense_forward(hidden, gain, shift, weights, at, in_bias, out_bias):
    rows, width = hidden.shape
    ff = in_bias.shape[1]
    return call(
        dense_fwd_kernel, (ff // FF_BLOCK,),
        [whole((rows, width)), whole((1, width)), whole((1, width))]
        + dense_specs(weights, at, ff) + [whole((1, width))],
        whole((rows, width)),
        jax.ShapeDtypeStruct((rows, width), F32),
        [pltpu.VMEM((rows, width), BF), pltpu.VMEM((rows, width), F32)],
        4.0 * rows * width * ff, 15.0e6, "dense_fwd",
    )(hidden, gain, shift, weights, weights, in_bias, out_bias)


def dense_bwd_kernel(
    core_ref, dx_ref, a_ref, g_ref, b_ref, win_ref, wout_ref, bin_ref, *rest,
):
    dw_refs = rest[: len(rest) - 8]
    da_ref, dbin_ref, dbout_ref, dg_ref, db_ref, m_sc, low_sc, acc = rest[len(rest) - 8 :]
    step = pl.program_id(0)

    @pl.when(step == 0)
    def _():
        unit, _ = norm_parts(a_ref[...])
        m_sc[...] = (unit * g_ref[...] + b_ref[...]).astype(BF)
        low = dx_ref[...].astype(BF)
        low_sc[...] = low
        dbout_ref[...] = jnp.sum(low.astype(F32), axis=0, keepdims=True)
        acc[...] = jnp.zeros_like(acc)

    normed = m_sc[...]
    low = low_sc[...]
    in_matrix = flat_rows(win_ref[...])
    preact = mm(normed, in_matrix) + bin_ref[...]
    active, slope = gelu_pair(preact)
    preact_grad = (slope * mm(low, flat_rows(wout_ref[...]))).astype(BF)
    dbin_ref[...] = jnp.sum(preact_grad.astype(F32), axis=0, keepdims=True)
    every = slice(None)
    put_grad(dw_refs, core_ref, 1, every, mm_at(low, active.astype(BF)).astype(BF))
    put_grad(dw_refs, core_ref, 0, every, mm_at(normed, preact_grad).astype(BF))
    acc[...] += mm_bt(preact_grad, in_matrix)

    @pl.when(step == pl.num_programs(0) - 1)
    def _():
        unit, scale = norm_parts(a_ref[...])
        hidden_grad, gain_grad, shift_grad = norm_pull(unit, scale, g_ref[...], acc[...])
        da_ref[...] = dx_ref[...] + hidden_grad
        dg_ref[...] = gain_grad
        db_ref[...] = shift_grad


def dense_back(core, incoming, hidden, gain, shift, weights, at, in_bias, devices, split,
               after=()):
    rows, width = hidden.shape
    ff = in_bias.shape[1]
    shapes = grad_shapes(devices, width, ff, split)
    short = jax.ShapeDtypeStruct((1, width), F32)
    made = call(
        dense_bwd_kernel, (ff // FF_BLOCK,),
        [whole((rows, width)), whole((rows, width)), whole((1, width)), whole((1, width))]
        + dense_specs(weights, at, ff),
        [grad_block(shape, FF_BLOCK, lambda c, *_: c) for shape in shapes] + [
            whole((rows, width)), pl.BlockSpec((1, FF_BLOCK), lambda c, *_: (0, c)),
            whole((1, width)), whole((1, width)), whole((1, width)),
        ],
        [jax.ShapeDtypeStruct(shape, BF) for shape in shapes] + [
            jax.ShapeDtypeStruct((rows, width), F32), jax.ShapeDtypeStruct((1, ff), F32),
            short, short, short,
        ],
        [
            pltpu.VMEM((rows, width), BF), pltpu.VMEM((rows, width), BF),
            pltpu.VMEM((rows, width), F32),
        ],
        10.0 * rows * width * ff, 35.0e6, "dense_bwd", after, prefetch=1,
    )(core, incoming, hidden, gain, shift, weights, weights, in_bias)
    return made[: len(shapes)], made[len(shapes) :]


def moe_kernel(
    capp,
    rb_own0, rb_own1, rb_oth0, rb_oth1, og_own, og_oth, dr_ref, dc_own, dc_oth, w_ref,
    win_ref, wout_ref, bin_ref, bout_ref,
    yc_own, yc_oth, rc_own, rc_oth0, rc_oth1, dg_own, dg_oth, dw_ref, dbin_ref, dbout_ref,
    b_sc, og_sc, dy_sc, w_sc, y_acc, r_acc, yo_acc, yt_acc, ro_acc, rt_acc,
):
    micro = 2
    expert = pl.program_id(0)
    chunk = pl.program_id(1)
    last_expert = expert == pl.num_programs(0) - 1
    last_chunk = chunk == pl.num_programs(1) - 1
    half = rb_own0.shape[0]
    rb_all = ((rb_own0, rb_oth0), (rb_own1, rb_oth1))

    @pl.when(chunk == 0)
    def _():
        for m in range(micro):
            slots = slice(m * capp, (m + 1) * capp)
            ids = lax.broadcasted_iota(jnp.int32, (capp, half), 0) + expert * capp
            tokens = None
            for side, og in enumerate((og_own, og_oth)):
                hit0 = dr_ref[m, 2 * side : 2 * side + 1, :] == ids
                hit1 = dr_ref[m, 2 * side + 1 : 2 * side + 2, :] == ids
                pick = jnp.where(hit0 | hit1, 1.0, 0.0).astype(BF)
                gate = jnp.sum(
                    jnp.where(hit0, w_ref[m, 2 * side : 2 * side + 1, :], 0.0)
                    + jnp.where(hit1, w_ref[m, 2 * side + 1 : 2 * side + 2, :], 0.0),
                    axis=-1, keepdims=True,
                )
                found = (mm(pick, rb_all[m][side][...]), mm(pick, og[m]), gate)
                tokens = found if tokens is None else tuple(
                    one + two for one, two in zip(tokens, found)
                )
            b_sc[slots, :] = tokens[0].astype(BF)
            og_sc[slots, :] = tokens[1].astype(BF)
            dy_sc[slots, :] = (tokens[1] * tokens[2]).astype(BF)
            w_sc[slots, :] = jnp.broadcast_to(tokens[2], (capp, w_sc.shape[1]))
        y_acc[...] = jnp.zeros_like(y_acc)
        r_acc[...] = jnp.zeros_like(r_acc)

    tokens = b_sc[...]
    low = dy_sc[...]
    preact = mm(tokens, win_ref[...]) + bin_ref[0]
    active, slope = gelu_pair(preact)
    active = active.astype(BF)
    preact_grad = (slope * mm(low, wout_ref[...])).astype(BF)
    dbin_ref[0] = jnp.sum(preact_grad.astype(F32), axis=0, keepdims=True)
    y_acc[...] += mm_bt(active, wout_ref[...])
    r_acc[...] += mm_bt(preact_grad, win_ref[...])
    every = slice(None)
    put_grad((dw_ref,), None, 1, every, mm_at(low, active).astype(BF))
    put_grad((dw_ref,), None, 0, every, mm_at(tokens, preact_grad).astype(BF))

    @pl.when(last_chunk)
    def _():
        dbout_ref[0] = jnp.sum(dy_sc[...].astype(F32), axis=0, keepdims=True)
        for m in range(micro):
            slots = slice(m * capp, (m + 1) * capp)
            result = y_acc[slots, :] + 0.5 * bout_ref[0]
            dots = jnp.sum(og_sc[slots, :].astype(F32) * result, axis=-1, keepdims=True)
            lanes = lax.broadcasted_iota(jnp.int32, (capp, 128), 1)
            dots = jnp.where(lanes == expert, dots, 0.0)
            weighted = (w_sc[slots, 0:1] * result).astype(BF)
            rows_grad = r_acc[slots, :].astype(BF)
            ids = lax.broadcasted_iota(jnp.int32, (half, capp), 1) + expert * capp
            for dc, yc, rc, dg in (
                (dc_own, yo_acc, ro_acc, dg_own), (dc_oth, yt_acc, rt_acc, dg_oth)
            ):
                hit = (dc[m, :, 0:1] == ids) | (dc[m, :, 1:2] == ids)
                pick = jnp.where(hit, 1.0, 0.0)
                low_pick = pick.astype(BF)
                y_new = mm(low_pick, weighted)
                r_new = mm(low_pick, rows_grad)
                d_new = lax.dot_general(
                    dots, pick, (((0,), (1,)), ((), ())), precision=EXACT,
                    preferred_element_type=F32,
                )[: dg.shape[1]]

                @pl.when(expert == 0)
                def _():
                    yc[m] = y_new
                    rc[m] = r_new
                    dg[m] = d_new

                @pl.when(expert > 0)
                def _():
                    yc[m] += y_new
                    rc[m] += r_new
                    dg[m] += d_new

    @pl.when(last_chunk & last_expert)
    def _():
        yc_own[...] = yo_acc[...].astype(BF)
        yc_oth[...] = yt_acc[...].astype(BF)
        rc_own[...] = ro_acc[...].astype(BF)
        rc_oth0[...] = rt_acc[0].astype(BF)
        rc_oth1[...] = rt_acc[1].astype(BF)


def mixture(rows_own, rows_oth, grad_own, grad_oth, place_rows, place_own, place_oth, gates,
            weights, in_bias, out_bias, capp, devices):
    micro, half, width = grad_own.shape
    experts, _, ff = in_bias.shape
    steps = ff // FF_BLOCK
    blocks = experts * steps
    slots = micro * capp
    w_block = (width, FF_BLOCK)
    group = (micro, half, width)
    dots = (micro, 8, half)
    flat = (half, width)
    (shape,) = grad_shapes(devices, width, experts * ff, False)
    return call(
        functools.partial(moe_kernel, capp),
        (experts, steps),
        [
            whole(flat), whole(flat), whole(flat), whole(flat), whole(group), whole(group),
            whole(place_rows.shape), whole(place_own.shape), whole(place_oth.shape),
            whole(gates.shape),
            pl.BlockSpec(w_block, lambda e, c: (0, e * steps + c)),
            pl.BlockSpec(w_block, lambda e, c: (0, blocks + e * steps + c)),
            pl.BlockSpec((1, 1, FF_BLOCK), lambda e, c: (e, 0, c)),
            pl.BlockSpec((1, 1, width), lambda e, c: (e, 0, 0)),
        ],
        [
            whole(group), whole(group), whole(group), whole(flat), whole(flat),
            whole(dots), whole(dots),
            grad_block(shape, FF_BLOCK, lambda e, c: e * steps + c),
            pl.BlockSpec((1, 1, FF_BLOCK), lambda e, c: (e, 0, c)),
            pl.BlockSpec((1, 1, width), lambda e, c: (e, 0, 0)),
        ],
        [
            jax.ShapeDtypeStruct(group, BF), jax.ShapeDtypeStruct(group, BF),
            jax.ShapeDtypeStruct(group, BF), jax.ShapeDtypeStruct(flat, BF),
            jax.ShapeDtypeStruct(flat, BF),
            jax.ShapeDtypeStruct(dots, F32), jax.ShapeDtypeStruct(dots, F32),
            jax.ShapeDtypeStruct(shape, BF),
            jax.ShapeDtypeStruct((experts, 1, ff), F32),
            jax.ShapeDtypeStruct((experts, 1, width), F32),
        ],
        [
            pltpu.VMEM((slots, width), BF), pltpu.VMEM((slots, width), BF),
            pltpu.VMEM((slots, width), BF), pltpu.VMEM((slots, 128), F32),
            pltpu.VMEM((slots, width), F32), pltpu.VMEM((slots, width), F32),
            pltpu.VMEM(group, F32), pltpu.VMEM(group, F32),
            pltpu.VMEM(group, F32), pltpu.VMEM(group, F32),
        ],
        12.0 * slots * experts * width * ff + 16.0 * experts * micro * capp * half * width,
        60.0e6, "experts",
    )(*rows_own, *rows_oth, grad_own, grad_oth, place_rows, place_own, place_oth, gates,
      weights, weights, in_bias, out_bias)


def gate_bwd_kernel(
    a_ref, og_ref, held_ref, ro_ref, rr_ref, do_ref, dr_ref, gp_ref, rt_ref, g_ref, b_ref,
    sent_ref, da_ref, drt_ref, dg_ref, db_ref,
):
    after = a_ref[...]
    incoming = og_ref[0].astype(F32)
    sent_ref[...] = held_ref[...]
    gates = gp_ref[...]
    found = do_ref[0] + dr_ref[0]
    spread = jnp.where(
        lax.broadcasted_iota(jnp.int32, (found.shape[0], gates.shape[1]), 0)
        == lax.broadcasted_iota(jnp.int32, (found.shape[0], gates.shape[1]), 1),
        1.0, 0.0,
    )
    gate_grad = lax.dot_general(
        found, spread, (((0,), (0,)), ((), ())), precision=EXACT, preferred_element_type=F32
    )
    logit_grad = gates * (gate_grad - jnp.sum(gates * gate_grad, axis=-1, keepdims=True))
    unit, scale = norm_parts(after)
    normed = unit * g_ref[...] + b_ref[...]
    drt_ref[...] = lax.dot_general(
        logit_grad, normed, (((0,), (0,)), ((), ())), precision=EXACT, preferred_element_type=F32
    )
    normed_grad = ro_ref[0].astype(F32) + rr_ref[...].astype(F32)
    normed_grad += lax.dot_general(
        logit_grad, rt_ref[...], (((1,), (1,)), ((), ())), precision=EXACT,
        preferred_element_type=F32,
    )
    hidden_grad, gain_grad, shift_grad = norm_pull(unit, scale, g_ref[...], normed_grad)
    da_ref[...] = incoming + hidden_grad
    dg_ref[...] = gain_grad
    db_ref[...] = shift_grad


def gate_back(after, incoming, held, r_own, r_got, d_own, d_got, gates, router, gain, shift,
              which, behind=()):
    block, width = after.shape
    lanes = gates.shape[1]
    one = pl.BlockSpec((1, block, width), lambda *_: (which, 0, 0))
    dots = pl.BlockSpec((1, 8, block), lambda *_: (which, 0, 0))
    flat = whole((block, width))
    low = whole((block, lanes))
    return call(
        gate_bwd_kernel, (1,),
        [
            flat, one, whole(held.shape), one, flat, dots, dots, low,
            whole((width, lanes)), whole((1, width)), whole((1, width)),
        ],
        [whole(held.shape), flat, whole((lanes, width)), whole((1, width)), whole((1, width))],
        [
            jax.ShapeDtypeStruct(held.shape, BF),
            jax.ShapeDtypeStruct((block, width), F32),
            jax.ShapeDtypeStruct((lanes, width), F32),
            jax.ShapeDtypeStruct((1, width), F32),
            jax.ShapeDtypeStruct((1, width), F32),
        ],
        [], 4.0 * block * width * lanes, 7.0e6, "gate_bwd", behind,
    )(after, incoming, held, r_own, r_got, d_own, d_got, gates, router, gain, shift)


def swap(value):
    return lax.ppermute(value, "tensor", [(0, 1), (1, 0)])


def in_order(mine, other, axis):
    first = lax.axis_index("tensor") == 0
    return jnp.stack([jnp.where(first, mine, other), jnp.where(first, other, mine)], axis=axis)


def gather_rows(share):
    return lax.all_gather(share, "dp", axis=0, tiled=True)


def chip_ring(chips):
    if chips == 8:
        return [0, 2, 4, 6, 7, 5, 3, 1]
    return list(range(chips))


def ring_add_kernel(kind, at_ref, *refs):
    def chunk(grads, given):
        return grads[0].astype(F32) + given[0].astype(F32)

    if kind == 0:
        grads, given, ahead, behind = refs
        total = chunk(grads, given).astype(BF)
        ahead[...] = total[0]
        behind[...] = total[1]
    elif kind == 3:
        grads, given, got_a, got_b, out = refs
        out[...] = chunk(grads, given) + (got_a[...].astype(F32) + got_b[...].astype(F32))
    else:
        grads_a, given_a, grads_b, given_b, got_a, got_b, ahead, behind = refs
        one, two = chunk(grads_a, given_a), chunk(grads_b, given_b)
        if kind == 1:
            ahead[0] = (one[0] + got_a[...].astype(F32)).astype(BF)
            ahead[1] = one[1].astype(BF)
            behind[0] = two[0].astype(BF)
            behind[1] = (two[1] + got_b[...].astype(F32)).astype(BF)
        else:
            ahead[...] = (one + got_a[...].astype(F32)).astype(BF)
            behind[...] = (two + got_b[...].astype(F32)).astype(BF)


class RingSum:
    def __init__(self, kept, sent):
        count = lax.axis_size("dp")
        self.chips = count // 2
        self.ring = chip_ring(self.chips)
        position = [self.ring.index(chip) for chip in range(self.chips)]
        self.here = jnp.array(position, jnp.int32)[lax.axis_index("dp") // 2]
        self.kept = kept
        self.away = self.chips // 2
        self.messages = (sent,)
        self.given = lax.ppermute(sent, "dp", [(at, at ^ 1) for at in range(count)])
        self.got = ()
        self.result = None

    def send(self, value, step):
        pairs = [
            (self.ring[at] * 2 + side, self.ring[(at + step) % self.chips] * 2 + side)
            for at in range(self.chips)
            for side in range(2)
        ]
        return lax.ppermute(value, "dp", pairs)

    def step(self, after=()):
        if self.result is not None:
            return
        table = jnp.array(self.ring, jnp.int32)
        away = self.away
        chips = [table[(self.here + away) % self.chips], table[(self.here - away) % self.chips]]
        places = jnp.stack(chips).astype(jnp.int32)
        shape = self.kept.shape[1:]

        def chunk_specs(which):
            return [
                pl.BlockSpec((1,) + shape, lambda _, at: (at[which], 0, 0, 0)),
                pl.BlockSpec((1,) + shape, lambda _, at: (at[which], 0, 0, 0)),
            ]

        far = self.chips // 2
        kind = 3 if away == 0 else 0 if away == far else 1 if away == far - 1 else 2
        two_ways = kind in (1, 2)
        in_specs = chunk_specs(0) + (chunk_specs(1) if two_ways else [])
        args = [self.kept, self.given] * (2 if two_ways else 1) + list(self.got)
        in_specs += [whole(got.shape) for got in self.got]
        out = shape if kind else shape[1:]
        kinds = [jax.ShapeDtypeStruct(out, F32 if kind == 3 else BF)] * (1 if kind == 3 else 2)
        sums = call(
            functools.partial(ring_add_kernel, kind), (1,), in_specs,
            [whole(out)] * len(kinds), kinds, [], 0, 1.0e6, "ring_add", after, prefetch=1,
        )(places, *args)
        self.away -= 1
        if kind == 3:
            self.result = sums[0]
            self.messages = ()
            return
        self.messages = tuple(sums)
        self.got = (self.send(sums[0], 1), self.send(sums[1], -1))


class PlainSum:
    def __init__(self, grad):
        axis = 1 if grad.ndim == 3 else 0
        done = lax.psum_scatter(grad, "dp", scatter_dimension=axis, tiled=True)
        self.messages = (done,)
        self.result = done.reshape((2,) + done.shape[-2:]).astype(F32)

    def step(self, after=()):
        return


def add_kernel(one_ref, two_ref, out_ref):
    out_ref[...] = one_ref[...] + two_ref[...]


class PairSum:
    def __init__(self, value):
        self.count = lax.axis_size("dp")
        self.value = value
        self.stage = 1
        self.send()

    def send(self):
        self.messages = (self.value,)
        if self.stage < self.count:
            pairs = [(at, at ^ self.stage) for at in range(self.count)]
            self.got = lax.ppermute(self.value, "dp", pairs)
        elif self.stage == self.count:
            self.got = swap(self.value)
        else:
            self.got = None
            self.messages = ()
        self.stage *= 2

    def step(self, after=()):
        if self.got is None:
            return
        shape = self.value.shape
        (self.value,) = call(
            add_kernel, (1,), [whole(shape)] * 2, [whole(shape)],
            [jax.ShapeDtypeStruct(shape, F32)], [], 0, 3.0e5, "small_add", after,
        )(self.value, self.got)
        self.send()


def pack_kernel(plan, side_ref, *refs):
    out_ref = refs[-1]
    width = out_ref.shape[1]
    out_ref[...] = jnp.zeros_like(out_ref)
    at = 0
    for inputs, rows, factor, sided in plan:
        total = None
        for which in inputs:
            ref = refs[which]
            value = ref[...].reshape(-1, ref.shape[-1])[:rows]
            total = value if total is None else total + value
        total = total * factor if factor != 1.0 else total
        parts = total.shape[1] // width
        for row in range(rows):
            for part in range(parts):
                piece = total[row : row + 1, part * width : (part + 1) * width]
                place = at + row * parts + part
                if sided:
                    place = place + side_ref[0] * (rows * parts)
                out_ref[pl.ds(place, 1), :] = piece
        at += rows * parts * (2 if sided else 1)


def pack_rows(groups, width):
    arrays, plan, total = [], [], 0
    for values, rows, factor, sided in groups:
        plan.append((tuple(range(len(arrays), len(arrays) + len(values))), rows, factor, sided))
        arrays += values
        total += rows * (values[0].shape[-1] // width) * (2 if sided else 1)
    shape = (round_up(total, 8), width)
    side = lax.axis_index("tensor").reshape(1)
    (out,) = call(
        functools.partial(pack_kernel, tuple(plan)), (1,),
        [whole(value.shape) for value in arrays], [whole(shape)],
        [jax.ShapeDtypeStruct(shape, F32)], [], 0, 3.0e5, "pack", (), prefetch=1,
    )(side, *arrays)
    return out


def out_kernel(a0_ref, a1_ref, y_ref, got_ref, out_ref):
    for m, a_ref in enumerate((a0_ref, a1_ref)):
        total = a_ref[...] + (y_ref[m].astype(F32) + got_ref[m].astype(F32))
        out_ref[m] = total.astype(BF)


def layer_output(hidden, y_own, y_got, after):
    shape = y_own.shape
    (out,) = call(
        out_kernel, (1,),
        [whole(hidden[0].shape)] * 2 + [whole(shape)] * 2, [whole(shape)],
        [jax.ShapeDtypeStruct(shape, BF)], [], 0, 8.0e6, "layer_output", after,
    )(*hidden, y_own, y_got)
    return out


def place_kernel(side_ref, own_ref, got_ref, out_ref):
    images, length = own_ref.shape[1], out_ref.shape[2]
    side = side_ref[0]
    for image in range(images):
        kept = own_ref[:, image, :length, :].astype(out_ref.dtype)
        out_ref[:, side * images + image] = kept
        other = got_ref[:, image, :length, :].astype(out_ref.dtype)
        out_ref[:, (1 - side) * images + image] = other


def place_images(own, got, shape, kind, after):
    micro, images, length, width = shape
    padded = (micro, images // 2, own.size // (micro * (images // 2) * width), width)
    side = lax.axis_index("tensor").reshape(1)
    (out,) = call(
        place_kernel, (micro,),
        [pl.BlockSpec((1,) + padded[1:], lambda m, *_: (m, 0, 0, 0))] * 2,
        [pl.BlockSpec((1,) + shape[1:], lambda m, *_: (m, 0, 0, 0))],
        [jax.ShapeDtypeStruct(shape, kind)], [], 0, 8.0e6, "place", after, prefetch=1,
    )(side, own.reshape(padded), got.reshape(padded))
    return out


def join_sides(mine_first):
    mine = lax.axis_index("tensor")
    kept = lax.dynamic_index_in_dim(mine_first, mine, 0, keepdims=False)
    sent = lax.dynamic_index_in_dim(mine_first, 1 - mine, 0, keepdims=False)
    return kept + swap(sent)


def own_half(value, axis):
    size = value.shape[axis] // 2
    return lax.dynamic_slice_in_dim(value, lax.axis_index("tensor") * size, size, axis)


def local(
    block_input, norm_gain, row_bias, qkv_weight, qkv_bias, out_weight, mlp_in, mlp_in_bias,
    mlp_out, mlp_out_bias, router, expert_in, expert_in_bias, expert_out, expert_out_bias,
    routes, slot_index, out_grad,
):
    micro, images, length, width = block_input.shape
    experts = router.shape[1]
    share_rows = mlp_in.shape[0]
    own_images = images // 2
    pad = round_up(length, ROW_PAD)
    half = own_images * pad
    rows = micro * half
    capp = round_up(CAP, ROW_PAD)
    side = lax.axis_index("tensor")

    def attn_share(layer):
        return jnp.concatenate(
            [qkv_weight[layer].reshape(share_rows, -1), out_weight[layer]], axis=1
        )

    devices = lax.axis_size("dp")
    first_mine = jnp.concatenate([attn_share(0), attn_share(1), mlp_in, mlp_out], axis=1)
    first_w = lax.all_gather(
        in_order(first_mine, swap(first_mine), 0), "dp", axis=0, tiled=False
    )
    if not whole_tiles(devices, width):
        first_w = jnp.moveaxis(first_w, 0, 1).reshape(1, 2, width, -1)
    dense_at = 4 * width
    expert_w = gather_rows(
        jnp.concatenate(
            [expert_in.reshape(share_rows, -1), expert_out.reshape(share_rows, -1)], axis=1
        )
    )

    biases = jnp.concatenate([qkv_bias.reshape(-1), mlp_in_bias])
    bias_pair = in_order(biases, swap(biases), 0)
    qkv_bias_pair = bias_pair[:, : qkv_bias.size].reshape((2,) + qkv_bias.shape)
    mlp_bias_full = bias_pair[:, qkv_bias.size :].reshape(1, -1)

    def qkv_bias_row(layer):
        pair = qkv_bias_pair[:, layer]
        zero = jnp.zeros_like(pair[:, 0])
        return jnp.concatenate([pair[:, 0], zero, pair[:, 1]], axis=1).reshape(1, -1)

    def padded(value, start):
        part = lax.dynamic_slice_in_dim(value, start, own_images, 1)
        return jnp.pad(part, ((0, 0), (0, 0), (0, pad - length), (0, 0)))

    mine_at = side * own_images
    other_at = (1 - side) * own_images
    hidden = padded(block_input, mine_at).astype(F32).reshape(rows, width)
    grad_own = padded(out_grad, mine_at).reshape(micro, half, width)
    grad_oth = padded(out_grad, other_at).reshape(micro, half, width)

    kept = slot_index < CAP
    place = jnp.where(kept, routes * capp + slot_index, -1)
    pick = jnp.where(kept, routes, -1)

    def lay(value, start):
        part = lax.dynamic_slice_in_dim(value, start, own_images, 1)
        part = jnp.pad(
            part, ((0, 0), (0, 0), (0, pad - length), (0, 0)), constant_values=-1
        )
        return part.reshape(micro, half, 2)

    place_own, place_oth = lay(place, mine_at), lay(place, other_at)
    place_rows = jnp.concatenate(
        [jnp.swapaxes(place_own, 1, 2), jnp.swapaxes(place_oth, 1, 2)], axis=1
    )
    select = lay(pick, mine_at).reshape(rows, 2)
    router_wide = jnp.pad(router, ((0, 0), (0, 128 - experts)))

    def row(vector):
        return vector.reshape(1, -1)

    qkv_one, lse_one, mix_one, after_one = attention_forward(
        hidden, row(norm_gain[0, 0]), row(row_bias[0, 0]), first_w, 0, qkv_bias_row(0),
        row(row_bias[0, 2]), length, pad, 0, micro,
    )
    after_ffn = dense_forward(
        after_one, row(norm_gain[0, 1]), row(row_bias[0, 1]), first_w, dense_at, mlp_bias_full,
        row(mlp_out_bias),
    )
    second = [
        attention_forward(
            after_ffn, row(norm_gain[1, 0]), row(row_bias[1, 0]), first_w, 1, qkv_bias_row(1),
            row(row_bias[1, 2]), length, pad, m, 1,
            (row(norm_gain[1, 1]), row(row_bias[1, 1]), router_wide, select, experts),
        )
        for m in range(micro)
    ]
    qkv_two, lse_two, mix_two, after_two, rows_own, gates, chosen = zip(*second)
    rows_oth = [swap(part) for part in rows_own]
    gate_own = jnp.stack([part[:, :2].T for part in chosen])
    gate_pair = jnp.concatenate([gate_own, swap(gate_own)], axis=1)
    ring = whole_tiles(devices, width)
    core = (lax.axis_index("dp") % 2).reshape(1)
    (
        y_own, y_oth, r_own, r_oth0, r_oth1, d_own, d_oth, expert_grad, ein_bias, eout_bias,
    ) = mixture(
        rows_own, rows_oth, grad_own, grad_oth, place_rows, place_own, place_oth, gate_pair,
        expert_w, expert_in_bias.reshape(experts, 1, -1),
        expert_out_bias.reshape(experts, 1, -1), capp, devices,
    )
    d_got = swap(d_oth)
    r_got = swap(r_oth0)
    expert_sum = PlainSum(expert_grad)
    grad_two, gate_parts, cores = [], [], []
    for m, held in enumerate((r_oth1, y_oth)):
        sent, grad_part, *small = gate_back(
            after_two[m], grad_own, held, r_own, r_got, d_own, d_got, gates[m],
            router_wide, row(norm_gain[1, 1]), row(row_bias[1, 1]), m,
            (cores[0][1],) if m else (),
        )
        r_got = swap(sent)
        grad_two.append(grad_part)
        gate_parts.append(small)
        cores.append(
            attention_core_back(
                grad_part, first_w, 1, (qkv_two[m], lse_two[m], half), length, pad, m, (sent,)
            )
        )
    y_got = r_got
    router_parts, gain_parts, shift_parts = (list(pair) for pair in zip(*gate_parts))
    two_grad, (grad_ffn, qb_two, ob_two, gain_two, shift_two) = attention_grad(
        core, grad_two, after_ffn, row(norm_gain[1, 0]), row(row_bias[1, 0]), first_w, 1, cores,
        mix_two, devices, ring, F32,
    )
    sum_two = RingSum(*two_grad) if ring else PlainSum(*two_grad)
    early_sum = PairSum(
        pack_rows(
            [
                ([gain_two], 1, 1.0, False), (gain_parts, 1, 1.0, False),
                ([shift_two], 1, 1.0, False), (shift_parts, 1, 1.0, False),
                ([ob_two], 1, 1.0, False), ([qb_two], 1, 1.0, False),
                (router_parts, experts, 1.0, False), ([eout_bias], experts, 0.5, False),
                ([ein_bias], experts, 1.0, True),
            ],
            width,
        )
    )
    dense_grad, (grad_one, in_bias_grad, out_bias_grad, gain_ffn, shift_ffn) = dense_back(
        core, grad_ffn, after_one, row(norm_gain[0, 1]), row(row_bias[0, 1]), first_w, dense_at,
        mlp_bias_full, devices, ring, sum_two.messages + early_sum.messages + (sent,),
    )
    done = (gain_ffn,)
    sum_two.step(done)
    early_sum.step(done)
    dense_sum = RingSum(*dense_grad) if ring else PlainSum(*dense_grad)
    out_own = layer_output(after_two, y_own, y_got, done)
    out_got = swap(out_own)
    chains = (sum_two, dense_sum, early_sum)

    def flying():
        return sum_two.messages + dense_sum.messages + early_sum.messages

    cores = []
    for which in range(2):
        cores.append(
            attention_core_back(
                grad_one, first_w, 0, (qkv_one, lse_one, half), length, pad, which,
                flying() + (out_own,),
            )
        )
        for chain in chains:
            chain.step((cores[-1][1],))
    block_output = place_images(out_own, out_got, block_input.shape, BF, (cores[-1][1],))
    one_grad, (grad_zero, qb_one, ob_one, gain_one, shift_one) = attention_grad(
        core, (grad_one, grad_one), hidden, row(norm_gain[0, 0]), row(row_bias[0, 0]), first_w,
        0, cores, (mix_one, mix_one), devices, ring, BF, flying(),
    )
    one_sum = RingSum(*one_grad) if ring else PlainSum(*one_grad)
    grad_got = swap(grad_zero)
    late_sum = PairSum(
        pack_rows(
            [
                ([gain_one], 1, 1.0, False), ([gain_ffn], 1, 1.0, False),
                ([shift_one], 1, 1.0, False), ([shift_ffn], 1, 1.0, False),
                ([ob_one], 1, 1.0, False), ([qb_one], 1, 1.0, False),
                ([in_bias_grad], 1, 1.0, False), ([out_bias_grad], 1, 1.0, False),
            ],
            width,
        )
    )
    last = (qb_one,)
    queue = [sum_two, one_sum]
    for _ in range(devices):
        queue += [dense_sum, sum_two, early_sum, late_sum, one_sum]
    for chain in queue:
        chain.step(last)
        if chain.messages:
            last = chain.messages
    input_grad = place_images(grad_zero, grad_got, block_input.shape, F32, last)

    expert_grads = expert_sum.result.reshape(2, share_rows, experts, -1)
    attn_grads = [join_sides(one_sum.result), join_sides(sum_two.result)]
    dense_done = join_sides(
        jnp.moveaxis(dense_sum.result.reshape(2, share_rows, 2, -1), 2, 0)
    )
    split_at = 3 * width // 2

    late, early = late_sum.value, early_sum.value
    gain_sum = jnp.concatenate([late[0:2], early[0:2]])
    shift_sum = jnp.concatenate([late[2:5], early[2:5]])
    qb_sum = jnp.stack([late[5:8], early[5:8]]).reshape(2, 2, 3, width // 2)
    qb_sum = lax.dynamic_index_in_dim(qb_sum, side, 1, keepdims=False)
    ff_rows = in_bias_grad.shape[1] // width
    in_bias_sum = late[8 : 8 + ff_rows]
    out_bias_sum = late[8 + ff_rows]
    at = 8 + experts
    router_sum = early[8:at]
    eout_sum = early[at : at + experts]
    at += experts
    ein_rows = expert_in_bias.size // width
    ein_sum = lax.dynamic_slice_in_dim(early, at + side * ein_rows, ein_rows, 0)
    return (
        block_output,
        input_grad,
        gain_sum.reshape(norm_gain.shape),
        shift_sum.reshape(row_bias.shape),
        jnp.stack([part[:, :split_at] for part in attn_grads]).reshape(qkv_weight.shape),
        jnp.stack([qb_sum[:, 0], qb_sum[:, 2]], axis=1),
        jnp.stack([part[:, split_at:] for part in attn_grads]),
        dense_done[0],
        own_half(in_bias_sum.reshape(-1), 0),
        dense_done[1],
        out_bias_sum.reshape(-1),
        router_sum.T,
        expert_grads[0],
        ein_sum.reshape(expert_in_bias.shape),
        expert_grads[1],
        eout_sum.reshape(experts, width),
    )


def solution(mesh):
    return jax.shard_map(
        local,
        mesh=mesh,
        in_specs=(
            P(None, "dp", None, None), P(), P(), P(None, "dp", None, "tensor"),
            P(None, None, "tensor"), P(None, "dp", "tensor"), P("dp", "tensor"), P("tensor"),
            P("dp", "tensor"), P(), P(), P("dp", None, "tensor"), P(None, "tensor"),
            P("dp", None, "tensor"), P(), P(None, "dp", None, None), P(None, "dp", None, None),
            P(None, "dp", None, None),
        ),
        out_specs=(
            P(None, "dp", None, None), P(None, "dp", None, None), P(), P(),
            P(None, "dp", None, "tensor"), P(None, None, "tensor"), P(None, "dp", "tensor"),
            P("dp", "tensor"), P("tensor"), P("dp", "tensor"), P(), P(),
            P("dp", None, "tensor"), P(None, "tensor"), P("dp", None, "tensor"), P(),
        ),
        check_vma=False,
    )
```

time: 811 us -> 737 us (0.909)
  waiting for transfers between devices: 204 us -> 149 us
  Pallas kernels: 383 us -> 409 us
  local copies, waits for them, and re-layouts: 91.3 us -> 74.9 us
  other arithmetic: 31.7 us -> 16.6 us
  starting transfers between devices: 69 us -> 57.7 us
    all_gather x2 -> x1, waiting for transfers between devices: 81 us -> 0.01 us  [gather_rows(): return lax.all_gather(share, 'dp', axis=0, tiled=True)]
    all_gather x0 -> x1, waiting for transfers between devices: none -> 76.6 us  [local(): lax.all_gather(in_order(first_mine, swap(first_mine), 0), 'dp', axis=0, t...]
    ppermute x14 -> x16, waiting for transfers between devices: 83.5 us -> 55.4 us  [swap(): return lax.ppermute(value, 'tensor', [(0, 1), (1, 0)])]
    pallas_call x34 -> x44, Pallas kernels: 383 us -> 409 us  [call(): return lambda *args: made(*args, *after)]
    ppermute x32 -> x24, starting transfers between devices: 40.4 us -> 28 us  [send(): return lax.ppermute(value, 'dp', pairs)]
    ppermute x32 -> x24, waiting for transfers between devices: 24.8 us -> 12.7 us  [send(): return lax.ppermute(value, 'dp', pairs)]
    ppermute x8, waiting for transfers between devices: 14.4 us -> 4.15 us  [send(): self.got = lax.ppermute(self.value, 'dp', pairs)]
    squeeze x6, local copies, waits for them, and re-layouts: 14.3 us -> 5.35 us  [the longest x2 2.67 us: join_sides(): sent = lax.dynamic_index_in_dim(mine_first, 1 - mine, 0, keepdims=False)]
  transfers between devices with their start and end apart: 62 -> 54, of which waited for: 25 -> 12; matrix products, arithmetic and copies ran while one was open for 11% -> 9% of each run, Pallas kernels for 36% -> 43%
where the time goes in v3:
time: 737 us; the launch traced here: 729 us
  Pallas kernels  409 us (55%)
  waiting for transfers between devices  149 us (20%)
  local copies, waits for them, and re-layouts  74.9 us (10%)
  starting transfers between devices  57.7 us (8%)
  between operations  22.3 us (3%)
  other arithmetic  16.6 us (2%)
    pallas_call x44, Pallas kernels, call(): return lambda *args: made(*args, *after)  409 us
    all_gather x1, waiting for transfers between devices, local(): lax.all_gather(in_order(first_mine, swap(first_mine), 0), 'dp', axis=0, t...  76.6 us
    ppermute x16, waiting for transfers between devices, swap(): return lax.ppermute(value, 'tensor', [(0, 1), (1, 0)])  55.4 us
    unnamed x161, local copies, waits for them, and re-layouts  34.9 us
    ppermute x24, starting transfers between devices, send(): return lax.ppermute(value, 'dp', pairs)  28 us
    ppermute x16, starting transfers between devices, swap(): return lax.ppermute(value, 'tensor', [(0, 1), (1, 0)])  20.2 us
  transfers between devices with their start and end apart: 54, of which 12 were waited for; matrix products, arithmetic and copies ran while one was open for 9% of the time, Pallas kernels for 43%

profile of v3, /device:TPU:0, one launch (start us, length us, event | category | flops | bytes accessed | tf_op | source)
XLA Modules:
  0.0 729.5 jit_solution(17508475871218762492)
XLA Ops:
  8.7 3.0 collective-permute-start
  11.7 13.3 %collective-permute-done = bf16[48,6144]{1,0:T(8,128)(2,1)S(1)} collective-permute-done((bf16[48,6144]{1,0:T(8,128)(2,1)S(1)}, bf16[48,6144]{1,0:T(8,128)(2,1)S(1)}, u32[]{:S(2)}, u32[]{:S(2)}) %collective-permute-start) | collective-permute-done | bytes 589856 | tf_op jit(solution)/shard_map/ppermute | solution.py:779
  30.5 6.9 constant_dynamic-slice_fusion.5
  50.2 76.6 %all-gather.6.cloned.1.call-done = bf16[32,48,6144]{2,1,0:T(8,128)(2,1)} async-done(((bf16[2,48,6144]{2,1,0:T(8,128)(2,1)}), bf16[32,48,6144]{2,1,0:T(8,128)(2,1)}) %all-gather.6.cloned.1.call-update) | async-done | bytes 18874384 | tf_op jit(solution)/shard_map/all_gather | solution.py:1037
  126.8 30.4 %attn_fwd.3 = (bf16[832,2304]{1,0:T(8,128)(2,1)}, f32[4,16,208]{2,1,0:T(8,128)}, bf16[832,768]{1,0:T(8,128)(2,1)}, f32[832,768]{1,0:T(8,128)}) custom-call(f32[832,768]{1,0:T(8,128)} %bitcast_convert_fusion.refs_0_.refs_3_, f32[1,768]{1,0:T(1,128)} %get-tuple-element.296.refs_1_.refs_4_, f32[1,768]{1,0:T(1,128)} %get-tuple-element.288.refs_2_.refs_5_, ...), custom_call_target="tpu_custom_call" | custom-call | flops 6052380672 | bytes 12000000 | tf_op jit(solution)/shard_map/attn_fwd/pallas_call | solution.py:102
  157.3 15.9 %dense_fwd.1.refs_0_.refs_3_ = f32[832,768]{1,0:T(8,128)} custom-call(f32[832,768]{1,0:T(8,128)} %get-tuple-element.107.refs_0_.refs_2_, f32[1,768]{1,0:T(1,128)} %get-tuple-element.295.refs_1_.refs_3_, f32[1,768]{1,0:T(1,128)} %get-tuple-element.286.refs_2_.refs_4_, bf16[16,2,48,6144]{3,2,1,0:T(8,128)(2,1)} %bitcast.123, ...), custom_call_target="tpu_custom_call" | custom-call | flops 7851737088 | bytes 15000000 | tf_op jit(solution)/shard_map/dense_fwd/pallas_call | solution.py:102
  173.2 19.6 %attn_fwd.4 = (bf16[416,2304]{1,0:T(8,128)(2,1)}, f32[2,16,208]{2,1,0:T(8,128)}, bf16[416,768]{1,0:T(8,128)(2,1)}, f32[416,768]{1,0:T(8,128)}, bf16[416,768]{1,0...) custom-call(f32[832,768]{1,0:T(8,128)} %dense_fwd.1.refs_0_.refs_3_, ...), custom_call_target="tpu_custom_call" | custom-call | flops 3026190336 | bytes 12000000 | tf_op jit(solution)/shard_map/attn_fwd/pallas_call | solution.py:102
  194.2 19.7 %attn_fwd.5 = (bf16[416,2304]{1,0:T(8,128)(2,1)}, f32[2,16,208]{2,1,0:T(8,128)}, bf16[416,768]{1,0:T(8,128)(2,1)}, f32[416,768]{1,0:T(8,128)}, bf16[416,768]{1,0...) custom-call(f32[832,768]{1,0:T(8,128)} %dense_fwd.1.refs_0_.refs_3_, ...), custom_call_target="tpu_custom_call" | custom-call | flops 3026190336 | bytes 12000000 | tf_op jit(solution)/shard_map/attn_fwd/pallas_call | solution.py:102
  221.8 8.7 %collective-permute-done.4 = f32[2,2,416]{2,1,0:T(2,128)S(1)} collective-permute-done((f32[2,2,416]{2,1,0:T(2,128)S(1)}, f32[2,2,416]{2,1,0:T(2,128)S(1)}, u32[]{:S(2)}, u32[]{:S(2)}) %collective-permute-start.4) | collective-permute-done | bytes 6688 | tf_op jit(solution)/shard_map/ppermute | solution.py:779
  231.1 92.6 %experts.1 = (bf16[2,416,768]{2,1,0:T(8,128)(2,1)}, bf16[2,416,768]{2,1,0:T(8,128)(2,1)}, bf16[2,416,768]{2,1,0:T(8,128)(2,1)}, bf16[416,768]{1,0:T(8,128)(2,1)}...) custom-call(bf16[416,768]{1,0:T(8,128)(2,1)} %get-tuple-element.110., ...), custom_call_target="tpu_custom_call" | custom-call | flops 46858764288 | bytes 60000000 | tf_op jit(solution)/shard_map/experts/pallas_call | solution.py:102
  326.8 14.0 %collective-permute-done.6.refs_6_ = f32[2,8,416]{2,1,0:T(8,128)S(1)} collective-permute-done((f32[2,8,416]{2,1,0:T(8,128)S(1)}, f32[2,8,416]{2,1,0:T(8,128)S(1)}, u32[]{:S(2)}, u32[]{:S(2)}) %collective-permute-start.6) | collective-permute-done | bytes 26656 | tf_op jit(solution)/shard_map/ppermute | solution.py:779
  341.7 7.6 %gate_bwd.2 = (bf16[416,768]{1,0:T(8,128)(2,1)}, f32[416,768]{1,0:T(8,128)}, f32[128,768]{1,0:T(8,128)}, f32[1,768]{1,0:T(1,128)}, f32[1,768]{1,0:T(1,128)}) custom-call(f32[416,768]{1,0:T(8,128)} %get-tuple-element.108.refs_0_, bf16[2,416,768]{2,1,0:T(8,128)(2,1)} %bitcast.136, bf16[416,768]{1,0:T(8,128)(2,1)} %get-tuple-element.117.refs_2_, ...), custom_call_target="tpu_custom_call" | custom-call | flops 163577856 | bytes 7000000 | tf_op jit(solution)/shard_map/gate_bwd/pallas_call | solution.py:102
  349.6 15.6 %attn_core.4 = (bf16[416,2304]{1,0:T(8,128)(2,1)}, bf16[416,768]{1,0:T(8,128)(2,1)}) custom-call(f32[416,768]{1,0:T(8,128)} %get-tuple-element.124.refs_0_.refs_1_, bf16[16,2,48,6144]{3,2,1,0:T(8,128)(2,1)} %bitcast.127, bf16[416,2304]{1,0:T(8,128)(2,1)} %get-tuple-element.125.refs_2_, f32[2,16,208]{2,1,0:T(8,128)} %get-tuple-element.126.refs_3_, ...), custom_call_target="tpu_custom_call" | custom-call | flops 5807013888 | bytes 8000000 | tf_op jit(solution)/shard_map/attn_core/pallas_call | solution.py:102
  366.1 7.1 gate_bwd.3
  373.2 15.4 %attn_core.5 = (bf16[416,2304]{1,0:T(8,128)(2,1)}, bf16[416,768]{1,0:T(8,128)(2,1)}) custom-call(f32[416,768]{1,0:T(8,128)} %get-tuple-element.129.refs_0_.refs_2_, bf16[16,2,48,6144]{3,2,1,0:T(8,128)(2,1)} %bitcast.128, bf16[416,2304]{1,0:T(8,128)(2,1)} %get-tuple-element.131.refs_2_, f32[2,16,208]{2,1,0:T(8,128)} %get-tuple-element.132.refs_3_, ...), custom_call_target="tpu_custom_call" | custom-call | flops 5807013888 | bytes 8000000 | tf_op jit(solution)/shard_map/attn_core/pallas_call | solution.py:102
  388.6 20.2 %attn_grad.2 = (bf16[8,2,48,1536]{3,2,1,0:T(8,128)(2,1)}, bf16[8,2,48,1536]{3,2,1,0:T(8,128)(2,1)}, f32[832,768]{1,0:T(8,128)}, f32[1,2304]{1,0:T(1,128)}, f32[1...) custom-call(s32[1]{0:T(128)} %bitcast.37.refs_0_, f32[416,768]{1,0:T(8,128)} %get-tuple-element.124.refs_0_.refs_1_, ...), custom_call_target="tpu_custom_call" | custom-call | flops 6870269952 | bytes 25000000 | tf_op jit(solution)/shard_map/attn_grad/pallas_call | solution.py:102
  410.7 39.0 %dense_bwd.1 = (bf16[8,2,48,3072]{3,2,1,0:T(8,128)(2,1)}, bf16[8,2,48,3072]{3,2,1,0:T(8,128)(2,1)}, f32[832,768]{1,0:T(8,128)}, f32[1,3072]{1,0:T(1,128)}, f32[1...) custom-call(s32[1]{0:T(128)} %bitcast.37.refs_0_, f32[832,768]{1,0:T(8,128)} %get-tuple-element.137.refs_1_, ...), custom_call_target="tpu_custom_call" | custom-call | flops 19629342720 | bytes 35000000 | tf_op jit(solution)/shard_map/dense_bwd/pallas_call | solution.py:102
  469.9 10.8 %collective-permute-done.8.refs_3_ = bf16[2,416,768]{2,1,0:T(8,128)(2,1)} collective-permute-done((bf16[2,416,768]{2,1,0:T(8,128)(2,1)}, bf16[2,416,768]{2,1,0:T(8,128)(2,1)}, u32[]{:S(2)}, u32[]{:S(2)}) %collective-permute-start.8) | collective-permute-done | bytes 1277984 | tf_op jit(solution)/shard_map/ppermute | solution.py:779
  480.7 3.9 layer_output.1.refs_8_.refs_9_
  486.0 2.5 ring_add.15
  490.5 15.3 %attn_core.6 = (bf16[416,2304]{1,0:T(8,128)(2,1)}, bf16[416,768]{1,0:T(8,128)(2,1)}) custom-call(f32[832,768]{1,0:T(8,128)} %get-tuple-element.152.refs_0_.refs_1_.refs_2_, bf16[16,2,48,6144]{3,2,1,0:T(8,128)(2,1)} %bitcast.132, bf16[832,2304]{1,0:T(8,128)(2,1)} %get-tuple-element.153.refs_2_, f32[4,16,208]{2,1,0:T(8,128)} %get-tuple-element.154.refs_3_, ...), custom_call_target="tpu_custom_call" | custom-call | flops 5807013888 | bytes 8000000 | tf_op jit(solution)/shard_map/attn_core/pallas_call | solution.py:102
  511.3 2.9 ring_add.16
  516.2 2.8 ring_add.17
  521.0 15.4 %attn_core.7 = (bf16[416,2304]{1,0:T(8,128)(2,1)}, bf16[416,768]{1,0:T(8,128)(2,1)}) custom-call(f32[832,768]{1,0:T(8,128)} %get-tuple-element.152.refs_0_.refs_1_.refs_2_, bf16[16,2,48,6144]{3,2,1,0:T(8,128)(2,1)} %bitcast.133, bf16[832,2304]{1,0:T(8,128)(2,1)} %get-tuple-element.153.refs_2_, f32[4,16,208]{2,1,0:T(8,128)} %get-tuple-element.154.refs_3_, ...), custom_call_target="tpu_custom_call" | custom-call | flops 5807013888 | bytes 8000000 | tf_op jit(solution)/shard_map/attn_core/pallas_call | solution.py:102
  540.1 3.0 ring_add.18
  544.5 3.6 ring_add.19
  548.1 20.1 %attn_grad.3 = (bf16[8,2,48,1536]{3,2,1,0:T(8,128)(2,1)}, bf16[8,2,48,1536]{3,2,1,0:T(8,128)(2,1)}, bf16[832,768]{1,0:T(8,128)(2,1)}, f32[1,2304]{1,0:T(1,128)},...) custom-call(s32[1]{0:T(128)} %bitcast.37.refs_0_, f32[832,768]{1,0:T(8,128)} %get-tuple-element.152.refs_0_.refs_1_.refs_2_, ...), custom_call_target="tpu_custom_call" | custom-call | flops 6870269952 | bytes 25000000 | tf_op jit(solution)/shard_map/attn_grad/pallas_call | solution.py:102
  572.8 7.0 collective-permute-done.27.refs_5_
  583.6 3.0 ring_add.20
  589.9 2.5 ring_add.21
  592.4 3.8 collective-permute-done.25.refs_6_
  597.1 3.9 ring_add.22
  601.0 3.0 ring_add.28
  606.2 2.3 collective-permute-start.23
  618.2 2.8 place.2
  621.0 4.1 copy.123
  628.1 3.0 ring_add.23
  636.5 3.9 ring_add.24
  643.4 3.0 ring_add.25
  659.5 3.0 ring_add.26
  662.5 3.4 collective-permute-done.37.refs_1_
  670.7 3.5 collective-permute-start.43
  674.1 3.7 place.3
  677.8 6.5 copy.124
  690.1 2.8 ring_add.27
  698.6 3.5 ring_add.29
  702.1 2.3 reshape.165
  708.2 8.5 %collective-permute-done.50 = f32[2,48,1536]{2,1,0:T(8,128)S(1)} collective-permute-done((f32[2,48,1536]{2,1,0:T(8,128)S(1)}, f32[2,48,1536]{2,1,0:T(8,128)S(1)}, u32[]{:S(2)}, u32[]{:S(2)}) %collective-permute-start.50) | collective-permute-done | bytes 589856 | tf_op jit(solution)/shard_map/ppermute | solution.py:779
  (359 shorter events, 141.9 us)
Async XLA Ops:
  7.2 119.6 %all-gather.6.cloned.1.call-start = ((), (), s32[]{:S(2)}) async-start(), calls=%async_computation.3 | async-start | bytes 20054016 | tf_op jit(solution)/shard_map/all_gather | solution.py:1037
  8.7 16.4 %collective-permute-start = (bf16[48,6144]{1,0:T(8,128)(2,1)S(1)}, bf16[48,6144]{1,0:T(8,128)(2,1)S(1)}, u32[]{:S(2)}, u32[]{:S(2)}) collective-permute-start(bf16[48,6144]{1,0:T(8,128)(2,1)S(1)} %constant_dynamic-update-slice_fusion), channel_id=1, source_target_pairs={{0,1},{1,0},{2,3},{3,2},{4,5},{5,4},{6,7},{7,6},{8,9},{9,8},{10,11... | collective-permute-start | bytes 1769480 | tf_op jit(solution)/shard_map/ppermute | solution.py:779
  26.3 204.8 %all-gather.4.cloned.1.call-start = ((), (), s32[]{:S(2)}) async-start(), calls=%async_computation.1 | async-start | bytes 20054016 | tf_op jit(solution)/shard_map/all_gather | solution.py:788
  28.6 689.1 %reduce-scatter.2.cloned.1.call-start = ((), (), s32[]{:S(2)}) async-start(), calls=%async_computation.2 | async-start | bytes 20054016 | tf_op jit(solution)/shard_map/reduce_scatter | solution.py:883
  28.7 19.6 %collective-permute-start.1 = (f32[3072]{0:T(1024)S(1)}, f32[3072]{0:T(1024)S(1)}, u32[]{:S(2)}, u32[]{:S(2)}) collective-permute-start(f32[3072]{0:T(1024)S(1)} %constant_dynamic-update-slice_fusion.5), channel_id=1, source_target_pairs={{0,1},{1,0},{2,3},{3,2},{4,5},{5,4},{6,7},{7,6},{8,9},{9,8},{10,11... | collective-permute-start | bytes 36872 | tf_op jit(solution)/shard_map/ppermute | solution.py:779
  192.7 38.4 %collective-permute-start.2 = (bf16[416,768]{1,0:T(8,128)(2,1)}, bf16[416,768]{1,0:T(8,128)(2,1)}, u32[]{:S(2)}, u32[]{:S(2)}) collective-permute-start(bf16[416,768]{1,0:T(8,128)(2,1)} %get-tuple-element.110.refs_0_), channel_id=1, source_target_pairs={{0,1},{1,0},{2,3},{3,2},{4,5},{5,4},{6,7},{7,6},{8,9},{9,8},{10,11... | collective-permute-start | bytes 1916936 | tf_op jit(solution)/shard_map/ppermute | solution.py:779
  214.0 17.2 %collective-permute-start.3 = (bf16[416,768]{1,0:T(8,128)(2,1)}, bf16[416,768]{1,0:T(8,128)(2,1)}, u32[]{:S(2)}, u32[]{:S(2)}) collective-permute-start(bf16[416,768]{1,0:T(8,128)(2,1)} %get-tuple-element.111.refs_1_), channel_id=1, source_target_pairs={{0,1},{1,0},{2,3},{3,2},{4,5},{5,4},{6,7},{7,6},{8,9},{9,8},{10,11... | collective-permute-start | bytes 1916936 | tf_op jit(solution)/shard_map/ppermute | solution.py:779
  215.7 14.8 %collective-permute-start.4 = (f32[2,2,416]{2,1,0:T(2,128)S(1)}, f32[2,2,416]{2,1,0:T(2,128)S(1)}, u32[]{:S(2)}, u32[]{:S(2)}) collective-permute-start(f32[2,2,416]{2,1,0:T(2,128)S(1)} %pad_maximum_fusion.8), channel_id=1, source_target_pairs={{0,1},{1,0},{2,3},{3,2},{4,5},{5,4},{6,7},{7,6},{8,9},{9,8},{10,11... | collective-permute-start | bytes 19976 | tf_op jit(solution)/shard_map/ppermute | solution.py:779
  324.8 16.1 %collective-permute-start.5 = (bf16[416,768]{1,0:T(8,128)(2,1)S(1)}, bf16[416,768]{1,0:T(8,128)(2,1)S(1)}, u32[]{:S(2)}, u32[]{:S(2)}) collective-permute-start(bf16[416,768]{1,0:T(8,128)(2,1)S(1)} %copy-done.65), channel_id=1, source_target_pairs={{0,1},{1,0},{2,3},{3,2},{4,5},{5,4},{6,7},{7,6},{8,9},{9,8},{10,11... | collective-permute-start | bytes 1916936 | tf_op jit(solution)/shard_map/ppermute | solution.py:779
  325.3 15.6 %collective-permute-start.6 = (f32[2,8,416]{2,1,0:T(8,128)S(1)}, f32[2,8,416]{2,1,0:T(8,128)S(1)}, u32[]{:S(2)}, u32[]{:S(2)}) collective-permute-start(f32[2,8,416]{2,1,0:T(8,128)S(1)} %copy-done.66), channel_id=1, source_target_pairs={{0,1},{1,0},{2,3},{3,2},{4,5},{5,4},{6,7},{7,6},{8,9},{9,8},{10,11... | collective-permute-start | bytes 79880 | tf_op jit(solution)/shard_map/ppermute | solution.py:779
  349.3 16.0 %collective-permute-start.7 = (bf16[416,768]{1,0:T(8,128)(2,1)}, bf16[416,768]{1,0:T(8,128)(2,1)S(1)}, u32[]{:S(2)}, u32[]{:S(2)}) collective-permute-start(bf16[416,768]{1,0:T(8,128)(2,1)} %get-tuple-element.122.refs_4_), channel_id=1, source_target_pairs={{0,1},{1,0},{2,3},{3,2},{4,5},{5,4},{6,7},{7,6},{8,9},{9,8},{10,11... | collective-permute-start | bytes 1916936 | tf_op jit(solution)/shard_map/ppermute | solution.py:779
  449.7 66.5 %collective-permute-start.14 = (bf16[8,2,48,3072]{3,2,1,0:T(8,128)(2,1)}, bf16[8,2,48,3072]{3,2,1,0:T(8,128)(2,1)}, u32[]{:S(2)}, u32[]{:S(2)}) collective-permute-start(bf16[8,2,48,3072]{3,2,1,0:T(8,128)(2,1)} %get-tuple-element.158.refs_6_), channel_id=1, source_target_pairs={{0,2},{2,0},{4,6},{6,4},{8,10},{10,8},{12,14},{14,12},{16,18},{18,... | collective-permute-start | bytes 14155784 | tf_op jit(solution)/shard_map/ppermute | solution.py:832
  449.8 34.8 %collective-permute-start.10 = (bf16[8,2,48,1536]{3,2,1,0:T(8,128)(2,1)}, bf16[8,2,48,1536]{3,2,1,0:T(8,128)(2,1)S(1)}, u32[]{:S(2)}, u32[]{:S(2)}) collective-permute-start(bf16[8,2,48,1536]{3,2,1,0:T(8,128)(2,1)} %get-tuple-element.138.refs_8_), channel_id=1, source_target_pairs={{0,2},{2,0},{4,6},{6,4},{8,10},{10,8},{12,14},{14,12},{16,18},{18,... | collective-permute-start | bytes 7077896 | tf_op jit(solution)/shard_map/ppermute | solution.py:832
  450.3 30.4 %collective-permute-start.8 = (bf16[2,416,768]{2,1,0:T(8,128)(2,1)}, bf16[2,416,768]{2,1,0:T(8,128)(2,1)}, u32[]{:S(2)}, u32[]{:S(2)}) collective-permute-start(bf16[2,416,768]{2,1,0:T(8,128)(2,1)} %get-tuple-element.128.refs_4_.refs_10_), channel_id=1, source_target_pairs={{0,1},{1,0},{2,3},{3,2},{4,5},{5,4},{6,7},{7,6},{8,9},{9,8},{10,11... | collective-permute-start | bytes 3833864 | tf_op jit(solution)/shard_map/ppermute | solution.py:779
  468.5 37.2 %collective-permute-start.15 = (f32[32,768]{1,0:T(8,128)}, f32[32,768]{1,0:T(8,128)S(1)}, u32[]{:S(2)}, u32[]{:S(2)}) collective-permute-start(f32[32,768]{1,0:T(8,128)} %small_add.10.refs_7_.refs_0_), channel_id=1, source_target_pairs={{0,4},{2,6},{4,0},{6,2},{8,12},{10,14},{12,8},{14,10},{16,20},{18,... | collective-permute-start | bytes 294920 | tf_op jit(solution)/shard_map/ppermute | solution.py:906
  488.4 21.5 %collective-permute-start.11 = (bf16[48,1536]{1,0:T(8,128)(2,1)}, bf16[48,1536]{1,0:T(8,128)(2,1)S(1)}, u32[]{:S(2)}, u32[]{:S(2)}) collective-permute-start(bf16[48,1536]{1,0:T(8,128)(2,1)} %get-tuple-element.156.refs_4_), channel_id=1, source_target_pairs={{0,8},{2,10},{8,16},{10,18},{16,24},{18,26},{24,28},{26,30},{28,20... | collective-permute-start | bytes 442376 | tf_op jit(solution)/shard_map/ppermute | solution.py:842
  490.4 19.6 %collective-permute-start.12 = (bf16[48,1536]{1,0:T(8,128)(2,1)}, bf16[48,1536]{1,0:T(8,128)(2,1)S(1)}, u32[]{:S(2)}, u32[]{:S(2)}) collective-permute-start(bf16[48,1536]{1,0:T(8,128)(2,1)} %get-tuple-element.157.refs_5_), channel_id=1, source_target_pairs={{0,4},{2,6},{8,0},{10,2},{16,8},{18,10},{24,16},{26,18},{28,24},{3... | collective-permute-start | bytes 442376 | tf_op jit(solution)/shard_map/ppermute | solution.py:842
  508.0 28.4 %collective-permute-start.20 = (f32[32,768]{1,0:T(8,128)}, f32[32,768]{1,0:T(8,128)S(1)}, u32[]{:S(2)}, u32[]{:S(2)}) collective-permute-start(f32[32,768]{1,0:T(8,128)} %small_add.11.refs_8_.refs_0_), channel_id=1, source_target_pairs={{0,8},{2,10},{4,12},{6,14},{8,0},{10,2},{12,4},{14,6},{16,24},{18,... | collective-permute-start | bytes 294920 | tf_op jit(solution)/shard_map/ppermute | solution.py:906
  514.2 24.5 %collective-permute-start.16 = (bf16[2,48,1536]{2,1,0:T(8,128)(2,1)}, bf16[2,48,1536]{2,1,0:T(8,128)(2,1)S(1)}, u32[]{:S(2)}, u32[]{:S(2)}) collective-permute-start(bf16[2,48,1536]{2,1,0:T(8,128)(2,1)} %get-tuple-element.160.refs_4_), channel_id=1, source_target_pairs={{0,8},{2,10},{8,16},{10,18},{16,24},{18,26},{24,28},{26,30},{28,20... | collective-permute-start | bytes 884744 | tf_op jit(solution)/shard_map/ppermute | solution.py:842
  514.2 24.4 %collective-permute-start.17 = (bf16[2,48,1536]{2,1,0:T(8,128)(2,1)}, bf16[2,48,1536]{2,1,0:T(8,128)(2,1)S(1)}, u32[]{:S(2)}, u32[]{:S(2)}) collective-permute-start(bf16[2,48,1536]{2,1,0:T(8,128)(2,1)} %get-tuple-element.161.refs_5_), channel_id=1, source_target_pairs={{0,4},{2,6},{8,0},{10,2},{16,8},{18,10},{24,16},{26,18},{28,24},{3... | collective-permute-start | bytes 884744 | tf_op jit(solution)/shard_map/ppermute | solution.py:842
  519.0 24.1 %collective-permute-start.18 = (bf16[48,3072]{1,0:T(8,128)(2,1)}, bf16[48,3072]{1,0:T(8,128)(2,1)S(1)}, u32[]{:S(2)}, u32[]{:S(2)}) collective-permute-start(bf16[48,3072]{1,0:T(8,128)(2,1)} %get-tuple-element.163.refs_6_), channel_id=1, source_target_pairs={{0,8},{2,10},{8,16},{10,18},{16,24},{18,26},{24,28},{26,30},{28,20... | collective-permute-start | bytes 884744 | tf_op jit(solution)/shard_map/ppermute | solution.py:842
  519.8 23.3 %collective-permute-start.19 = (bf16[48,3072]{1,0:T(8,128)(2,1)}, bf16[48,3072]{1,0:T(8,128)(2,1)S(1)}, u32[]{:S(2)}, u32[]{:S(2)}) collective-permute-start(bf16[48,3072]{1,0:T(8,128)(2,1)} %get-tuple-element.164.refs_7_), channel_id=1, source_target_pairs={{0,4},{2,6},{8,0},{10,2},{16,8},{18,10},{24,16},{26,18},{28,24},{3... | collective-permute-start | bytes 884744 | tf_op jit(solution)/shard_map/ppermute | solution.py:842
  568.2 19.0 %collective-permute-start.26 = (bf16[8,2,48,1536]{3,2,1,0:T(8,128)(2,1)}, bf16[8,2,48,1536]{3,2,1,0:T(8,128)(2,1)S(1)}, u32[]{:S(2)}, u32[]{:S(2)}) collective-permute-start(bf16[8,2,48,1536]{3,2,1,0:T(8,128)(2,1)} %get-tuple-element.182), channel_id=1, source_target_pairs={{0,2},{2,0},{4,6},{6,4},{8,10},{10,8},{12,14},{14,12},{16,18},{18,... | collective-permute-start | bytes 7077896 | tf_op jit(solution)/shard_map/ppermute | solution.py:832
  568.3 42.4 %collective-permute-start.9 = (bf16[2,416,768]{2,1,0:T(8,128)(2,1)}, bf16[2,416,768]{2,1,0:T(8,128)(2,1)}, u32[]{:S(2)}, u32[]{:S(2)}) collective-permute-start(bf16[2,416,768]{2,1,0:T(8,128)(2,1)} %layer_output.1.refs_8_.refs_9_), channel_id=1, source_target_pairs={{0,1},{1,0},{2,3},{3,2},{4,5},{5,4},{6,7},{7,6},{8,9},{9,8},{10,11... | collective-permute-start | bytes 3833864 | tf_op jit(solution)/shard_map/ppermute | solution.py:779
  569.9 9.9 %collective-permute-start.27 = (bf16[2,48,1536]{2,1,0:T(8,128)(2,1)S(1)}, bf16[2,48,1536]{2,1,0:T(8,128)(2,1)S(1)}, u32[]{:S(2)}, u32[]{:S(2)}) collective-permute-start(bf16[2,48,1536]{2,1,0:T(8,128)(2,1)S(1)} %copy-done.25), channel_id=1, source_target_pairs={{0,8},{2,10},{8,16},{10,18},{16,24},{18,26},{24,28},{26,30},{28,20... | collective-permute-start | bytes 884744 | tf_op jit(solution)/shard_map/ppermute | solution.py:842
  570.8 12.1 %collective-permute-start.28 = (bf16[2,48,1536]{2,1,0:T(8,128)(2,1)S(1)}, bf16[2,48,1536]{2,1,0:T(8,128)(2,1)S(1)}, u32[]{:S(2)}, u32[]{:S(2)}) collective-permute-start(bf16[2,48,1536]{2,1,0:T(8,128)(2,1)S(1)} %copy-done.24), channel_id=1, source_target_pairs={{0,4},{2,6},{8,0},{10,2},{16,8},{18,10},{24,16},{26,18},{28,24},{3... | collective-permute-start | bytes 884744 | tf_op jit(solution)/shard_map/ppermute | solution.py:842
  572.0 20.5 %collective-permute-start.24 = (bf16[2,48,3072]{2,1,0:T(8,128)(2,1)}, bf16[2,48,3072]{2,1,0:T(8,128)(2,1)S(1)}, u32[]{:S(2)}, u32[]{:S(2)}) collective-permute-start(bf16[2,48,3072]{2,1,0:T(8,128)(2,1)} %get-tuple-element.171.refs_15_), channel_id=1, source_target_pairs={{0,8},{2,10},{8,16},{10,18},{16,24},{18,26},{24,28},{26,30},{28,20... | collective-permute-start | bytes 1769480 | tf_op jit(solution)/shard_map/ppermute | solution.py:842
  579.8 16.5 %collective-permute-start.25 = (bf16[2,48,3072]{2,1,0:T(8,128)(2,1)}, bf16[2,48,3072]{2,1,0:T(8,128)(2,1)S(1)}, u32[]{:S(2)}, u32[]{:S(2)}) collective-permute-start(bf16[2,48,3072]{2,1,0:T(8,128)(2,1)} %get-tuple-element.172.refs_16_), channel_id=1, source_target_pairs={{0,4},{2,6},{8,0},{10,2},{16,8},{18,10},{24,16},{26,18},{28,24},{3... | collective-permute-start | bytes 1769480 | tf_op jit(solution)/shard_map/ppermute | solution.py:842
  586.6 14.4 %collective-permute-start.45 = (bf16[2,48,1536]{2,1,0:T(8,128)(2,1)}, bf16[2,48,1536]{2,1,0:T(8,128)(2,1)}, u32[]{:S(2)}, u32[]{:S(2)}) collective-permute-start(bf16[2,48,1536]{2,1,0:T(8,128)(2,1)} %get-tuple-element.183.refs_3_), channel_id=1, source_target_pairs={{0,8},{2,10},{8,16},{10,18},{16,24},{18,26},{24,28},{26,30},{28,20... | collective-permute-start | bytes 884744 | tf_op jit(solution)/shard_map/ppermute | solution.py:842
  587.2 13.7 %collective-permute-start.46 = (bf16[2,48,1536]{2,1,0:T(8,128)(2,1)}, bf16[2,48,1536]{2,1,0:T(8,128)(2,1)}, u32[]{:S(2)}, u32[]{:S(2)}) collective-permute-start(bf16[2,48,1536]{2,1,0:T(8,128)(2,1)} %get-tuple-element.184.refs_4_), channel_id=1, source_target_pairs={{0,4},{2,6},{8,0},{10,2},{16,8},{18,10},{24,16},{26,18},{28,24},{3... | collective-permute-start | bytes 884744 | tf_op jit(solution)/shard_map/ppermute | solution.py:842
  605.7 26.1 %collective-permute-start.47 = (f32[48,1536]{1,0:T(8,128)}, f32[48,1536]{1,0:T(8,128)}, u32[]{:S(2)}, u32[]{:S(2)}) collective-permute-start(f32[48,1536]{1,0:T(8,128)} %dynamic-slice_bitcast_fusion), channel_id=1, source_target_pairs={{0,1},{1,0},{2,3},{3,2},{4,5},{5,4},{6,7},{7,6},{8,9},{9,8},{10,11... | collective-permute-start | bytes 884744 | tf_op jit(solution)/shard_map/ppermute | solution.py:779
  610.7 17.4 %collective-permute-start.33 = (bf16[48,1536]{1,0:T(8,128)(2,1)}, bf16[48,1536]{1,0:T(8,128)(2,1)}, u32[]{:S(2)}, u32[]{:S(2)}) collective-permute-start(bf16[48,1536]{1,0:T(8,128)(2,1)} %get-tuple-element.186.refs_8_), channel_id=1, source_target_pairs={{0,4},{2,6},{8,0},{10,2},{16,8},{18,10},{24,16},{26,18},{28,24},{3... | collective-permute-start | bytes 442376 | tf_op jit(solution)/shard_map/ppermute | solution.py:842
  612.7 21.4 %collective-permute-start.30 = (bf16[2,48,3072]{2,1,0:T(8,128)(2,1)S(1)}, bf16[2,48,3072]{2,1,0:T(8,128)(2,1)S(1)}, u32[]{:S(2)}, u32[]{:S(2)}) collective-permute-start(bf16[2,48,3072]{2,1,0:T(8,128)(2,1)S(1)} %copy-done.5), channel_id=1, source_target_pairs={{0,8},{2,10},{8,16},{10,18},{16,24},{18,26},{24,28},{26,30},{28,20... | collective-permute-start | bytes 1769480 | tf_op jit(solution)/shard_map/ppermute | solution.py:842
  612.8 22.4 %collective-permute-start.31 = (bf16[2,48,3072]{2,1,0:T(8,128)(2,1)S(1)}, bf16[2,48,3072]{2,1,0:T(8,128)(2,1)}, u32[]{:S(2)}, u32[]{:S(2)}) collective-permute-start(bf16[2,48,3072]{2,1,0:T(8,128)(2,1)S(1)} %copy-done.4), channel_id=1, source_target_pairs={{0,4},{2,6},{8,0},{10,2},{16,8},{18,10},{24,16},{26,18},{28,24},{3... | collective-permute-start | bytes 1769480 | tf_op jit(solution)/shard_map/ppermute | solution.py:842
  616.6 54.1 %collective-permute-start.21 = (bf16[832,768]{1,0:T(8,128)(2,1)S(1)}, bf16[832,768]{1,0:T(8,128)(2,1)}, u32[]{:S(2)}, u32[]{:S(2)}) collective-permute-start(bf16[832,768]{1,0:T(8,128)(2,1)S(1)} %copy-done.10), channel_id=1, source_target_pairs={{0,1},{1,0},{2,3},{3,2},{4,5},{5,4},{6,7},{7,6},{8,9},{9,8},{10,11... | collective-permute-start | bytes 3833864 | tf_op jit(solution)/shard_map/ppermute | solution.py:779
  631.1 12.3 %collective-permute-start.35 = (bf16[2,48,1536]{2,1,0:T(8,128)(2,1)}, bf16[2,48,1536]{2,1,0:T(8,128)(2,1)}, u32[]{:S(2)}, u32[]{:S(2)}) collective-permute-start(bf16[2,48,1536]{2,1,0:T(8,128)(2,1)} %get-tuple-element.189.refs_7_), channel_id=1, source_target_pairs={{0,8},{2,10},{8,16},{10,18},{16,24},{18,26},{24,28},{26,30},{28,20... | collective-permute-start | bytes 884744 | tf_op jit(solution)/shard_map/ppermute | solution.py:842
  631.8 11.6 %collective-permute-start.36 = (bf16[2,48,1536]{2,1,0:T(8,128)(2,1)}, bf16[2,48,1536]{2,1,0:T(8,128)(2,1)}, u32[]{:S(2)}, u32[]{:S(2)}) collective-permute-start(bf16[2,48,1536]{2,1,0:T(8,128)(2,1)} %get-tuple-element.190.refs_8_), channel_id=1, source_target_pairs={{0,4},{2,6},{8,0},{10,2},{16,8},{18,10},{24,16},{26,18},{28,24},{3... | collective-permute-start | bytes 884744 | tf_op jit(solution)/shard_map/ppermute | solution.py:842
  635.2 13.3 %collective-permute-start.41 = (f32[32,768]{1,0:T(8,128)S(1)}, f32[32,768]{1,0:T(8,128)}, u32[]{:S(2)}, u32[]{:S(2)}) collective-permute-start(f32[32,768]{1,0:T(8,128)S(1)} %copy-done.12), channel_id=1, source_target_pairs={{0,1},{1,0},{2,3},{3,2},{4,5},{5,4},{6,7},{7,6},{8,9},{9,8},{10,11... | collective-permute-start | bytes 294920 | tf_op jit(solution)/shard_map/ppermute | solution.py:779
  646.5 10.1 %collective-permute-start.38 = (bf16[2,48,1536]{2,1,0:T(8,128)(2,1)}, bf16[2,48,1536]{2,1,0:T(8,128)(2,1)S(1)}, u32[]{:S(2)}, u32[]{:S(2)}) collective-permute-start(bf16[2,48,1536]{2,1,0:T(8,128)(2,1)} %get-tuple-element.193.refs_2_.refs_5_), channel_id=1, source_target_pairs={{0,8},{2,10},{8,16},{10,18},{16,24},{18,26},{24,28},{26,30},{28,20... | collective-permute-start | bytes 884744 | tf_op jit(solution)/shard_map/ppermute | solution.py:842
  647.5 11.3 %collective-permute-start.39 = (bf16[2,48,1536]{2,1,0:T(8,128)(2,1)}, bf16[2,48,1536]{2,1,0:T(8,128)(2,1)S(1)}, u32[]{:S(2)}, u32[]{:S(2)}) collective-permute-start(bf16[2,48,1536]{2,1,0:T(8,128)(2,1)} %get-tuple-element.194.refs_3_.refs_6_), channel_id=1, source_target_pairs={{0,4},{2,6},{8,0},{10,2},{16,8},{18,10},{24,16},{26,18},{28,24},{3... | collective-permute-start | bytes 884744 | tf_op jit(solution)/shard_map/ppermute | solution.py:842
  650.9 46.8 %collective-permute-start.48 = (bf16[2,48,3072]{2,1,0:T(8,128)(2,1)S(1)}, bf16[2,48,3072]{2,1,0:T(8,128)(2,1)S(1)}, u32[]{:S(2)}, u32[]{:S(2)}) collective-permute-start(bf16[2,48,3072]{2,1,0:T(8,128)(2,1)S(1)} %copy-done.7), channel_id=1, source_target_pairs={{0,8},{2,10},{8,16},{10,18},{16,24},{18,26},{24,28},{26,30},{28,20... | collective-permute-start | bytes 1769480 | tf_op jit(solution)/shard_map/ppermute | solution.py:842
  654.0 11.8 %collective-permute-start.37 = (f32[16,768]{1,0:T(8,128)}, f32[16,768]{1,0:T(8,128)S(1)}, u32[]{:S(2)}, u32[]{:S(2)}) collective-permute-start(f32[16,768]{1,0:T(8,128)} %small_add.16.refs_7_.refs_0_), channel_id=1, source_target_pairs={{0,16},{2,18},{4,20},{6,22},{8,24},{10,26},{12,28},{14,30},{16,0},... | collective-permute-start | bytes 147464 | tf_op jit(solution)/shard_map/ppermute | solution.py:906
  656.6 41.1 %collective-permute-start.49 = (bf16[2,48,3072]{2,1,0:T(8,128)(2,1)S(1)}, bf16[2,48,3072]{2,1,0:T(8,128)(2,1)}, u32[]{:S(2)}, u32[]{:S(2)}) collective-permute-start(bf16[2,48,3072]{2,1,0:T(8,128)(2,1)S(1)} %copy-done.6), channel_id=1, source_target_pairs={{0,4},{2,6},{8,0},{10,2},{16,8},{18,10},{24,16},{26,18},{28,24},{3... | collective-permute-start | bytes 1769480 | tf_op jit(solution)/shard_map/ppermute | solution.py:842
  667.9 16.4 %collective-permute-start.40 = (f32[16,768]{1,0:T(8,128)}, f32[16,768]{1,0:T(8,128)S(1)}, u32[]{:S(2)}, u32[]{:S(2)}) collective-permute-start(f32[16,768]{1,0:T(8,128)} %small_add.17.refs_3_.refs_0_.refs_2_.refs_5_), channel_id=1, source_target_pairs={{0,1},{1,0},{2,3},{3,2},{4,5},{5,4},{6,7},{7,6},{8,9},{9,8},{10,11... | collective-permute-start | bytes 147464 | tf_op jit(solution)/shard_map/ppermute | solution.py:779
  669.9 19.5 %collective-permute-start.42 = (bf16[2,48,1536]{2,1,0:T(8,128)(2,1)}, bf16[2,48,1536]{2,1,0:T(8,128)(2,1)}, u32[]{:S(2)}, u32[]{:S(2)}) collective-permute-start(bf16[2,48,1536]{2,1,0:T(8,128)(2,1)} %get-tuple-element.195.refs_2_), channel_id=1, source_target_pairs={{0,8},{2,10},{8,16},{10,18},{16,24},{18,26},{24,28},{26,30},{28,20... | collective-permute-start | bytes 884744 | tf_op jit(solution)/shard_map/ppermute | solution.py:842
  670.7 18.7 %collective-permute-start.43 = (bf16[2,48,1536]{2,1,0:T(8,128)(2,1)}, bf16[2,48,1536]{2,1,0:T(8,128)(2,1)S(1)}, u32[]{:S(2)}, u32[]{:S(2)}) collective-permute-start(bf16[2,48,1536]{2,1,0:T(8,128)(2,1)} %get-tuple-element.196.refs_3_), channel_id=1, source_target_pairs={{0,4},{2,6},{8,0},{10,2},{16,8},{18,10},{24,16},{26,18},{28,24},{3... | collective-permute-start | bytes 884744 | tf_op jit(solution)/shard_map/ppermute | solution.py:842
  694.0 12.5 %collective-permute-start.44 = (f32[48,1536]{1,0:T(8,128)S(1)}, f32[48,1536]{1,0:T(8,128)S(1)}, u32[]{:S(2)}, u32[]{:S(2)}) collective-permute-start(f32[48,1536]{1,0:T(8,128)S(1)} %dynamic-slice_bitcast_fusion.1), channel_id=1, source_target_pairs={{0,1},{1,0},{2,3},{3,2},{4,5},{5,4},{6,7},{7,6},{8,9},{9,8},{10,11... | collective-permute-start | bytes 884744 | tf_op jit(solution)/shard_map/ppermute | solution.py:779
  705.5 11.2 %collective-permute-start.50 = (f32[2,48,1536]{2,1,0:T(8,128)S(1)}, f32[2,48,1536]{2,1,0:T(8,128)S(1)}, u32[]{:S(2)}, u32[]{:S(2)}) collective-permute-start(f32[2,48,1536]{2,1,0:T(8,128)S(1)} %bitcast.150), channel_id=1, source_target_pairs={{0,1},{1,0},{2,3},{3,2},{4,5},{5,4},{6,7},{7,6},{8,9},{9,8},{10,11... | collective-permute-start | bytes 1769480 | tf_op jit(solution)/shard_map/ppermute | solution.py:779
  (76 other events, 551.1 us)
Sparse Core Ops, SparseCore 0:
  26.4 100.4 all-gather.5
  129.0 98.9 all-gather.3
  323.9 200.3 reduce-scatter.1

commit v4 on v3

--- a/solution.py
+++ b/solution.py
@@ -15,6 +15,7 @@
 F32 = jnp.float32
 VMEM_LIMIT = 58 * 1024 * 1024
 FF_BLOCK = 512
+EXPERT_BLOCK = 768
 ROW_PAD = 16
 GELU_SLOPE = 0.7978845608028654
 GELU_CUBE = 0.044715
@@ -73,7 +74,7 @@
 
 
 def call(kernel, grid, in_specs, out_specs, out_shape, scratch, flops, traffic, name,
-         after=(), prefetch=0):
+         after=(), prefetch=0, aliases=None):
     taken = prefetch + len(in_specs)
     skipped = len(after)
 
@@ -90,6 +91,7 @@
             scratch_shapes=scratch,
         ),
         out_shape=out_shape,
+        input_output_aliases=aliases or {},
         name=name,
         compiler_params=pltpu.CompilerParams(
             vmem_limit_bytes=VMEM_LIMIT,
@@ -219,7 +221,7 @@
         o_ref[rows, place] = jnp.where(lane < HD, mixed[0], mixed[1]).astype(BF)
         return carry
 
-    lax.fori_loop(0, images * pairs, pair_step, 0)
+    lax.fori_loop(0, images * pairs, pair_step, 0, unroll=6)
     out_matrix = jnp.concatenate(
         [flat_rows(w_ref[:, t, :, 3 * third :]) for t in range(2)], axis=1
     )
@@ -323,6 +325,7 @@
         key = qkv_ref[rows, col(1)]
         value = qkv_ref[rows, col(2)]
         mixed = grad_sc[rows, place]
+        key_turned = key.T
         parts = []
         for half in range(2):
             mine = (lane >= HD) if half else (lane < HD)
@@ -334,17 +337,20 @@
             delta = jnp.sum(product, axis=0, keepdims=True)
             score_grad = (product - probs * delta).astype(BF)
             parts.append((
-                mm_at(score_grad, key) * HD ** (-0.5),
+                mm(key_turned, score_grad) * HD ** (-0.5),
                 mm(score_grad, query),
                 mm(probs.astype(BF), mixed),
             ))
-        for part in range(3):
+        turned = lax.broadcasted_iota(jnp.int32, (2 * HD, pad), 0)
+        query_grad = jnp.where(turned < HD, parts[0][0], parts[1][0])
+        dqkv_ref[rows, col(0)] = query_grad.T.astype(BF)
+        for part in range(1, 3):
             dqkv_ref[rows, col(part)] = jnp.where(
                 lane < HD, parts[0][part], parts[1][part]
             ).astype(BF)
         return carry
 
-    lax.fori_loop(0, images * pairs, pair_step, 0)
+    lax.fori_loop(0, images * pairs, pair_step, 0, unroll=6)
 
 
 def attention_core_back(incoming, weights, layer, stored, length, pad, which, after=()):
@@ -374,50 +380,55 @@
 
 def attn_grad_kernel(
     core_ref, da0_ref, da1_ref, h_ref, g_ref, b_ref, w_ref, dq0_ref, dq1_ref,
-    low0_ref, low1_ref, o0_ref, o1_ref, *outs,
+    low0_ref, low1_ref, o0_ref, o1_ref, *rest,
 ):
-    dw_refs = outs[: len(outs) - 5]
-    dh_ref, dqb_ref, dob_ref, dg_ref, db_ref = outs[len(outs) - 5 :]
-    width = h_ref.shape[1]
+    dw_refs = rest[: len(rest) - 7]
+    dh_ref, dqb_ref, dob_ref, dg_ref, db_ref, n_sc, acc = rest[len(rest) - 7 :]
+    step = pl.program_id(0)
     block = dq0_ref.shape[0]
+    wide = dq0_ref.shape[1]
     gain = g_ref[...]
-    unit, scale = norm_parts(h_ref[...])
-    normed = (unit * gain + b_ref[...]).astype(BF)
     half = (slice(0, block), slice(block, 2 * block))
-    third = width // 2
-    normed_grad = [None, None]
-    for t in range(2):
-        cols = slice(t * 3 * third, (t + 1) * 3 * third)
-        matrix = flat_rows(w_ref[:, t, :, : 3 * third])
-        piece = sums = mix = None
-        sides = ((dq0_ref, low0_ref, o0_ref), (dq1_ref, low1_ref, o1_ref))
-        for side, (dq_ref, low_ref, o_ref) in enumerate(sides):
-            grads = dq_ref[:, cols]
-            term = mm_bt(grads, matrix)
-            normed_grad[side] = term if t == 0 else normed_grad[side] + term
-            outer = mm_at(normed[half[side]], grads)
-            total = jnp.sum(grads.astype(F32), axis=0, keepdims=True)
-            out = mm_at(low_ref[...], o_ref[:, t * third : (t + 1) * third])
-            piece = outer if side == 0 else piece + outer
-            sums = total if side == 0 else sums + total
-            mix = out if side == 0 else mix + out
-        put_grad(dw_refs, core_ref, t, slice(0, 3 * third), piece.astype(BF))
-        put_grad(dw_refs, core_ref, t, slice(3 * third, 4 * third), mix.astype(BF))
-        dqb_ref[:, cols] = sums
-    dob_ref[...] = jnp.sum(low0_ref[...].astype(F32), axis=0, keepdims=True) + jnp.sum(
-        low1_ref[...].astype(F32), axis=0, keepdims=True
-    )
-    for side, da_ref in enumerate((da0_ref, da1_ref)):
-        hidden_grad, gain_grad, shift_grad = norm_pull(
-            unit[half[side]], scale[half[side]], gain, normed_grad[side]
+
+    @pl.when(step == 0)
+    def _():
+        unit, _ = norm_parts(h_ref[...])
+        n_sc[...] = (unit * gain + b_ref[...]).astype(BF)
+        acc[...] = jnp.zeros_like(acc)
+        dob_ref[...] = jnp.sum(low0_ref[...].astype(F32), axis=0, keepdims=True) + jnp.sum(
+            low1_ref[...].astype(F32), axis=0, keepdims=True
         )
-        dh_ref[half[side], :] = (da_ref[...] + hidden_grad).astype(dh_ref.dtype)
-        if side == 0:
-            dg_ref[...] = gain_grad
-            db_ref[...] = shift_grad
-        else:
-            dg_ref[...] += gain_grad
-            db_ref[...] += shift_grad
+
+    matrix = flat_rows(w_ref[:, 0, :, :wide])
+    piece = sums = mix = None
+    sides = ((dq0_ref, low0_ref, o0_ref), (dq1_ref, low1_ref, o1_ref))
+    for side, (dq_ref, low_ref, o_ref) in enumerate(sides):
+        grads = dq_ref[...]
+        acc[half[side], :] += mm_bt(grads, matrix)
+        outer = mm_at(n_sc[half[side], :], grads)
+        total = jnp.sum(grads.astype(F32), axis=0, keepdims=True)
+        out = mm_at(low_ref[...], o_ref[...])
+        piece = outer if side == 0 else piece + outer
+        sums = total if side == 0 else sums + total
+        mix = out if side == 0 else mix + out
+    put_grad(dw_refs, core_ref, 0, slice(0, wide), piece.astype(BF))
+    put_grad(dw_refs, core_ref, 0, slice(wide, w_ref.shape[3]), mix.astype(BF))
+    dqb_ref[...] = sums
+
+    @pl.when(step == pl.num_programs(0) - 1)
+    def _():
+        unit, scale = norm_parts(h_ref[...])
+        for side, da_ref in enumerate((da0_ref, da1_ref)):
+            hidden_grad, gain_grad, shift_grad = norm_pull(
+                unit[half[side]], scale[half[side]], gain, acc[half[side], :]
+            )
+            dh_ref[half[side], :] = (da_ref[...] + hidden_grad).astype(dh_ref.dtype)
+            if side == 0:
+                dg_ref[...] = gain_grad
+                db_ref[...] = shift_grad
+            else:
+                dg_ref[...] += gain_grad
+                db_ref[...] += shift_grad
 
 
 def attention_grad(
@@ -428,18 +439,34 @@
     shapes = grad_shapes(devices, width, 2 * width, split)
     block = rows // 2
     short = jax.ShapeDtypeStruct((1, width), F32)
+    third = width // 2
+
+    def side_block(shape):
+        if len(shape) == 3:
+            return pl.BlockSpec((1,) + shape[1:], lambda t, *_: (t, 0, 0))
+        return pl.BlockSpec(
+            (shape[0], 1) + shape[2:], lambda t, *_: (0, t, 0, 0)
+        )
+
+    def columns_of(value, which, columns):
+        at = which if value.shape[0] > block else 0
+        return pl.BlockSpec((block, columns), lambda t, *_: (at, t))
+
     made = call(
-        attn_grad_kernel, (1,),
+        attn_grad_kernel, (2,),
         [
             half_of(incoming[0], block, 0), half_of(incoming[1], block, 1),
             whole((rows, width)), whole((1, width)), whole((1, width)),
-            weight_spec(weights, 2, 2 * width, lambda *_: (0, 0, 0, layer)),
-            whole((block, 3 * width)), whole((block, 3 * width)),
+            pl.BlockSpec(
+                (weights.shape[0], 1, weights.shape[2], 2 * width),
+                lambda t, *_: (0, t, 0, layer),
+            ),
+            columns_of(cores[0][0], 0, 3 * third), columns_of(cores[1][0], 0, 3 * third),
             whole((block, width)), whole((block, width)),
-            half_of(mixed[0], block, 0), half_of(mixed[1], block, 1),
+            columns_of(mixed[0], 0, third), columns_of(mixed[1], 1, third),
         ],
-        [whole(shape) for shape in shapes] + [
-            whole((rows, width)), whole((1, 3 * width)),
+        [side_block(shape) for shape in shapes] + [
+            whole((rows, width)), pl.BlockSpec((1, 3 * third), lambda t, *_: (0, t)),
             whole((1, width)), whole((1, width)), whole((1, width)),
         ],
         [jax.ShapeDtypeStruct(shape, BF) for shape in shapes] + [
@@ -447,7 +474,7 @@
             jax.ShapeDtypeStruct((1, 3 * width), F32),
             short, short, short,
         ],
-        [],
+        [pltpu.VMEM((rows, width), BF), pltpu.VMEM((rows, width), F32)],
         14.0 * rows * width * width, 25.0e6, "attn_grad", after, prefetch=1,
     )(core, *incoming, hidden, gain, shift, weights, cores[0][0], cores[1][0], cores[0][1],
       cores[1][1], *mixed)
@@ -562,46 +589,71 @@
     return made[: len(shapes)], made[len(shapes) :]
 
 
+def pick_rows(place_ref, m, expert, capp):
+    half = place_ref.shape[2]
+    ids = lax.broadcasted_iota(jnp.int32, (capp, half), 0) + expert * capp
+    return place_ref[m, 0:1, :] == ids, place_ref[m, 1:2, :] == ids
+
+
+def as_pick(hit):
+    return jnp.where(hit, 1.0, 0.0).astype(BF)
+
+
+def spread_kernel(capp, own_ref, oth_ref, po_ref, pt_ref, out_ref):
+    expert = pl.program_id(0)
+    for m in range(own_ref.shape[0]):
+        total = None
+        for ref, place_ref in ((own_ref, po_ref), (oth_ref, pt_ref)):
+            hit0, hit1 = pick_rows(place_ref, m, expert, capp)
+            part = mm(as_pick(hit0 | hit1), ref[m])
+            total = part if total is None else total + part
+        out_ref[0, m * capp : (m + 1) * capp, :] = total.astype(BF)
+
+
+def spread_rows(own, oth, place_own, place_oth, experts, capp):
+    micro, half, width = own.shape
+    slots = micro * capp
+    (out,) = call(
+        functools.partial(spread_kernel, capp), (experts,),
+        [whole(own.shape), whole(oth.shape), whole(place_own.shape), whole(place_oth.shape)],
+        [pl.BlockSpec((1, slots, width), lambda e: (e, 0, 0))],
+        [jax.ShapeDtypeStruct((experts, slots, width), BF)],
+        [], 4.0 * experts * slots * half * width, 9.0e6, "spread",
+    )(own, oth, place_own, place_oth)
+    return out
+
+
 def moe_kernel(
     capp,
-    rb_own0, rb_own1, rb_oth0, rb_oth1, og_own, og_oth, dr_ref, dc_own, dc_oth, w_ref,
+    rb_own0, rb_own1, rb_oth0, rb_oth1, og_ref, po_ref, pt_ref, w_ref,
     win_ref, wout_ref, bin_ref, bout_ref,
-    yc_own, yc_oth, rc_own, rc_oth0, rc_oth1, dg_own, dg_oth, dw_ref, dbin_ref, dbout_ref,
-    b_sc, og_sc, dy_sc, w_sc, y_acc, r_acc, yo_acc, yt_acc, ro_acc, rt_acc,
+    y_ref, r_ref, d_ref, dw_ref, dbin_ref, dbout_ref,
+    b_sc, dy_sc, w_sc, y_acc, r_acc,
 ):
     micro = 2
     expert = pl.program_id(0)
     chunk = pl.program_id(1)
-    last_expert = expert == pl.num_programs(0) - 1
     last_chunk = chunk == pl.num_programs(1) - 1
-    half = rb_own0.shape[0]
     rb_all = ((rb_own0, rb_oth0), (rb_own1, rb_oth1))
 
     @pl.when(chunk == 0)
     def _():
         for m in range(micro):
             slots = slice(m * capp, (m + 1) * capp)
-            ids = lax.broadcasted_iota(jnp.int32, (capp, half), 0) + expert * capp
-            tokens = None
-            for side, og in enumerate((og_own, og_oth)):
-                hit0 = dr_ref[m, 2 * side : 2 * side + 1, :] == ids
-                hit1 = dr_ref[m, 2 * side + 1 : 2 * side + 2, :] == ids
-                pick = jnp.where(hit0 | hit1, 1.0, 0.0).astype(BF)
-                gate = jnp.sum(
+            rows = gate = None
+            for side, place_ref in enumerate((po_ref, pt_ref)):
+                hit0, hit1 = pick_rows(place_ref, m, expert, capp)
+                part = mm(as_pick(hit0 | hit1), rb_all[m][side][...])
+                weight = jnp.sum(
                     jnp.where(hit0, w_ref[m, 2 * side : 2 * side + 1, :], 0.0)
                     + jnp.where(hit1, w_ref[m, 2 * side + 1 : 2 * side + 2, :], 0.0),
                     axis=-1, keepdims=True,
                 )
-                found = (mm(pick, rb_all[m][side][...]), mm(pick, og[m]), gate)
-                tokens = found if tokens is None else tuple(
-                    one + two for one, two in zip(tokens, found)
-                )
-            b_sc[slots, :] = tokens[0].astype(BF)
-            og_sc[slots, :] = tokens[1].astype(BF)
-            dy_sc[slots, :] = (tokens[1] * tokens[2]).astype(BF)
-            w_sc[slots, :] = jnp.broadcast_to(tokens[2], (capp, w_sc.shape[1]))
-        y_acc[...] = jnp.zeros_like(y_acc)
-        r_acc[...] = jnp.zeros_like(r_acc)
+                rows = part if side == 0 else rows + part
+                gate = weight if side == 0 else gate + weight
+            b_sc[slots, :] = rows.astype(BF)
+            dy_sc[slots, :] = (og_ref[0, slots, :].astype(F32) * gate).astype(BF)
+            w_sc[slots, :] = jnp.broadcast_to(gate, (capp, w_sc.shape[1]))
 
     tokens = b_sc[...]
     low = dy_sc[...]
@@ -610,109 +662,128 @@
     active = active.astype(BF)
     preact_grad = (slope * mm(low, wout_ref[...])).astype(BF)
     dbin_ref[0] = jnp.sum(preact_grad.astype(F32), axis=0, keepdims=True)
-    y_acc[...] += mm_bt(active, wout_ref[...])
-    r_acc[...] += mm_bt(preact_grad, win_ref[...])
+    result = mm_bt(active, wout_ref[...])
+    rows_grad = mm_bt(preact_grad, win_ref[...])
     every = slice(None)
     put_grad((dw_ref,), None, 1, every, mm_at(low, active).astype(BF))
     put_grad((dw_ref,), None, 0, every, mm_at(tokens, preact_grad).astype(BF))
 
+    @pl.when(chunk == 0)
+    def _():
+        y_acc[...] = result
+        r_acc[...] = rows_grad
+
+    @pl.when((chunk > 0) & jnp.logical_not(last_chunk))
+    def _():
+        y_acc[...] += result
+        r_acc[...] += rows_grad
+
     @pl.when(last_chunk)
     def _():
         dbout_ref[0] = jnp.sum(dy_sc[...].astype(F32), axis=0, keepdims=True)
-        for m in range(micro):
-            slots = slice(m * capp, (m + 1) * capp)
-            result = y_acc[slots, :] + 0.5 * bout_ref[0]
-            dots = jnp.sum(og_sc[slots, :].astype(F32) * result, axis=-1, keepdims=True)
-            lanes = lax.broadcasted_iota(jnp.int32, (capp, 128), 1)
-            dots = jnp.where(lanes == expert, dots, 0.0)
-            weighted = (w_sc[slots, 0:1] * result).astype(BF)
-            rows_grad = r_acc[slots, :].astype(BF)
-            ids = lax.broadcasted_iota(jnp.int32, (half, capp), 1) + expert * capp
-            for dc, yc, rc, dg in (
-                (dc_own, yo_acc, ro_acc, dg_own), (dc_oth, yt_acc, rt_acc, dg_oth)
-            ):
-                hit = (dc[m, :, 0:1] == ids) | (dc[m, :, 1:2] == ids)
-                pick = jnp.where(hit, 1.0, 0.0)
-                low_pick = pick.astype(BF)
-                y_new = mm(low_pick, weighted)
-                r_new = mm(low_pick, rows_grad)
-                d_new = lax.dot_general(
-                    dots, pick, (((0,), (1,)), ((), ())), precision=EXACT,
-                    preferred_element_type=F32,
-                )[: dg.shape[1]]
-
-                @pl.when(expert == 0)
-                def _():
-                    yc[m] = y_new
-                    rc[m] = r_new
-                    dg[m] = d_new
-
-                @pl.when(expert > 0)
-                def _():
-                    yc[m] += y_new
-                    rc[m] += r_new
-                    dg[m] += d_new
-
-    @pl.when(last_chunk & last_expert)
-    def _():
-        yc_own[...] = yo_acc[...].astype(BF)
-        yc_oth[...] = yt_acc[...].astype(BF)
-        rc_own[...] = ro_acc[...].astype(BF)
-        rc_oth0[...] = rt_acc[0].astype(BF)
-        rc_oth1[...] = rt_acc[1].astype(BF)
-
-
-def mixture(rows_own, rows_oth, grad_own, grad_oth, place_rows, place_own, place_oth, gates,
-            weights, in_bias, out_bias, capp, devices):
-    micro, half, width = grad_own.shape
-    experts, _, ff = in_bias.shape
-    steps = ff // FF_BLOCK
+        total = y_acc[...] + result + 0.5 * bout_ref[0]
+        dots = jnp.sum(og_ref[0].astype(F32) * total, axis=-1, keepdims=True)
+        high = dots.astype(BF)
+        rest = dots - high.astype(F32)
+        mid = rest.astype(BF)
+        tiny = (rest - mid.astype(F32)).astype(BF)
+        lanes = lax.broadcasted_iota(jnp.int32, d_ref.shape[1:], 1)
+        zero = jnp.zeros(d_ref.shape[1:], BF)
+        d_ref[0] = jnp.where(
+            lanes == expert, high,
+            jnp.where(lanes == 8 + expert, mid, jnp.where(lanes == 16 + expert, tiny, zero)),
+        )
+        y_ref[0] = (w_sc[:, 0:1] * total).astype(BF)
+        r_ref[0] = (r_acc[...] + rows_grad).astype(BF)
+
+
+def mixture(rows_own, rows_oth, grad_rows, place_own, place_oth, gates, weights, in_bias,
+            out_bias, capp, devices):
+    half, width = rows_own[0].shape
+    experts, slots, _ = grad_rows.shape
+    ff = in_bias.shape[2]
+    block = EXPERT_BLOCK
+    steps = ff // block
     blocks = experts * steps
-    slots = micro * capp
-    w_block = (width, FF_BLOCK)
-    group = (micro, half, width)
-    dots = (micro, 8, half)
+    w_block = (width, block)
     flat = (half, width)
     (shape,) = grad_shapes(devices, width, experts * ff, False)
+    by_expert = pl.BlockSpec((1, slots, width), lambda e, c: (e, 0, 0))
     return call(
         functools.partial(moe_kernel, capp),
         (experts, steps),
         [
-            whole(flat), whole(flat), whole(flat), whole(flat), whole(group), whole(group),
-            whole(place_rows.shape), whole(place_own.shape), whole(place_oth.shape),
-            whole(gates.shape),
+            whole(flat), whole(flat), whole(flat), whole(flat), by_expert,
+            whole(place_own.shape), whole(place_oth.shape), whole(gates.shape),
             pl.BlockSpec(w_block, lambda e, c: (0, e * steps + c)),
             pl.BlockSpec(w_block, lambda e, c: (0, blocks + e * steps + c)),
-            pl.BlockSpec((1, 1, FF_BLOCK), lambda e, c: (e, 0, c)),
+            pl.BlockSpec((1, 1, block), lambda e, c: (e, 0, c)),
             pl.BlockSpec((1, 1, width), lambda e, c: (e, 0, 0)),
         ],
         [
-            whole(group), whole(group), whole(group), whole(flat), whole(flat),
-            whole(dots), whole(dots),
-            grad_block(shape, FF_BLOCK, lambda e, c: e * steps + c),
-            pl.BlockSpec((1, 1, FF_BLOCK), lambda e, c: (e, 0, c)),
+            by_expert, by_expert, pl.BlockSpec((1, slots, 128), lambda e, c: (e, 0, 0)),
+            grad_block(shape, block, lambda e, c: e * steps + c),
+            pl.BlockSpec((1, 1, block), lambda e, c: (e, 0, c)),
             pl.BlockSpec((1, 1, width), lambda e, c: (e, 0, 0)),
         ],
         [
-            jax.ShapeDtypeStruct(group, BF), jax.ShapeDtypeStruct(group, BF),
-            jax.ShapeDtypeStruct(group, BF), jax.ShapeDtypeStruct(flat, BF),
-            jax.ShapeDtypeStruct(flat, BF),
-            jax.ShapeDtypeStruct(dots, F32), jax.ShapeDtypeStruct(dots, F32),
+            jax.ShapeDtypeStruct((experts, slots, width), BF),
+            jax.ShapeDtypeStruct((experts, slots, width), BF),
+            jax.ShapeDtypeStruct((experts, slots, 128), BF),
             jax.ShapeDtypeStruct(shape, BF),
             jax.ShapeDtypeStruct((experts, 1, ff), F32),
             jax.ShapeDtypeStruct((experts, 1, width), F32),
         ],
         [
             pltpu.VMEM((slots, width), BF), pltpu.VMEM((slots, width), BF),
-            pltpu.VMEM((slots, width), BF), pltpu.VMEM((slots, 128), F32),
+            pltpu.VMEM((slots, 128), F32),
             pltpu.VMEM((slots, width), F32), pltpu.VMEM((slots, width), F32),
-            pltpu.VMEM(group, F32), pltpu.VMEM(group, F32),
-            pltpu.VMEM(group, F32), pltpu.VMEM(group, F32),
         ],
-        12.0 * slots * experts * width * ff + 16.0 * experts * micro * capp * half * width,
+        12.0 * slots * experts * width * ff + 4.0 * experts * slots * half * width,
         60.0e6, "experts",
-    )(*rows_own, *rows_oth, grad_own, grad_oth, place_rows, place_own, place_oth, gates,
-      weights, weights, in_bias, out_bias)
+    )(*rows_own, *rows_oth, grad_rows, place_own, place_oth, gates, weights, weights,
+      in_bias, out_bias)
+
+
+def collect_kernel(capp, jobs, *refs):
+    picks = {}
+    for m, place, source, out, kind in jobs:
+        rows_ref, out_ref = refs[source], refs[out]
+        experts = rows_ref.shape[0]
+        half = refs[place].shape[1]
+        if (m, place) not in picks:
+            hits = []
+            for expert in range(experts):
+                ids = lax.broadcasted_iota(jnp.int32, (half, capp), 1) + expert * capp
+                hit = (refs[place][m, :, 0:1] == ids) | (refs[place][m, :, 1:2] == ids)
+                hits.append(as_pick(hit))
+            picks[m, place] = hits
+        total = None
+        for expert, pick in enumerate(picks[m, place]):
+            rows = rows_ref[expert, m * capp : (m + 1) * capp, :]
+            if kind == "dots":
+                part = lax.dot_general(
+                    rows, pick, (((0,), (1,)), ((), ())), preferred_element_type=F32
+                )
+            else:
+                part = mm(pick, rows)
+            total = part if total is None else total + part
+        if kind == "dots":
+            total = total[0:8] + total[8:16] + total[16:24]
+        if len(out_ref.shape) == 3:
+            out_ref[m] = total.astype(out_ref.dtype)
+        else:
+            out_ref[...] = total.astype(out_ref.dtype)
+
+
+def collect(capp, arrays, outs, jobs, name, after=()):
+    experts, slots, width = arrays[-1].shape
+    return call(
+        functools.partial(collect_kernel, capp, tuple(jobs)), (1,),
+        [whole(value.shape) for value in arrays], [whole(shape) for shape, _ in outs],
+        [jax.ShapeDtypeStruct(shape, kind) for shape, kind in outs], [],
+        2.0 * len(jobs) * arrays[0].shape[1] * experts * capp * width, 8.0e6, name, after,
+    )(*arrays)
 
 
 def gate_bwd_kernel(
@@ -788,13 +859,16 @@
     return lax.all_gather(share, "dp", axis=0, tiled=True)
 
 
-def chip_ring(chips):
-    if chips == 8:
-        return [0, 2, 4, 6, 7, 5, 3, 1]
-    return list(range(chips))
-
-
-def ring_add_kernel(kind, at_ref, *refs):
+def ring_chip(place, chips):
+    half = chips // 2
+    even = 2 * place
+    odd = 2 * (chips - 1 - place) + 1
+    if isinstance(place, int):
+        return even if place < half else odd
+    return jnp.where(place < half, even, odd)
+
+
+def ring_add(kind, refs):
     def chunk(grads, given):
         return grads[0].astype(F32) + given[0].astype(F32)
 
@@ -806,6 +880,9 @@
     elif kind == 3:
         grads, given, got_a, got_b, out = refs
         out[...] = chunk(grads, given) + (got_a[...].astype(F32) + got_b[...].astype(F32))
+    elif kind == 4:
+        one, two, out = refs
+        out[...] = one[...] + two[...]
     else:
         grads_a, given_a, grads_b, given_b, got_a, got_b, ahead, behind = refs
         one, two = chunk(grads_a, given_a), chunk(grads_b, given_b)
@@ -819,13 +896,44 @@
             behind[...] = (two + got_b[...].astype(F32)).astype(BF)
 
 
+def step_kernel(plans, _, *refs):
+    taken = sum(ins for _, ins, _ in plans)
+    at, out_at = 0, taken
+    for kind, ins, outs in plans:
+        ring_add(kind, refs[at : at + ins] + refs[out_at : out_at + outs])
+        at += ins
+        out_at += outs
+
+
+def step_all(chains, after=()):
+    live = [chain for chain in chains if not chain.finished()]
+    if not live:
+        return tuple(after)
+    stages = [chain.stage(index) for index, chain in enumerate(live)]
+    places = jnp.stack([place for stage in stages for place in stage[1]]).astype(jnp.int32)
+    sums = call(
+        functools.partial(
+            step_kernel, tuple((stage[0], len(stage[2]), len(stage[4])) for stage in stages)
+        ),
+        (1,), [spec for stage in stages for spec in stage[2]],
+        [whole(out.shape) for stage in stages for out in stage[4]],
+        [out for stage in stages for out in stage[4]], [], 0, 2.0e6, "ring_add", after,
+        prefetch=1,
+    )(places, *[value for stage in stages for value in stage[3]])
+    at = 0
+    for chain, stage in zip(live, stages):
+        chain.take(sums[at : at + len(stage[4])])
+        at += len(stage[4])
+    return tuple(sums[:1])
+
+
 class RingSum:
     def __init__(self, kept, sent):
         count = lax.axis_size("dp")
         self.chips = count // 2
-        self.ring = chip_ring(self.chips)
-        position = [self.ring.index(chip) for chip in range(self.chips)]
-        self.here = jnp.array(position, jnp.int32)[lax.axis_index("dp") // 2]
+        self.ring = [ring_chip(place, self.chips) for place in range(self.chips)]
+        chip = lax.axis_index("dp") // 2
+        self.here = jnp.where(chip % 2 == 0, chip // 2, self.chips - 1 - chip // 2)
         self.kept = kept
         self.away = self.chips // 2
         self.messages = (sent,)
@@ -841,38 +949,37 @@
         ]
         return lax.ppermute(value, "dp", pairs)
 
-    def step(self, after=()):
-        if self.result is not None:
-            return
-        table = jnp.array(self.ring, jnp.int32)
+    def finished(self):
+        return self.result is not None
+
+    def stage(self, index):
         away = self.away
-        chips = [table[(self.here + away) % self.chips], table[(self.here - away) % self.chips]]
-        places = jnp.stack(chips).astype(jnp.int32)
+        chips = [
+            ring_chip((self.here + far) % self.chips, self.chips)
+            for far in (away, self.chips - away)
+        ]
         shape = self.kept.shape[1:]
 
         def chunk_specs(which):
-            return [
-                pl.BlockSpec((1,) + shape, lambda _, at: (at[which], 0, 0, 0)),
-                pl.BlockSpec((1,) + shape, lambda _, at: (at[which], 0, 0, 0)),
-            ]
+            slot = 2 * index + which
+            return [pl.BlockSpec((1,) + shape, lambda _, at: (at[slot], 0, 0, 0))] * 2
 
         far = self.chips // 2
         kind = 3 if away == 0 else 0 if away == far else 1 if away == far - 1 else 2
         two_ways = kind in (1, 2)
         in_specs = chunk_specs(0) + (chunk_specs(1) if two_ways else [])
+        in_specs += [whole(got.shape) for got in self.got]
         args = [self.kept, self.given] * (2 if two_ways else 1) + list(self.got)
-        in_specs += [whole(got.shape) for got in self.got]
         out = shape if kind else shape[1:]
-        kinds = [jax.ShapeDtypeStruct(out, F32 if kind == 3 else BF)] * (1 if kind == 3 else 2)
-        sums = call(
-            functools.partial(ring_add_kernel, kind), (1,), in_specs,
-            [whole(out)] * len(kinds), kinds, [], 0, 1.0e6, "ring_add", after, prefetch=1,
-        )(places, *args)
-        self.away -= 1
-        if kind == 3:
+        outs = [jax.ShapeDtypeStruct(out, F32 if kind == 3 else BF)] * (1 if kind == 3 else 2)
+        return kind, chips, in_specs, args, outs
+
+    def take(self, sums):
+        if self.away == 0:
             self.result = sums[0]
             self.messages = ()
             return
+        self.away -= 1
         self.messages = tuple(sums)
         self.got = (self.send(sums[0], 1), self.send(sums[1], -1))
 
@@ -884,41 +991,68 @@
         self.messages = (done,)
         self.result = done.reshape((2,) + done.shape[-2:]).astype(F32)
 
-    def step(self, after=()):
-        return
-
-
-def add_kernel(one_ref, two_ref, out_ref):
-    out_ref[...] = one_ref[...] + two_ref[...]
+    def finished(self):
+        return True
+
+
+def hold_kernel(value_ref, out_ref):
+    return
+
+
+def hold(value, after):
+    anywhere = pl.BlockSpec(memory_space=pl.ANY)
+    return call(
+        hold_kernel, (1,), [anywhere], anywhere, jax.ShapeDtypeStruct(value.shape, value.dtype),
+        [], 0, 1.0e3, "hold", after, aliases={0: 0},
+    )(value)
+
+
+def expert_out_kernel(sum_ref, in_ref, out_ref):
+    experts, ff = in_ref.shape[1], in_ref.shape[2]
+    for part, ref in enumerate((in_ref, out_ref)):
+        for expert in range(experts):
+            ref[:, expert, :] = sum_ref[part, :, expert * ff : (expert + 1) * ff].astype(F32)
+
+
+def expert_outputs(total, shape, after):
+    return call(
+        expert_out_kernel, (1,), [whole(total.shape)], [whole(shape)] * 2,
+        [jax.ShapeDtypeStruct(shape, F32)] * 2, [], 0, 4.0e6, "expert_out", after,
+    )(total)
 
 
 class PairSum:
     def __init__(self, value):
         self.count = lax.axis_size("dp")
         self.value = value
-        self.stage = 1
+        self.reach = 1
         self.send()
 
     def send(self):
         self.messages = (self.value,)
-        if self.stage < self.count:
-            pairs = [(at, at ^ self.stage) for at in range(self.count)]
+        if self.reach < self.count:
+            pairs = [(at, at ^ self.reach) for at in range(self.count)]
             self.got = lax.ppermute(self.value, "dp", pairs)
-        elif self.stage == self.count:
+        elif self.reach == self.count:
             self.got = swap(self.value)
         else:
             self.got = None
             self.messages = ()
-        self.stage *= 2
-
-    def step(self, after=()):
-        if self.got is None:
-            return
+        self.reach *= 2
+
+    def finished(self):
+        return self.got is None
+
+    def stage(self, index):
+        zero = jnp.zeros((), jnp.int32)
         shape = self.value.shape
-        (self.value,) = call(
-            add_kernel, (1,), [whole(shape)] * 2, [whole(shape)],
-            [jax.ShapeDtypeStruct(shape, F32)], [], 0, 3.0e5, "small_add", after,
-        )(self.value, self.got)
+        return (
+            4, [zero, zero], [whole(shape)] * 2, [self.value, self.got],
+            [jax.ShapeDtypeStruct(shape, F32)],
+        )
+
+    def take(self, sums):
+        (self.value,) = sums
         self.send()
 
 
@@ -987,10 +1121,31 @@
         out_ref[:, (1 - side) * images + image] = other
 
 
+def place_rows_kernel(side_ref, own_ref, got_ref, out_ref):
+    images, length = own_ref.shape[1], out_ref.shape[1]
+    for side, (first, second) in enumerate(((own_ref, got_ref), (got_ref, own_ref))):
+        @pl.when(side_ref[0] == side)
+        def _():
+            for image in range(images):
+                out_ref[0, :, image, :] = first[0, image, :length, :].astype(out_ref.dtype)
+                out_ref[0, :, images + image, :] = second[0, image, :length, :].astype(
+                    out_ref.dtype
+                )
+
+
 def place_images(own, got, shape, kind, after):
     micro, images, length, width = shape
     padded = (micro, images // 2, own.size // (micro * (images // 2) * width), width)
     side = lax.axis_index("tensor").reshape(1)
+    if kind == F32:
+        turned = (micro, length, images, width)
+        (out,) = call(
+            place_rows_kernel, (micro,),
+            [pl.BlockSpec((1,) + padded[1:], lambda m, *_: (m, 0, 0, 0))] * 2,
+            [pl.BlockSpec((1,) + turned[1:], lambda m, *_: (m, 0, 0, 0))],
+            [jax.ShapeDtypeStruct(turned, kind)], [], 0, 8.0e6, "place", after, prefetch=1,
+        )(side, own.reshape(padded), got.reshape(padded))
+        return jnp.swapaxes(out, 1, 2)
     (out,) = call(
         place_kernel, (micro,),
         [pl.BlockSpec((1,) + padded[1:], lambda m, *_: (m, 0, 0, 0))] * 2,
@@ -1004,7 +1159,7 @@
     mine = lax.axis_index("tensor")
     kept = lax.dynamic_index_in_dim(mine_first, mine, 0, keepdims=False)
     sent = lax.dynamic_index_in_dim(mine_first, 1 - mine, 0, keepdims=False)
-    return kept + swap(sent)
+    return kept + swap(sent.astype(BF)).astype(F32)
 
 
 def own_half(value, axis):
@@ -1078,8 +1233,10 @@
         return part.reshape(micro, half, 2)
 
     place_own, place_oth = lay(place, mine_at), lay(place, other_at)
-    place_rows = jnp.concatenate(
-        [jnp.swapaxes(place_own, 1, 2), jnp.swapaxes(place_oth, 1, 2)], axis=1
+    place_own_rows = jnp.swapaxes(place_own, 1, 2)
+    place_oth_rows = jnp.swapaxes(place_oth, 1, 2)
+    grad_rows = spread_rows(
+        grad_own, grad_oth, place_own_rows, place_oth_rows, experts, capp
     )
     select = lay(pick, mine_at).reshape(rows, 2)
     router_wide = jnp.pad(router, ((0, 0), (0, 128 - experts)))
@@ -1109,12 +1266,29 @@
     gate_pair = jnp.concatenate([gate_own, swap(gate_own)], axis=1)
     ring = whole_tiles(devices, width)
     core = (lax.axis_index("dp") % 2).reshape(1)
-    (
-        y_own, y_oth, r_own, r_oth0, r_oth1, d_own, d_oth, expert_grad, ein_bias, eout_bias,
-    ) = mixture(
-        rows_own, rows_oth, grad_own, grad_oth, place_rows, place_own, place_oth, gate_pair,
-        expert_w, expert_in_bias.reshape(experts, 1, -1),
-        expert_out_bias.reshape(experts, 1, -1), capp, devices,
+    y_slots, r_slots, d_slots, expert_grad, ein_bias, eout_bias = mixture(
+        rows_own, rows_oth, grad_rows, place_own_rows, place_oth_rows, gate_pair, expert_w,
+        expert_in_bias.reshape(experts, 1, -1), expert_out_bias.reshape(experts, 1, -1), capp,
+        devices,
+    )
+    group, one, dots = (micro, half, width), (half, width), (micro, 8, half)
+    r_oth0, r_oth1, d_oth = collect(
+        capp, (place_oth, d_slots, r_slots), ((one, BF), (one, BF), (dots, F32)),
+        (
+            (0, 0, 2, 3, "rows"), (1, 0, 2, 4, "rows"), (0, 0, 1, 5, "dots"),
+            (1, 0, 1, 5, "dots"),
+        ),
+        "collect_first",
+    )
+    y_own, y_oth, r_own, d_own = collect(
+        capp, (place_own, place_oth, d_slots, r_slots, y_slots),
+        ((group, BF), (group, BF), (group, BF), (dots, F32)),
+        (
+            (0, 0, 3, 7, "rows"), (1, 0, 3, 7, "rows"), (0, 0, 2, 8, "dots"),
+            (1, 0, 2, 8, "dots"), (0, 0, 4, 5, "rows"), (1, 0, 4, 5, "rows"),
+            (0, 1, 4, 6, "rows"), (1, 1, 4, 6, "rows"),
+        ),
+        "collect_rest", (r_oth0,),
     )
     d_got = swap(d_oth)
     r_got = swap(r_oth0)
@@ -1141,50 +1315,44 @@
         mix_two, devices, ring, F32,
     )
     sum_two = RingSum(*two_grad) if ring else PlainSum(*two_grad)
-    early_sum = PairSum(
-        pack_rows(
+    out_own = layer_output(after_two, y_own, y_got, (gain_two,))
+    out_got = swap(out_own)
+    early = (
             [
                 ([gain_two], 1, 1.0, False), (gain_parts, 1, 1.0, False),
                 ([shift_two], 1, 1.0, False), (shift_parts, 1, 1.0, False),
                 ([ob_two], 1, 1.0, False), ([qb_two], 1, 1.0, False),
                 (router_parts, experts, 1.0, False), ([eout_bias], experts, 0.5, False),
                 ([ein_bias], experts, 1.0, True),
-            ],
-            width,
-        )
+            ]
     )
     dense_grad, (grad_one, in_bias_grad, out_bias_grad, gain_ffn, shift_ffn) = dense_back(
         core, grad_ffn, after_one, row(norm_gain[0, 1]), row(row_bias[0, 1]), first_w, dense_at,
-        mlp_bias_full, devices, ring, sum_two.messages + early_sum.messages + (sent,),
-    )
-    done = (gain_ffn,)
-    sum_two.step(done)
-    early_sum.step(done)
-    dense_sum = RingSum(*dense_grad) if ring else PlainSum(*dense_grad)
-    out_own = layer_output(after_two, y_own, y_got, done)
-    out_got = swap(out_own)
-    chains = (sum_two, dense_sum, early_sum)
-
-    def flying():
-        return sum_two.messages + dense_sum.messages + early_sum.messages
-
+        mlp_bias_full, devices, ring, sum_two.messages + (out_own,),
+    )
+    last = step_all([sum_two], (gain_ffn, out_got))
+    if ring:
+        dense_sum = RingSum(dense_grad[0], hold(dense_grad[1], last))
+    else:
+        dense_sum = PlainSum(*dense_grad)
+    block_output = place_images(out_own, out_got, block_input.shape, BF, last)
+    step_all([dense_sum], (block_output,))
     cores = []
     for which in range(2):
         cores.append(
             attention_core_back(
                 grad_one, first_w, 0, (qkv_one, lse_one, half), length, pad, which,
-                flying() + (out_own,),
+                sum_two.messages + dense_sum.messages + (block_output,),
             )
         )
-        for chain in chains:
-            chain.step((cores[-1][1],))
-    block_output = place_images(out_own, out_got, block_input.shape, BF, (cores[-1][1],))
+        step_all([sum_two, dense_sum], (cores[-1][1],))
     one_grad, (grad_zero, qb_one, ob_one, gain_one, shift_one) = attention_grad(
         core, (grad_one, grad_one), hidden, row(norm_gain[0, 0]), row(row_bias[0, 0]), first_w,
-        0, cores, (mix_one, mix_one), devices, ring, BF, flying(),
-    )
-    one_sum = RingSum(*one_grad) if ring else PlainSum(*one_grad)
-    grad_got = swap(grad_zero)
+        0, cores, (mix_one, mix_one), devices, False, BF,
+        sum_two.messages + dense_sum.messages,
+    )
+    last = step_all([sum_two, dense_sum], (qb_one,))
+    one_sum = PlainSum(hold(one_grad[0], expert_sum.messages + last))
     late_sum = PairSum(
         pack_rows(
             [
@@ -1192,33 +1360,40 @@
                 ([shift_one], 1, 1.0, False), ([shift_ffn], 1, 1.0, False),
                 ([ob_one], 1, 1.0, False), ([qb_one], 1, 1.0, False),
                 ([in_bias_grad], 1, 1.0, False), ([out_bias_grad], 1, 1.0, False),
-            ],
+            ] + early,
             width,
         )
     )
-    last = (qb_one,)
-    queue = [sum_two, one_sum]
-    for _ in range(devices):
-        queue += [dense_sum, sum_two, early_sum, late_sum, one_sum]
-    for chain in queue:
-        chain.step(last)
-        if chain.messages:
-            last = chain.messages
-    input_grad = place_images(grad_zero, grad_got, block_input.shape, F32, last)
-
-    expert_grads = expert_sum.result.reshape(2, share_rows, experts, -1)
-    attn_grads = [join_sides(one_sum.result), join_sides(sum_two.result)]
-    dense_done = join_sides(
-        jnp.moveaxis(dense_sum.result.reshape(2, share_rows, 2, -1), 2, 0)
-    )
+    expert_total = expert_sum.messages[0].reshape((2, share_rows, -1))
+    expert_grads = expert_outputs(expert_total, expert_in.shape, last)
+    last = (expert_grads[0],)
+    grad_got = swap(grad_zero)
+    for turn in range(devices):
+        last = step_all([sum_two, dense_sum, late_sum], last)
+        if turn == 2:
+            input_grad = place_images(grad_zero, grad_got, block_input.shape, F32, last)
+            last = (input_grad,)
+
+    one_done = join_sides(one_sum.result)
+    joined = join_sides(
+        jnp.concatenate(
+            [
+                sum_two.result[:, None],
+                jnp.moveaxis(dense_sum.result.reshape(2, share_rows, 2, -1), 2, 0),
+            ],
+            axis=1,
+        )
+    )
+    attn_grads, dense_done = [one_done, joined[0]], joined[1:]
     split_at = 3 * width // 2
 
-    late, early = late_sum.value, early_sum.value
+    late = late_sum.value
+    ff_rows = in_bias_grad.shape[1] // width
+    early = late[9 + ff_rows :]
     gain_sum = jnp.concatenate([late[0:2], early[0:2]])
     shift_sum = jnp.concatenate([late[2:5], early[2:5]])
     qb_sum = jnp.stack([late[5:8], early[5:8]]).reshape(2, 2, 3, width // 2)
     qb_sum = lax.dynamic_index_in_dim(qb_sum, side, 1, keepdims=False)
-    ff_rows = in_bias_grad.shape[1] // width
     in_bias_sum = late[8 : 8 + ff_rows]
     out_bias_sum = late[8 + ff_rows]
     at = 8 + experts

time: 737 us -> 647 us (0.88)
  Pallas kernels: 409 us -> 336 us
  waiting for transfers between devices: 149 us -> 176 us
  starting transfers between devices: 57.7 us -> 42.1 us
  local copies, waits for them, and re-layouts: 74.9 us -> 60.4 us
    pallas_call x44 -> x34, Pallas kernels: 409 us -> 336 us  [call(): return lambda *args: made(*args, *after)]
    ppermute x16 -> x14, waiting for transfers between devices: 55.4 us -> 23.8 us  [swap(): return lax.ppermute(value, 'tensor', [(0, 1), (1, 0)])]
    ppermute x24 -> x16, waiting for transfers between devices: 12.7 us -> 39.9 us  [send(): return lax.ppermute(value, 'dp', pairs)]
    all_gather x1, waiting for transfers between devices: 0.01 us -> 24.9 us  [gather_rows(): return lax.all_gather(share, 'dp', axis=0, tiled=True)]
    ppermute x24 -> x16, starting transfers between devices: 28 us -> 17.3 us  [send(): return lax.ppermute(value, 'dp', pairs)]
    unnamed x161 -> x142, local copies, waits for them, and re-layouts: 34.9 us -> 27.7 us
    ppermute x16 -> x14, starting transfers between devices: 20.2 us -> 20 us  [swap(): return lax.ppermute(value, 'tensor', [(0, 1), (1, 0)])]
  transfers between devices with their start and end apart: 54 -> 40, of which waited for: 12 -> 16; matrix products, arithmetic and copies ran while one was open for 9% -> 8% of each run, Pallas kernels for 43% -> 43%
where the time goes in v4:
time: 647 us; the launch traced here: 640 us
  Pallas kernels  336 us (52%)
  waiting for transfers between devices  176 us (27%)
  local copies, waits for them, and re-layouts  60.4 us (9%)
  starting transfers between devices  42.1 us (7%)
  between operations  15.3 us (2%)
  other arithmetic  9.84 us (2%)
    pallas_call x34, Pallas kernels, call(): return lambda *args: made(*args, *after)  336 us
    all_gather x1, waiting for transfers between devices, local(): lax.all_gather(in_order(first_mine, swap(first_mine), 0), 'dp', axis=0, t...  73.9 us
    ppermute x16, waiting for transfers between devices, send(): return lax.ppermute(value, 'dp', pairs)  39.9 us
    unnamed x142, local copies, waits for them, and re-layouts  27.7 us
    all_gather x1, waiting for transfers between devices, gather_rows(): return lax.all_gather(share, 'dp', axis=0, tiled=True)  24.9 us
    ppermute x14, waiting for transfers between devices, swap(): return lax.ppermute(value, 'tensor', [(0, 1), (1, 0)])  23.8 us
    ppermute x14, starting transfers between devices, swap(): return lax.ppermute(value, 'tensor', [(0, 1), (1, 0)])  20 us
    ppermute x16, starting transfers between devices, send(): return lax.ppermute(value, 'dp', pairs)  17.3 us
  transfers between devices with their start and end apart: 40, of which 16 were waited for; matrix products, arithmetic and copies ran while one was open for 8% of the time, Pallas kernels for 43%

profile of v4, /device:TPU:0, one launch (start us, length us, event | category | flops | bytes accessed | tf_op | source)
XLA Modules:
  0.0 640.4 jit_solution(5158258590807631328)
XLA Ops:
  9.4 3.0 collective-permute-start
  12.4 13.3 %collective-permute-done = bf16[48,6144]{1,0:T(8,128)(2,1)S(1)} collective-permute-done((bf16[48,6144]{1,0:T(8,128)(2,1)S(1)}, bf16[48,6144]{1,0:T(8,128)(2,1)S(1)}, u32[]{:S(2)}, u32[]{:S(2)}) %collective-permute-start) | collective-permute-done | bytes 589856 | tf_op jit(solution)/shard_map/ppermute | solution.py:850
  31.2 6.9 %constant_dynamic-slice_fusion.1 = (bf16[2,2,197,768]{3,1,2,0:T(2,128)(2,1)S(1)}, bf16[2,2,197,768]{3,1,2,0:T(2,128)(2,1)S(1)}, bf16[2,2,197,768]{3,1,2,0:T(2,128)(2,1)S(1)}) fusion(bf16[2,4,197,768]{3,1,2,0:T(4,128)(2,1)} %param.35, s32[]{:T(128)S(6)} %select_n.192, s32[]{:T(128)S(6)} %select_n.183, bf16[2,4,197,768]{3,1,2,0:T(4,128)(2,1)} %param.18), kind=kLoop, calls=%fused_computation.62 | loop fusion | bytes 7262216 | tf_op jit(solution)/shard_map/dynamic_slice | solution.py:1215
  53.7 73.9 %all-gather.6.cloned.1.call-done = bf16[32,48,6144]{2,1,0:T(8,128)(2,1)} async-done(((bf16[2,48,6144]{2,1,0:T(8,128)(2,1)}), bf16[32,48,6144]{2,1,0:T(8,128)(2,1)}) %all-gather.6.cloned.1.call-update) | async-done | bytes 18874384 | tf_op jit(solution)/shard_map/all_gather | solution.py:1192
  127.6 16.4 %attn_fwd.3 = (bf16[832,2304]{1,0:T(8,128)(2,1)}, f32[4,16,208]{2,1,0:T(8,128)}, bf16[832,768]{1,0:T(8,128)(2,1)}, f32[832,768]{1,0:T(8,128)}) custom-call(f32[832,768]{1,0:T(8,128)} %bitcast_convert_fusion.refs_0_.refs_3_, f32[1,768]{1,0:T(1,128)} %get-tuple-element.294.refs_1_.refs_4_, f32[1,768]{1,0:T(1,128)} %get-tuple-element.286.refs_2_.refs_5_, ...), custom_call_target="tpu_custom_call" | custom-call | flops 6052380672 | bytes 12000000 | tf_op jit(solution)/shard_map/attn_fwd/pallas_call | solution.py:104
  144.0 15.8 %dense_fwd.1.refs_0_.refs_3_ = f32[832,768]{1,0:T(8,128)} custom-call(f32[832,768]{1,0:T(8,128)} %get-tuple-element.106.refs_0_.refs_2_, f32[1,768]{1,0:T(1,128)} %get-tuple-element.293.refs_1_.refs_3_, f32[1,768]{1,0:T(1,128)} %get-tuple-element.284.refs_2_.refs_4_, bf16[16,2,48,6144]{3,2,1,0:T(8,128)(2,1)} %bitcast.138, ...), custom_call_target="tpu_custom_call" | custom-call | flops 7851737088 | bytes 15000000 | tf_op jit(solution)/shard_map/dense_fwd/pallas_call | solution.py:104
  159.8 12.6 %attn_fwd.4 = (bf16[416,2304]{1,0:T(8,128)(2,1)}, f32[2,16,208]{2,1,0:T(8,128)}, bf16[416,768]{1,0:T(8,128)(2,1)}, f32[416,768]{1,0:T(8,128)}, bf16[416,768]{1,0...) custom-call(f32[832,768]{1,0:T(8,128)} %dense_fwd.1.refs_0_.refs_3_, ...), custom_call_target="tpu_custom_call" | custom-call | flops 3026190336 | bytes 12000000 | tf_op jit(solution)/shard_map/attn_fwd/pallas_call | solution.py:104
  174.0 12.3 %attn_fwd.5 = (bf16[416,2304]{1,0:T(8,128)(2,1)}, f32[2,16,208]{2,1,0:T(8,128)}, bf16[416,768]{1,0:T(8,128)(2,1)}, f32[416,768]{1,0:T(8,128)}, bf16[416,768]{1,0...) custom-call(f32[832,768]{1,0:T(8,128)} %dense_fwd.1.refs_0_.refs_3_, ...), custom_call_target="tpu_custom_call" | custom-call | flops 3026190336 | bytes 12000000 | tf_op jit(solution)/shard_map/attn_fwd/pallas_call | solution.py:104
  189.6 7.4 %spread.1.refs_4_ = bf16[4,608,768]{2,1,0:T(8,128)(2,1)} custom-call(bf16[2,416,768]{2,1,0:T(8,128)(2,1)} %bitcast.152, bf16[2,416,768]{2,1,0:T(8,128)(2,1)} %bitcast.171, s32[2,2,416]{2,1,0:T(2,128)} %copy.116.refs_2_.refs_5_, s32[2,2,416]{2,1,0:T(2,128)} %copy.117.refs_3_.refs_6_), custom_call_target="tpu_custom_call" | custom-call | flops 3107979264 | bytes 9000000 | tf_op jit(solution)/shard_map/spread/pallas_call | solution.py:104
  198.3 5.0 collective-permute-done.4
  203.9 24.9 %all-gather.4.cloned.1.call-done.refs_8_.refs_9_ = bf16[768,12288]{1,0:T(8,128)(2,1)} async-done(((bf16[48,12288]{1,0:T(8,128)(2,1)}), bf16[768,12288]{1,0:T(8,128)(2,1)}) %all-gather.4.cloned.1.call-update) | async-done | bytes 18874384 | tf_op jit(solution)/shard_map/all_gather | solution.py:859
  230.4 58.8 %experts.1 = (bf16[4,608,768]{2,1,0:T(8,128)(2,1)}, bf16[4,608,768]{2,1,0:T(8,128)(2,1)}, bf16[4,608,128]{2,1,0:T(8,128)(2,1)}, bf16[16,2,48,6144]{3,2,1,0:T(8,1...) custom-call(bf16[416,768]{1,0:T(8,128)(2,1)} %get-tuple-element.109.refs_0_, ...), custom_call_target="tpu_custom_call" | custom-call | flops 37534826496 | bytes 60000000 | tf_op jit(solution)/shard_map/experts/pallas_call | solution.py:104
  289.4 6.9 %collect_first.1 = (bf16[416,768]{1,0:T(8,128)(2,1)}, bf16[416,768]{1,0:T(8,128)(2,1)}, f32[2,8,416]{2,1,0:T(8,128)}) custom-call(s32[2,416,2]{2,1,0:T(8,128)} %bitcast.169, bf16[4,608,128]{2,1,0:T(8,128)(2,1)} %get-tuple-element.113.refs_1_.refs_2_, bf16[4,608,768]{2,1,0:T(8,128)(2,1)} %get-tuple-element.114.refs_2_.refs_3_), custom_call_target="tpu_custom_call" | custom-call | flops 3107979264 | bytes 8000000 | tf_op jit(solution)/shard_map/collect_first/pallas_call | solution.py:104
  298.4 16.4 %collect_rest.1 = (bf16[2,416,768]{2,1,0:T(8,128)(2,1)}, bf16[2,416,768]{2,1,0:T(8,128)(2,1)}, bf16[2,416,768]{2,1,0:T(8,128)(2,1)}, f32[2,8,416]{2,1,0:T(8,128)}) custom-call(s32[2,416,2]{2,1,0:T(8,128)} %bitcast.167, s32[2,416,2]{2,1,0:T(8,128)} %bitcast.170, bf16[4,608,128]{2,1,0:T(8,128)(2,1)} %get-tuple-element.113.refs_1_.refs_2_, ...), custom_call_target="tpu_custom_call" | custom-call | flops 6215958528 | bytes 8000000 | tf_op jit(solution)/shard_map/collect_rest/pallas_call | solution.py:104
  315.6 7.4 %gate_bwd.2 = (bf16[416,768]{1,0:T(8,128)(2,1)}, f32[416,768]{1,0:T(8,128)}, f32[128,768]{1,0:T(8,128)}, f32[1,768]{1,0:T(1,128)}, f32[1,768]{1,0:T(1,128)}) custom-call(f32[416,768]{1,0:T(8,128)} %get-tuple-element.107.refs_0_, bf16[2,416,768]{2,1,0:T(8,128)(2,1)} %bitcast.153, bf16[416,768]{1,0:T(8,128)(2,1)} %get-tuple-element.120.refs_2_, ...), custom_call_target="tpu_custom_call" | custom-call | flops 163577856 | bytes 7000000 | tf_op jit(solution)/shard_map/gate_bwd/pallas_call | solution.py:104
  324.6 12.2 %attn_core.4 = (bf16[416,2304]{1,0:T(8,128)(2,1)}, bf16[416,768]{1,0:T(8,128)(2,1)}) custom-call(f32[416,768]{1,0:T(8,128)} %get-tuple-element.126.refs_0_.refs_1_, bf16[16,2,48,6144]{3,2,1,0:T(8,128)(2,1)} %bitcast.142, bf16[416,2304]{1,0:T(8,128)(2,1)} %get-tuple-element.127.refs_2_, f32[2,16,208]{2,1,0:T(8,128)} %get-tuple-element.128.refs_3_, ...), custom_call_target="tpu_custom_call" | custom-call | flops 5807013888 | bytes 8000000 | tf_op jit(solution)/shard_map/attn_core/pallas_call | solution.py:104
  336.8 2.6 collective-permute-done.7.refs_4_
  340.3 7.2 %gate_bwd.3 = (bf16[2,416,768]{2,1,0:T(8,128)(2,1)}, f32[416,768]{1,0:T(8,128)}, f32[128,768]{1,0:T(8,128)}, f32[1,768]{1,0:T(1,128)}, f32[1,768]{1,0:T(1,128)}) custom-call(f32[416,768]{1,0:T(8,128)} %get-tuple-element.108.refs_0_.refs_1_, bf16[2,416,768]{2,1,0:T(8,128)(2,1)} %bitcast.154, bf16[2,416,768]{2,1,0:T(8,128)(2,1)} %get-tuple-element.118.refs_2_, ...), custom_call_target="tpu_custom_call" | custom-call | flops 163577856 | bytes 7000000 | tf_op jit(solution)/shard_map/gate_bwd/pallas_call | solution.py:104
  349.0 12.2 %attn_core.5 = (bf16[416,2304]{1,0:T(8,128)(2,1)}, bf16[416,768]{1,0:T(8,128)(2,1)}) custom-call(f32[416,768]{1,0:T(8,128)} %get-tuple-element.131.refs_0_.refs_2_, bf16[16,2,48,6144]{3,2,1,0:T(8,128)(2,1)} %bitcast.143, bf16[416,2304]{1,0:T(8,128)(2,1)} %get-tuple-element.133.refs_2_, f32[2,16,208]{2,1,0:T(8,128)} %get-tuple-element.134.refs_3_, ...), custom_call_target="tpu_custom_call" | custom-call | flops 5807013888 | bytes 8000000 | tf_op jit(solution)/shard_map/attn_core/pallas_call | solution.py:104
  361.2 20.1 %attn_grad.2 = (bf16[8,2,48,1536]{3,2,1,0:T(8,128)(2,1)}, bf16[8,2,48,1536]{3,2,1,0:T(8,128)(2,1)}, f32[832,768]{1,0:T(8,128)}, f32[1,2304]{1,0:T(1,128)}, f32[1...) custom-call(s32[1]{0:T(128)} %bitcast.37.refs_0_, f32[416,768]{1,0:T(8,128)} %get-tuple-element.126.refs_0_.refs_1_, ...), custom_call_target="tpu_custom_call" | custom-call | flops 6870269952 | bytes 25000000 | tf_op jit(solution)/shard_map/attn_grad/pallas_call | solution.py:104
  382.1 4.0 layer_output.1.refs_9_
  386.7 38.8 %dense_bwd.1 = (bf16[8,2,48,3072]{3,2,1,0:T(8,128)(2,1)}, bf16[8,2,48,3072]{3,2,1,0:T(8,128)(2,1)}, f32[832,768]{1,0:T(8,128)}, f32[1,3072]{1,0:T(1,128)}, f32[1...) custom-call(s32[1]{0:T(128)} %bitcast.37.refs_0_, f32[832,768]{1,0:T(8,128)} %get-tuple-element.142.refs_1_, ...), custom_call_target="tpu_custom_call" | custom-call | flops 19629342720 | bytes 35000000 | tf_op jit(solution)/shard_map/dense_bwd/pallas_call | solution.py:104
  427.3 2.5 ring_add.10
  433.4 2.8 place.2.refs_3_.refs_8_
  438.1 2.8 ring_add.11
  442.9 12.4 %attn_core.6 = (bf16[416,2304]{1,0:T(8,128)(2,1)}, bf16[416,768]{1,0:T(8,128)(2,1)}) custom-call(f32[832,768]{1,0:T(8,128)} %get-tuple-element.145.refs_0_.refs_1_.refs_2_, bf16[16,2,48,6144]{3,2,1,0:T(8,128)(2,1)} %bitcast.147, bf16[832,2304]{1,0:T(8,128)(2,1)} %get-tuple-element.146.refs_2_, f32[4,16,208]{2,1,0:T(8,128)} %get-tuple-element.147.refs_3_, ...), custom_call_target="tpu_custom_call" | custom-call | flops 5807013888 | bytes 8000000 | tf_op jit(solution)/shard_map/attn_core/pallas_call | solution.py:104
  456.7 8.3 %collective-permute-done.15.refs_12_ = bf16[48,3072]{1,0:T(8,128)(2,1)S(1)} collective-permute-done((bf16[48,3072]{1,0:T(8,128)(2,1)}, bf16[48,3072]{1,0:T(8,128)(2,1)S(1)}, u32[]{:S(2)}, u32[]{:S(2)}) %collective-permute-start.15) | collective-permute-done | bytes 294944 | tf_op jit(solution)/shard_map/ppermute | solution.py:950
  465.7 4.3 ring_add.12
  474.6 12.2 %attn_core.7 = (bf16[416,2304]{1,0:T(8,128)(2,1)}, bf16[416,768]{1,0:T(8,128)(2,1)}) custom-call(f32[832,768]{1,0:T(8,128)} %get-tuple-element.145.refs_0_.refs_1_.refs_2_, bf16[16,2,48,6144]{3,2,1,0:T(8,128)(2,1)} %bitcast.148, bf16[832,2304]{1,0:T(8,128)(2,1)} %get-tuple-element.146.refs_2_, f32[4,16,208]{2,1,0:T(8,128)} %get-tuple-element.147.refs_3_, ...), custom_call_target="tpu_custom_call" | custom-call | flops 5807013888 | bytes 8000000 | tf_op jit(solution)/shard_map/attn_core/pallas_call | solution.py:104
  486.9 18.0 %collective-permute-done.16.refs_5_ = bf16[2,48,1536]{2,1,0:T(8,128)(2,1)S(1)} collective-permute-done((bf16[2,48,1536]{2,1,0:T(8,128)(2,1)}, bf16[2,48,1536]{2,1,0:T(8,128)(2,1)S(1)}, u32[]{:S(2)}, u32[]{:S(2)}) %collective-permute-start.16) | collective-permute-done | bytes 294944 | tf_op jit(solution)/shard_map/ppermute | solution.py:950
  507.9 4.6 ring_add.13
  516.6 18.8 %attn_grad.3 = (bf16[16,2,48,1536]{3,2,1,0:T(8,128)(2,1)}, bf16[832,768]{1,0:T(8,128)(2,1)}, f32[1,2304]{1,0:T(1,128)}, f32[1,768]{1,0:T(1,128)}, f32[1,768]{1,0:T(1,128)}, /*index=5*/f32[1,768]{1,0:T(1,128)}) custom-call(s32[1]{0:T(128)} %bitcast.37.refs_0_, f32[832,768]{1,0:T(8,128)} %get-tuple-element.145.refs_0_.refs_1_.refs_2_, ...), custom_call_target="tpu_custom_call" | custom-call | flops 6870269952 | bytes 25000000 | tf_op jit(solution)/shard_map/attn_grad/pallas_call | solution.py:104
  536.5 4.6 ring_add.14
  550.5 3.0 expert_out.1
  553.4 9.4 %collective-permute-done.25.refs_3_ = bf16[2,48,1536]{2,1,0:T(8,128)(2,1)S(1)} collective-permute-done((bf16[2,48,1536]{2,1,0:T(8,128)(2,1)S(1)}, bf16[2,48,1536]{2,1,0:T(8,128)(2,1)S(1)}, u32[]{:S(2)}, u32[]{:S(2)}) %collective-permute-start.25) | collective-permute-done | bytes 294944 | tf_op jit(solution)/shard_map/ppermute | solution.py:950
  564.8 4.2 ring_add.15
  573.8 3.0 collective-permute-done.30.refs_2_
  577.5 2.3 ring_add.16.refs_1_.refs_3_
  580.8 5.9 collective-permute-done.31.refs_2_
  587.4 2.3 ring_add.17.refs_3_.refs_1_
  591.9 2.4 copy.124
  594.2 4.3 place.3
  598.6 3.4 copy.144
  601.9 4.1 copy.125
  606.7 2.3 ring_add.18.refs_1_.refs_3_
  611.5 2.8 collective-permute-done.33.refs_2_
  615.0 2.3 ring_add.19
  621.5 3.0 reduce-scatter.5.cloned.1.call-done
  (294 shorter events, 100.7 us)
Async XLA Ops:
  7.2 120.4 %all-gather.6.cloned.1.call-start = ((), (), s32[]{:S(2)}) async-start(), calls=%async_computation.5 | async-start | bytes 20054016 | tf_op jit(solution)/shard_map/all_gather | solution.py:1192
  9.4 16.4 %collective-permute-start = (bf16[48,6144]{1,0:T(8,128)(2,1)S(1)}, bf16[48,6144]{1,0:T(8,128)(2,1)S(1)}, u32[]{:S(2)}, u32[]{:S(2)}) collective-permute-start(bf16[48,6144]{1,0:T(8,128)(2,1)S(1)} %constant_dynamic-update-slice_fusion), channel_id=1, source_target_pairs={{0,1},{1,0},{2,3},{3,2},{4,5},{5,4},{6,7},{7,6},{8,9},{9,8},{10,11... | collective-permute-start | bytes 1769480 | tf_op jit(solution)/shard_map/ppermute | solution.py:850
  27.0 201.7 %all-gather.4.cloned.1.call-start = ((), (), s32[]{:S(2)}) async-start(), calls=%async_computation.2 | async-start | bytes 20054016 | tf_op jit(solution)/shard_map/all_gather | solution.py:859
  29.3 511.8 %reduce-scatter.3.cloned.1.call-start = ((), (), s32[]{:S(2)}) async-start(), calls=%async_computation.3 | async-start | bytes 20054016 | tf_op jit(solution)/shard_map/reduce_scatter | solution.py:990
  29.4 22.4 %collective-permute-start.1 = (f32[3072]{0:T(1024)S(1)}, f32[3072]{0:T(1024)S(1)}, u32[]{:S(2)}, u32[]{:S(2)}) collective-permute-start(f32[3072]{0:T(1024)S(1)} %constant_dynamic-update-slice_fusion.5), channel_id=1, source_target_pairs={{0,1},{1,0},{2,3},{3,2},{4,5},{5,4},{6,7},{7,6},{8,9},{9,8},{10,11... | collective-permute-start | bytes 36872 | tf_op jit(solution)/shard_map/ppermute | solution.py:850
  172.4 15.5 %copy-start.31 = (f32[416,128]{1,0:T(8,128)S(1)}, f32[416,128]{1,0:T(8,128)}, u32[]{:S(2)}) copy-start(f32[416,128]{1,0:T(8,128)} %get-tuple-element.111) | copy-start | bytes 638980
  172.4 56.3 %collective-permute-start.2 = (bf16[416,768]{1,0:T(8,128)(2,1)}, bf16[416,768]{1,0:T(8,128)(2,1)S(1)}, u32[]{:S(2)}, u32[]{:S(2)}) collective-permute-start(bf16[416,768]{1,0:T(8,128)(2,1)} %get-tuple-element.109.refs_0_), channel_id=1, source_target_pairs={{0,1},{1,0},{2,3},{3,2},{4,5},{5,4},{6,7},{7,6},{8,9},{9,8},{10,11... | collective-permute-start | bytes 1916936 | tf_op jit(solution)/shard_map/ppermute | solution.py:850
  186.3 42.5 %collective-permute-start.3 = (bf16[416,768]{1,0:T(8,128)(2,1)}, bf16[416,768]{1,0:T(8,128)(2,1)S(1)}, u32[]{:S(2)}, u32[]{:S(2)}) collective-permute-start(bf16[416,768]{1,0:T(8,128)(2,1)} %get-tuple-element.110.refs_1_), channel_id=1, source_target_pairs={{0,1},{1,0},{2,3},{3,2},{4,5},{5,4},{6,7},{7,6},{8,9},{9,8},{10,11... | collective-permute-start | bytes 1916936 | tf_op jit(solution)/shard_map/ppermute | solution.py:850
  188.1 15.1 %collective-permute-start.4 = (f32[2,2,416]{2,1,0:T(2,128)S(1)}, f32[2,2,416]{2,1,0:T(2,128)S(1)}, u32[]{:S(2)}, u32[]{:S(2)}) collective-permute-start(f32[2,2,416]{2,1,0:T(2,128)S(1)} %pad_maximum_fusion.8), channel_id=1, source_target_pairs={{0,1},{1,0},{2,3},{3,2},{4,5},{5,4},{6,7},{7,6},{8,9},{9,8},{10,11... | collective-permute-start | bytes 19976 | tf_op jit(solution)/shard_map/ppermute | solution.py:850
  189.6 8.0 %copy-start.51 = (f32[4,768]{1,0:T(4,128)S(1)}, f32[4,768]{1,0:T(4,128)}, u32[]{:S(2)}) copy-start(f32[4,768]{1,0:T(4,128)} %param.32) | copy-start | bytes 36868
  289.2 335.2 %reduce-scatter.5.cloned.1.call-start = ((), (), s32[]{:S(2)}) async-start(), calls=%async_computation.4 | async-start | bytes 5013504 | tf_op jit(solution)/shard_map/reduce_scatter | solution.py:990
  296.3 18.4 %collective-permute-start.5 = (bf16[416,768]{1,0:T(8,128)(2,1)}, bf16[416,768]{1,0:T(8,128)(2,1)S(1)}, u32[]{:S(2)}, u32[]{:S(2)}) collective-permute-start(bf16[416,768]{1,0:T(8,128)(2,1)} %get-tuple-element.116.refs_5_), channel_id=1, source_target_pairs={{0,1},{1,0},{2,3},{3,2},{4,5},{5,4},{6,7},{7,6},{8,9},{9,8},{10,11... | collective-permute-start | bytes 1916936 | tf_op jit(solution)/shard_map/ppermute | solution.py:850
  297.8 16.9 %collective-permute-start.6 = (f32[2,8,416]{2,1,0:T(8,128)}, f32[2,8,416]{2,1,0:T(8,128)S(1)}, u32[]{:S(2)}, u32[]{:S(2)}) collective-permute-start(f32[2,8,416]{2,1,0:T(8,128)} %get-tuple-element.122), channel_id=1, source_target_pairs={{0,1},{1,0},{2,3},{3,2},{4,5},{5,4},{6,7},{7,6},{8,9},{9,8},{10,11... | collective-permute-start | bytes 79880 | tf_op jit(solution)/shard_map/ppermute | solution.py:850
  323.0 16.4 %collective-permute-start.7 = (bf16[416,768]{1,0:T(8,128)(2,1)}, bf16[416,768]{1,0:T(8,128)(2,1)S(1)}, u32[]{:S(2)}, u32[]{:S(2)}) collective-permute-start(bf16[416,768]{1,0:T(8,128)(2,1)} %get-tuple-element.124.refs_4_), channel_id=1, source_target_pairs={{0,1},{1,0},{2,3},{3,2},{4,5},{5,4},{6,7},{7,6},{8,9},{9,8},{10,11... | collective-permute-start | bytes 1916936 | tf_op jit(solution)/shard_map/ppermute | solution.py:850
  347.5 34.6 %collective-permute-start.8 = (bf16[2,416,768]{2,1,0:T(8,128)(2,1)}, bf16[2,416,768]{2,1,0:T(8,128)(2,1)}, u32[]{:S(2)}, u32[]{:S(2)}) collective-permute-start(bf16[2,416,768]{2,1,0:T(8,128)(2,1)} %get-tuple-element.130.refs_4_), channel_id=1, source_target_pairs={{0,1},{1,0},{2,3},{3,2},{4,5},{5,4},{6,7},{7,6},{8,9},{9,8},{10,11... | collective-permute-start | bytes 3833864 | tf_op jit(solution)/shard_map/ppermute | solution.py:850
  381.4 44.1 %collective-permute-start.10 = (bf16[8,2,48,1536]{3,2,1,0:T(8,128)(2,1)}, bf16[8,2,48,1536]{3,2,1,0:T(8,128)(2,1)S(1)}, u32[]{:S(2)}, u32[]{:S(2)}) collective-permute-start(bf16[8,2,48,1536]{3,2,1,0:T(8,128)(2,1)} %get-tuple-element.141.refs_8_), channel_id=1, source_target_pairs={{0,2},{2,0},{4,6},{6,4},{8,10},{10,8},{12,14},{14,12},{16,18},{18,... | collective-permute-start | bytes 7077896 | tf_op jit(solution)/shard_map/ppermute | solution.py:940
  386.1 39.4 %collective-permute-start.9 = (bf16[2,416,768]{2,1,0:T(8,128)(2,1)}, bf16[2,416,768]{2,1,0:T(8,128)(2,1)S(1)}, u32[]{:S(2)}, u32[]{:S(2)}) collective-permute-start(bf16[2,416,768]{2,1,0:T(8,128)(2,1)} %layer_output.1.refs_9_), channel_id=1, source_target_pairs={{0,1},{1,0},{2,3},{3,2},{4,5},{5,4},{6,7},{7,6},{8,9},{9,8},{10,11... | collective-permute-start | bytes 3833864 | tf_op jit(solution)/shard_map/ppermute | solution.py:850
  429.8 8.3 %collective-permute-start.11 = (bf16[8,2,48,3072]{3,2,1,0:T(8,128)(2,1)}, bf16[8,2,48,3072]{3,2,1,0:T(8,128)(2,1)}, u32[]{:S(2)}, u32[]{:S(2)}) collective-permute-start(bf16[8,2,48,3072]{3,2,1,0:T(8,128)(2,1)} %hold.2), channel_id=1, source_target_pairs={{0,2},{2,0},{4,6},{6,4},{8,10},{10,8},{12,14},{14,12},{16,18},{18,... | collective-permute-start | bytes 14155784 | tf_op jit(solution)/shard_map/ppermute | solution.py:940
  431.4 23.9 %collective-permute-start.12 = (bf16[48,1536]{1,0:T(8,128)(2,1)S(1)}, bf16[48,1536]{1,0:T(8,128)(2,1)S(1)}, u32[]{:S(2)}, u32[]{:S(2)}) collective-permute-start(bf16[48,1536]{1,0:T(8,128)(2,1)S(1)} %copy-done.11), channel_id=1, source_target_pairs={{0,8},{2,10},{8,16},{10,18},{16,24},{18,26},{24,28},{26,30},{28,20... | collective-permute-start | bytes 442376 | tf_op jit(solution)/shard_map/ppermute | solution.py:950
  432.8 22.5 %collective-permute-start.13 = (bf16[48,1536]{1,0:T(8,128)(2,1)S(1)}, bf16[48,1536]{1,0:T(8,128)(2,1)S(1)}, u32[]{:S(2)}, u32[]{:S(2)}) collective-permute-start(bf16[48,1536]{1,0:T(8,128)(2,1)S(1)} %copy-done.34), channel_id=1, source_target_pairs={{0,4},{2,6},{8,0},{10,2},{16,8},{18,10},{24,16},{26,18},{28,24},{3... | collective-permute-start | bytes 442376 | tf_op jit(solution)/shard_map/ppermute | solution.py:950
  440.9 15.8 %collective-permute-start.14 = (bf16[48,3072]{1,0:T(8,128)(2,1)}, bf16[48,3072]{1,0:T(8,128)(2,1)S(1)}, u32[]{:S(2)}, u32[]{:S(2)}) collective-permute-start(bf16[48,3072]{1,0:T(8,128)(2,1)} %get-tuple-element.151.refs_6_), channel_id=1, source_target_pairs={{0,8},{2,10},{8,16},{10,18},{16,24},{18,26},{24,28},{26,30},{28,20... | collective-permute-start | bytes 884744 | tf_op jit(solution)/shard_map/ppermute | solution.py:950
  442.4 22.5 %collective-permute-start.15 = (bf16[48,3072]{1,0:T(8,128)(2,1)}, bf16[48,3072]{1,0:T(8,128)(2,1)S(1)}, u32[]{:S(2)}, u32[]{:S(2)}) collective-permute-start(bf16[48,3072]{1,0:T(8,128)(2,1)} %get-tuple-element.152.refs_7_), channel_id=1, source_target_pairs={{0,4},{2,6},{8,0},{10,2},{16,8},{18,10},{24,16},{26,18},{28,24},{3... | collective-permute-start | bytes 884744 | tf_op jit(solution)/shard_map/ppermute | solution.py:950
  455.3 9.7 %copy-start.32 = (bf16[48,1536]{1,0:T(8,128)(2,1)}, bf16[48,1536]{1,0:T(8,128)(2,1)S(1)}, u32[]{:S(2)}) copy-start(bf16[48,1536]{1,0:T(8,128)(2,1)S(1)} %collective-permute-done.12.refs_5_) | copy-start | bytes 442372
  455.3 9.7 %copy-start.33 = (bf16[48,1536]{1,0:T(8,128)(2,1)}, bf16[48,1536]{1,0:T(8,128)(2,1)S(1)}, u32[]{:S(2)}) copy-start(bf16[48,1536]{1,0:T(8,128)(2,1)S(1)} %collective-permute-done.13.refs_6_) | copy-start | bytes 442372
  456.7 8.3 %copy-start.24 = (bf16[48,3072]{1,0:T(8,128)(2,1)}, bf16[48,3072]{1,0:T(8,128)(2,1)S(1)}, u32[]{:S(2)}) copy-start(bf16[48,3072]{1,0:T(8,128)(2,1)S(1)} %collective-permute-done.14.refs_11_) | copy-start | bytes 884740
  470.0 36.8 %collective-permute-start.18 = (bf16[2,48,3072]{2,1,0:T(8,128)(2,1)}, bf16[2,48,3072]{2,1,0:T(8,128)(2,1)S(1)}, u32[]{:S(2)}, u32[]{:S(2)}) collective-permute-start(bf16[2,48,3072]{2,1,0:T(8,128)(2,1)} %get-tuple-element.157.refs_6_), channel_id=1, source_target_pairs={{0,8},{2,10},{8,16},{10,18},{16,24},{18,26},{24,28},{26,30},{28,20... | collective-permute-start | bytes 1769480 | tf_op jit(solution)/shard_map/ppermute | solution.py:950
  470.3 36.5 %collective-permute-start.19 = (bf16[2,48,3072]{2,1,0:T(8,128)(2,1)}, bf16[2,48,3072]{2,1,0:T(8,128)(2,1)S(1)}, u32[]{:S(2)}, u32[]{:S(2)}) collective-permute-start(bf16[2,48,3072]{2,1,0:T(8,128)(2,1)} %get-tuple-element.158.refs_7_), channel_id=1, source_target_pairs={{0,4},{2,6},{8,0},{10,2},{16,8},{18,10},{24,16},{26,18},{28,24},{3... | collective-permute-start | bytes 1769480 | tf_op jit(solution)/shard_map/ppermute | solution.py:950
  472.6 32.3 %collective-permute-start.16 = (bf16[2,48,1536]{2,1,0:T(8,128)(2,1)}, bf16[2,48,1536]{2,1,0:T(8,128)(2,1)S(1)}, u32[]{:S(2)}, u32[]{:S(2)}) collective-permute-start(bf16[2,48,1536]{2,1,0:T(8,128)(2,1)} %get-tuple-element.155.refs_4_), channel_id=1, source_target_pairs={{0,8},{2,10},{8,16},{10,18},{16,24},{18,26},{24,28},{26,30},{28,20... | collective-permute-start | bytes 884744 | tf_op jit(solution)/shard_map/ppermute | solution.py:950
  472.9 33.9 %collective-permute-start.17 = (bf16[2,48,1536]{2,1,0:T(8,128)(2,1)}, bf16[2,48,1536]{2,1,0:T(8,128)(2,1)S(1)}, u32[]{:S(2)}, u32[]{:S(2)}) collective-permute-start(bf16[2,48,1536]{2,1,0:T(8,128)(2,1)} %get-tuple-element.156.refs_5_), channel_id=1, source_target_pairs={{0,4},{2,6},{8,0},{10,2},{16,8},{18,10},{24,16},{26,18},{28,24},{3... | collective-permute-start | bytes 884744 | tf_op jit(solution)/shard_map/ppermute | solution.py:950
  512.5 22.8 %collective-permute-start.21 = (bf16[2,48,1536]{2,1,0:T(8,128)(2,1)}, bf16[2,48,1536]{2,1,0:T(8,128)(2,1)S(1)}, u32[]{:S(2)}, u32[]{:S(2)}) collective-permute-start(bf16[2,48,1536]{2,1,0:T(8,128)(2,1)} %get-tuple-element.162.refs_13_), channel_id=1, source_target_pairs={{0,8},{2,10},{8,16},{10,18},{16,24},{18,26},{24,28},{26,30},{28,20... | collective-permute-start | bytes 884744 | tf_op jit(solution)/shard_map/ppermute | solution.py:950
  514.1 21.3 %collective-permute-start.22 = (bf16[2,48,1536]{2,1,0:T(8,128)(2,1)}, bf16[2,48,1536]{2,1,0:T(8,128)(2,1)S(1)}, u32[]{:S(2)}, u32[]{:S(2)}) collective-permute-start(bf16[2,48,1536]{2,1,0:T(8,128)(2,1)} %get-tuple-element.163.refs_14_), channel_id=1, source_target_pairs={{0,4},{2,6},{8,0},{10,2},{16,8},{18,10},{24,16},{26,18},{28,24},{3... | collective-permute-start | bytes 884744 | tf_op jit(solution)/shard_map/ppermute | solution.py:950
  514.5 20.8 %collective-permute-start.23 = (bf16[2,48,3072]{2,1,0:T(8,128)(2,1)}, bf16[2,48,3072]{2,1,0:T(8,128)(2,1)S(1)}, u32[]{:S(2)}, u32[]{:S(2)}) collective-permute-start(bf16[2,48,3072]{2,1,0:T(8,128)(2,1)} %get-tuple-element.164.refs_15_), channel_id=1, source_target_pairs={{0,8},{2,10},{8,16},{10,18},{16,24},{18,26},{24,28},{26,30},{28,20... | collective-permute-start | bytes 1769480 | tf_op jit(solution)/shard_map/ppermute | solution.py:950
  516.1 19.3 %collective-permute-start.24 = (bf16[2,48,3072]{2,1,0:T(8,128)(2,1)}, bf16[2,48,3072]{2,1,0:T(8,128)(2,1)S(1)}, u32[]{:S(2)}, u32[]{:S(2)}) collective-permute-start(bf16[2,48,3072]{2,1,0:T(8,128)(2,1)} %get-tuple-element.165.refs_16_), channel_id=1, source_target_pairs={{0,4},{2,6},{8,0},{10,2},{16,8},{18,10},{24,16},{26,18},{28,24},{3... | collective-permute-start | bytes 1769480 | tf_op jit(solution)/shard_map/ppermute | solution.py:950
  541.2 53.0 %collective-permute-start.20 = (bf16[832,768]{1,0:T(8,128)(2,1)}, bf16[832,768]{1,0:T(8,128)(2,1)}, u32[]{:S(2)}, u32[]{:S(2)}) collective-permute-start(bf16[832,768]{1,0:T(8,128)(2,1)} %get-tuple-element.166), channel_id=1, source_target_pairs={{0,1},{1,0},{2,3},{3,2},{4,5},{5,4},{6,7},{7,6},{8,9},{9,8},{10,11... | collective-permute-start | bytes 3833864 | tf_op jit(solution)/shard_map/ppermute | solution.py:850
  542.7 21.0 %collective-permute-start.27 = (bf16[2,48,3072]{2,1,0:T(8,128)(2,1)S(1)}, bf16[2,48,3072]{2,1,0:T(8,128)(2,1)S(1)}, u32[]{:S(2)}, u32[]{:S(2)}) collective-permute-start(bf16[2,48,3072]{2,1,0:T(8,128)(2,1)S(1)} %copy-done.58), channel_id=1, source_target_pairs={{0,8},{2,10},{8,16},{10,18},{16,24},{18,26},{24,28},{26,30},{28,20... | collective-permute-start | bytes 1769480 | tf_op jit(solution)/shard_map/ppermute | solution.py:950
  544.3 19.4 %collective-permute-start.28 = (bf16[2,48,3072]{2,1,0:T(8,128)(2,1)S(1)}, bf16[2,48,3072]{2,1,0:T(8,128)(2,1)S(1)}, u32[]{:S(2)}, u32[]{:S(2)}) collective-permute-start(bf16[2,48,3072]{2,1,0:T(8,128)(2,1)S(1)} %copy-done.57), channel_id=1, source_target_pairs={{0,4},{2,6},{8,0},{10,2},{16,8},{18,10},{24,16},{26,18},{28,24},{3... | collective-permute-start | bytes 1769480 | tf_op jit(solution)/shard_map/ppermute | solution.py:950
  546.7 1.7 collective-permute-start.29
  546.7 16.1 %collective-permute-start.25 = (bf16[2,48,1536]{2,1,0:T(8,128)(2,1)S(1)}, bf16[2,48,1536]{2,1,0:T(8,128)(2,1)S(1)}, u32[]{:S(2)}, u32[]{:S(2)}) collective-permute-start(bf16[2,48,1536]{2,1,0:T(8,128)(2,1)S(1)} %copy-done.12), channel_id=1, source_target_pairs={{0,8},{2,10},{8,16},{10,18},{16,24},{18,26},{24,28},{26,30},{28,20... | collective-permute-start | bytes 884744 | tf_op jit(solution)/shard_map/ppermute | solution.py:950
  548.4 15.4 %copy-start.35 = (f32[48,768]{1,0:T(8,128)}, f32[48,768]{1,0:T(8,128)S(1)}, u32[]{:S(2)}) copy-start(f32[48,768]{1,0:T(8,128)S(1)} %collective-permute-done.29.refs_10_) | copy-start | bytes 442372
  548.4 15.4 %collective-permute-start.26 = (bf16[2,48,1536]{2,1,0:T(8,128)(2,1)}, bf16[2,48,1536]{2,1,0:T(8,128)(2,1)S(1)}, u32[]{:S(2)}, u32[]{:S(2)}) collective-permute-start(bf16[2,48,1536]{2,1,0:T(8,128)(2,1)} %get-tuple-element.169), channel_id=1, source_target_pairs={{0,4},{2,6},{8,0},{10,2},{16,8},{18,10},{24,16},{26,18},{28,24},{3... | collective-permute-start | bytes 884744 | tf_op jit(solution)/shard_map/ppermute | solution.py:950
  549.9 19.2 %copy-start.48 = (s32[2]{0:T(128)}, s32[2]{0:T(128)S(1)}, u32[]{:S(2)}) copy-start(s32[2]{0:T(128)S(1)} %broadcast_2_refs_0_.2.refs_0_) | copy-start | bytes 28
  569.1 7.7 %collective-permute-start.30 = (f32[48,768]{1,0:T(8,128)}, f32[48,768]{1,0:T(8,128)S(1)}, u32[]{:S(2)}, u32[]{:S(2)}) collective-permute-start(f32[48,768]{1,0:T(8,128)} %get-tuple-element.191.refs_1_), channel_id=1, source_target_pairs={{0,4},{2,6},{4,0},{6,2},{8,12},{10,14},{12,8},{14,10},{16,20},{18,... | collective-permute-start | bytes 442376 | tf_op jit(solution)/shard_map/ppermute | solution.py:1035
  572.4 19.5 %copy-start.1 = (bf16[2,4,197,768]{3,2,1,0:T(8,128)(2,1)S(1)}, bf16[2,4,197,768]{3,2,1,0:T(8,128)(2,1)}, u32[]{:S(2)}) copy-start(bf16[2,4,197,768]{3,2,1,0:T(8,128)(2,1)} %place.2.refs_3_.refs_8_) | copy-start | bytes 7262212
  572.4 38.0 %collective-permute-start.35 = (bf16[3,48,1536]{2,1,0:T(8,128)(2,1)S(1)}, bf16[3,48,1536]{2,1,0:T(8,128)(2,1)S(1)}, u32[]{:S(2)}, u32[]{:S(2)}) collective-permute-start(bf16[3,48,1536]{2,1,0:T(8,128)(2,1)S(1)} %fusion.5), channel_id=1, source_target_pairs={{0,1},{1,0},{2,3},{3,2},{4,5},{5,4},{6,7},{7,6},{8,9},{9,8},{10,11... | collective-permute-start | bytes 1327112 | tf_op jit(solution)/shard_map/ppermute | solution.py:850
  579.8 6.9 %collective-permute-start.31 = (f32[48,768]{1,0:T(8,128)}, f32[48,768]{1,0:T(8,128)S(1)}, u32[]{:S(2)}, u32[]{:S(2)}) collective-permute-start(f32[48,768]{1,0:T(8,128)} %ring_add.16.refs_1_.refs_3_), channel_id=1, source_target_pairs={{0,8},{2,10},{4,12},{6,14},{8,0},{10,2},{12,4},{14,6},{16,24},{18,... | collective-permute-start | bytes 442376 | tf_op jit(solution)/shard_map/ppermute | solution.py:1035
  589.7 16.4 %collective-permute-start.32 = (f32[48,768]{1,0:T(8,128)}, f32[48,768]{1,0:T(8,128)S(1)}, u32[]{:S(2)}, u32[]{:S(2)}) collective-permute-start(f32[48,768]{1,0:T(8,128)} %ring_add.17.refs_3_.refs_1_), channel_id=1, source_target_pairs={{0,16},{2,18},{4,20},{6,22},{8,24},{10,26},{12,28},{14,30},{16,0},... | collective-permute-start | bytes 442376 | tf_op jit(solution)/shard_map/ppermute | solution.py:1035
  609.0 5.4 collective-permute-start.33
  625.5 6.0 collective-permute-start.34
  (51 other events, 94.0 us)
Sparse Core Ops, SparseCore 0:
  27.1 100.4 all-gather.5
  129.8 98.9 all-gather.3
  289.3 212.9 reduce-scatter.2
  541.3 83.0 reduce-scatter.4

commit v5 on v4

--- a/solution.py
+++ b/solution.py
@@ -15,7 +15,7 @@
 F32 = jnp.float32
 VMEM_LIMIT = 58 * 1024 * 1024
 FF_BLOCK = 512
-EXPERT_BLOCK = 768
+EXPERT_BLOCK = 1536
 ROW_PAD = 16
 GELU_SLOPE = 0.7978845608028654
 GELU_CUBE = 0.044715
@@ -670,10 +670,10 @@
 
     @pl.when(chunk == 0)
     def _():
-        y_acc[...] = result
-        r_acc[...] = rows_grad
-
-    @pl.when((chunk > 0) & jnp.logical_not(last_chunk))
+        y_acc[...] = jnp.zeros_like(y_acc)
+        r_acc[...] = jnp.zeros_like(r_acc)
+
+    @pl.when(jnp.logical_not(last_chunk))
     def _():
         y_acc[...] += result
         r_acc[...] += rows_grad
@@ -1121,31 +1121,10 @@
         out_ref[:, (1 - side) * images + image] = other
 
 
-def place_rows_kernel(side_ref, own_ref, got_ref, out_ref):
-    images, length = own_ref.shape[1], out_ref.shape[1]
-    for side, (first, second) in enumerate(((own_ref, got_ref), (got_ref, own_ref))):
-        @pl.when(side_ref[0] == side)
-        def _():
-            for image in range(images):
-                out_ref[0, :, image, :] = first[0, image, :length, :].astype(out_ref.dtype)
-                out_ref[0, :, images + image, :] = second[0, image, :length, :].astype(
-                    out_ref.dtype
-                )
-
-
 def place_images(own, got, shape, kind, after):
     micro, images, length, width = shape
     padded = (micro, images // 2, own.size // (micro * (images // 2) * width), width)
     side = lax.axis_index("tensor").reshape(1)
-    if kind == F32:
-        turned = (micro, length, images, width)
-        (out,) = call(
-            place_rows_kernel, (micro,),
-            [pl.BlockSpec((1,) + padded[1:], lambda m, *_: (m, 0, 0, 0))] * 2,
-            [pl.BlockSpec((1,) + turned[1:], lambda m, *_: (m, 0, 0, 0))],
-            [jax.ShapeDtypeStruct(turned, kind)], [], 0, 8.0e6, "place", after, prefetch=1,
-        )(side, own.reshape(padded), got.reshape(padded))
-        return jnp.swapaxes(out, 1, 2)
     (out,) = call(
         place_kernel, (micro,),
         [pl.BlockSpec((1,) + padded[1:], lambda m, *_: (m, 0, 0, 0))] * 2,

time: 647 us -> 642 us (level)
    unnamed x142 -> x140, local copies, waits for them, and re-layouts: 27.7 us -> 29.4 us
  transfers between devices with their start and end apart: 40 -> 40, of which waited for: 16 -> 16; matrix products, arithmetic and copies ran while one was open for 8% -> 8% of each run, Pallas kernels for 43% -> 44%
where the time goes in v5:
time: 642 us; the launch traced here: 636 us
  Pallas kernels  332 us (52%)
  waiting for transfers between devices  178 us (28%)
  local copies, waits for them, and re-layouts  58.7 us (9%)
  starting transfers between devices  41.8 us (7%)
  between operations  15.3 us (2%)
  other arithmetic  9.74 us (2%)
    pallas_call x34, Pallas kernels, call(): return lambda *args: made(*args, *after)  332 us
    all_gather x1, waiting for transfers between devices, local(): lax.all_gather(in_order(first_mine, swap(first_mine), 0), 'dp', axis=0, t...  73.9 us
    ppermute x16, waiting for transfers between devices, send(): return lax.ppermute(value, 'dp', pairs)  39.8 us
    unnamed x140, local copies, waits for them, and re-layouts  29.4 us
    all_gather x1, waiting for transfers between devices, gather_rows(): return lax.all_gather(share, 'dp', axis=0, tiled=True)  25 us
    ppermute x14, waiting for transfers between devices, swap(): return lax.ppermute(value, 'tensor', [(0, 1), (1, 0)])  23.7 us
    ppermute x14, starting transfers between devices, swap(): return lax.ppermute(value, 'tensor', [(0, 1), (1, 0)])  20 us
    ppermute x16, starting transfers between devices, send(): return lax.ppermute(value, 'dp', pairs)  17.3 us
  transfers between devices with their start and end apart: 40, of which 16 were waited for; matrix products, arithmetic and copies ran while one was open for 8% of the time, Pallas kernels for 44%

profile of v5, /device:TPU:0, one launch (start us, length us, event | category | flops | bytes accessed | tf_op | source)
XLA Modules:
  0.0 635.8 jit_solution(1697691401141862022)
XLA Ops:
  8.7 3.0 collective-permute-start
  11.7 13.3 %collective-permute-done = bf16[48,6144]{1,0:T(8,128)(2,1)S(1)} collective-permute-done((bf16[48,6144]{1,0:T(8,128)(2,1)S(1)}, bf16[48,6144]{1,0:T(8,128)(2,1)S(1)}, u32[]{:S(2)}, u32[]{:S(2)}) %collective-permute-start) | collective-permute-done | bytes 589856 | tf_op jit(solution)/shard_map/ppermute | solution.py:850
  30.5 6.9 %constant_dynamic-slice_fusion.1 = (bf16[2,2,197,768]{3,1,2,0:T(2,128)(2,1)S(1)}, bf16[2,2,197,768]{3,1,2,0:T(2,128)(2,1)S(1)}, bf16[2,2,197,768]{3,1,2,0:T(2,128)(2,1)S(1)}) fusion(bf16[2,4,197,768]{3,1,2,0:T(4,128)(2,1)} %param.35, s32[]{:T(128)S(6)} %select_n.192, s32[]{:T(128)S(6)} %select_n.183, bf16[2,4,197,768]{3,1,2,0:T(4,128)(2,1)} %param.18), kind=kLoop, calls=%fused_computation.61 | loop fusion | bytes 7262216 | tf_op jit(solution)/shard_map/dynamic_slice | solution.py:1194
  53.0 73.9 %all-gather.6.cloned.1.call-done = bf16[32,48,6144]{2,1,0:T(8,128)(2,1)} async-done(((bf16[2,48,6144]{2,1,0:T(8,128)(2,1)}), bf16[32,48,6144]{2,1,0:T(8,128)(2,1)}) %all-gather.6.cloned.1.call-update) | async-done | bytes 18874384 | tf_op jit(solution)/shard_map/all_gather | solution.py:1171
  126.8 16.4 %attn_fwd.3 = (bf16[832,2304]{1,0:T(8,128)(2,1)}, f32[4,16,208]{2,1,0:T(8,128)}, bf16[832,768]{1,0:T(8,128)(2,1)}, f32[832,768]{1,0:T(8,128)}) custom-call(f32[832,768]{1,0:T(8,128)} %bitcast_convert_fusion.refs_0_.refs_3_, f32[1,768]{1,0:T(1,128)} %get-tuple-element.294.refs_1_.refs_4_, f32[1,768]{1,0:T(1,128)} %get-tuple-element.286.refs_2_.refs_5_, ...), custom_call_target="tpu_custom_call" | custom-call | flops 6052380672 | bytes 12000000 | tf_op jit(solution)/shard_map/attn_fwd/pallas_call | solution.py:104
  143.2 15.8 %dense_fwd.1.refs_0_.refs_3_ = f32[832,768]{1,0:T(8,128)} custom-call(f32[832,768]{1,0:T(8,128)} %get-tuple-element.106.refs_0_.refs_2_, f32[1,768]{1,0:T(1,128)} %get-tuple-element.293.refs_1_.refs_3_, f32[1,768]{1,0:T(1,128)} %get-tuple-element.284.refs_2_.refs_4_, bf16[16,2,48,6144]{3,2,1,0:T(8,128)(2,1)} %bitcast.135, ...), custom_call_target="tpu_custom_call" | custom-call | flops 7851737088 | bytes 15000000 | tf_op jit(solution)/shard_map/dense_fwd/pallas_call | solution.py:104
  159.0 12.6 %attn_fwd.4 = (bf16[416,2304]{1,0:T(8,128)(2,1)}, f32[2,16,208]{2,1,0:T(8,128)}, bf16[416,768]{1,0:T(8,128)(2,1)}, f32[416,768]{1,0:T(8,128)}, bf16[416,768]{1,0...) custom-call(f32[832,768]{1,0:T(8,128)} %dense_fwd.1.refs_0_.refs_3_, ...), custom_call_target="tpu_custom_call" | custom-call | flops 3026190336 | bytes 12000000 | tf_op jit(solution)/shard_map/attn_fwd/pallas_call | solution.py:104
  173.1 12.4 %attn_fwd.5 = (bf16[416,2304]{1,0:T(8,128)(2,1)}, f32[2,16,208]{2,1,0:T(8,128)}, bf16[416,768]{1,0:T(8,128)(2,1)}, f32[416,768]{1,0:T(8,128)}, bf16[416,768]{1,0...) custom-call(f32[832,768]{1,0:T(8,128)} %dense_fwd.1.refs_0_.refs_3_, ...), custom_call_target="tpu_custom_call" | custom-call | flops 3026190336 | bytes 12000000 | tf_op jit(solution)/shard_map/attn_fwd/pallas_call | solution.py:104
  188.8 7.4 %spread.1.refs_4_ = bf16[4,608,768]{2,1,0:T(8,128)(2,1)} custom-call(bf16[2,416,768]{2,1,0:T(8,128)(2,1)} %bitcast.147, bf16[2,416,768]{2,1,0:T(8,128)(2,1)} %bitcast.166, s32[2,2,416]{2,1,0:T(2,128)} %copy.113.refs_2_.refs_5_, s32[2,2,416]{2,1,0:T(2,128)} %copy.114.refs_3_.refs_6_), custom_call_target="tpu_custom_call" | custom-call | flops 3107979264 | bytes 9000000 | tf_op jit(solution)/shard_map/spread/pallas_call | solution.py:104
  197.5 4.9 collective-permute-done.4
  203.0 25.0 %all-gather.4.cloned.1.call-done.refs_8_.refs_9_ = bf16[768,12288]{1,0:T(8,128)(2,1)} async-done(((bf16[48,12288]{1,0:T(8,128)(2,1)}), bf16[768,12288]{1,0:T(8,128)(2,1)}) %all-gather.4.cloned.1.call-update) | async-done | bytes 18874384 | tf_op jit(solution)/shard_map/all_gather | solution.py:859
  229.7 55.1 %experts.1 = (bf16[4,608,768]{2,1,0:T(8,128)(2,1)}, bf16[4,608,768]{2,1,0:T(8,128)(2,1)}, bf16[4,608,128]{2,1,0:T(8,128)(2,1)}, bf16[16,2,48,6144]{3,2,1,0:T(8,1...) custom-call(bf16[416,768]{1,0:T(8,128)(2,1)} %get-tuple-element.109.refs_0_, ...), custom_call_target="tpu_custom_call" | custom-call | flops 37534826496 | bytes 60000000 | tf_op jit(solution)/shard_map/experts/pallas_call | solution.py:104
  285.0 6.9 %collect_first.1 = (bf16[416,768]{1,0:T(8,128)(2,1)}, bf16[416,768]{1,0:T(8,128)(2,1)}, f32[2,8,416]{2,1,0:T(8,128)}) custom-call(s32[2,416,2]{2,1,0:T(8,128)} %bitcast.164, bf16[4,608,128]{2,1,0:T(8,128)(2,1)} %get-tuple-element.113.refs_1_.refs_2_, bf16[4,608,768]{2,1,0:T(8,128)(2,1)} %get-tuple-element.114.refs_2_.refs_3_), custom_call_target="tpu_custom_call" | custom-call | flops 3107979264 | bytes 8000000 | tf_op jit(solution)/shard_map/collect_first/pallas_call | solution.py:104
  294.0 16.4 %collect_rest.1 = (bf16[2,416,768]{2,1,0:T(8,128)(2,1)}, bf16[2,416,768]{2,1,0:T(8,128)(2,1)}, bf16[2,416,768]{2,1,0:T(8,128)(2,1)}, f32[2,8,416]{2,1,0:T(8,128)}) custom-call(s32[2,416,2]{2,1,0:T(8,128)} %bitcast.162, s32[2,416,2]{2,1,0:T(8,128)} %bitcast.165, bf16[4,608,128]{2,1,0:T(8,128)(2,1)} %get-tuple-element.113.refs_1_.refs_2_, ...), custom_call_target="tpu_custom_call" | custom-call | flops 6215958528 | bytes 8000000 | tf_op jit(solution)/shard_map/collect_rest/pallas_call | solution.py:104
  311.2 7.4 %gate_bwd.2 = (bf16[416,768]{1,0:T(8,128)(2,1)}, f32[416,768]{1,0:T(8,128)}, f32[128,768]{1,0:T(8,128)}, f32[1,768]{1,0:T(1,128)}, f32[1,768]{1,0:T(1,128)}) custom-call(f32[416,768]{1,0:T(8,128)} %get-tuple-element.107.refs_0_, bf16[2,416,768]{2,1,0:T(8,128)(2,1)} %bitcast.148, bf16[416,768]{1,0:T(8,128)(2,1)} %get-tuple-element.120.refs_2_, ...), custom_call_target="tpu_custom_call" | custom-call | flops 163577856 | bytes 7000000 | tf_op jit(solution)/shard_map/gate_bwd/pallas_call | solution.py:104
  320.2 12.2 %attn_core.4 = (bf16[416,2304]{1,0:T(8,128)(2,1)}, bf16[416,768]{1,0:T(8,128)(2,1)}) custom-call(f32[416,768]{1,0:T(8,128)} %get-tuple-element.126.refs_0_.refs_1_, bf16[16,2,48,6144]{3,2,1,0:T(8,128)(2,1)} %bitcast.139, bf16[416,2304]{1,0:T(8,128)(2,1)} %get-tuple-element.127.refs_2_, f32[2,16,208]{2,1,0:T(8,128)} %get-tuple-element.128.refs_3_, ...), custom_call_target="tpu_custom_call" | custom-call | flops 5807013888 | bytes 8000000 | tf_op jit(solution)/shard_map/attn_core/pallas_call | solution.py:104
  332.4 2.6 collective-permute-done.7.refs_4_
  335.9 7.2 %gate_bwd.3 = (bf16[2,416,768]{2,1,0:T(8,128)(2,1)}, f32[416,768]{1,0:T(8,128)}, f32[128,768]{1,0:T(8,128)}, f32[1,768]{1,0:T(1,128)}, f32[1,768]{1,0:T(1,128)}) custom-call(f32[416,768]{1,0:T(8,128)} %get-tuple-element.108.refs_0_.refs_1_, bf16[2,416,768]{2,1,0:T(8,128)(2,1)} %bitcast.149, bf16[2,416,768]{2,1,0:T(8,128)(2,1)} %get-tuple-element.118.refs_2_, ...), custom_call_target="tpu_custom_call" | custom-call | flops 163577856 | bytes 7000000 | tf_op jit(solution)/shard_map/gate_bwd/pallas_call | solution.py:104
  344.6 12.2 %attn_core.5 = (bf16[416,2304]{1,0:T(8,128)(2,1)}, bf16[416,768]{1,0:T(8,128)(2,1)}) custom-call(f32[416,768]{1,0:T(8,128)} %get-tuple-element.131.refs_0_.refs_2_, bf16[16,2,48,6144]{3,2,1,0:T(8,128)(2,1)} %bitcast.140, bf16[416,2304]{1,0:T(8,128)(2,1)} %get-tuple-element.133.refs_2_, f32[2,16,208]{2,1,0:T(8,128)} %get-tuple-element.134.refs_3_, ...), custom_call_target="tpu_custom_call" | custom-call | flops 5807013888 | bytes 8000000 | tf_op jit(solution)/shard_map/attn_core/pallas_call | solution.py:104
  356.8 20.1 %attn_grad.2 = (bf16[8,2,48,1536]{3,2,1,0:T(8,128)(2,1)}, bf16[8,2,48,1536]{3,2,1,0:T(8,128)(2,1)}, f32[832,768]{1,0:T(8,128)}, f32[1,2304]{1,0:T(1,128)}, f32[1...) custom-call(s32[1]{0:T(128)} %bitcast.37.refs_0_, f32[416,768]{1,0:T(8,128)} %get-tuple-element.126.refs_0_.refs_1_, ...), custom_call_target="tpu_custom_call" | custom-call | flops 6870269952 | bytes 25000000 | tf_op jit(solution)/shard_map/attn_grad/pallas_call | solution.py:104
  377.7 4.0 layer_output.1.refs_9_
  382.3 38.8 %dense_bwd.1 = (bf16[8,2,48,3072]{3,2,1,0:T(8,128)(2,1)}, bf16[8,2,48,3072]{3,2,1,0:T(8,128)(2,1)}, f32[832,768]{1,0:T(8,128)}, f32[1,3072]{1,0:T(1,128)}, f32[1...) custom-call(s32[1]{0:T(128)} %bitcast.37.refs_0_, f32[832,768]{1,0:T(8,128)} %get-tuple-element.142.refs_1_, ...), custom_call_target="tpu_custom_call" | custom-call | flops 19629342720 | bytes 35000000 | tf_op jit(solution)/shard_map/dense_bwd/pallas_call | solution.py:104
  422.9 2.5 ring_add.10
  428.8 2.9 place.2.refs_3_.refs_8_
  433.6 2.8 ring_add.11
  438.4 12.4 %attn_core.6 = (bf16[416,2304]{1,0:T(8,128)(2,1)}, bf16[416,768]{1,0:T(8,128)(2,1)}) custom-call(f32[832,768]{1,0:T(8,128)} %get-tuple-element.145.refs_0_.refs_1_.refs_2_, bf16[16,2,48,6144]{3,2,1,0:T(8,128)(2,1)} %bitcast.144, bf16[832,2304]{1,0:T(8,128)(2,1)} %get-tuple-element.146.refs_2_, f32[4,16,208]{2,1,0:T(8,128)} %get-tuple-element.147.refs_3_, ...), custom_call_target="tpu_custom_call" | custom-call | flops 5807013888 | bytes 8000000 | tf_op jit(solution)/shard_map/attn_core/pallas_call | solution.py:104
  452.2 8.2 %collective-permute-done.15.refs_12_ = bf16[48,3072]{1,0:T(8,128)(2,1)S(1)} collective-permute-done((bf16[48,3072]{1,0:T(8,128)(2,1)}, bf16[48,3072]{1,0:T(8,128)(2,1)S(1)}, u32[]{:S(2)}, u32[]{:S(2)}) %collective-permute-start.15) | collective-permute-done | bytes 294944 | tf_op jit(solution)/shard_map/ppermute | solution.py:950
  461.2 4.3 ring_add.12
  470.2 12.2 %attn_core.7 = (bf16[416,2304]{1,0:T(8,128)(2,1)}, bf16[416,768]{1,0:T(8,128)(2,1)}) custom-call(f32[832,768]{1,0:T(8,128)} %get-tuple-element.145.refs_0_.refs_1_.refs_2_, bf16[16,2,48,6144]{3,2,1,0:T(8,128)(2,1)} %bitcast.145, bf16[832,2304]{1,0:T(8,128)(2,1)} %get-tuple-element.146.refs_2_, f32[4,16,208]{2,1,0:T(8,128)} %get-tuple-element.147.refs_3_, ...), custom_call_target="tpu_custom_call" | custom-call | flops 5807013888 | bytes 8000000 | tf_op jit(solution)/shard_map/attn_core/pallas_call | solution.py:104
  482.4 18.0 %collective-permute-done.16.refs_5_ = bf16[2,48,1536]{2,1,0:T(8,128)(2,1)S(1)} collective-permute-done((bf16[2,48,1536]{2,1,0:T(8,128)(2,1)}, bf16[2,48,1536]{2,1,0:T(8,128)(2,1)S(1)}, u32[]{:S(2)}, u32[]{:S(2)}) %collective-permute-start.16) | collective-permute-done | bytes 294944 | tf_op jit(solution)/shard_map/ppermute | solution.py:950
  503.4 4.6 ring_add.13
  512.1 18.8 %attn_grad.3 = (bf16[16,2,48,1536]{3,2,1,0:T(8,128)(2,1)}, bf16[832,768]{1,0:T(8,128)(2,1)}, f32[1,2304]{1,0:T(1,128)}, f32[1,768]{1,0:T(1,128)}, f32[1,768]{1,0:T(1,128)}, /*index=5*/f32[1,768]{1,0:T(1,128)}) custom-call(s32[1]{0:T(128)} %bitcast.37.refs_0_, f32[832,768]{1,0:T(8,128)} %get-tuple-element.145.refs_0_.refs_1_.refs_2_, ...), custom_call_target="tpu_custom_call" | custom-call | flops 6870269952 | bytes 25000000 | tf_op jit(solution)/shard_map/attn_grad/pallas_call | solution.py:104
  532.0 4.6 ring_add.14
  545.9 3.0 expert_out.1
  548.9 9.4 %collective-permute-done.25.refs_3_ = bf16[2,48,1536]{2,1,0:T(8,128)(2,1)S(1)} collective-permute-done((bf16[2,48,1536]{2,1,0:T(8,128)(2,1)S(1)}, bf16[2,48,1536]{2,1,0:T(8,128)(2,1)S(1)}, u32[]{:S(2)}, u32[]{:S(2)}) %collective-permute-start.25) | collective-permute-done | bytes 294944 | tf_op jit(solution)/shard_map/ppermute | solution.py:950
  560.4 4.2 ring_add.15
  569.2 3.3 collective-permute-done.30.refs_2_
  573.2 2.3 ring_add.16.refs_1_.refs_3_
  576.3 5.9 collective-permute-done.31.refs_2_
  582.9 2.3 ring_add.17.refs_3_.refs_1_
  585.2 2.1 collective-permute-start.32
  587.3 2.4 copy.120
  589.7 4.0 place.3.refs_3_
  593.7 6.5 %copy.121 = f32[2,4,197,768]{3,1,2,0:T(4,128)} copy(f32[2,4,197,768]{3,2,1,0:T(8,128)} %place.3.refs_3_) | data formatting | bytes 9682944
  600.9 2.3 ring_add.18.refs_1_.refs_3_
  605.8 2.8 collective-permute-done.33.refs_2_
  609.2 2.3 ring_add.19
  615.7 4.3 reduce-scatter.5.cloned.1.call-done
  (291 shorter events, 97.6 us)
Async XLA Ops:
  7.2 119.6 %all-gather.6.cloned.1.call-start = ((), (), s32[]{:S(2)}) async-start(), calls=%async_computation.5 | async-start | bytes 20054016 | tf_op jit(solution)/shard_map/all_gather | solution.py:1171
  8.7 16.4 %collective-permute-start = (bf16[48,6144]{1,0:T(8,128)(2,1)S(1)}, bf16[48,6144]{1,0:T(8,128)(2,1)S(1)}, u32[]{:S(2)}, u32[]{:S(2)}) collective-permute-start(bf16[48,6144]{1,0:T(8,128)(2,1)S(1)} %constant_dynamic-update-slice_fusion), channel_id=1, source_target_pairs={{0,1},{1,0},{2,3},{3,2},{4,5},{5,4},{6,7},{7,6},{8,9},{9,8},{10,11... | collective-permute-start | bytes 1769480 | tf_op jit(solution)/shard_map/ppermute | solution.py:850
  26.3 201.7 %all-gather.4.cloned.1.call-start = ((), (), s32[]{:S(2)}) async-start(), calls=%async_computation.2 | async-start | bytes 20054016 | tf_op jit(solution)/shard_map/all_gather | solution.py:859
  28.6 508.1 %reduce-scatter.3.cloned.1.call-start = ((), (), s32[]{:S(2)}) async-start(), calls=%async_computation.3 | async-start | bytes 20054016 | tf_op jit(solution)/shard_map/reduce_scatter | solution.py:990
  28.7 22.4 %collective-permute-start.1 = (f32[3072]{0:T(1024)S(1)}, f32[3072]{0:T(1024)S(1)}, u32[]{:S(2)}, u32[]{:S(2)}) collective-permute-start(f32[3072]{0:T(1024)S(1)} %constant_dynamic-update-slice_fusion.5), channel_id=1, source_target_pairs={{0,1},{1,0},{2,3},{3,2},{4,5},{5,4},{6,7},{7,6},{8,9},{9,8},{10,11... | collective-permute-start | bytes 36872 | tf_op jit(solution)/shard_map/ppermute | solution.py:850
  171.6 15.5 %copy-start.30 = (f32[416,128]{1,0:T(8,128)S(1)}, f32[416,128]{1,0:T(8,128)}, u32[]{:S(2)}) copy-start(f32[416,128]{1,0:T(8,128)} %get-tuple-element.111) | copy-start | bytes 638980
  171.6 56.4 %collective-permute-start.2 = (bf16[416,768]{1,0:T(8,128)(2,1)}, bf16[416,768]{1,0:T(8,128)(2,1)S(1)}, u32[]{:S(2)}, u32[]{:S(2)}) collective-permute-start(bf16[416,768]{1,0:T(8,128)(2,1)} %get-tuple-element.109.refs_0_), channel_id=1, source_target_pairs={{0,1},{1,0},{2,3},{3,2},{4,5},{5,4},{6,7},{7,6},{8,9},{9,8},{10,11... | collective-permute-start | bytes 1916936 | tf_op jit(solution)/shard_map/ppermute | solution.py:850
  185.5 42.5 %collective-permute-start.3 = (bf16[416,768]{1,0:T(8,128)(2,1)}, bf16[416,768]{1,0:T(8,128)(2,1)S(1)}, u32[]{:S(2)}, u32[]{:S(2)}) collective-permute-start(bf16[416,768]{1,0:T(8,128)(2,1)} %get-tuple-element.110.refs_1_), channel_id=1, source_target_pairs={{0,1},{1,0},{2,3},{3,2},{4,5},{5,4},{6,7},{7,6},{8,9},{9,8},{10,11... | collective-permute-start | bytes 1916936 | tf_op jit(solution)/shard_map/ppermute | solution.py:850
  187.3 15.1 %collective-permute-start.4 = (f32[2,2,416]{2,1,0:T(2,128)S(1)}, f32[2,2,416]{2,1,0:T(2,128)S(1)}, u32[]{:S(2)}, u32[]{:S(2)}) collective-permute-start(f32[2,2,416]{2,1,0:T(2,128)S(1)} %pad_maximum_fusion.8), channel_id=1, source_target_pairs={{0,1},{1,0},{2,3},{3,2},{4,5},{5,4},{6,7},{7,6},{8,9},{9,8},{10,11... | collective-permute-start | bytes 19976 | tf_op jit(solution)/shard_map/ppermute | solution.py:850
  188.8 8.1 %copy-start.50 = (f32[4,768]{1,0:T(4,128)S(1)}, f32[4,768]{1,0:T(4,128)}, u32[]{:S(2)}) copy-start(f32[4,768]{1,0:T(4,128)} %param.32) | copy-start | bytes 36868
  284.8 335.2 %reduce-scatter.5.cloned.1.call-start = ((), (), s32[]{:S(2)}) async-start(), calls=%async_computation.4 | async-start | bytes 5013504 | tf_op jit(solution)/shard_map/reduce_scatter | solution.py:990
  291.9 18.4 %collective-permute-start.5 = (bf16[416,768]{1,0:T(8,128)(2,1)}, bf16[416,768]{1,0:T(8,128)(2,1)S(1)}, u32[]{:S(2)}, u32[]{:S(2)}) collective-permute-start(bf16[416,768]{1,0:T(8,128)(2,1)} %get-tuple-element.116.refs_5_), channel_id=1, source_target_pairs={{0,1},{1,0},{2,3},{3,2},{4,5},{5,4},{6,7},{7,6},{8,9},{9,8},{10,11... | collective-permute-start | bytes 1916936 | tf_op jit(solution)/shard_map/ppermute | solution.py:850
  293.4 16.9 %collective-permute-start.6 = (f32[2,8,416]{2,1,0:T(8,128)}, f32[2,8,416]{2,1,0:T(8,128)S(1)}, u32[]{:S(2)}, u32[]{:S(2)}) collective-permute-start(f32[2,8,416]{2,1,0:T(8,128)} %get-tuple-element.122), channel_id=1, source_target_pairs={{0,1},{1,0},{2,3},{3,2},{4,5},{5,4},{6,7},{7,6},{8,9},{9,8},{10,11... | collective-permute-start | bytes 79880 | tf_op jit(solution)/shard_map/ppermute | solution.py:850
  318.6 16.5 %collective-permute-start.7 = (bf16[416,768]{1,0:T(8,128)(2,1)}, bf16[416,768]{1,0:T(8,128)(2,1)S(1)}, u32[]{:S(2)}, u32[]{:S(2)}) collective-permute-start(bf16[416,768]{1,0:T(8,128)(2,1)} %get-tuple-element.124.refs_4_), channel_id=1, source_target_pairs={{0,1},{1,0},{2,3},{3,2},{4,5},{5,4},{6,7},{7,6},{8,9},{9,8},{10,11... | collective-permute-start | bytes 1916936 | tf_op jit(solution)/shard_map/ppermute | solution.py:850
  343.1 34.6 %collective-permute-start.8 = (bf16[2,416,768]{2,1,0:T(8,128)(2,1)}, bf16[2,416,768]{2,1,0:T(8,128)(2,1)}, u32[]{:S(2)}, u32[]{:S(2)}) collective-permute-start(bf16[2,416,768]{2,1,0:T(8,128)(2,1)} %get-tuple-element.130.refs_4_), channel_id=1, source_target_pairs={{0,1},{1,0},{2,3},{3,2},{4,5},{5,4},{6,7},{7,6},{8,9},{9,8},{10,11... | collective-permute-start | bytes 3833864 | tf_op jit(solution)/shard_map/ppermute | solution.py:850
  376.9 44.1 %collective-permute-start.10 = (bf16[8,2,48,1536]{3,2,1,0:T(8,128)(2,1)}, bf16[8,2,48,1536]{3,2,1,0:T(8,128)(2,1)S(1)}, u32[]{:S(2)}, u32[]{:S(2)}) collective-permute-start(bf16[8,2,48,1536]{3,2,1,0:T(8,128)(2,1)} %get-tuple-element.141.refs_8_), channel_id=1, source_target_pairs={{0,2},{2,0},{4,6},{6,4},{8,10},{10,8},{12,14},{14,12},{16,18},{18,... | collective-permute-start | bytes 7077896 | tf_op jit(solution)/shard_map/ppermute | solution.py:940
  381.7 39.4 %collective-permute-start.9 = (bf16[2,416,768]{2,1,0:T(8,128)(2,1)}, bf16[2,416,768]{2,1,0:T(8,128)(2,1)S(1)}, u32[]{:S(2)}, u32[]{:S(2)}) collective-permute-start(bf16[2,416,768]{2,1,0:T(8,128)(2,1)} %layer_output.1.refs_9_), channel_id=1, source_target_pairs={{0,1},{1,0},{2,3},{3,2},{4,5},{5,4},{6,7},{7,6},{8,9},{9,8},{10,11... | collective-permute-start | bytes 3833864 | tf_op jit(solution)/shard_map/ppermute | solution.py:850
  425.3 8.3 %collective-permute-start.11 = (bf16[8,2,48,3072]{3,2,1,0:T(8,128)(2,1)}, bf16[8,2,48,3072]{3,2,1,0:T(8,128)(2,1)}, u32[]{:S(2)}, u32[]{:S(2)}) collective-permute-start(bf16[8,2,48,3072]{3,2,1,0:T(8,128)(2,1)} %hold.2), channel_id=1, source_target_pairs={{0,2},{2,0},{4,6},{6,4},{8,10},{10,8},{12,14},{14,12},{16,18},{18,... | collective-permute-start | bytes 14155784 | tf_op jit(solution)/shard_map/ppermute | solution.py:940
  426.8 24.0 %collective-permute-start.12 = (bf16[48,1536]{1,0:T(8,128)(2,1)S(1)}, bf16[48,1536]{1,0:T(8,128)(2,1)S(1)}, u32[]{:S(2)}, u32[]{:S(2)}) collective-permute-start(bf16[48,1536]{1,0:T(8,128)(2,1)S(1)} %copy-done.10), channel_id=1, source_target_pairs={{0,8},{2,10},{8,16},{10,18},{16,24},{18,26},{24,28},{26,30},{28,20... | collective-permute-start | bytes 442376 | tf_op jit(solution)/shard_map/ppermute | solution.py:950
  428.2 22.6 %collective-permute-start.13 = (bf16[48,1536]{1,0:T(8,128)(2,1)S(1)}, bf16[48,1536]{1,0:T(8,128)(2,1)S(1)}, u32[]{:S(2)}, u32[]{:S(2)}) collective-permute-start(bf16[48,1536]{1,0:T(8,128)(2,1)S(1)} %copy-done.33), channel_id=1, source_target_pairs={{0,4},{2,6},{8,0},{10,2},{16,8},{18,10},{24,16},{26,18},{28,24},{3... | collective-permute-start | bytes 442376 | tf_op jit(solution)/shard_map/ppermute | solution.py:950
  436.4 15.8 %collective-permute-start.14 = (bf16[48,3072]{1,0:T(8,128)(2,1)}, bf16[48,3072]{1,0:T(8,128)(2,1)S(1)}, u32[]{:S(2)}, u32[]{:S(2)}) collective-permute-start(bf16[48,3072]{1,0:T(8,128)(2,1)} %get-tuple-element.151.refs_6_), channel_id=1, source_target_pairs={{0,8},{2,10},{8,16},{10,18},{16,24},{18,26},{24,28},{26,30},{28,20... | collective-permute-start | bytes 884744 | tf_op jit(solution)/shard_map/ppermute | solution.py:950
  438.0 22.5 %collective-permute-start.15 = (bf16[48,3072]{1,0:T(8,128)(2,1)}, bf16[48,3072]{1,0:T(8,128)(2,1)S(1)}, u32[]{:S(2)}, u32[]{:S(2)}) collective-permute-start(bf16[48,3072]{1,0:T(8,128)(2,1)} %get-tuple-element.152.refs_7_), channel_id=1, source_target_pairs={{0,4},{2,6},{8,0},{10,2},{16,8},{18,10},{24,16},{26,18},{28,24},{3... | collective-permute-start | bytes 884744 | tf_op jit(solution)/shard_map/ppermute | solution.py:950
  450.9 9.6 %copy-start.31 = (bf16[48,1536]{1,0:T(8,128)(2,1)}, bf16[48,1536]{1,0:T(8,128)(2,1)S(1)}, u32[]{:S(2)}) copy-start(bf16[48,1536]{1,0:T(8,128)(2,1)S(1)} %collective-permute-done.12.refs_5_) | copy-start | bytes 442372
  450.9 9.6 %copy-start.32 = (bf16[48,1536]{1,0:T(8,128)(2,1)}, bf16[48,1536]{1,0:T(8,128)(2,1)S(1)}, u32[]{:S(2)}) copy-start(bf16[48,1536]{1,0:T(8,128)(2,1)S(1)} %collective-permute-done.13.refs_6_) | copy-start | bytes 442372
  452.2 8.2 %copy-start.23 = (bf16[48,3072]{1,0:T(8,128)(2,1)}, bf16[48,3072]{1,0:T(8,128)(2,1)S(1)}, u32[]{:S(2)}) copy-start(bf16[48,3072]{1,0:T(8,128)(2,1)S(1)} %collective-permute-done.14.refs_11_) | copy-start | bytes 884740
  465.5 36.8 %collective-permute-start.18 = (bf16[2,48,3072]{2,1,0:T(8,128)(2,1)}, bf16[2,48,3072]{2,1,0:T(8,128)(2,1)S(1)}, u32[]{:S(2)}, u32[]{:S(2)}) collective-permute-start(bf16[2,48,3072]{2,1,0:T(8,128)(2,1)} %get-tuple-element.157.refs_6_), channel_id=1, source_target_pairs={{0,8},{2,10},{8,16},{10,18},{16,24},{18,26},{24,28},{26,30},{28,20... | collective-permute-start | bytes 1769480 | tf_op jit(solution)/shard_map/ppermute | solution.py:950
  465.8 36.5 %collective-permute-start.19 = (bf16[2,48,3072]{2,1,0:T(8,128)(2,1)}, bf16[2,48,3072]{2,1,0:T(8,128)(2,1)S(1)}, u32[]{:S(2)}, u32[]{:S(2)}) collective-permute-start(bf16[2,48,3072]{2,1,0:T(8,128)(2,1)} %get-tuple-element.158.refs_7_), channel_id=1, source_target_pairs={{0,4},{2,6},{8,0},{10,2},{16,8},{18,10},{24,16},{26,18},{28,24},{3... | collective-permute-start | bytes 1769480 | tf_op jit(solution)/shard_map/ppermute | solution.py:950
  468.1 32.2 %collective-permute-start.16 = (bf16[2,48,1536]{2,1,0:T(8,128)(2,1)}, bf16[2,48,1536]{2,1,0:T(8,128)(2,1)S(1)}, u32[]{:S(2)}, u32[]{:S(2)}) collective-permute-start(bf16[2,48,1536]{2,1,0:T(8,128)(2,1)} %get-tuple-element.155.refs_4_), channel_id=1, source_target_pairs={{0,8},{2,10},{8,16},{10,18},{16,24},{18,26},{24,28},{26,30},{28,20... | collective-permute-start | bytes 884744 | tf_op jit(solution)/shard_map/ppermute | solution.py:950
  468.4 33.9 %collective-permute-start.17 = (bf16[2,48,1536]{2,1,0:T(8,128)(2,1)}, bf16[2,48,1536]{2,1,0:T(8,128)(2,1)S(1)}, u32[]{:S(2)}, u32[]{:S(2)}) collective-permute-start(bf16[2,48,1536]{2,1,0:T(8,128)(2,1)} %get-tuple-element.156.refs_5_), channel_id=1, source_target_pairs={{0,4},{2,6},{8,0},{10,2},{16,8},{18,10},{24,16},{26,18},{28,24},{3... | collective-permute-start | bytes 884744 | tf_op jit(solution)/shard_map/ppermute | solution.py:950
  508.0 22.8 %collective-permute-start.21 = (bf16[2,48,1536]{2,1,0:T(8,128)(2,1)}, bf16[2,48,1536]{2,1,0:T(8,128)(2,1)S(1)}, u32[]{:S(2)}, u32[]{:S(2)}) collective-permute-start(bf16[2,48,1536]{2,1,0:T(8,128)(2,1)} %get-tuple-element.162.refs_13_), channel_id=1, source_target_pairs={{0,8},{2,10},{8,16},{10,18},{16,24},{18,26},{24,28},{26,30},{28,20... | collective-permute-start | bytes 884744 | tf_op jit(solution)/shard_map/ppermute | solution.py:950
  509.6 21.3 %collective-permute-start.22 = (bf16[2,48,1536]{2,1,0:T(8,128)(2,1)}, bf16[2,48,1536]{2,1,0:T(8,128)(2,1)S(1)}, u32[]{:S(2)}, u32[]{:S(2)}) collective-permute-start(bf16[2,48,1536]{2,1,0:T(8,128)(2,1)} %get-tuple-element.163.refs_14_), channel_id=1, source_target_pairs={{0,4},{2,6},{8,0},{10,2},{16,8},{18,10},{24,16},{26,18},{28,24},{3... | collective-permute-start | bytes 884744 | tf_op jit(solution)/shard_map/ppermute | solution.py:950
  510.0 20.8 %collective-permute-start.23 = (bf16[2,48,3072]{2,1,0:T(8,128)(2,1)}, bf16[2,48,3072]{2,1,0:T(8,128)(2,1)S(1)}, u32[]{:S(2)}, u32[]{:S(2)}) collective-permute-start(bf16[2,48,3072]{2,1,0:T(8,128)(2,1)} %get-tuple-element.164.refs_15_), channel_id=1, source_target_pairs={{0,8},{2,10},{8,16},{10,18},{16,24},{18,26},{24,28},{26,30},{28,20... | collective-permute-start | bytes 1769480 | tf_op jit(solution)/shard_map/ppermute | solution.py:950
  511.6 19.3 %collective-permute-start.24 = (bf16[2,48,3072]{2,1,0:T(8,128)(2,1)}, bf16[2,48,3072]{2,1,0:T(8,128)(2,1)S(1)}, u32[]{:S(2)}, u32[]{:S(2)}) collective-permute-start(bf16[2,48,3072]{2,1,0:T(8,128)(2,1)} %get-tuple-element.165.refs_16_), channel_id=1, source_target_pairs={{0,4},{2,6},{8,0},{10,2},{16,8},{18,10},{24,16},{26,18},{28,24},{3... | collective-permute-start | bytes 1769480 | tf_op jit(solution)/shard_map/ppermute | solution.py:950
  536.7 53.0 %collective-permute-start.20 = (bf16[832,768]{1,0:T(8,128)(2,1)}, bf16[832,768]{1,0:T(8,128)(2,1)}, u32[]{:S(2)}, u32[]{:S(2)}) collective-permute-start(bf16[832,768]{1,0:T(8,128)(2,1)} %get-tuple-element.166), channel_id=1, source_target_pairs={{0,1},{1,0},{2,3},{3,2},{4,5},{5,4},{6,7},{7,6},{8,9},{9,8},{10,11... | collective-permute-start | bytes 3833864 | tf_op jit(solution)/shard_map/ppermute | solution.py:850
  538.2 21.1 %collective-permute-start.27 = (bf16[2,48,3072]{2,1,0:T(8,128)(2,1)S(1)}, bf16[2,48,3072]{2,1,0:T(8,128)(2,1)S(1)}, u32[]{:S(2)}, u32[]{:S(2)}) collective-permute-start(bf16[2,48,3072]{2,1,0:T(8,128)(2,1)S(1)} %copy-done.57), channel_id=1, source_target_pairs={{0,8},{2,10},{8,16},{10,18},{16,24},{18,26},{24,28},{26,30},{28,20... | collective-permute-start | bytes 1769480 | tf_op jit(solution)/shard_map/ppermute | solution.py:950
  539.8 19.5 %collective-permute-start.28 = (bf16[2,48,3072]{2,1,0:T(8,128)(2,1)S(1)}, bf16[2,48,3072]{2,1,0:T(8,128)(2,1)S(1)}, u32[]{:S(2)}, u32[]{:S(2)}) collective-permute-start(bf16[2,48,3072]{2,1,0:T(8,128)(2,1)S(1)} %copy-done.56), channel_id=1, source_target_pairs={{0,4},{2,6},{8,0},{10,2},{16,8},{18,10},{24,16},{26,18},{28,24},{3... | collective-permute-start | bytes 1769480 | tf_op jit(solution)/shard_map/ppermute | solution.py:950
  542.2 1.7 collective-permute-start.29
  542.2 16.1 %collective-permute-start.25 = (bf16[2,48,1536]{2,1,0:T(8,128)(2,1)S(1)}, bf16[2,48,1536]{2,1,0:T(8,128)(2,1)S(1)}, u32[]{:S(2)}, u32[]{:S(2)}) collective-permute-start(bf16[2,48,1536]{2,1,0:T(8,128)(2,1)S(1)} %copy-done.11), channel_id=1, source_target_pairs={{0,8},{2,10},{8,16},{10,18},{16,24},{18,26},{24,28},{26,30},{28,20... | collective-permute-start | bytes 884744 | tf_op jit(solution)/shard_map/ppermute | solution.py:950
  543.8 15.5 %copy-start.34 = (f32[48,768]{1,0:T(8,128)}, f32[48,768]{1,0:T(8,128)S(1)}, u32[]{:S(2)}) copy-start(f32[48,768]{1,0:T(8,128)S(1)} %collective-permute-done.29.refs_10_) | copy-start | bytes 442372
  543.8 15.4 %collective-permute-start.26 = (bf16[2,48,1536]{2,1,0:T(8,128)(2,1)}, bf16[2,48,1536]{2,1,0:T(8,128)(2,1)S(1)}, u32[]{:S(2)}, u32[]{:S(2)}) collective-permute-start(bf16[2,48,1536]{2,1,0:T(8,128)(2,1)} %get-tuple-element.169), channel_id=1, source_target_pairs={{0,4},{2,6},{8,0},{10,2},{16,8},{18,10},{24,16},{26,18},{28,24},{3... | collective-permute-start | bytes 884744 | tf_op jit(solution)/shard_map/ppermute | solution.py:950
  545.3 19.3 %copy-start.47 = (s32[2]{0:T(128)}, s32[2]{0:T(128)S(1)}, u32[]{:S(2)}) copy-start(s32[2]{0:T(128)S(1)} %broadcast_2_refs_0_.2.refs_0_) | copy-start | bytes 28
  564.6 7.9 %collective-permute-start.30 = (f32[48,768]{1,0:T(8,128)}, f32[48,768]{1,0:T(8,128)S(1)}, u32[]{:S(2)}, u32[]{:S(2)}) collective-permute-start(f32[48,768]{1,0:T(8,128)} %get-tuple-element.191.refs_1_), channel_id=1, source_target_pairs={{0,4},{2,6},{4,0},{6,2},{8,12},{10,14},{12,8},{14,10},{16,20},{18,... | collective-permute-start | bytes 442376 | tf_op jit(solution)/shard_map/ppermute | solution.py:1035
  567.9 19.4 %copy-start.1 = (bf16[2,4,197,768]{3,2,1,0:T(8,128)(2,1)S(1)}, bf16[2,4,197,768]{3,2,1,0:T(8,128)(2,1)}, u32[]{:S(2)}) copy-start(bf16[2,4,197,768]{3,2,1,0:T(8,128)(2,1)} %place.2.refs_3_.refs_8_) | copy-start | bytes 7262212
  567.9 36.7 %collective-permute-start.35 = (bf16[3,48,1536]{2,1,0:T(8,128)(2,1)S(1)}, bf16[3,48,1536]{2,1,0:T(8,128)(2,1)S(1)}, u32[]{:S(2)}, u32[]{:S(2)}) collective-permute-start(bf16[3,48,1536]{2,1,0:T(8,128)(2,1)S(1)} %fusion.5), channel_id=1, source_target_pairs={{0,1},{1,0},{2,3},{3,2},{4,5},{5,4},{6,7},{7,6},{8,9},{9,8},{10,11... | collective-permute-start | bytes 1327112 | tf_op jit(solution)/shard_map/ppermute | solution.py:850
  575.5 6.7 %collective-permute-start.31 = (f32[48,768]{1,0:T(8,128)}, f32[48,768]{1,0:T(8,128)S(1)}, u32[]{:S(2)}, u32[]{:S(2)}) collective-permute-start(f32[48,768]{1,0:T(8,128)} %ring_add.16.refs_1_.refs_3_), channel_id=1, source_target_pairs={{0,8},{2,10},{4,12},{6,14},{8,0},{10,2},{12,4},{14,6},{16,24},{18,... | collective-permute-start | bytes 442376 | tf_op jit(solution)/shard_map/ppermute | solution.py:1035
  585.2 15.0 %collective-permute-start.32 = (f32[48,768]{1,0:T(8,128)}, f32[48,768]{1,0:T(8,128)S(1)}, u32[]{:S(2)}, u32[]{:S(2)}) collective-permute-start(f32[48,768]{1,0:T(8,128)} %ring_add.17.refs_3_.refs_1_), channel_id=1, source_target_pairs={{0,16},{2,18},{4,20},{6,22},{8,24},{10,26},{12,28},{14,30},{16,0},... | collective-permute-start | bytes 442376 | tf_op jit(solution)/shard_map/ppermute | solution.py:1035
  603.2 5.4 collective-permute-start.33
  621.0 6.0 collective-permute-start.34
  (50 other events, 87.5 us)
Sparse Core Ops, SparseCore 0:
  26.4 100.4 all-gather.5
  129.0 98.9 all-gather.3
  284.9 212.8 reduce-scatter.2
  536.8 83.0 reduce-scatter.4

commit v6 on v5

--- a/solution.py
+++ b/solution.py
@@ -810,10 +810,8 @@
         logit_grad, normed, (((0,), (0,)), ((), ())), precision=EXACT, preferred_element_type=F32
     )
     normed_grad = ro_ref[0].astype(F32) + rr_ref[...].astype(F32)
-    normed_grad += lax.dot_general(
-        logit_grad, rt_ref[...], (((1,), (1,)), ((), ())), precision=EXACT,
-        preferred_element_type=F32,
-    )
+    for expert in range(rt_ref.shape[0]):
+        normed_grad += logit_grad[:, expert : expert + 1] * rt_ref[expert : expert + 1, :]
     hidden_grad, gain_grad, shift_grad = norm_pull(unit, scale, g_ref[...], normed_grad)
     da_ref[...] = incoming + hidden_grad
     dg_ref[...] = gain_grad
@@ -832,7 +830,7 @@
         gate_bwd_kernel, (1,),
         [
             flat, one, whole(held.shape), one, flat, dots, dots, low,
-            whole((width, lanes)), whole((1, width)), whole((1, width)),
+            whole(router.shape), whole((1, width)), whole((1, width)),
         ],
         [whole(held.shape), flat, whole((lanes, width)), whole((1, width)), whole((1, width))],
         [
@@ -1276,7 +1274,7 @@
     for m, held in enumerate((r_oth1, y_oth)):
         sent, grad_part, *small = gate_back(
             after_two[m], grad_own, held, r_own, r_got, d_own, d_got, gates[m],
-            router_wide, row(norm_gain[1, 1]), row(row_bias[1, 1]), m,
+            router.T, row(norm_gain[1, 1]), row(row_bias[1, 1]), m,
             (cores[0][1],) if m else (),
         )
         r_got = swap(sent)

time: 642 us -> 641 us (level)
  transfers between devices with their start and end apart: 40 -> 40, of which waited for: 16 -> 17; matrix products, arithmetic and copies ran while one was open for 8% -> 8% of each run, Pallas kernels for 44% -> 44%
where the time goes in v6:
time: 641 us; the launch traced here: 635 us
  Pallas kernels  331 us (52%)
  waiting for transfers between devices  180 us (28%)
  local copies, waits for them, and re-layouts  58.8 us (9%)
  starting transfers between devices  39 us (6%)
  between operations  15.4 us (2%)
  other arithmetic  9.86 us (2%)
    pallas_call x34, Pallas kernels, call(): return lambda *args: made(*args, *after)  331 us
    all_gather x1, waiting for transfers between devices, local(): lax.all_gather(in_order(first_mine, swap(first_mine), 0), 'dp', axis=0, t...  73.9 us
    ppermute x16, waiting for transfers between devices, send(): return lax.ppermute(value, 'dp', pairs)  43 us
    unnamed x140, local copies, waits for them, and re-layouts  29.1 us
    all_gather x1, waiting for transfers between devices, gather_rows(): return lax.all_gather(share, 'dp', axis=0, tiled=True)  25 us
    ppermute x14, waiting for transfers between devices, swap(): return lax.ppermute(value, 'tensor', [(0, 1), (1, 0)])  23.5 us
    ppermute x14, starting transfers between devices, swap(): return lax.ppermute(value, 'tensor', [(0, 1), (1, 0)])  19.8 us
    ppermute x16, starting transfers between devices, send(): return lax.ppermute(value, 'dp', pairs)  16.3 us
  transfers between devices with their start and end apart: 40, of which 17 were waited for; matrix products, arithmetic and copies ran while one was open for 8% of the time, Pallas kernels for 44%

profile of v6, /device:TPU:0, one launch (start us, length us, event | category | flops | bytes accessed | tf_op | source)
XLA Modules:
  0.0 634.6 jit_solution(9936855935317294949)
XLA Ops:
  8.7 3.0 collective-permute-start
  11.7 13.3 %collective-permute-done = bf16[48,6144]{1,0:T(8,128)(2,1)S(1)} collective-permute-done((bf16[48,6144]{1,0:T(8,128)(2,1)S(1)}, bf16[48,6144]{1,0:T(8,128)(2,1)S(1)}, u32[]{:S(2)}, u32[]{:S(2)}) %collective-permute-start) | collective-permute-done | bytes 589856 | tf_op jit(solution)/shard_map/ppermute | solution.py:848
  30.5 6.9 %constant_dynamic-slice_fusion.1 = (bf16[2,2,197,768]{3,1,2,0:T(2,128)(2,1)S(1)}, bf16[2,2,197,768]{3,1,2,0:T(2,128)(2,1)S(1)}, bf16[2,2,197,768]{3,1,2,0:T(2,128)(2,1)S(1)}) fusion(bf16[2,4,197,768]{3,1,2,0:T(4,128)(2,1)} %param.35, s32[]{:T(128)S(6)} %select_n.192, s32[]{:T(128)S(6)} %select_n.183, bf16[2,4,197,768]{3,1,2,0:T(4,128)(2,1)} %param.18), kind=kLoop, calls=%fused_computation.61 | loop fusion | bytes 7262216 | tf_op jit(solution)/shard_map/dynamic_slice | solution.py:1192
  53.0 73.9 %all-gather.6.cloned.1.call-done = bf16[32,48,6144]{2,1,0:T(8,128)(2,1)} async-done(((bf16[2,48,6144]{2,1,0:T(8,128)(2,1)}), bf16[32,48,6144]{2,1,0:T(8,128)(2,1)}) %all-gather.6.cloned.1.call-update) | async-done | bytes 18874384 | tf_op jit(solution)/shard_map/all_gather | solution.py:1169
  126.8 16.4 %attn_fwd.3 = (bf16[832,2304]{1,0:T(8,128)(2,1)}, f32[4,16,208]{2,1,0:T(8,128)}, bf16[832,768]{1,0:T(8,128)(2,1)}, f32[832,768]{1,0:T(8,128)}) custom-call(f32[832,768]{1,0:T(8,128)} %bitcast_convert_fusion.refs_0_.refs_3_, f32[1,768]{1,0:T(1,128)} %get-tuple-element.294.refs_1_.refs_4_, f32[1,768]{1,0:T(1,128)} %get-tuple-element.286.refs_2_.refs_5_, ...), custom_call_target="tpu_custom_call" | custom-call | flops 6052380672 | bytes 12000000 | tf_op jit(solution)/shard_map/attn_fwd/pallas_call | solution.py:104
  143.2 15.8 %dense_fwd.1.refs_0_.refs_3_ = f32[832,768]{1,0:T(8,128)} custom-call(f32[832,768]{1,0:T(8,128)} %get-tuple-element.106.refs_0_.refs_2_, f32[1,768]{1,0:T(1,128)} %get-tuple-element.293.refs_1_.refs_3_, f32[1,768]{1,0:T(1,128)} %get-tuple-element.284.refs_2_.refs_4_, bf16[16,2,48,6144]{3,2,1,0:T(8,128)(2,1)} %bitcast.136, ...), custom_call_target="tpu_custom_call" | custom-call | flops 7851737088 | bytes 15000000 | tf_op jit(solution)/shard_map/dense_fwd/pallas_call | solution.py:104
  159.0 12.6 %attn_fwd.4 = (bf16[416,2304]{1,0:T(8,128)(2,1)}, f32[2,16,208]{2,1,0:T(8,128)}, bf16[416,768]{1,0:T(8,128)(2,1)}, f32[416,768]{1,0:T(8,128)}, bf16[416,768]{1,0...) custom-call(f32[832,768]{1,0:T(8,128)} %dense_fwd.1.refs_0_.refs_3_, ...), custom_call_target="tpu_custom_call" | custom-call | flops 3026190336 | bytes 12000000 | tf_op jit(solution)/shard_map/attn_fwd/pallas_call | solution.py:104
  173.1 12.4 %attn_fwd.5 = (bf16[416,2304]{1,0:T(8,128)(2,1)}, f32[2,16,208]{2,1,0:T(8,128)}, bf16[416,768]{1,0:T(8,128)(2,1)}, f32[416,768]{1,0:T(8,128)}, bf16[416,768]{1,0...) custom-call(f32[832,768]{1,0:T(8,128)} %dense_fwd.1.refs_0_.refs_3_, ...), custom_call_target="tpu_custom_call" | custom-call | flops 3026190336 | bytes 12000000 | tf_op jit(solution)/shard_map/attn_fwd/pallas_call | solution.py:104
  188.8 7.4 %spread.1.refs_4_ = bf16[4,608,768]{2,1,0:T(8,128)(2,1)} custom-call(bf16[2,416,768]{2,1,0:T(8,128)(2,1)} %bitcast.148, bf16[2,416,768]{2,1,0:T(8,128)(2,1)} %bitcast.167, s32[2,2,416]{2,1,0:T(2,128)} %copy.113.refs_2_.refs_5_, s32[2,2,416]{2,1,0:T(2,128)} %copy.114.refs_3_.refs_6_), custom_call_target="tpu_custom_call" | custom-call | flops 3107979264 | bytes 9000000 | tf_op jit(solution)/shard_map/spread/pallas_call | solution.py:104
  197.5 4.9 collective-permute-done.4
  203.0 25.0 %all-gather.4.cloned.1.call-done.refs_8_.refs_9_ = bf16[768,12288]{1,0:T(8,128)(2,1)} async-done(((bf16[48,12288]{1,0:T(8,128)(2,1)}), bf16[768,12288]{1,0:T(8,128)(2,1)}) %all-gather.4.cloned.1.call-update) | async-done | bytes 18874384 | tf_op jit(solution)/shard_map/all_gather | solution.py:857
  229.7 55.1 %experts.1 = (bf16[4,608,768]{2,1,0:T(8,128)(2,1)}, bf16[4,608,768]{2,1,0:T(8,128)(2,1)}, bf16[4,608,128]{2,1,0:T(8,128)(2,1)}, bf16[16,2,48,6144]{3,2,1,0:T(8,1...) custom-call(bf16[416,768]{1,0:T(8,128)(2,1)} %get-tuple-element.109.refs_0_, ...), custom_call_target="tpu_custom_call" | custom-call | flops 37534826496 | bytes 60000000 | tf_op jit(solution)/shard_map/experts/pallas_call | solution.py:104
  285.0 6.9 %collect_first.1 = (bf16[416,768]{1,0:T(8,128)(2,1)}, bf16[416,768]{1,0:T(8,128)(2,1)}, f32[2,8,416]{2,1,0:T(8,128)}) custom-call(s32[2,416,2]{2,1,0:T(8,128)} %bitcast.165, bf16[4,608,128]{2,1,0:T(8,128)(2,1)} %get-tuple-element.113.refs_1_.refs_2_, bf16[4,608,768]{2,1,0:T(8,128)(2,1)} %get-tuple-element.114.refs_2_.refs_3_), custom_call_target="tpu_custom_call" | custom-call | flops 3107979264 | bytes 8000000 | tf_op jit(solution)/shard_map/collect_first/pallas_call | solution.py:104
  294.0 16.4 %collect_rest.1 = (bf16[2,416,768]{2,1,0:T(8,128)(2,1)}, bf16[2,416,768]{2,1,0:T(8,128)(2,1)}, bf16[2,416,768]{2,1,0:T(8,128)(2,1)}, f32[2,8,416]{2,1,0:T(8,128)}) custom-call(s32[2,416,2]{2,1,0:T(8,128)} %bitcast.163, s32[2,416,2]{2,1,0:T(8,128)} %bitcast.166, bf16[4,608,128]{2,1,0:T(8,128)(2,1)} %get-tuple-element.113.refs_1_.refs_2_, ...), custom_call_target="tpu_custom_call" | custom-call | flops 6215958528 | bytes 8000000 | tf_op jit(solution)/shard_map/collect_rest/pallas_call | solution.py:104
  311.2 6.6 %gate_bwd.2 = (bf16[416,768]{1,0:T(8,128)(2,1)}, f32[416,768]{1,0:T(8,128)}, f32[128,768]{1,0:T(8,128)}, f32[1,768]{1,0:T(1,128)}, f32[1,768]{1,0:T(1,128)}) custom-call(f32[416,768]{1,0:T(8,128)} %get-tuple-element.107.refs_0_, bf16[2,416,768]{2,1,0:T(8,128)(2,1)} %bitcast.149, bf16[416,768]{1,0:T(8,128)(2,1)} %get-tuple-element.120.refs_2_, ...), custom_call_target="tpu_custom_call" | custom-call | flops 163577856 | bytes 7000000 | tf_op jit(solution)/shard_map/gate_bwd/pallas_call | solution.py:104
  319.4 12.2 %attn_core.4 = (bf16[416,2304]{1,0:T(8,128)(2,1)}, bf16[416,768]{1,0:T(8,128)(2,1)}) custom-call(f32[416,768]{1,0:T(8,128)} %get-tuple-element.126.refs_0_.refs_1_, bf16[16,2,48,6144]{3,2,1,0:T(8,128)(2,1)} %bitcast.140, bf16[416,2304]{1,0:T(8,128)(2,1)} %get-tuple-element.127.refs_2_, f32[2,16,208]{2,1,0:T(8,128)} %get-tuple-element.128.refs_3_, ...), custom_call_target="tpu_custom_call" | custom-call | flops 5807013888 | bytes 8000000 | tf_op jit(solution)/shard_map/attn_core/pallas_call | solution.py:104
  331.6 2.6 collective-permute-done.7.refs_4_
  335.1 6.4 %gate_bwd.3 = (bf16[2,416,768]{2,1,0:T(8,128)(2,1)}, f32[416,768]{1,0:T(8,128)}, f32[128,768]{1,0:T(8,128)}, f32[1,768]{1,0:T(1,128)}, f32[1,768]{1,0:T(1,128)}) custom-call(f32[416,768]{1,0:T(8,128)} %get-tuple-element.108.refs_0_.refs_1_, bf16[2,416,768]{2,1,0:T(8,128)(2,1)} %bitcast.150, bf16[2,416,768]{2,1,0:T(8,128)(2,1)} %get-tuple-element.118.refs_2_, ...), custom_call_target="tpu_custom_call" | custom-call | flops 163577856 | bytes 7000000 | tf_op jit(solution)/shard_map/gate_bwd/pallas_call | solution.py:104
  343.0 12.3 %attn_core.5 = (bf16[416,2304]{1,0:T(8,128)(2,1)}, bf16[416,768]{1,0:T(8,128)(2,1)}) custom-call(f32[416,768]{1,0:T(8,128)} %get-tuple-element.131.refs_0_.refs_2_, bf16[16,2,48,6144]{3,2,1,0:T(8,128)(2,1)} %bitcast.141, bf16[416,2304]{1,0:T(8,128)(2,1)} %get-tuple-element.133.refs_2_, f32[2,16,208]{2,1,0:T(8,128)} %get-tuple-element.134.refs_3_, ...), custom_call_target="tpu_custom_call" | custom-call | flops 5807013888 | bytes 8000000 | tf_op jit(solution)/shard_map/attn_core/pallas_call | solution.py:104
  355.3 20.2 %attn_grad.2 = (bf16[8,2,48,1536]{3,2,1,0:T(8,128)(2,1)}, bf16[8,2,48,1536]{3,2,1,0:T(8,128)(2,1)}, f32[832,768]{1,0:T(8,128)}, f32[1,2304]{1,0:T(1,128)}, f32[1...) custom-call(s32[1]{0:T(128)} %bitcast.38.refs_0_, f32[416,768]{1,0:T(8,128)} %get-tuple-element.126.refs_0_.refs_1_, ...), custom_call_target="tpu_custom_call" | custom-call | flops 6870269952 | bytes 25000000 | tf_op jit(solution)/shard_map/attn_grad/pallas_call | solution.py:104
  376.3 4.0 layer_output.1.refs_9_
  380.8 38.9 %dense_bwd.1 = (bf16[8,2,48,3072]{3,2,1,0:T(8,128)(2,1)}, bf16[8,2,48,3072]{3,2,1,0:T(8,128)(2,1)}, f32[832,768]{1,0:T(8,128)}, f32[1,3072]{1,0:T(1,128)}, f32[1...) custom-call(s32[1]{0:T(128)} %bitcast.38.refs_0_, f32[832,768]{1,0:T(8,128)} %get-tuple-element.142.refs_1_, ...), custom_call_target="tpu_custom_call" | custom-call | flops 19629342720 | bytes 35000000 | tf_op jit(solution)/shard_map/dense_bwd/pallas_call | solution.py:104
  421.4 2.5 ring_add.10
  427.4 2.9 place.2.refs_3_.refs_8_
  432.2 2.8 ring_add.11
  437.0 12.6 %attn_core.6 = (bf16[416,2304]{1,0:T(8,128)(2,1)}, bf16[416,768]{1,0:T(8,128)(2,1)}) custom-call(f32[832,768]{1,0:T(8,128)} %get-tuple-element.145.refs_0_.refs_1_.refs_2_, bf16[16,2,48,6144]{3,2,1,0:T(8,128)(2,1)} %bitcast.145, bf16[832,2304]{1,0:T(8,128)(2,1)} %get-tuple-element.146.refs_2_, f32[4,16,208]{2,1,0:T(8,128)} %get-tuple-element.147.refs_3_, ...), custom_call_target="tpu_custom_call" | custom-call | flops 5807013888 | bytes 8000000 | tf_op jit(solution)/shard_map/attn_core/pallas_call | solution.py:104
  450.3 8.0 %collective-permute-done.15.refs_12_ = bf16[48,3072]{1,0:T(8,128)(2,1)S(1)} collective-permute-done((bf16[48,3072]{1,0:T(8,128)(2,1)}, bf16[48,3072]{1,0:T(8,128)(2,1)S(1)}, u32[]{:S(2)}, u32[]{:S(2)}) %collective-permute-start.15) | collective-permute-done | bytes 294944 | tf_op jit(solution)/shard_map/ppermute | solution.py:948
  459.0 4.3 ring_add.12
  467.9 12.2 %attn_core.7 = (bf16[416,2304]{1,0:T(8,128)(2,1)}, bf16[416,768]{1,0:T(8,128)(2,1)}) custom-call(f32[832,768]{1,0:T(8,128)} %get-tuple-element.145.refs_0_.refs_1_.refs_2_, bf16[16,2,48,6144]{3,2,1,0:T(8,128)(2,1)} %bitcast.146, bf16[832,2304]{1,0:T(8,128)(2,1)} %get-tuple-element.146.refs_2_, f32[4,16,208]{2,1,0:T(8,128)} %get-tuple-element.147.refs_3_, ...), custom_call_target="tpu_custom_call" | custom-call | flops 5807013888 | bytes 8000000 | tf_op jit(solution)/shard_map/attn_core/pallas_call | solution.py:104
  480.1 20.2 %collective-permute-done.16.refs_5_ = bf16[2,48,1536]{2,1,0:T(8,128)(2,1)S(1)} collective-permute-done((bf16[2,48,1536]{2,1,0:T(8,128)(2,1)}, bf16[2,48,1536]{2,1,0:T(8,128)(2,1)S(1)}, u32[]{:S(2)}, u32[]{:S(2)}) %collective-permute-start.16) | collective-permute-done | bytes 294944 | tf_op jit(solution)/shard_map/ppermute | solution.py:948
  503.3 4.6 ring_add.13
  512.0 18.8 %attn_grad.3 = (bf16[16,2,48,1536]{3,2,1,0:T(8,128)(2,1)}, bf16[832,768]{1,0:T(8,128)(2,1)}, f32[1,2304]{1,0:T(1,128)}, f32[1,768]{1,0:T(1,128)}, f32[1,768]{1,0:T(1,128)}, /*index=5*/f32[1,768]{1,0:T(1,128)}) custom-call(s32[1]{0:T(128)} %bitcast.38.refs_0_, f32[832,768]{1,0:T(8,128)} %get-tuple-element.145.refs_0_.refs_1_.refs_2_, ...), custom_call_target="tpu_custom_call" | custom-call | flops 6870269952 | bytes 25000000 | tf_op jit(solution)/shard_map/attn_grad/pallas_call | solution.py:104
  532.0 4.6 ring_add.14
  540.2 1.9 pack.1.refs_9_
  544.9 3.0 expert_out.1
  547.8 10.6 %collective-permute-done.25.refs_3_ = bf16[2,48,1536]{2,1,0:T(8,128)(2,1)S(1)} collective-permute-done((bf16[2,48,1536]{2,1,0:T(8,128)(2,1)S(1)}, bf16[2,48,1536]{2,1,0:T(8,128)(2,1)S(1)}, u32[]{:S(2)}, u32[]{:S(2)}) %collective-permute-start.25) | collective-permute-done | bytes 294944 | tf_op jit(solution)/shard_map/ppermute | solution.py:948
  560.9 4.2 ring_add.15
  569.2 4.2 collective-permute-done.30.refs_2_
  574.1 2.3 ring_add.16.refs_1_.refs_3_
  577.5 5.0 collective-permute-done.31.refs_2_
  583.1 2.3 ring_add.17.refs_3_.refs_1_
  586.4 2.4 copy.120
  588.8 4.0 place.3.refs_3_
  592.8 6.5 %copy.121 = f32[2,4,197,768]{3,1,2,0:T(4,128)} copy(f32[2,4,197,768]{3,2,1,0:T(8,128)} %place.3.refs_3_) | data formatting | bytes 9682944
  600.0 2.3 ring_add.18.refs_1_.refs_3_
  605.0 2.6 collective-permute-done.33.refs_2_
  608.3 2.3 ring_add.19
  614.7 4.0 reduce-scatter.5.cloned.1.call-done
  (291 shorter events, 95.1 us)
Async XLA Ops:
  7.2 119.6 %all-gather.6.cloned.1.call-start = ((), (), s32[]{:S(2)}) async-start(), calls=%async_computation.5 | async-start | bytes 20054016 | tf_op jit(solution)/shard_map/all_gather | solution.py:1169
  8.7 16.4 %collective-permute-start = (bf16[48,6144]{1,0:T(8,128)(2,1)S(1)}, bf16[48,6144]{1,0:T(8,128)(2,1)S(1)}, u32[]{:S(2)}, u32[]{:S(2)}) collective-permute-start(bf16[48,6144]{1,0:T(8,128)(2,1)S(1)} %constant_dynamic-update-slice_fusion), channel_id=1, source_target_pairs={{0,1},{1,0},{2,3},{3,2},{4,5},{5,4},{6,7},{7,6},{8,9},{9,8},{10,11... | collective-permute-start | bytes 1769480 | tf_op jit(solution)/shard_map/ppermute | solution.py:848
  26.3 201.7 %all-gather.4.cloned.1.call-start = ((), (), s32[]{:S(2)}) async-start(), calls=%async_computation.2 | async-start | bytes 20054016 | tf_op jit(solution)/shard_map/all_gather | solution.py:857
  28.6 508.1 %reduce-scatter.3.cloned.1.call-start = ((), (), s32[]{:S(2)}) async-start(), calls=%async_computation.3 | async-start | bytes 20054016 | tf_op jit(solution)/shard_map/reduce_scatter | solution.py:988
  28.7 22.4 %collective-permute-start.1 = (f32[3072]{0:T(1024)S(1)}, f32[3072]{0:T(1024)S(1)}, u32[]{:S(2)}, u32[]{:S(2)}) collective-permute-start(f32[3072]{0:T(1024)S(1)} %constant_dynamic-update-slice_fusion.5), channel_id=1, source_target_pairs={{0,1},{1,0},{2,3},{3,2},{4,5},{5,4},{6,7},{7,6},{8,9},{9,8},{10,11... | collective-permute-start | bytes 36872 | tf_op jit(solution)/shard_map/ppermute | solution.py:848
  171.6 15.5 %copy-start.30 = (f32[416,128]{1,0:T(8,128)S(1)}, f32[416,128]{1,0:T(8,128)}, u32[]{:S(2)}) copy-start(f32[416,128]{1,0:T(8,128)} %get-tuple-element.111) | copy-start | bytes 638980
  171.6 56.4 %collective-permute-start.2 = (bf16[416,768]{1,0:T(8,128)(2,1)}, bf16[416,768]{1,0:T(8,128)(2,1)S(1)}, u32[]{:S(2)}, u32[]{:S(2)}) collective-permute-start(bf16[416,768]{1,0:T(8,128)(2,1)} %get-tuple-element.109.refs_0_), channel_id=1, source_target_pairs={{0,1},{1,0},{2,3},{3,2},{4,5},{5,4},{6,7},{7,6},{8,9},{9,8},{10,11... | collective-permute-start | bytes 1916936 | tf_op jit(solution)/shard_map/ppermute | solution.py:848
  185.5 42.5 %collective-permute-start.3 = (bf16[416,768]{1,0:T(8,128)(2,1)}, bf16[416,768]{1,0:T(8,128)(2,1)S(1)}, u32[]{:S(2)}, u32[]{:S(2)}) collective-permute-start(bf16[416,768]{1,0:T(8,128)(2,1)} %get-tuple-element.110.refs_1_), channel_id=1, source_target_pairs={{0,1},{1,0},{2,3},{3,2},{4,5},{5,4},{6,7},{7,6},{8,9},{9,8},{10,11... | collective-permute-start | bytes 1916936 | tf_op jit(solution)/shard_map/ppermute | solution.py:848
  187.3 15.1 %collective-permute-start.4 = (f32[2,2,416]{2,1,0:T(2,128)S(1)}, f32[2,2,416]{2,1,0:T(2,128)S(1)}, u32[]{:S(2)}, u32[]{:S(2)}) collective-permute-start(f32[2,2,416]{2,1,0:T(2,128)S(1)} %pad_maximum_fusion.8), channel_id=1, source_target_pairs={{0,1},{1,0},{2,3},{3,2},{4,5},{5,4},{6,7},{7,6},{8,9},{9,8},{10,11... | collective-permute-start | bytes 19976 | tf_op jit(solution)/shard_map/ppermute | solution.py:848
  188.8 8.1 %copy-start.50 = (f32[4,768]{1,0:T(4,128)S(1)}, f32[4,768]{1,0:T(4,128)}, u32[]{:S(2)}) copy-start(f32[4,768]{1,0:T(4,128)} %param.32) | copy-start | bytes 36868
  284.8 333.9 %reduce-scatter.5.cloned.1.call-start = ((), (), s32[]{:S(2)}) async-start(), calls=%async_computation.4 | async-start | bytes 5013504 | tf_op jit(solution)/shard_map/reduce_scatter | solution.py:988
  291.9 18.4 %collective-permute-start.5 = (bf16[416,768]{1,0:T(8,128)(2,1)}, bf16[416,768]{1,0:T(8,128)(2,1)S(1)}, u32[]{:S(2)}, u32[]{:S(2)}) collective-permute-start(bf16[416,768]{1,0:T(8,128)(2,1)} %get-tuple-element.116.refs_5_), channel_id=1, source_target_pairs={{0,1},{1,0},{2,3},{3,2},{4,5},{5,4},{6,7},{7,6},{8,9},{9,8},{10,11... | collective-permute-start | bytes 1916936 | tf_op jit(solution)/shard_map/ppermute | solution.py:848
  293.4 16.9 %collective-permute-start.6 = (f32[2,8,416]{2,1,0:T(8,128)}, f32[2,8,416]{2,1,0:T(8,128)S(1)}, u32[]{:S(2)}, u32[]{:S(2)}) collective-permute-start(f32[2,8,416]{2,1,0:T(8,128)} %get-tuple-element.122), channel_id=1, source_target_pairs={{0,1},{1,0},{2,3},{3,2},{4,5},{5,4},{6,7},{7,6},{8,9},{9,8},{10,11... | collective-permute-start | bytes 79880 | tf_op jit(solution)/shard_map/ppermute | solution.py:848
  317.8 16.5 %collective-permute-start.7 = (bf16[416,768]{1,0:T(8,128)(2,1)}, bf16[416,768]{1,0:T(8,128)(2,1)S(1)}, u32[]{:S(2)}, u32[]{:S(2)}) collective-permute-start(bf16[416,768]{1,0:T(8,128)(2,1)} %get-tuple-element.124.refs_4_), channel_id=1, source_target_pairs={{0,1},{1,0},{2,3},{3,2},{4,5},{5,4},{6,7},{7,6},{8,9},{9,8},{10,11... | collective-permute-start | bytes 1916936 | tf_op jit(solution)/shard_map/ppermute | solution.py:848
  341.5 34.8 %collective-permute-start.8 = (bf16[2,416,768]{2,1,0:T(8,128)(2,1)}, bf16[2,416,768]{2,1,0:T(8,128)(2,1)}, u32[]{:S(2)}, u32[]{:S(2)}) collective-permute-start(bf16[2,416,768]{2,1,0:T(8,128)(2,1)} %get-tuple-element.130.refs_4_), channel_id=1, source_target_pairs={{0,1},{1,0},{2,3},{3,2},{4,5},{5,4},{6,7},{7,6},{8,9},{9,8},{10,11... | collective-permute-start | bytes 3833864 | tf_op jit(solution)/shard_map/ppermute | solution.py:848
  375.5 44.1 %collective-permute-start.10 = (bf16[8,2,48,1536]{3,2,1,0:T(8,128)(2,1)}, bf16[8,2,48,1536]{3,2,1,0:T(8,128)(2,1)S(1)}, u32[]{:S(2)}, u32[]{:S(2)}) collective-permute-start(bf16[8,2,48,1536]{3,2,1,0:T(8,128)(2,1)} %get-tuple-element.141.refs_8_), channel_id=1, source_target_pairs={{0,2},{2,0},{4,6},{6,4},{8,10},{10,8},{12,14},{14,12},{16,18},{18,... | collective-permute-start | bytes 7077896 | tf_op jit(solution)/shard_map/ppermute | solution.py:938
  380.2 39.4 %collective-permute-start.9 = (bf16[2,416,768]{2,1,0:T(8,128)(2,1)}, bf16[2,416,768]{2,1,0:T(8,128)(2,1)S(1)}, u32[]{:S(2)}, u32[]{:S(2)}) collective-permute-start(bf16[2,416,768]{2,1,0:T(8,128)(2,1)} %layer_output.1.refs_9_), channel_id=1, source_target_pairs={{0,1},{1,0},{2,3},{3,2},{4,5},{5,4},{6,7},{7,6},{8,9},{9,8},{10,11... | collective-permute-start | bytes 3833864 | tf_op jit(solution)/shard_map/ppermute | solution.py:848
  423.9 8.3 %collective-permute-start.11 = (bf16[8,2,48,3072]{3,2,1,0:T(8,128)(2,1)}, bf16[8,2,48,3072]{3,2,1,0:T(8,128)(2,1)}, u32[]{:S(2)}, u32[]{:S(2)}) collective-permute-start(bf16[8,2,48,3072]{3,2,1,0:T(8,128)(2,1)} %hold.2), channel_id=1, source_target_pairs={{0,2},{2,0},{4,6},{6,4},{8,10},{10,8},{12,14},{14,12},{16,18},{18,... | collective-permute-start | bytes 14155784 | tf_op jit(solution)/shard_map/ppermute | solution.py:938
  425.4 24.2 %collective-permute-start.12 = (bf16[48,1536]{1,0:T(8,128)(2,1)S(1)}, bf16[48,1536]{1,0:T(8,128)(2,1)S(1)}, u32[]{:S(2)}, u32[]{:S(2)}) collective-permute-start(bf16[48,1536]{1,0:T(8,128)(2,1)S(1)} %copy-done.10), channel_id=1, source_target_pairs={{0,8},{2,10},{8,16},{10,18},{16,24},{18,26},{24,28},{26,30},{28,20... | collective-permute-start | bytes 442376 | tf_op jit(solution)/shard_map/ppermute | solution.py:948
  426.9 22.7 %collective-permute-start.13 = (bf16[48,1536]{1,0:T(8,128)(2,1)S(1)}, bf16[48,1536]{1,0:T(8,128)(2,1)S(1)}, u32[]{:S(2)}, u32[]{:S(2)}) collective-permute-start(bf16[48,1536]{1,0:T(8,128)(2,1)S(1)} %copy-done.33), channel_id=1, source_target_pairs={{0,4},{2,6},{8,0},{10,2},{16,8},{18,10},{24,16},{26,18},{28,24},{3... | collective-permute-start | bytes 442376 | tf_op jit(solution)/shard_map/ppermute | solution.py:948
  435.0 15.3 %collective-permute-start.14 = (bf16[48,3072]{1,0:T(8,128)(2,1)}, bf16[48,3072]{1,0:T(8,128)(2,1)S(1)}, u32[]{:S(2)}, u32[]{:S(2)}) collective-permute-start(bf16[48,3072]{1,0:T(8,128)(2,1)} %get-tuple-element.151.refs_6_), channel_id=1, source_target_pairs={{0,8},{2,10},{8,16},{10,18},{16,24},{18,26},{24,28},{26,30},{28,20... | collective-permute-start | bytes 884744 | tf_op jit(solution)/shard_map/ppermute | solution.py:948
  436.4 21.8 %collective-permute-start.15 = (bf16[48,3072]{1,0:T(8,128)(2,1)}, bf16[48,3072]{1,0:T(8,128)(2,1)S(1)}, u32[]{:S(2)}, u32[]{:S(2)}) collective-permute-start(bf16[48,3072]{1,0:T(8,128)(2,1)} %get-tuple-element.152.refs_7_), channel_id=1, source_target_pairs={{0,4},{2,6},{8,0},{10,2},{16,8},{18,10},{24,16},{26,18},{28,24},{3... | collective-permute-start | bytes 884744 | tf_op jit(solution)/shard_map/ppermute | solution.py:948
  449.6 8.7 %copy-start.31 = (bf16[48,1536]{1,0:T(8,128)(2,1)}, bf16[48,1536]{1,0:T(8,128)(2,1)S(1)}, u32[]{:S(2)}) copy-start(bf16[48,1536]{1,0:T(8,128)(2,1)S(1)} %collective-permute-done.12.refs_5_) | copy-start | bytes 442372
  449.6 8.7 %copy-start.32 = (bf16[48,1536]{1,0:T(8,128)(2,1)}, bf16[48,1536]{1,0:T(8,128)(2,1)S(1)}, u32[]{:S(2)}) copy-start(bf16[48,1536]{1,0:T(8,128)(2,1)S(1)} %collective-permute-done.13.refs_6_) | copy-start | bytes 442372
  450.3 8.0 %copy-start.23 = (bf16[48,3072]{1,0:T(8,128)(2,1)}, bf16[48,3072]{1,0:T(8,128)(2,1)S(1)}, u32[]{:S(2)}) copy-start(bf16[48,3072]{1,0:T(8,128)(2,1)S(1)} %collective-permute-done.14.refs_11_) | copy-start | bytes 884740
  463.3 39.0 %collective-permute-start.18 = (bf16[2,48,3072]{2,1,0:T(8,128)(2,1)}, bf16[2,48,3072]{2,1,0:T(8,128)(2,1)S(1)}, u32[]{:S(2)}, u32[]{:S(2)}) collective-permute-start(bf16[2,48,3072]{2,1,0:T(8,128)(2,1)} %get-tuple-element.157.refs_6_), channel_id=1, source_target_pairs={{0,8},{2,10},{8,16},{10,18},{16,24},{18,26},{24,28},{26,30},{28,20... | collective-permute-start | bytes 1769480 | tf_op jit(solution)/shard_map/ppermute | solution.py:948
  464.9 37.3 %collective-permute-start.19 = (bf16[2,48,3072]{2,1,0:T(8,128)(2,1)}, bf16[2,48,3072]{2,1,0:T(8,128)(2,1)S(1)}, u32[]{:S(2)}, u32[]{:S(2)}) collective-permute-start(bf16[2,48,3072]{2,1,0:T(8,128)(2,1)} %get-tuple-element.158.refs_7_), channel_id=1, source_target_pairs={{0,4},{2,6},{8,0},{10,2},{16,8},{18,10},{24,16},{26,18},{28,24},{3... | collective-permute-start | bytes 1769480 | tf_op jit(solution)/shard_map/ppermute | solution.py:948
  465.9 34.5 %collective-permute-start.16 = (bf16[2,48,1536]{2,1,0:T(8,128)(2,1)}, bf16[2,48,1536]{2,1,0:T(8,128)(2,1)S(1)}, u32[]{:S(2)}, u32[]{:S(2)}) collective-permute-start(bf16[2,48,1536]{2,1,0:T(8,128)(2,1)} %get-tuple-element.155.refs_4_), channel_id=1, source_target_pairs={{0,8},{2,10},{8,16},{10,18},{16,24},{18,26},{24,28},{26,30},{28,20... | collective-permute-start | bytes 884744 | tf_op jit(solution)/shard_map/ppermute | solution.py:948
  467.5 34.7 %collective-permute-start.17 = (bf16[2,48,1536]{2,1,0:T(8,128)(2,1)}, bf16[2,48,1536]{2,1,0:T(8,128)(2,1)S(1)}, u32[]{:S(2)}, u32[]{:S(2)}) collective-permute-start(bf16[2,48,1536]{2,1,0:T(8,128)(2,1)} %get-tuple-element.156.refs_5_), channel_id=1, source_target_pairs={{0,4},{2,6},{8,0},{10,2},{16,8},{18,10},{24,16},{26,18},{28,24},{3... | collective-permute-start | bytes 884744 | tf_op jit(solution)/shard_map/ppermute | solution.py:948
  508.0 22.8 %collective-permute-start.21 = (bf16[2,48,1536]{2,1,0:T(8,128)(2,1)}, bf16[2,48,1536]{2,1,0:T(8,128)(2,1)S(1)}, u32[]{:S(2)}, u32[]{:S(2)}) collective-permute-start(bf16[2,48,1536]{2,1,0:T(8,128)(2,1)} %get-tuple-element.162.refs_13_), channel_id=1, source_target_pairs={{0,8},{2,10},{8,16},{10,18},{16,24},{18,26},{24,28},{26,30},{28,20... | collective-permute-start | bytes 884744 | tf_op jit(solution)/shard_map/ppermute | solution.py:948
  509.6 21.3 %collective-permute-start.22 = (bf16[2,48,1536]{2,1,0:T(8,128)(2,1)}, bf16[2,48,1536]{2,1,0:T(8,128)(2,1)S(1)}, u32[]{:S(2)}, u32[]{:S(2)}) collective-permute-start(bf16[2,48,1536]{2,1,0:T(8,128)(2,1)} %get-tuple-element.163.refs_14_), channel_id=1, source_target_pairs={{0,4},{2,6},{8,0},{10,2},{16,8},{18,10},{24,16},{26,18},{28,24},{3... | collective-permute-start | bytes 884744 | tf_op jit(solution)/shard_map/ppermute | solution.py:948
  510.0 20.8 %collective-permute-start.23 = (bf16[2,48,3072]{2,1,0:T(8,128)(2,1)}, bf16[2,48,3072]{2,1,0:T(8,128)(2,1)S(1)}, u32[]{:S(2)}, u32[]{:S(2)}) collective-permute-start(bf16[2,48,3072]{2,1,0:T(8,128)(2,1)} %get-tuple-element.164.refs_15_), channel_id=1, source_target_pairs={{0,8},{2,10},{8,16},{10,18},{16,24},{18,26},{24,28},{26,30},{28,20... | collective-permute-start | bytes 1769480 | tf_op jit(solution)/shard_map/ppermute | solution.py:948
  511.6 19.6 %collective-permute-start.24 = (bf16[2,48,3072]{2,1,0:T(8,128)(2,1)}, bf16[2,48,3072]{2,1,0:T(8,128)(2,1)S(1)}, u32[]{:S(2)}, u32[]{:S(2)}) collective-permute-start(bf16[2,48,3072]{2,1,0:T(8,128)(2,1)} %get-tuple-element.165.refs_16_), channel_id=1, source_target_pairs={{0,4},{2,6},{8,0},{10,2},{16,8},{18,10},{24,16},{26,18},{28,24},{3... | collective-permute-start | bytes 1769480 | tf_op jit(solution)/shard_map/ppermute | solution.py:948
  536.7 52.1 %collective-permute-start.20 = (bf16[832,768]{1,0:T(8,128)(2,1)}, bf16[832,768]{1,0:T(8,128)(2,1)}, u32[]{:S(2)}, u32[]{:S(2)}) collective-permute-start(bf16[832,768]{1,0:T(8,128)(2,1)} %get-tuple-element.166), channel_id=1, source_target_pairs={{0,1},{1,0},{2,3},{3,2},{4,5},{5,4},{6,7},{7,6},{8,9},{9,8},{10,11... | collective-permute-start | bytes 3833864 | tf_op jit(solution)/shard_map/ppermute | solution.py:848
  538.2 21.6 %collective-permute-start.27 = (bf16[2,48,3072]{2,1,0:T(8,128)(2,1)S(1)}, bf16[2,48,3072]{2,1,0:T(8,128)(2,1)S(1)}, u32[]{:S(2)}, u32[]{:S(2)}) collective-permute-start(bf16[2,48,3072]{2,1,0:T(8,128)(2,1)S(1)} %copy-done.57), channel_id=1, source_target_pairs={{0,8},{2,10},{8,16},{10,18},{16,24},{18,26},{24,28},{26,30},{28,20... | collective-permute-start | bytes 1769480 | tf_op jit(solution)/shard_map/ppermute | solution.py:948
  539.8 20.0 %collective-permute-start.28 = (bf16[2,48,3072]{2,1,0:T(8,128)(2,1)S(1)}, bf16[2,48,3072]{2,1,0:T(8,128)(2,1)S(1)}, u32[]{:S(2)}, u32[]{:S(2)}) collective-permute-start(bf16[2,48,3072]{2,1,0:T(8,128)(2,1)S(1)} %copy-done.56), channel_id=1, source_target_pairs={{0,4},{2,6},{8,0},{10,2},{16,8},{18,10},{24,16},{26,18},{28,24},{3... | collective-permute-start | bytes 1769480 | tf_op jit(solution)/shard_map/ppermute | solution.py:948
  542.2 1.7 collective-permute-start.29
  542.2 16.2 %collective-permute-start.25 = (bf16[2,48,1536]{2,1,0:T(8,128)(2,1)S(1)}, bf16[2,48,1536]{2,1,0:T(8,128)(2,1)S(1)}, u32[]{:S(2)}, u32[]{:S(2)}) collective-permute-start(bf16[2,48,1536]{2,1,0:T(8,128)(2,1)S(1)} %copy-done.11), channel_id=1, source_target_pairs={{0,8},{2,10},{8,16},{10,18},{16,24},{18,26},{24,28},{26,30},{28,20... | collective-permute-start | bytes 884744 | tf_op jit(solution)/shard_map/ppermute | solution.py:948
  543.8 16.0 %copy-start.34 = (f32[48,768]{1,0:T(8,128)}, f32[48,768]{1,0:T(8,128)S(1)}, u32[]{:S(2)}) copy-start(f32[48,768]{1,0:T(8,128)S(1)} %collective-permute-done.29.refs_10_) | copy-start | bytes 442372
  543.8 16.0 %collective-permute-start.26 = (bf16[2,48,1536]{2,1,0:T(8,128)(2,1)}, bf16[2,48,1536]{2,1,0:T(8,128)(2,1)S(1)}, u32[]{:S(2)}, u32[]{:S(2)}) collective-permute-start(bf16[2,48,1536]{2,1,0:T(8,128)(2,1)} %get-tuple-element.169), channel_id=1, source_target_pairs={{0,4},{2,6},{8,0},{10,2},{16,8},{18,10},{24,16},{26,18},{28,24},{3... | collective-permute-start | bytes 884744 | tf_op jit(solution)/shard_map/ppermute | solution.py:948
  544.3 20.8 %copy-start.48 = (s32[2]{0:T(128)}, s32[2]{0:T(128)S(1)}, u32[]{:S(2)}) copy-start(s32[2]{0:T(128)S(1)} %broadcast_2_refs_0_.2.refs_0_) | copy-start | bytes 28
  565.1 8.4 %collective-permute-start.30 = (f32[48,768]{1,0:T(8,128)}, f32[48,768]{1,0:T(8,128)S(1)}, u32[]{:S(2)}, u32[]{:S(2)}) collective-permute-start(f32[48,768]{1,0:T(8,128)} %get-tuple-element.191.refs_1_), channel_id=1, source_target_pairs={{0,4},{2,6},{4,0},{6,2},{8,12},{10,14},{12,8},{14,10},{16,20},{18,... | collective-permute-start | bytes 442376 | tf_op jit(solution)/shard_map/ppermute | solution.py:1033
  568.2 18.2 %copy-start.1 = (bf16[2,4,197,768]{3,2,1,0:T(8,128)(2,1)S(1)}, bf16[2,4,197,768]{3,2,1,0:T(8,128)(2,1)}, u32[]{:S(2)}) copy-start(bf16[2,4,197,768]{3,2,1,0:T(8,128)(2,1)} %place.2.refs_3_.refs_8_) | copy-start | bytes 7262212
  568.2 35.7 %collective-permute-start.35 = (bf16[3,48,1536]{2,1,0:T(8,128)(2,1)S(1)}, bf16[3,48,1536]{2,1,0:T(8,128)(2,1)S(1)}, u32[]{:S(2)}, u32[]{:S(2)}) collective-permute-start(bf16[3,48,1536]{2,1,0:T(8,128)(2,1)S(1)} %fusion.5), channel_id=1, source_target_pairs={{0,1},{1,0},{2,3},{3,2},{4,5},{5,4},{6,7},{7,6},{8,9},{9,8},{10,11... | collective-permute-start | bytes 1327112 | tf_op jit(solution)/shard_map/ppermute | solution.py:848
  576.4 6.0 collective-permute-start.31
  585.4 13.9 %collective-permute-start.32 = (f32[48,768]{1,0:T(8,128)}, f32[48,768]{1,0:T(8,128)S(1)}, u32[]{:S(2)}, u32[]{:S(2)}) collective-permute-start(f32[48,768]{1,0:T(8,128)} %ring_add.17.refs_3_.refs_1_), channel_id=1, source_target_pairs={{0,16},{2,18},{4,20},{6,22},{8,24},{10,26},{12,28},{14,30},{16,0},... | collective-permute-start | bytes 442376 | tf_op jit(solution)/shard_map/ppermute | solution.py:1033
  602.3 5.4 collective-permute-start.33
  619.8 6.0 collective-permute-start.34
  (50 other events, 87.9 us)
Sparse Core Ops, SparseCore 0:
  26.4 100.4 all-gather.5
  129.0 98.9 all-gather.3
  284.9 213.6 reduce-scatter.2
  536.8 81.9 reduce-scatter.4
